TPU v7x, 32 devices: a whole 2x2x4 slice. The times are simulated.
32 devices in a mesh: scene: 2 (over y), brick: 4 (over z), chan: 2 (over x), rep: 2 (over core).
Axes of the slice: x: 2, y: 2, z: 4, core: 2. Of those that a mesh axis runs over, the one named last changes fastest.
Arguments:
- features: bfloat16 [128, 73728], P('chan', ('scene', 'brick', 'rep')), parts along dimension 1, may hold values from -6 to 6
- conv_weight: bfloat16 [27, 128, 128], P(None, None, 'chan'), may hold values from -0.109375 to 0.109375
- neighbours: int32 [27, 73728], P(None, ('scene', 'brick', 'rep')), parts along dimension 1, may hold values from -1 to 36863, as said below
- cotangent: bfloat16 [128, 73728], P('chan', ('scene', 'brick', 'rep')), parts along dimension 1, may hold values from -6 to 6
Outputs:
- output: bfloat16 [128, 73728], P('chan', ('scene', 'brick', 'rep')), parts along dimension 1
- grad_features: bfloat16 [128, 73728], P('chan', ('scene', 'brick', 'rep')), parts along dimension 1
- grad_weight: float32 [54, 128, 128], P('scene', None, 'chan'), parts along dimension 0
There are 2 independent parts, one for each index of `scene`. A program takes and returns all parts, laid end to end along the dimension named above; an argument that names none is the same for every part. Nothing has to cross between parts.
Inputs may be any that keep to these rules, and one draw needn't show every extreme that they name: Each entry neighbours[k, s] is -1 or s + (k // 9 - 1) * 256 + (k // 3 % 3 - 1) * 16 + (k % 3 - 1), the site beside s at that offset on a column of 16 x 16 cross-sections; neighbours[26 - k, neighbours[k, s]] = s wherever neighbours[k, s] >= 0; neighbours[13, s] is s or -1.
All inputs are finite; a program needn't handle non-finite values.
Results may differ from a plain program's by a relative error of at most 0.0065.
Values may be sent and summed in bfloat16 or wider, within the bound.
No kernel may reach another device: no remote copies, remote signals or barrier semaphores. Data moves between devices by JAX's collectives and lax.ppermute only.
A program may use at most 64 MiB of HBM per device.

v0:
```python
import jax
import jax.numpy as jnp
from jax import lax
from jax.sharding import PartitionSpec as P

EDGE = 16
TAPS = 27


def extended_2(cells, sides, width):
    for axis, dim in sides:
        count = lax.axis_size(axis)
        ends = count - 1
        head = lax.slice_in_dim(cells, 0, width, axis=dim)
        tail = lax.slice_in_dim(cells, cells.shape[dim] - width, cells.shape[dim], axis=dim)
        cells = jnp.concatenate(
            [
                lax.ppermute(tail, axis, [(i, (i + 1) % count) for i in range(ends)]),
                cells,
                lax.ppermute(head, axis, [((i + 1) % count, i) for i in range(ends)]),
            ],
            axis=dim,
        )
    return cells


def tap_shift(offset):
    return (offset // 9 - 1) * EDGE * EDGE + (offset // 3 % 3 - 1) * EDGE + (offset % 3 - 1)


def shifted(extended, width, sites_here, offset, valid_row):
    begin = width + tap_shift(offset)
    piece = extended[:, begin : begin + sites_here]
    return jnp.where(valid_row[None, :], piece, jnp.zeros((), extended.dtype))


def local(features, conv_weight, neighbours, cotangent):
    sites_here = features.shape[1]
    share = features.shape[0]
    valid = neighbours >= 0
    full_here = lax.all_gather(features, "chan", axis=0, tiled=True)
    extended = extended_2(full_here, ((("brick", "rep"), 1),), sites_here)
    hidden = jnp.zeros((share, sites_here), jnp.float32)
    for offset in range(TAPS):
        gathered = shifted(extended, sites_here, sites_here, offset, valid[offset])
        hidden = hidden + lax.dot_general(
            conv_weight[offset],
            gathered,
            (((0,), (0,)), ((), ())),
            preferred_element_type=jnp.float32,
        )
    output = (features.astype(jnp.float32) + jax.nn.silu(hidden)).astype(jnp.bfloat16)
    sigma = jax.nn.sigmoid(hidden)
    grad_hidden = (cotangent.astype(jnp.float32) * sigma * (1.0 + hidden * (1.0 - sigma))).astype(
        jnp.bfloat16
    )
    grad_extended = extended_2(grad_hidden, ((("brick", "rep"), 1),), sites_here)
    reversed_rows = jnp.stack(
        [
            shifted(
                grad_extended, sites_here, sites_here, TAPS - 1 - offset, valid[TAPS - 1 - offset]
            )
            for offset in range(TAPS)
        ],
        axis=0,
    )
    stacked = reversed_rows.reshape(TAPS * share, sites_here)
    weight_stack = jnp.transpose(conv_weight, (1, 0, 2)).reshape(conv_weight.shape[1], TAPS * share)
    grad_conv = lax.psum_scatter(
        jnp.dot(weight_stack, stacked, preferred_element_type=jnp.float32).astype(jnp.bfloat16),
        "chan",
        scatter_dimension=0,
        tiled=True,
    ).astype(jnp.float32)
    weight_terms = lax.dot_general(
        full_here, stacked, (((1,), (1,)), ((), ())), preferred_element_type=jnp.float32
    )
    weight_terms = jnp.transpose(weight_terms.reshape(conv_weight.shape[1], TAPS, share), (1, 0, 2))
    grad_features = (cotangent.astype(jnp.float32) + grad_conv).astype(jnp.bfloat16)
    grad_weight = lax.psum(weight_terms, ("brick", "rep"))
    return (output, grad_features, grad_weight)


def solution(mesh):
    return jax.shard_map(
        local,
        mesh=mesh,
        in_specs=(
            P("chan", ("scene", "brick", "rep")),
            P(None, None, "chan"),
            P(None, ("scene", "brick", "rep")),
            P("chan", ("scene", "brick", "rep")),
        ),
        out_specs=(
            P("chan", ("scene", "brick", "rep")),
            P("chan", ("scene", "brick", "rep")),
            P("scene", None, "chan"),
        ),
        check_vma=False,
    )
```

profile of v0, /device:TPU:0, one launch (start us, length us, event | category | flops | bytes accessed | tf_op | source)
XLA Modules:
  0.0 194.6 jit_solution(2604356106981183995)
XLA Ops:
  7.2 0.7 all-gather.2.cloned.1.call-update
  7.9 27.1 %all-gather.2.cloned.1.call-done = bf16[128,4608]{1,0:T(8,128)(2,1)} async-done(((bf16[64,4608]{1,0:T(8,128)(2,1)}), bf16[128,4608]{1,0:T(8,128)(2,1)}) %all-gather.2.cloned.1.call-update) | async-done | bytes 1179664 | tf_op jit(solution)/shard_map/all_gather | solution.py:41
  35.1 1.9 collective-permute-start
  37.0 1.1 broadcast_compare_fusion
  38.1 0.4 slice_reduce_fusion.19
  38.5 1.0 slice_reduce_fusion
  39.6 1.3 collective-permute-start.1
  41.2 4.3 %collective-permute-done.1 = bf16[128,4608]{1,0:T(8,128)(2,1)S(1)} collective-permute-done((bf16[128,4608]{1,0:T(8,128)(2,1)S(1)}, bf16[128,4608]{1,0:T(8,128)(2,1)S(1)}, u32[]{:S(2)}, u32[]{:S(2)}) %collective-permute-start.1) | collective-permute-done | bytes 1179680 | tf_op jit(solution)/shard_map/ppermute | solution.py:20
  45.6 0.9 copy-done.3
  46.5 0.6 convolution_bitcast_fusion.2
  47.1 0.6 convolution_bitcast_fusion.3
  47.7 0.6 convolution_bitcast_fusion.4
  48.4 0.3 convolution_bitcast_fusion.5
  48.7 0.6 convolution_bitcast_fusion.6
  49.3 0.6 convolution_bitcast_fusion.7
  49.9 0.6 convolution_bitcast_fusion.8
  50.6 0.6 convolution_bitcast_fusion.9
  51.2 0.6 convolution_bitcast_fusion.10
  51.8 0.6 fusion.18
  52.4 0.6 fusion.19
  53.1 0.6 fusion.20
  53.7 0.6 convolution_add_fusion.13
  54.3 0.6 convolution_add_fusion.12
  55.0 0.6 convolution_add_fusion.11
  55.6 0.3 convolution_add_fusion.10
  55.9 0.6 convolution_add_fusion.9
  56.6 0.6 convolution_add_fusion.8
  57.2 0.6 convolution_add_fusion.7
  57.8 0.6 convolution_add_fusion.6
  58.5 0.6 convolution_add_fusion.5
  59.1 0.8 convolution_add_fusion.4
  59.9 0.6 convolution_add_fusion.3
  60.6 0.6 convolution_add_fusion.2
  61.2 0.3 convolution_add_fusion.1
  61.6 1.1 fusion.14
  62.8 1.9 fusion.16
  64.7 1.3 collective-permute-start.2
  66.0 15.8 %collective-permute-start.3 = (bf16[64,4608]{1,0:T(8,128)(2,1)S(1)}, bf16[64,4608]{1,0:T(8,128)(2,1)S(1)}, u32[]{:S(2)}, u32[]{:S(2)}) collective-permute-start(bf16[64,4608]{1,0:T(8,128)(2,1)S(1)} %get-tuple-element.30), channel_id=1, source_target_pairs={{0,1},{1,4},{4,5},{5,8},{8,9},{9,12},{12,13},{2,3},{3,6},{6,7},{7,... | collective-permute-start | bytes 1769480 | tf_op jit(solution)/shard_map/ppermute | solution.py:18
  84.0 0.3 fusion.140
  84.2 0.3 fusion.144
  84.5 0.3 fusion.100
  88.3 5.6 %copy-done.4 = bf16[27,64,4608]{2,1,0:T(8,128)(2,1)} copy-done((bf16[27,64,4608]{2,1,0:T(8,128)(2,1)}, bf16[27,64,4608]{2,1,0:T(8,128)(2,1)S(1)}, u32[]{:S(2)}) %copy-start.4) | copy-done | bytes 15925272
  93.9 3.4 %fusion.12 = bf16[128,4608]{1,0:T(8,128)(2,1)} fusion(bf16[27,64,4608]{2,1,0:T(8,128)(2,1)S(1)} %fusion.147, bf16[27,128,64]{1,2,0:T(8,128)(2,1)S(1)} %copy-done.3), kind=kOutput, calls=%fused_computation.37 | convolution fusion | flops 2039021568 | bytes 17547264 | tf_op jit(solution)/shard_map/dot_general | solution.py:70
  97.3 8.7 %fusion.260 = f32[1728,128]{1,0:T(8,128)} fusion(bf16[1728,4608]{1,0:T(8,128)(2,1)} %bitcast.252, bf16[128,4608]{1,0:T(8,128)(2,1)S(1)} %copy-done), kind=kOutput, calls=%fused_computation.398 | convolution fusion | flops 2038431744 | bytes 17989632 | tf_op jit(solution)/shard_map/dot_general | solution.py:75
  106.1 19.5 %reduce-scatter.2.cloned.1.call-done = bf16[64,4608]{1,0:T(8,128)(2,1)} async-done(((bf16[128,4608]{1,0:T(8,128)(2,1)}), bf16[64,4608]{1,0:T(8,128)(2,1)}) %reduce-scatter.2.cloned.1.call-update) | async-done | bytes 589840 | tf_op jit(solution)/shard_map/reduce_scatter | solution.py:69
  125.5 2.0 %fusion.17 = bf16[64,4608]{1,0:T(8,128)(2,1)} fusion(bf16[64,4608]{1,0:T(8,128)(2,1)S(1)} %copy-done.1, bf16[64,4608]{1,0:T(8,128)(2,1)} %reduce-scatter.2.cloned.1.call-done), kind=kLoop, calls=%fused_computation.92 | loop fusion | flops 1179648 | bytes 1769472 | tf_op jit(solution)/shard_map/convert_element_type | solution.py:79
  127.6 58.4 %all-reduce.2.cloned.1.call-done = f32[27,128,64]{1,2,0:T(8,128)} async-done(((f32[27,128,64]{1,2,0:T(8,128)}), f32[27,128,64]{1,2,0:T(8,128)}) %all-reduce.2.cloned.1.call-update) | async-done | bytes 884752 | tf_op jit(solution)/shard_map/psum | solution.py:80
  185.9 2.2 %copy.39 = f32[27,128,64]{1,2,0:T(8,128)} copy(f32[27,128,64]{1,2,0:T(8,128)} %all-reduce.2.cloned.1.call-done) | data formatting | bytes 1769472
  (43 shorter events, 6.3 us)
Async XLA Ops:
  7.2 27.9 %all-gather.2.cloned.1.call-start = ((), (), s32[]{:S(2)}) async-start(), calls=%async_computation.1 | async-start | bytes 1769472 | tf_op jit(solution)/shard_map/all_gather | solution.py:41
  7.9 117.6 %reduce-scatter.2.cloned.1.call-start = ((), (), s32[]{:S(2)}) async-start(), calls=%async_computation.2 | async-start | bytes 1769472 | tf_op jit(solution)/shard_map/reduce_scatter | solution.py:69
  35.0 4.5 %copy-start = (bf16[128,4608]{1,0:T(8,128)(2,1)S(1)}, bf16[128,4608]{1,0:T(8,128)(2,1)}, u32[]{:S(2)}) copy-start(bf16[128,4608]{1,0:T(8,128)(2,1)} %all-gather.2.cloned.1.call-done) | copy-start | bytes 3538948
  35.1 5.8 %collective-permute-start = (bf16[128,4608]{1,0:T(8,128)(2,1)}, bf16[128,4608]{1,0:T(8,128)(2,1)S(1)}, u32[]{:S(2)}, u32[]{:S(2)}) collective-permute-start(bf16[128,4608]{1,0:T(8,128)(2,1)} %all-gather.2.cloned.1.call-done), channel_id=1, source_target_pairs={{0,1},{1,4},{4,5},{5,8},{8,9},{9,12},{12,13},{2,3},{3,6},{6,7},{7,... | collective-permute-start | bytes 3538952 | tf_op jit(solution)/shard_map/ppermute | solution.py:18
  39.6 5.9 %collective-permute-start.1 = (bf16[128,4608]{1,0:T(8,128)(2,1)S(1)}, bf16[128,4608]{1,0:T(8,128)(2,1)S(1)}, u32[]{:S(2)}, u32[]{:S(2)}) collective-permute-start(bf16[128,4608]{1,0:T(8,128)(2,1)S(1)} %copy-done), channel_id=1, source_target_pairs={{1,0},{4,1},{5,4},{8,5},{9,8},{12,9},{13,12},{3,2},{6,3},{7,6},{10... | collective-permute-start | bytes 3538952 | tf_op jit(solution)/shard_map/ppermute | solution.py:20
  45.5 1.0 copy-start.3
  61.5 1.1 copy-start.1
  61.5 1.2 copy-start.2
  64.7 17.1 %collective-permute-start.2 = (bf16[64,4608]{1,0:T(8,128)(2,1)S(1)}, bf16[64,4608]{1,0:T(8,128)(2,1)S(1)}, u32[]{:S(2)}, u32[]{:S(2)}) collective-permute-start(bf16[64,4608]{1,0:T(8,128)(2,1)S(1)} %get-tuple-element.30), channel_id=1, source_target_pairs={{1,0},{4,1},{5,4},{8,5},{9,8},{12,9},{13,12},{3,2},{6,3},{7,6},{10... | collective-permute-start | bytes 1769480 | tf_op jit(solution)/shard_map/ppermute | solution.py:20
  66.0 19.2 %collective-permute-start.3 = (bf16[64,4608]{1,0:T(8,128)(2,1)S(1)}, bf16[64,4608]{1,0:T(8,128)(2,1)S(1)}, u32[]{:S(2)}, u32[]{:S(2)}) collective-permute-start(bf16[64,4608]{1,0:T(8,128)(2,1)S(1)} %get-tuple-element.30), channel_id=1, source_target_pairs={{0,1},{1,4},{4,5},{5,8},{8,9},{9,12},{12,13},{2,3},{3,6},{6,7},{7,... | collective-permute-start | bytes 1769480 | tf_op jit(solution)/shard_map/ppermute | solution.py:18
  88.3 5.6 %copy-start.4 = (bf16[27,64,4608]{2,1,0:T(8,128)(2,1)}, bf16[27,64,4608]{2,1,0:T(8,128)(2,1)S(1)}, u32[]{:S(2)}) copy-start(bf16[27,64,4608]{2,1,0:T(8,128)(2,1)S(1)} %fusion.147) | copy-start | bytes 47775748
  97.3 88.6 %all-reduce.2.cloned.1.call-start = ((), (), s32[]{:S(2)}) async-start(), calls=%async_computation.3 | async-start | bytes 1769472 | tf_op jit(solution)/shard_map/psum | solution.py:80
Sparse Core Ops, SparseCore 0:
  9.5 25.4 all-gather.1
  97.4 28.0 reduce-scatter.1
  128.6 57.2 all-reduce.1
where the time goes:
time: 195 us
  waiting for transfers between devices  110 us (56%)
  matrix products  29.9 us (15%)
  starting transfers between devices  20.5 us (11%)
  between operations  14.2 us (7%)
  local copies, waits for them, and re-layouts  10.5 us (5%)
  other arithmetic  9.56 us (5%)
    psum x1, waiting for transfers between devices, local(): grad_weight = lax.psum(weight_terms, ('brick', 'rep'))  58.4 us
    all_gather x1, waiting for transfers between devices, local(): full_here = lax.all_gather(features, 'chan', axis=0, tiled=True)  27.1 us
    reduce_scatter x1, waiting for transfers between devices, local(): lax.psum_scatter(jnp.dot(weight_stack, stacked, preferred_element_type=jn...  19.5 us
    dot_general x27, matrix products, local(): lax.dot_general(conv_weight[offset], gathered, (((0,), (0,)), ((), ())),...  17.8 us
    ppermute x2, starting transfers between devices, extended_2(): lax.ppermute(tail, axis, [(i, (i + 1) % count) for i in range(ends)])  17.8 us
    unnamed x12, local copies, waits for them, and re-layouts  8.87 us
    dot_general x1, matrix products, local(): lax.dot_general(full_here, stacked, (((1,), (1,)), ((), ())), preferred_e...  8.69 us
    unnamed x26, other arithmetic  6.13 us
  transfers between devices with their start and end apart: 7, of which 4 were waited for; matrix products, arithmetic and copies ran while one was open for 9% of the time, Pallas kernels for 0%

commit v1 on v0

v1 whole, which is shorter than its diff:
```python
import functools

import jax
import jax.numpy as jnp
from jax import lax
from jax.experimental import pallas as pl
from jax.experimental.pallas import tpu as pltpu
from jax.sharding import PartitionSpec as P

EDGE = 16
FACE = EDGE * EDGE
TAPS = 27
HALO = 384
ROWS = 16
GROUP = 4
SITES = ("brick", "rep")
LINE = ("brick", "chan", "rep")
VMEM = 56 * 1024 * 1024

STEPS = [(k // 3 - 1) * EDGE + k % 3 - 1 for k in range(9)]


def cost(flops, moved):
    return pl.CostEstimate(flops=flops, bytes_accessed=moved, transcendentals=0)


def call(body, outs, scratch, flops, moved, name, scalars=0):
    return pl.pallas_call(
        body,
        out_shape=outs,
        grid_spec=pltpu.PrefetchScalarGridSpec(
            num_scalar_prefetch=scalars, grid=(), scratch_shapes=scratch
        ),
        compiler_params=pltpu.CompilerParams(vmem_limit_bytes=VMEM),
        cost_estimate=cost(flops, moved),
        name=name,
    )


def lay_out(left, middle, right, shifts):
    sites = middle.shape[1]
    length = sites + 2 * HALO
    for at in range(0, middle.shape[0], ROWS):
        rows = pl.ds(at, ROWS)
        shifts[4, rows, :HALO] = left[rows, :]
        shifts[4, rows, HALO : HALO + sites] = middle[rows, :]
        shifts[4, rows, HALO + sites :] = right[rows, :]
        for j, step in enumerate(STEPS):
            if j != 4:
                shifts[j, rows, 128 : length - 128] = shifts[
                    4, rows, 128 + step : length - 128 + step
                ]


def masked(shifts, valid, tap, mask_tap, start, width):
    channels = shifts.shape[1]
    row = valid[pl.ds(mask_tap, 1), pl.ds(start, width)]
    keep = jnp.broadcast_to((row >= 0).astype(jnp.float32), (ROWS, width)).astype(jnp.bfloat16)
    begin = pl.multiple_of(start + HALO + (tap // 9 - 1) * FACE, 128)
    return [
        shifts[tap % 9, at : at + ROWS, pl.ds(begin, width)] * keep
        for at in range(0, channels, ROWS)
    ]


def forward(width, left, middle, right, weights, valid, shifts, start):
    channels = middle.shape[0]
    total = None
    for first in range(0, TAPS, GROUP):
        last = min(first + GROUP, TAPS)
        rows = []
        for tap in range(first, last):
            rows += masked(shifts, valid, tap, tap, start, width)
        part = jnp.dot(
            weights[:, first * channels : last * channels],
            jnp.concatenate(rows, axis=0),
            preferred_element_type=jnp.float32,
        )
        total = part if total is None else total + part
    return total


def own_body(width, left, middle, right, weights, valid, hidden, shifts):
    lay_out(left, middle, right, shifts)

    def block(j, carry):
        start = pl.multiple_of(j * width, width)
        hidden[:, pl.ds(start, width)] = forward(
            width, left, middle, right, weights, valid, shifts, start
        )
        return carry

    lax.fori_loop(0, middle.shape[1] // width, block, 0)


def rest_body(
    width, left, middle, right, weights, valid, begun, features, cotangent, output, grad, first, last, shifts
):
    lay_out(left, middle, right, shifts)

    def block(j, carry):
        start = pl.multiple_of(j * width, width)
        here = pl.ds(start, width)
        hidden = begun[:, here] + forward(width, left, middle, right, weights, valid, shifts, start)
        sigma = jax.nn.sigmoid(hidden)
        output[:, here] = (features[:, here].astype(jnp.float32) + hidden * sigma).astype(jnp.bfloat16)
        grad[:, here] = (
            cotangent[:, here].astype(jnp.float32) * sigma * (1.0 + hidden * (1.0 - sigma))
        ).astype(jnp.bfloat16)
        return carry

    lax.fori_loop(0, middle.shape[1] // width, block, 0)
    first[...] = grad[:, :HALO]
    last[...] = grad[:, grad.shape[1] - HALO :]


def weight_body(
    width, half, rep, left, middle, right, valid, own, rest, kept, sent, shifts, total
):
    lay_out(left, middle, right, shifts)
    share = middle.shape[0]
    total[...] = jnp.zeros_like(total)

    def block(j, carry):
        start = pl.multiple_of(j * width, width)
        here = pl.ds(start, width)
        features = jnp.concatenate([own[:, here], rest[:, here]], axis=0)
        for first in range(0, TAPS, GROUP):
            last = min(first + GROUP, TAPS)
            rows = []
            for tap in range(first, last):
                rows += masked(shifts, valid, TAPS - 1 - tap, TAPS - 1 - tap, start, width)
            total[first * share : last * share, :] += lax.dot_general(
                jnp.concatenate(rows, axis=0),
                features,
                (((1,), (1,)), ((), ())),
                preferred_element_type=jnp.float32,
            )
        return carry

    lax.fori_loop(0, middle.shape[1] // width, block, 0)
    mine = rep[0]
    kept[...] = total[pl.ds(pl.multiple_of(mine * half, ROWS), half), :]
    sent[...] = total[pl.ds(pl.multiple_of((1 - mine) * half, ROWS), half), :].astype(jnp.bfloat16)


def feature_body(width, left, middle, right, valid, weights, own, rest, shifts):
    lay_out(left, middle, right, shifts)
    share = middle.shape[0]

    def block(j, carry):
        start = pl.multiple_of(j * width, width)
        here = pl.ds(start, width)
        total = None
        for first in range(0, TAPS, GROUP):
            last = min(first + GROUP, TAPS)
            rows = []
            for tap in range(first, last):
                rows += masked(shifts, valid, TAPS - 1 - tap, TAPS - 1 - tap, start, width)
            part = jnp.dot(
                weights[:, first * share : last * share],
                jnp.concatenate(rows, axis=0),
                preferred_element_type=jnp.float32,
            )
            total = part if total is None else total + part
        own[:, here] = total[:share]
        rest[:, here] = total[share:].astype(jnp.bfloat16)
        return carry

    lax.fori_loop(0, middle.shape[1] // width, block, 0)


def split_body(bricks, brick, kept, arrived, mine, *pieces):
    size = mine.shape[0]
    for d in range(bricks):
        rows = pl.ds(pl.multiple_of((brick[0] + d) % bricks * size, ROWS), size)
        summed = kept[rows, :] + arrived[rows, :].astype(jnp.float32)
        if d == 0:
            mine[...] = summed
        else:
            pieces[d - 1][...] = summed.astype(jnp.bfloat16)


def merge_body(mine, *rest):
    *pieces, done = rest
    total = mine[...]
    for piece in pieces:
        total += piece[...].astype(jnp.float32)
    done[...] = total.astype(jnp.bfloat16)


def gather_body(bricks, brick, *rest):
    *pieces, side = rest
    size = pieces[0].shape[0]
    for d, piece in enumerate(pieces):
        at = (brick[0] + bricks - d) % bricks * size
        side[pl.ds(pl.multiple_of(at, ROWS), size), :] = piece[...]


def join_body(half, rep, turn, side, other, out, both):
    mine = rep[0]
    both[pl.ds(pl.multiple_of(mine * half, ROWS), half), :] = side[...]
    both[pl.ds(pl.multiple_of((1 - mine) * half, ROWS), half), :] = other[...]
    out[...] = pltpu.roll(both[: out.shape[0], :].astype(jnp.float32), turn[0], 1)


def hop(x, step, over):
    bricks, chans, reps = (lax.axis_size(axis) for axis in LINE)
    pairs = []
    for at in range(bricks * reps):
        to = at + step
        if not 0 <= to < bricks * reps:
            continue
        for chan in range(chans):
            pairs.append(
                (
                    (at // reps * chans + (chan + over) % chans) * reps + at % reps,
                    (to // reps * chans + chan) * reps + to % reps,
                )
            )
    return lax.ppermute(x, LINE, pairs)


def local(features, conv_weight, neighbours, cotangent):
    share, sites = features.shape
    total = conv_weight.shape[1]
    chans, bricks, reps = (lax.axis_size(axis) for axis in ("chan", "brick", "rep"))
    chan, brick, rep = (lax.axis_index(axis) for axis in ("chan", "brick", "rep"))
    width = 512
    f32, bf16 = jnp.float32, jnp.bfloat16
    shape = jax.ShapeDtypeStruct
    length = sites + 2 * HALO
    flops = 2 * TAPS * share * sites

    others = [
        lax.ppermute(features, "chan", [((i + over) % chans, i) for i in range(chans)])
        for over in range(1, chans)
    ]
    head, tail = features[:, :HALO], features[:, sites - HALO :]
    lefts = [hop(tail, 1, over) for over in range(chans)]
    rights = [hop(head, -1, over) for over in range(chans)]
    rest = jnp.concatenate(others, axis=0)
    rest_left = jnp.concatenate(lefts[1:], axis=0)
    rest_right = jnp.concatenate(rights[1:], axis=0)

    ring = lax.dynamic_slice_in_dim(
        jnp.concatenate([conv_weight, conv_weight], axis=1), chan * share, total, axis=1
    )
    by_out = jnp.transpose(ring, (2, 0, 1))
    own_weights = by_out[:, :, :share].reshape(share, TAPS * share)
    rest_weights = by_out[:, :, share:].reshape(share, TAPS * (total - share))
    by_in = jnp.transpose(ring, (1, 0, 2)).reshape(total, TAPS * share)

    begun = call(
        functools.partial(own_body, width),
        shape((share, sites), f32),
        [pltpu.VMEM((9, share, length), bf16)],
        flops * share,
        4 * share * sites,
        "forward_own",
    )(lefts[0], features, rights[0], own_weights, neighbours)
    output, grad, first, last = call(
        functools.partial(rest_body, width),
        (
            shape((share, sites), bf16),
            shape((share, sites), bf16),
            shape((share, HALO), bf16),
            shape((share, HALO), bf16),
        ),
        [pltpu.VMEM((9, total - share, length), bf16)],
        flops * (total - share),
        4 * share * sites,
        "forward_rest",
    )(rest_left, rest, rest_right, rest_weights, neighbours, begun, features, cotangent)

    grad_left, grad_right = hop(last, 1, 0), hop(first, -1, 0)

    piece = -(-TAPS * share // (reps * bricks * ROWS)) * ROWS
    half = piece * bricks
    kept, sent = call(
        functools.partial(weight_body, width, half),
        (shape((half, total), f32), shape((half, total), bf16)),
        [pltpu.VMEM((9, share, length), bf16), pltpu.VMEM((reps * half, total), f32)],
        flops * total,
        4 * share * sites,
        "grad_weight",
        scalars=1,
    )(rep[None], grad_left, grad, grad_right, neighbours, features, rest)
    swap = [(0, 1), (1, 0)]
    arrived = lax.ppermute(sent, "rep", swap)

    own_part, rest_part = call(
        functools.partial(feature_body, width),
        (shape((share, sites), f32), shape((total - share, sites), bf16)),
        [pltpu.VMEM((9, share, length), bf16)],
        flops * total,
        4 * share * sites,
        "grad_features",
    )(grad_left, grad, grad_right, neighbours, by_in)
    terms = [
        lax.ppermute(
            rest_part[(over - 1) * share : over * share],
            "chan",
            [(i, (i + over) % chans) for i in range(chans)],
        )
        for over in range(1, chans)
    ]

    mine, *pieces = call(
        functools.partial(split_body, bricks),
        (shape((piece, total), f32),) + (shape((piece, total), bf16),) * (bricks - 1),
        [],
        0,
        6 * half * total,
        "split",
        scalars=1,
    )(brick[None], kept, arrived)
    turns = [[(i, (i + d) % bricks) for i in range(bricks)] for d in range(1, bricks)]
    pieces = [lax.ppermute(x, "brick", turn) for x, turn in zip(pieces, turns)]
    done = call(
        merge_body,
        shape((piece, total), bf16),
        [],
        0,
        2 * half * total,
        "merge",
    )(mine, *pieces)
    pieces = [done] + [lax.ppermute(done, "brick", turn) for turn in turns]
    side = call(
        functools.partial(gather_body, bricks),
        shape((half, total), bf16),
        [],
        0,
        4 * half * total,
        "gather",
        scalars=1,
    )(brick[None], *pieces)
    other = lax.ppermute(side, "rep", swap)
    grad_weight = call(
        functools.partial(join_body, half),
        shape((TAPS * share, total), f32),
        [pltpu.VMEM((reps * half, total), bf16)],
        0,
        12 * half * total,
        "join",
        scalars=2,
    )(rep[None], (chan * share)[None], side, other)

    grad_features = cotangent.astype(f32) + own_part
    for term in terms:
        grad_features = grad_features + term.astype(f32)
    grad_weight = jnp.transpose(grad_weight.reshape(TAPS, share, total), (0, 2, 1))
    return output, grad_features.astype(bf16), grad_weight


def solution(mesh):
    return jax.shard_map(
        local,
        mesh=mesh,
        in_specs=(
            P("chan", ("scene", "brick", "rep")),
            P(None, None, "chan"),
            P(None, ("scene", "brick", "rep")),
            P("chan", ("scene", "brick", "rep")),
        ),
        out_specs=(
            P("chan", ("scene", "brick", "rep")),
            P("chan", ("scene", "brick", "rep")),
            P("scene", None, "chan"),
        ),
        check_vma=False,
    )
```

time: 195 us -> 99.7 us (0.51)
  waiting for transfers between devices: 110 us -> 12.7 us
  Pallas kernels: 0 us -> 41.8 us
  matrix products: 29.9 us -> 0 us
  between operations: 14.2 us -> 0.79 us
  starting transfers between devices: 20.5 us -> 29.7 us
  other arithmetic: 9.56 us -> 3.05 us
    psum x1 -> x0, waiting for transfers between devices: 58.4 us -> none  [local(): grad_weight = lax.psum(weight_terms, ('brick', 'rep'))]
    pallas_call x0 -> x8, Pallas kernels: none -> 41.8 us  [the longest x1 9.89 us: local(): call(functools.partial(weight_body, width, half), (shape((half, total), f...]
    dot_general x29 -> x0, matrix products: 29.9 us -> none  [the longest x27 17.8 us: local(): lax.dot_general(conv_weight[offset], gathered, (((0,), (0,)), ((), ())),...]
    all_gather x1 -> x0, waiting for transfers between devices: 27.1 us -> none  [local(): full_here = lax.all_gather(features, 'chan', axis=0, tiled=True)]
    reduce_scatter x1 -> x0, waiting for transfers between devices: 19.5 us -> none  [local(): lax.psum_scatter(jnp.dot(weight_stack, stacked, preferred_element_type=jn...]
    ppermute x4 -> x16, starting transfers between devices: 20.4 us -> 29.7 us  [the longest x6 14.1 us: hop(): return lax.ppermute(x, LINE, pairs)]
    ppermute x4 -> x16, waiting for transfers between devices: 4.33 us -> 12.7 us  [the longest x3 4.57 us: local(): pieces = [done] + [lax.ppermute(done, 'brick', turn) for turn in turns]]
    unnamed x26 -> x0, other arithmetic: 6.13 us -> none
  transfers between devices with their start and end apart: 7 -> 16, of which waited for: 4 -> 8; matrix products, arithmetic and copies ran while one was open for 9% -> 7% of each run, Pallas kernels for 0% -> 25%
where the time goes in v1:
time: 99.7 us; the launch traced here: 99.1 us
  Pallas kernels  41.8 us (42%)
  starting transfers between devices  29.7 us (30%)
  waiting for transfers between devices  12.7 us (13%)
  local copies, waits for them, and re-layouts  11.1 us (11%)
  other arithmetic  3.05 us (3%)
    ppermute x6, starting transfers between devices, hop(): return lax.ppermute(x, LINE, pairs)  14.1 us
    pallas_call x1, Pallas kernels, local(): call(functools.partial(weight_body, width, half), (shape((half, total), f...  9.89 us
    pallas_call x1, Pallas kernels, local(): call(functools.partial(rest_body, width), (shape((share, sites), bf16), s...  8.93 us
    pallas_call x1, Pallas kernels, local(): call(functools.partial(feature_body, width), (shape((share, sites), f32),...  7.94 us
    pallas_call x1, Pallas kernels, local(): call(functools.partial(own_body, width), shape((share, sites), f32), [plt...  7.82 us
    unnamed x36, local copies, waits for them, and re-layouts  6.25 us
    ppermute x3, starting transfers between devices, local(): pieces = [lax.ppermute(x, 'brick', turn) for x, turn in zip(pieces, turns)]  5.57 us
    ppermute x3, waiting for transfers between devices, local(): pieces = [done] + [lax.ppermute(done, 'brick', turn) for turn in turns]  4.57 us
  transfers between devices with their start and end apart: 16, of which 8 were waited for; matrix products, arithmetic and copies ran while one was open for 7% of the time, Pallas kernels for 25%

profile of v1, /device:TPU:0, one launch (start us, length us, event | category | flops | bytes accessed | tf_op | source)
XLA Modules:
  0.0 99.1 jit_solution(6102694226697305816)
XLA Ops:
  0.6 3.0 %collective-permute-start.1 = (bf16[64,4608]{1,0:T(8,128)(2,1)}, bf16[64,4608]{1,0:T(8,128)(2,1)S(1)}, u32[]{:S(2)}, u32[]{:S(2)}) collective-permute-start(bf16[64,4608]{1,0:T(8,128)(2,1)} %own.1), channel_id=1, source_target_pairs={{2,0},{0,2},{3,1},{1,3},{6,4},{4,6},{7,5},{5,7},{10,8},{8,10},{11,... | collective-permute-start | bytes 1769480 | tf_op jit(solution)/shard_map/ppermute | solution.py:236
  3.6 0.8 fusion.1
  4.5 1.4 %collective-permute-start = (bf16[64,384]{1,0:T(8,128)(2,1)S(1)}, bf16[64,384]{1,0:T(8,128)(2,1)S(1)}, u32[]{:S(2)}, u32[]{:S(2)}) collective-permute-start(bf16[64,384]{1,0:T(8,128)(2,1)S(1)} %get-tuple-element.28), channel_id=1, source_target_pairs={{2,1},{0,3},{3,4},{1,6},{6,5},{4,7},{7,8},{5,10},{10,9},{8,11},{11... | collective-permute-start | bytes 147464 | tf_op jit(solution)/shard_map/ppermute | solution.py:221
  5.8 4.1 %collective-permute-start.3 = (bf16[64,384]{1,0:T(8,128)(2,1)S(1)}, bf16[64,384]{1,0:T(8,128)(2,1)S(1)}, u32[]{:S(2)}, u32[]{:S(2)}) collective-permute-start(bf16[64,384]{1,0:T(8,128)(2,1)S(1)} %get-tuple-element.28), channel_id=1, source_target_pairs={{0,1},{2,3},{1,4},{3,6},{4,5},{6,7},{5,8},{7,10},{8,9},{10,11},{9,... | collective-permute-start | bytes 147464 | tf_op jit(solution)/shard_map/ppermute | solution.py:221
  10.0 1.3 %collective-permute-start.2 = (bf16[64,384]{1,0:T(8,128)(2,1)S(1)}, bf16[64,384]{1,0:T(8,128)(2,1)S(1)}, u32[]{:S(2)}, u32[]{:S(2)}) collective-permute-start(bf16[64,384]{1,0:T(8,128)(2,1)S(1)} %get-tuple-element.27), channel_id=1, source_target_pairs={{3,0},{1,2},{6,1},{4,3},{7,4},{5,6},{10,5},{8,7},{11,8},{9,10},{14... | collective-permute-start | bytes 147464 | tf_op jit(solution)/shard_map/ppermute | solution.py:221
  11.3 1.3 %collective-permute-start.4 = (bf16[64,384]{1,0:T(8,128)(2,1)S(1)}, bf16[64,384]{1,0:T(8,128)(2,1)S(1)}, u32[]{:S(2)}, u32[]{:S(2)}) collective-permute-start(bf16[64,384]{1,0:T(8,128)(2,1)S(1)} %get-tuple-element.27), channel_id=1, source_target_pairs={{1,0},{3,2},{4,1},{6,3},{5,4},{7,6},{8,5},{10,7},{9,8},{11,10},{12... | collective-permute-start | bytes 147464 | tf_op jit(solution)/shard_map/ppermute | solution.py:221
  12.6 1.7 %fusion.3 = bf16[64,27,128]{2,0,1:T(8,128)(2,1)S(1)} fusion(s32[]{:T(128)S(6)} %select_n.3, bf16[27,128,64]{1,2,0:T(8,128)(2,1)} %param.5), kind=kLoop, calls=%fused_computation.6 | loop fusion | flops 884736 | bytes 884740 | tf_op jit(solution)/shard_map/transpose | solution.py:249
  14.5 0.3 copy.10
  14.8 1.1 %reshape.18.weights = bf16[64,1728]{1,0:T(8,128)(2,1)} reshape(bf16[64,27,64]{2,1,0:T(8,128)(2,1)S(1)} %copy.10) | data formatting | bytes 442368 | tf_op jit(solution)/shard_map/reshape | solution.py:251
  16.2 1.1 %reshape.19.weights = bf16[64,1728]{1,0:T(8,128)(2,1)} reshape(bf16[64,27,64]{2,1,0:T(8,128)(2,1)S(1)} %copy.11) | data formatting | bytes 442368 | tf_op jit(solution)/shard_map/reshape | solution.py:250
  17.3 0.6 copy-done.14
  17.9 0.6 copy-done.15
  18.5 7.8 %forward_own.1.begun = f32[64,4608]{1,0:T(8,128)} custom-call(bf16[64,384]{1,0:T(8,128)(2,1)} %copy-done.14, bf16[64,4608]{1,0:T(8,128)(2,1)} %own.1, bf16[64,384]{1,0:T(8,128)(2,1)} %copy-done.15, bf16[64,1728]{1,0:T(8,128)(2,1)} %reshape.19.weights, s32[27,4608]{1,0:T(8,128)} %valid.7), custom_call_target="tpu_custom_call" | custom-call | flops 1019215872 | bytes 1179648 | tf_op jit(solution)/shard_map/forward_own/pallas_call | solution.py:254
  26.4 0.6 copy-done.12
  27.0 0.8 copy-done.3
  27.8 8.9 %forward_rest.1 = (bf16[64,4608]{1,0:T(8,128)(2,1)}, bf16[64,4608]{1,0:T(8,128)(2,1)}, bf16[64,384]{1,0:T(8,128)(2,1)}, bf16[64,384]{1,0:T(8,128)(2,1)}) custom-call(bf16[64,384]{1,0:T(8,128)(2,1)} %copy-done.12, bf16[64,4608]{1,0:T(8,128)(2,1)} %copy-done.3, bf16[64,384]{1,0:T(8,128)(2,1)} %copy-done.13, bf16[64,1728]{1,0:T(8,128)(2,1)} %reshape.18.weights, ...), custom_call_target="tpu_custom_call" | custom-call | flops 1019215872 | bytes 1179648 | tf_op jit(solution)/shard_map/forward_rest/pallas_call | solution.py:262
  36.7 4.7 %collective-permute-start.5 = (bf16[64,384]{1,0:T(8,128)(2,1)}, bf16[64,384]{1,0:T(8,128)(2,1)S(1)}, u32[]{:S(2)}, u32[]{:S(2)}) collective-permute-start(bf16[64,384]{1,0:T(8,128)(2,1)} %get-tuple-element.16), channel_id=1, source_target_pairs={{0,1},{2,3},{1,4},{3,6},{4,5},{6,7},{5,8},{7,10},{8,9},{10,11},{9,... | collective-permute-start | bytes 147464 | tf_op jit(solution)/shard_map/ppermute | solution.py:221
  41.5 1.3 %collective-permute-start.6 = (bf16[64,384]{1,0:T(8,128)(2,1)}, bf16[64,384]{1,0:T(8,128)(2,1)S(1)}, u32[]{:S(2)}, u32[]{:S(2)}) collective-permute-start(bf16[64,384]{1,0:T(8,128)(2,1)} %get-tuple-element.18), channel_id=1, source_target_pairs={{1,0},{3,2},{4,1},{6,3},{5,4},{7,6},{8,5},{10,7},{9,8},{11,10},{12... | collective-permute-start | bytes 147464 | tf_op jit(solution)/shard_map/ppermute | solution.py:221
  42.8 0.4 fusion
  43.2 1.0 %copy.12.weights = bf16[128,1728]{1,0:T(8,128)(2,1)} copy(bf16[128,1728]{0,1:T(8,128)(2,1)S(1)} %bitcast.11) | data formatting | bytes 884736 | tf_op jit(solution)/shard_map/reshape | solution.py:252
  44.2 1.9 %collective-permute-done.6.right = bf16[64,384]{1,0:T(8,128)(2,1)S(1)} collective-permute-done((bf16[64,384]{1,0:T(8,128)(2,1)}, bf16[64,384]{1,0:T(8,128)(2,1)S(1)}, u32[]{:S(2)}, u32[]{:S(2)}) %collective-permute-start.6) | collective-permute-done | bytes 49184 | tf_op jit(solution)/shard_map/ppermute | solution.py:221
  46.1 0.6 copy-done.17
  46.7 7.9 %grad_features.1 = (f32[64,4608]{1,0:T(8,128)}, bf16[64,4608]{1,0:T(8,128)(2,1)}) custom-call(bf16[64,384]{1,0:T(8,128)(2,1)} %copy-done.16, bf16[64,4608]{1,0:T(8,128)(2,1)} %get-tuple-element.17.middle, bf16[64,384]{1,0:T(8,128)(2,1)} %copy-done.17, s32[27,4608]{1,0:T(8,128)} %valid.7, bf16[128,1728]{1,0:T(8,128)(2,1)} %copy.12.weights), custom_call_target="tpu_custom_call" | custom-call | flops 2038431744 | bytes 1179648 | tf_op jit(solution)/shard_map/grad_features/pallas_call | solution.py:292
  54.6 0.5 collective-permute-start.7
  55.2 9.9 %grad_weight.1 = (f32[896,128]{1,0:T(8,128)}, bf16[896,128]{1,0:T(8,128)(2,1)}) custom-call(s32[1]{0:T(128)} %bitcast.3.rep, bf16[64,384]{1,0:T(8,128)(2,1)} %copy-done.16, bf16[64,4608]{1,0:T(8,128)(2,1)} %get-tuple-element.17.middle, bf16[64,384]{1,0:T(8,128)(2,1)} %copy-done.17, s32[27,4608]{1,0:T(8,128)} %valid.7, bf16[64,4608]{1,0:T(8,128)(2,1)} %own.1, ...), custom_call_target="tpu_custom_call" | custom-call | flops 2038431744 | bytes 1179648 | tf_op jit(solution)/shard_map/grad_weight/pallas_call | solution.py:280
  65.1 2.5 %collective-permute-start.8 = (bf16[896,128]{1,0:T(8,128)(2,1)}, bf16[896,128]{1,0:T(8,128)(2,1)S(1)}, u32[]{:S(2)}, u32[]{:S(2)}) collective-permute-start(bf16[896,128]{1,0:T(8,128)(2,1)} %get-tuple-element.22), channel_id=1, source_target_pairs={{0,1},{1,0},{2,3},{3,2},{4,5},{5,4},{6,7},{7,6},{8,9},{9,8},{10,11... | collective-permute-start | bytes 688136 | tf_op jit(solution)/shard_map/ppermute | solution.py:290
  67.6 1.3 %collective-permute-done.8.arrived = bf16[896,128]{1,0:T(8,128)(2,1)S(1)} collective-permute-done((bf16[896,128]{1,0:T(8,128)(2,1)}, bf16[896,128]{1,0:T(8,128)(2,1)S(1)}, u32[]{:S(2)}, u32[]{:S(2)}) %collective-permute-start.8) | collective-permute-done | bytes 229408 | tf_op jit(solution)/shard_map/ppermute | solution.py:290
  68.9 0.7 copy-done.4
  69.6 1.8 %split.1 = (f32[224,128]{1,0:T(8,128)}, bf16[224,128]{1,0:T(8,128)(2,1)}, bf16[224,128]{1,0:T(8,128)(2,1)}, bf16[224,128]{1,0:T(8,128)(2,1)}) custom-call(s32[1]{0:T(128)} %bitcast.5.brick, f32[896,128]{1,0:T(8,128)} %get-tuple-element.21.kept, bf16[896,128]{1,0:T(8,128)(2,1)} %copy-done.4), custom_call_target="tpu_custom_call" | custom-call | bytes 688128 | tf_op jit(solution)/shard_map/split/pallas_call | solution.py:309
  71.4 1.6 %collective-permute-start.9 = (bf16[224,128]{1,0:T(8,128)(2,1)}, bf16[224,128]{1,0:T(8,128)(2,1)S(1)}, u32[]{:S(2)}, u32[]{:S(2)}) collective-permute-start(bf16[224,128]{1,0:T(8,128)(2,1)} %get-tuple-element.24), channel_id=1, source_target_pairs={{0,4},{4,8},{8,12},{12,0},{1,5},{5,9},{9,13},{13,1},{2,6},{6,10},{... | collective-permute-start | bytes 172040 | tf_op jit(solution)/shard_map/ppermute | solution.py:319
  73.0 1.6 %collective-permute-start.10 = (bf16[224,128]{1,0:T(8,128)(2,1)}, bf16[224,128]{1,0:T(8,128)(2,1)S(1)}, u32[]{:S(2)}, u32[]{:S(2)}) collective-permute-start(bf16[224,128]{1,0:T(8,128)(2,1)} %get-tuple-element.25), channel_id=1, source_target_pairs={{0,8},{4,12},{8,0},{12,4},{1,9},{5,13},{9,1},{13,5},{2,10},{6,14},... | collective-permute-start | bytes 172040 | tf_op jit(solution)/shard_map/ppermute | solution.py:319
  74.6 2.3 %collective-permute-start.11 = (bf16[224,128]{1,0:T(8,128)(2,1)}, bf16[224,128]{1,0:T(8,128)(2,1)S(1)}, u32[]{:S(2)}, u32[]{:S(2)}) collective-permute-start(bf16[224,128]{1,0:T(8,128)(2,1)} %get-tuple-element.26), channel_id=1, source_target_pairs={{0,12},{4,0},{8,4},{12,8},{1,13},{5,1},{9,5},{13,9},{2,14},{6,2},{... | collective-permute-start | bytes 172040 | tf_op jit(solution)/shard_map/ppermute | solution.py:319
  76.9 0.8 collective-permute-done.9.rest_0_
  77.8 2.4 %collective-permute-done.10.rest_1_ = bf16[224,128]{1,0:T(8,128)(2,1)S(1)} collective-permute-done((bf16[224,128]{1,0:T(8,128)(2,1)}, bf16[224,128]{1,0:T(8,128)(2,1)S(1)}, u32[]{:S(2)}, u32[]{:S(2)}) %collective-permute-start.10) | collective-permute-done | bytes 57376 | tf_op jit(solution)/shard_map/ppermute | solution.py:319
  80.2 0.6 copy-done.7
  80.8 1.6 %merge.1.rest_0_ = bf16[224,128]{1,0:T(8,128)(2,1)} custom-call(f32[224,128]{1,0:T(8,128)} %get-tuple-element.23.mine, bf16[224,128]{1,0:T(8,128)(2,1)} %copy-done.6, bf16[224,128]{1,0:T(8,128)(2,1)} %copy-done.7, bf16[224,128]{1,0:T(8,128)(2,1)} %copy-done.9), custom_call_target="tpu_custom_call" | custom-call | bytes 229376 | tf_op jit(solution)/shard_map/merge/pallas_call | solution.py:320
  82.4 1.7 %collective-permute-start.12 = (bf16[224,128]{1,0:T(8,128)(2,1)}, bf16[224,128]{1,0:T(8,128)(2,1)S(1)}, u32[]{:S(2)}, u32[]{:S(2)}) collective-permute-start(bf16[224,128]{1,0:T(8,128)(2,1)} %merge.1.rest_0_), channel_id=1, source_target_pairs={{0,4},{4,8},{8,12},{12,0},{1,5},{5,9},{9,13},{13,1},{2,6},{6,10},{... | collective-permute-start | bytes 172040 | tf_op jit(solution)/shard_map/ppermute | solution.py:328
  84.1 1.8 %collective-permute-start.13 = (bf16[224,128]{1,0:T(8,128)(2,1)}, bf16[224,128]{1,0:T(8,128)(2,1)S(1)}, u32[]{:S(2)}, u32[]{:S(2)}) collective-permute-start(bf16[224,128]{1,0:T(8,128)(2,1)} %merge.1.rest_0_), channel_id=1, source_target_pairs={{0,8},{4,12},{8,0},{12,4},{1,9},{5,13},{9,1},{13,5},{2,10},{6,14},... | collective-permute-start | bytes 172040 | tf_op jit(solution)/shard_map/ppermute | solution.py:328
  85.9 0.5 collective-permute-start.14
  86.4 2.5 %collective-permute-done.12.rest_1_ = bf16[224,128]{1,0:T(8,128)(2,1)S(1)} collective-permute-done((bf16[224,128]{1,0:T(8,128)(2,1)}, bf16[224,128]{1,0:T(8,128)(2,1)S(1)}, u32[]{:S(2)}, u32[]{:S(2)}) %collective-permute-start.12) | collective-permute-done | bytes 57376 | tf_op jit(solution)/shard_map/ppermute | solution.py:328
  88.9 1.8 %collective-permute-done.13.rest_2_ = bf16[224,128]{1,0:T(8,128)(2,1)S(1)} collective-permute-done((bf16[224,128]{1,0:T(8,128)(2,1)}, bf16[224,128]{1,0:T(8,128)(2,1)S(1)}, u32[]{:S(2)}, u32[]{:S(2)}) %collective-permute-start.13) | collective-permute-done | bytes 57376 | tf_op jit(solution)/shard_map/ppermute | solution.py:328
  91.0 0.3 copy-done.10
  91.3 0.6 copy-done.11
  92.0 1.6 %gather.1.side = bf16[896,128]{1,0:T(8,128)(2,1)} custom-call(s32[1]{0:T(128)} %bitcast.5.brick, bf16[224,128]{1,0:T(8,128)(2,1)} %merge.1.rest_0_, bf16[224,128]{1,0:T(8,128)(2,1)} %copy-done.8, bf16[224,128]{1,0:T(8,128)(2,1)} %copy-done.10, bf16[224,128]{1,0:T(8,128)(2,1)} %copy-done.11), custom_call_target="tpu_custom_call" | custom-call | bytes 458752 | tf_op jit(solution)/shard_map/gather/pallas_call | solution.py:329
  93.6 1.7 %collective-permute-done.15.other = bf16[896,128]{1,0:T(8,128)(2,1)S(1)} collective-permute-done((bf16[896,128]{1,0:T(8,128)(2,1)}, bf16[896,128]{1,0:T(8,128)(2,1)S(1)}, u32[]{:S(2)}, u32[]{:S(2)}) %collective-permute-start.15) | collective-permute-done | bytes 229408 | tf_op jit(solution)/shard_map/ppermute | solution.py:338
  95.3 0.7 copy-done.5
  96.0 2.2 %join.1 = f32[1728,128]{1,0:T(8,128)} custom-call(s32[1]{0:T(128)} %bitcast.3.rep, s32[1]{0:T(128)} %bitcast.4.turn, bf16[896,128]{1,0:T(8,128)(2,1)} %gather.1.side, bf16[896,128]{1,0:T(8,128)(2,1)} %copy-done.5), custom_call_target="tpu_custom_call" | custom-call | bytes 1376256 | tf_op jit(solution)/shard_map/join/pallas_call | solution.py:339
  98.1 1.0 add_convert_fusion
  (38 shorter events, 0.9 us)
Async XLA Ops:
  0.6 25.8 %collective-permute-start.1 = (bf16[64,4608]{1,0:T(8,128)(2,1)}, bf16[64,4608]{1,0:T(8,128)(2,1)S(1)}, u32[]{:S(2)}, u32[]{:S(2)}) collective-permute-start(bf16[64,4608]{1,0:T(8,128)(2,1)} %own.1), channel_id=1, source_target_pairs={{2,0},{0,2},{3,1},{1,3},{6,4},{4,6},{7,5},{5,7},{10,8},{8,10},{11,... | collective-permute-start | bytes 1769480 | tf_op jit(solution)/shard_map/ppermute | solution.py:236
  4.5 21.9 %collective-permute-start = (bf16[64,384]{1,0:T(8,128)(2,1)S(1)}, bf16[64,384]{1,0:T(8,128)(2,1)S(1)}, u32[]{:S(2)}, u32[]{:S(2)}) collective-permute-start(bf16[64,384]{1,0:T(8,128)(2,1)S(1)} %get-tuple-element.28), channel_id=1, source_target_pairs={{2,1},{0,3},{3,4},{1,6},{6,5},{4,7},{7,8},{5,10},{10,9},{8,11},{11... | collective-permute-start | bytes 147464 | tf_op jit(solution)/shard_map/ppermute | solution.py:221
  5.8 11.4 %collective-permute-start.3 = (bf16[64,384]{1,0:T(8,128)(2,1)S(1)}, bf16[64,384]{1,0:T(8,128)(2,1)S(1)}, u32[]{:S(2)}, u32[]{:S(2)}) collective-permute-start(bf16[64,384]{1,0:T(8,128)(2,1)S(1)} %get-tuple-element.28), channel_id=1, source_target_pairs={{0,1},{2,3},{1,4},{3,6},{4,5},{6,7},{5,8},{7,10},{8,9},{10,11},{9,... | collective-permute-start | bytes 147464 | tf_op jit(solution)/shard_map/ppermute | solution.py:221
  10.0 16.4 %collective-permute-start.2 = (bf16[64,384]{1,0:T(8,128)(2,1)S(1)}, bf16[64,384]{1,0:T(8,128)(2,1)S(1)}, u32[]{:S(2)}, u32[]{:S(2)}) collective-permute-start(bf16[64,384]{1,0:T(8,128)(2,1)S(1)} %get-tuple-element.27), channel_id=1, source_target_pairs={{3,0},{1,2},{6,1},{4,3},{7,4},{5,6},{10,5},{8,7},{11,8},{9,10},{14... | collective-permute-start | bytes 147464 | tf_op jit(solution)/shard_map/ppermute | solution.py:221
  11.3 6.0 %collective-permute-start.4 = (bf16[64,384]{1,0:T(8,128)(2,1)S(1)}, bf16[64,384]{1,0:T(8,128)(2,1)S(1)}, u32[]{:S(2)}, u32[]{:S(2)}) collective-permute-start(bf16[64,384]{1,0:T(8,128)(2,1)S(1)} %get-tuple-element.27), channel_id=1, source_target_pairs={{1,0},{3,2},{4,1},{6,3},{5,4},{7,6},{8,5},{10,7},{9,8},{11,10},{12... | collective-permute-start | bytes 147464 | tf_op jit(solution)/shard_map/ppermute | solution.py:221
  17.3 0.6 copy-start.14
  17.9 0.6 copy-start.15
  26.4 16.4 %copy-start.1 = (bf16[27,128,64]{1,2,0:T(8,128)(2,1)S(1)}, bf16[27,128,64]{1,2,0:T(8,128)(2,1)}, u32[]{:S(2)}) copy-start(bf16[27,128,64]{1,2,0:T(8,128)(2,1)} %param.5) | copy-start | bytes 1327108
  26.4 0.6 copy-start.12
  26.4 0.6 copy-start.13
  27.0 0.8 copy-start.3
  36.7 7.5 %collective-permute-start.5 = (bf16[64,384]{1,0:T(8,128)(2,1)}, bf16[64,384]{1,0:T(8,128)(2,1)S(1)}, u32[]{:S(2)}, u32[]{:S(2)}) collective-permute-start(bf16[64,384]{1,0:T(8,128)(2,1)} %get-tuple-element.16), channel_id=1, source_target_pairs={{0,1},{2,3},{1,4},{3,6},{4,5},{6,7},{5,8},{7,10},{8,9},{10,11},{9,... | collective-permute-start | bytes 147464 | tf_op jit(solution)/shard_map/ppermute | solution.py:221
  41.5 4.6 %collective-permute-start.6 = (bf16[64,384]{1,0:T(8,128)(2,1)}, bf16[64,384]{1,0:T(8,128)(2,1)S(1)}, u32[]{:S(2)}, u32[]{:S(2)}) collective-permute-start(bf16[64,384]{1,0:T(8,128)(2,1)} %get-tuple-element.18), channel_id=1, source_target_pairs={{1,0},{3,2},{4,1},{6,3},{5,4},{7,6},{8,5},{10,7},{9,8},{11,10},{12... | collective-permute-start | bytes 147464 | tf_op jit(solution)/shard_map/ppermute | solution.py:221
  44.2 1.9 %copy-start.16 = (bf16[64,384]{1,0:T(8,128)(2,1)}, bf16[64,384]{1,0:T(8,128)(2,1)S(1)}, u32[]{:S(2)}) copy-start(bf16[64,384]{1,0:T(8,128)(2,1)S(1)} %collective-permute-done.5.left) | copy-start | bytes 147460
  46.1 0.6 copy-start.17
  54.6 43.5 %collective-permute-start.7 = (bf16[64,4608]{1,0:T(8,128)(2,1)}, bf16[64,4608]{1,0:T(8,128)(2,1)S(1)}, u32[]{:S(2)}, u32[]{:S(2)}) collective-permute-start(bf16[64,4608]{1,0:T(8,128)(2,1)} %get-tuple-element.20), channel_id=1, source_target_pairs={{0,2},{2,0},{1,3},{3,1},{4,6},{6,4},{5,7},{7,5},{8,10},{10,8},{9,1... | collective-permute-start | bytes 1769480 | tf_op jit(solution)/shard_map/ppermute | solution.py:301
  65.1 3.8 %collective-permute-start.8 = (bf16[896,128]{1,0:T(8,128)(2,1)}, bf16[896,128]{1,0:T(8,128)(2,1)S(1)}, u32[]{:S(2)}, u32[]{:S(2)}) collective-permute-start(bf16[896,128]{1,0:T(8,128)(2,1)} %get-tuple-element.22), channel_id=1, source_target_pairs={{0,1},{1,0},{2,3},{3,2},{4,5},{5,4},{6,7},{7,6},{8,9},{9,8},{10,11... | collective-permute-start | bytes 688136 | tf_op jit(solution)/shard_map/ppermute | solution.py:290
  68.9 0.7 copy-start.4
  71.4 26.8 %copy-start = (bf16[64,4608]{1,0:T(8,128)(2,1)S(1)}, bf16[64,4608]{1,0:T(8,128)(2,1)}, u32[]{:S(2)}) copy-start(bf16[64,4608]{1,0:T(8,128)(2,1)} %cotangent.1) | copy-start | bytes 1769476
  71.4 26.8 %copy-start.2 = (f32[64,4608]{1,0:T(8,128)S(1)}, f32[64,4608]{1,0:T(8,128)}, u32[]{:S(2)}) copy-start(f32[64,4608]{1,0:T(8,128)} %get-tuple-element.19) | copy-start | bytes 3538948
  71.4 6.4 %collective-permute-start.9 = (bf16[224,128]{1,0:T(8,128)(2,1)}, bf16[224,128]{1,0:T(8,128)(2,1)S(1)}, u32[]{:S(2)}, u32[]{:S(2)}) collective-permute-start(bf16[224,128]{1,0:T(8,128)(2,1)} %get-tuple-element.24), channel_id=1, source_target_pairs={{0,4},{4,8},{8,12},{12,0},{1,5},{5,9},{9,13},{13,1},{2,6},{6,10},{... | collective-permute-start | bytes 172040 | tf_op jit(solution)/shard_map/ppermute | solution.py:319
  73.0 7.1 %collective-permute-start.10 = (bf16[224,128]{1,0:T(8,128)(2,1)}, bf16[224,128]{1,0:T(8,128)(2,1)S(1)}, u32[]{:S(2)}, u32[]{:S(2)}) collective-permute-start(bf16[224,128]{1,0:T(8,128)(2,1)} %get-tuple-element.25), channel_id=1, source_target_pairs={{0,8},{4,12},{8,0},{12,4},{1,9},{5,13},{9,1},{13,5},{2,10},{6,14},... | collective-permute-start | bytes 172040 | tf_op jit(solution)/shard_map/ppermute | solution.py:319
  74.6 5.5 %collective-permute-start.11 = (bf16[224,128]{1,0:T(8,128)(2,1)}, bf16[224,128]{1,0:T(8,128)(2,1)S(1)}, u32[]{:S(2)}, u32[]{:S(2)}) collective-permute-start(bf16[224,128]{1,0:T(8,128)(2,1)} %get-tuple-element.26), channel_id=1, source_target_pairs={{0,12},{4,0},{8,4},{12,8},{1,13},{5,1},{9,5},{13,9},{2,14},{6,2},{... | collective-permute-start | bytes 172040 | tf_op jit(solution)/shard_map/ppermute | solution.py:319
  77.8 2.4 %copy-start.6 = (bf16[224,128]{1,0:T(8,128)(2,1)}, bf16[224,128]{1,0:T(8,128)(2,1)S(1)}, u32[]{:S(2)}) copy-start(bf16[224,128]{1,0:T(8,128)(2,1)S(1)} %collective-permute-done.9.rest_0_) | copy-start | bytes 172036
  80.2 0.6 copy-start.7
  80.2 0.6 copy-start.9
  82.4 6.5 %collective-permute-start.12 = (bf16[224,128]{1,0:T(8,128)(2,1)}, bf16[224,128]{1,0:T(8,128)(2,1)S(1)}, u32[]{:S(2)}, u32[]{:S(2)}) collective-permute-start(bf16[224,128]{1,0:T(8,128)(2,1)} %merge.1.rest_0_), channel_id=1, source_target_pairs={{0,4},{4,8},{8,12},{12,0},{1,5},{5,9},{9,13},{13,1},{2,6},{6,10},{... | collective-permute-start | bytes 172040 | tf_op jit(solution)/shard_map/ppermute | solution.py:328
  84.1 6.7 %collective-permute-start.13 = (bf16[224,128]{1,0:T(8,128)(2,1)}, bf16[224,128]{1,0:T(8,128)(2,1)S(1)}, u32[]{:S(2)}, u32[]{:S(2)}) collective-permute-start(bf16[224,128]{1,0:T(8,128)(2,1)} %merge.1.rest_0_), channel_id=1, source_target_pairs={{0,8},{4,12},{8,0},{12,4},{1,9},{5,13},{9,1},{13,5},{2,10},{6,14},... | collective-permute-start | bytes 172040 | tf_op jit(solution)/shard_map/ppermute | solution.py:328
  85.9 5.1 %collective-permute-start.14 = (bf16[224,128]{1,0:T(8,128)(2,1)}, bf16[224,128]{1,0:T(8,128)(2,1)S(1)}, u32[]{:S(2)}, u32[]{:S(2)}) collective-permute-start(bf16[224,128]{1,0:T(8,128)(2,1)} %merge.1.rest_0_), channel_id=1, source_target_pairs={{0,12},{4,0},{8,4},{12,8},{1,13},{5,1},{9,5},{13,9},{2,14},{6,2},{... | collective-permute-start | bytes 172040 | tf_op jit(solution)/shard_map/ppermute | solution.py:328
  88.9 2.1 %copy-start.8 = (bf16[224,128]{1,0:T(8,128)(2,1)}, bf16[224,128]{1,0:T(8,128)(2,1)S(1)}, u32[]{:S(2)}) copy-start(bf16[224,128]{1,0:T(8,128)(2,1)S(1)} %collective-permute-done.12.rest_1_) | copy-start | bytes 172036
  90.7 0.6 copy-start.10
  91.3 0.6 copy-start.11
  93.6 1.7 %collective-permute-start.15 = (bf16[896,128]{1,0:T(8,128)(2,1)}, bf16[896,128]{1,0:T(8,128)(2,1)S(1)}, u32[]{:S(2)}, u32[]{:S(2)}) collective-permute-start(bf16[896,128]{1,0:T(8,128)(2,1)} %gather.1.side), channel_id=1, source_target_pairs={{0,1},{1,0},{2,3},{3,2},{4,5},{5,4},{6,7},{7,6},{8,9},{9,8},{10,11... | collective-permute-start | bytes 688136 | tf_op jit(solution)/shard_map/ppermute | solution.py:338
  95.3 0.7 copy-start.5

commit v2 on v0

v2 whole, which is shorter than its diff:
```python
import functools

import jax
import jax.numpy as jnp
from jax import lax
from jax.experimental import pallas as pl
from jax.experimental.pallas import tpu as pltpu
from jax.sharding import PartitionSpec as P

EDGE = 16
FACE = EDGE * EDGE
TAPS = 27
HALO = 384
FAR = 2 * HALO
ROWS = 16
GROUP = 4
WIDTH = 768
BACK = 512
LINE = ("brick", "chan", "rep")
MIB = 1024 * 1024
F32, BF16 = jnp.float32, jnp.bfloat16

STEPS = [(k // 3 - 1) * EDGE + k % 3 - 1 for k in range(9)]

HERE = pl.BlockSpec(memory_space=pltpu.VMEM)
SCALAR = pl.BlockSpec(memory_space=pltpu.SMEM)


def kernel(body, name, outs, args, scalars=(), scratch=(), out_specs=None, limit=8, flops=0, moved=MIB):
    single = not isinstance(outs, (tuple, list))
    specs = out_specs or [HERE] * (1 if single else len(outs))
    return pl.pallas_call(
        body,
        out_shape=outs,
        in_specs=[SCALAR] * len(scalars) + [HERE] * len(args),
        out_specs=specs[0] if single else specs,
        scratch_shapes=list(scratch),
        compiler_params=pltpu.CompilerParams(vmem_limit_bytes=limit * MIB),
        cost_estimate=pl.CostEstimate(flops=flops, bytes_accessed=moved, transcendentals=0),
        name=name,
    )(*(x[None] for x in scalars), *args)


def shape(dims, kind=BF16):
    return jax.ShapeDtypeStruct(dims, kind)


def shift(shifts):
    length = shifts.shape[2]
    for at in range(0, shifts.shape[1], ROWS):
        rows = pl.ds(at, ROWS)
        for j, step in enumerate(STEPS):
            if j != 4:
                shifts[j, rows, 128 : length - 128] = shifts[4, rows, 128 + step : length - 128 + step]


def masked(shifts, valid, tap, at_shift, at_valid, width):
    keep = valid[tap, :, pl.ds(at_valid, width)]
    begin = pl.multiple_of(at_shift + (tap // 9 - 1) * FACE, 128)
    return [
        shifts[tap % 9, at : at + ROWS, pl.ds(begin, width)] * keep
        for at in range(0, shifts.shape[1], ROWS)
    ]


def groups():
    return [range(first, min(first + GROUP, TAPS)) for first in range(0, TAPS, GROUP)]


def product(weights, shifts, valid, at_shift, at_valid, width, taps_of):
    channels = shifts.shape[1]
    total = None
    for group in groups():
        rows = []
        for tap in group:
            rows += masked(shifts, valid, taps_of(tap), at_shift, at_valid, width)
        part = jnp.dot(
            weights[:, group[0] * channels : (group[-1] + 1) * channels],
            jnp.concatenate(rows, axis=0),
            preferred_element_type=F32,
        )
        total = part if total is None else total + part
    return total


def pack_body(*refs):
    ends, outs = refs[:6], refs[6:]
    for (features, cotangent, neighbours), out in zip((ends[:3], ends[3:]), outs):
        share = features.shape[0]
        out[...] = jnp.zeros_like(out)
        out[:share, :] = features[...]
        out[share : 2 * share, :HALO] = cotangent[...]
        kept = (neighbours[...] >= 0).astype(F32)
        kept = jnp.concatenate([kept, jnp.zeros((32 - TAPS, HALO), F32)], axis=0)
        out[share : share + 32, HALO:] = kept.astype(BF16)


def pack(features, cotangent, neighbours):
    share, sites = features.shape

    def end(rows, width, at):
        return pl.BlockSpec((rows, width), lambda i: (0, at * (sites // width - 1)))

    rows = share + max(share, 32)
    return pl.pallas_call(
        pack_body,
        grid=(1,),
        out_shape=[shape((rows, FAR))] * 2,
        in_specs=[
            spec
            for at in (1, 0)
            for spec in (end(share, FAR, at), end(share, HALO, at), end(TAPS, HALO, at))
        ],
        out_specs=[pl.BlockSpec((rows, FAR), lambda i: (0, 0))] * 2,
        cost_estimate=pl.CostEstimate(flops=0, bytes_accessed=MIB, transcendentals=0),
        name="pack",
    )(*(features, cotangent, neighbours) * 2)


def weights_body(share, turn, by_out, own, rest, by_in, flat):
    total = by_out.shape[2]
    flat[...] = jnp.zeros_like(flat)
    for group in groups():
        taps = []
        for tap in group:
            ring = pltpu.roll(by_out[tap].astype(F32), turn[0], 1)
            flat[tap * share : (tap + 1) * share, :] = ring
            taps.append(ring)
        first, last = group[0], group[-1] + 1
        own[:, first * share : last * share] = jnp.concatenate(
            [x[:, :share] for x in taps], axis=1
        ).astype(BF16)
        left = total - share
        rest[:, first * left : last * left] = jnp.concatenate(
            [x[:, share:] for x in taps], axis=1
        ).astype(BF16)
    by_in[...] = flat[...].T.astype(BF16)


def own_body(left, middle, right, weights, neighbours, begun, valid, shifts, kept):
    share, sites = middle.shape
    shifts[4, :, :FAR] = left[:share, :]
    shifts[4, :, FAR : FAR + sites] = middle[...]
    shifts[4, :, FAR + sites :] = right[:share, :]
    shift(shifts)
    kept[:, :HALO] = left[share : share + 32, HALO:].astype(F32)
    kept[:TAPS, HALO : HALO + sites] = (neighbours[...] >= 0).astype(F32)
    kept[:, HALO + sites :] = right[share : share + 32, HALO:].astype(F32)
    for tap in range(TAPS):
        valid[tap] = jnp.broadcast_to(kept[tap : tap + 1, :], (ROWS, kept.shape[1])).astype(BF16)

    def block(j, carry):
        start = pl.multiple_of(j * WIDTH, 128)
        begun[:, pl.ds(start, WIDTH)] = product(
            weights, shifts, valid, start + HALO, start, WIDTH, lambda tap: tap
        )
        return carry

    lax.fori_loop(0, begun.shape[1] // WIDTH, block, 0)


def rest_body(
    ends, middle, weights, valid, begun, left, features, right, cotangent, output, grad, shifts, kept
):
    share, sites = features.shape
    shifts[4, :, :FAR] = ends[:, :FAR]
    shifts[4, :, FAR : FAR + sites] = middle[...]
    shifts[4, :, FAR + sites :] = ends[:, FAR:]
    shift(shifts)
    grad[:, :HALO] = left[share : 2 * share, :HALO]
    grad[:, HALO : HALO + sites] = cotangent[...]
    grad[:, HALO + sites :] = right[share : 2 * share, :HALO]
    kept[:, HALO : HALO + sites] = features[...]

    def block(j, carry):
        start = pl.multiple_of(j * WIDTH, 128)
        here = pl.ds(start, WIDTH)
        hidden = begun[:, here] + product(
            weights, shifts, valid, start + HALO, start, WIDTH, lambda tap: tap
        )
        sigma = jax.nn.sigmoid(hidden)
        kept[:, here] = (kept[:, here].astype(F32) + hidden * sigma).astype(BF16)
        grad[:, here] = (
            grad[:, here].astype(F32) * sigma * (1.0 + hidden * (1.0 - sigma))
        ).astype(BF16)
        return carry

    lax.fori_loop(0, begun.shape[1] // WIDTH, block, 0)
    output[...] = kept[:, HALO : HALO + sites]


def weight_body(half, rep, grad, valid, own, rest, kept, sent, shifts, total):
    share, sites = own.shape
    shifts[4] = grad[...]
    shift(shifts)
    total[...] = jnp.zeros_like(total)

    def block(j, carry):
        start = pl.multiple_of(j * BACK, 128)
        here = pl.ds(start, BACK)
        features = jnp.concatenate([own[:, here], rest[:, here]], axis=0)
        for group in groups():
            rows = []
            for tap in group:
                rows += masked(shifts, valid, TAPS - 1 - tap, start + HALO, start + HALO, BACK)
            total[group[0] * share : (group[-1] + 1) * share, :] += lax.dot_general(
                jnp.concatenate(rows, axis=0),
                features,
                (((1,), (1,)), ((), ())),
                preferred_element_type=F32,
            )
        return carry

    lax.fori_loop(0, sites // BACK, block, 0)
    mine = rep[0]
    kept[...] = total[pl.ds(pl.multiple_of(mine * half, ROWS), half), :]
    sent[...] = total[pl.ds(pl.multiple_of((1 - mine) * half, ROWS), half), :].astype(BF16)


def feature_body(shifts, valid, weights, own, rest):
    share, sites = own.shape

    def block(j, carry):
        start = pl.multiple_of(j * BACK, 128)
        here = pl.ds(start, BACK)
        total = product(
            weights, shifts, valid, start + HALO, start + HALO, BACK, lambda tap: TAPS - 1 - tap
        )
        own[:, here] = total[:share]
        rest[:, here] = total[share:].astype(BF16)
        return carry

    lax.fori_loop(0, sites // BACK, block, 0)


def split_body(bricks, brick, kept, arrived, mine, *pieces):
    size = mine.shape[0]
    for d in range(bricks):
        rows = pl.ds(pl.multiple_of((brick[0] + d) % bricks * size, ROWS), size)
        summed = kept[rows, :] + arrived[rows, :].astype(F32)
        if d == 0:
            mine[...] = summed
        else:
            pieces[d - 1][...] = summed.astype(BF16)


def merge_body(mine, *rest):
    *pieces, done = rest
    total = mine[...]
    for piece in pieces:
        total += piece[...].astype(F32)
    done[...] = total.astype(BF16)


def gather_body(bricks, brick, *rest):
    *pieces, side = rest
    size = pieces[0].shape[0]
    for d, piece in enumerate(pieces):
        at = (brick[0] + bricks - d) % bricks * size
        side[pl.ds(pl.multiple_of(at, ROWS), size), :] = piece[...]


def join_body(half, rep, turn, side, other, out, both):
    mine = rep[0]
    both[pl.ds(pl.multiple_of(mine * half, ROWS), half), :] = side[...]
    both[pl.ds(pl.multiple_of((1 - mine) * half, ROWS), half), :] = other[...]
    out[...] = pltpu.roll(both[: out.shape[0], :].astype(F32), turn[0], 1)


def add_body(cotangent, own, *rest):
    *terms, out = rest
    total = cotangent[...].astype(F32) + own[...]
    for term in terms:
        total += term[...].astype(F32)
    out[...] = total.astype(BF16)


def hop(x, step):
    count = lax.axis_size(("brick", "rep"))
    pairs = [(i, i + step) for i in range(count) if 0 <= i + step < count]
    return lax.ppermute(x, ("brick", "rep"), pairs)


def local(features, conv_weight, neighbours, cotangent):
    share, sites = features.shape
    total = conv_weight.shape[1]
    left = total - share
    chans, bricks, reps = (lax.axis_size(axis) for axis in ("chan", "brick", "rep"))
    chan, brick, rep = (lax.axis_index(axis) for axis in ("chan", "brick", "rep"))
    margin = sites + 2 * HALO
    flops = 2 * TAPS * share * sites

    def around(x):
        return [
            lax.ppermute(x, "chan", [((i + over) % chans, i) for i in range(chans)])
            for over in range(1, chans)
        ]

    def stack(parts):
        return parts[0] if len(parts) == 1 else jnp.concatenate(parts, axis=0)

    rest = stack(around(features))
    to_next, to_last = pack(features, cotangent, neighbours)
    before, behind = hop(to_next, 1), hop(to_last, -1)
    ends = stack(around(jnp.concatenate([before[:share], behind[:share]], axis=1)))

    lanes = -(-TAPS * share // 128) * 128
    own_weights, rest_weights, by_in = kernel(
        functools.partial(weights_body, share),
        "weights",
        [shape((share, TAPS * share)), shape((share, TAPS * left)), shape((total, lanes))],
        [jnp.transpose(conv_weight, (0, 2, 1))],
        scalars=[(total - chan * share) % total],
        scratch=[pltpu.VMEM((lanes, total), F32)],
    )
    begun, valid = kernel(
        own_body,
        "forward_own",
        [shape((share, margin), F32), shape((TAPS, ROWS, margin))],
        [before, features, behind, own_weights, neighbours],
        scratch=[pltpu.VMEM((9, share, sites + 2 * FAR), BF16), pltpu.VMEM((32, margin), F32)],
        limit=20,
        flops=flops * share,
    )
    output, grad = kernel(
        rest_body,
        "forward_rest",
        [shape((share, sites)), shape((share, margin))],
        [ends, rest, rest_weights, valid, begun, before, features, behind, cotangent],
        scratch=[
            pltpu.VMEM((9, left, sites + 2 * FAR), BF16),
            pltpu.VMEM((share, margin), BF16),
        ],
        limit=24,
        flops=flops * left,
    )

    piece = -(-TAPS * share // (reps * bricks * ROWS)) * ROWS
    half = piece * bricks
    kept, sent, shifts = kernel(
        functools.partial(weight_body, half),
        "grad_weight",
        [shape((half, total), F32), shape((half, total)), shape((9, share, margin))],
        [grad, valid, features, rest],
        scalars=[rep],
        scratch=[pltpu.VMEM((reps * half, total), F32)],
        limit=12,
        flops=flops * total,
    )
    swap = [(0, 1), (1, 0)]
    arrived = lax.ppermute(sent, "rep", swap)

    own_part, rest_part = kernel(
        feature_body,
        "grad_features",
        [shape((share, sites), F32), shape((left, sites))],
        [shifts, valid, by_in],
        limit=12,
        flops=flops * total,
    )
    terms = [
        lax.ppermute(
            rest_part if left == share else rest_part[(over - 1) * share : over * share],
            "chan",
            [(i, (i + over) % chans) for i in range(chans)],
        )
        for over in range(1, chans)
    ]

    mine, *pieces = kernel(
        functools.partial(split_body, bricks),
        "split",
        [shape((piece, total), F32)] + [shape((piece, total))] * (bricks - 1),
        [kept, arrived],
        scalars=[brick],
    )
    turns = [[(i, (i + d) % bricks) for i in range(bricks)] for d in range(1, bricks)]
    pieces = [lax.ppermute(x, "brick", turn) for x, turn in zip(pieces, turns)]
    done = kernel(merge_body, "merge", shape((piece, total)), [mine, *pieces])
    pieces = [done] + [lax.ppermute(done, "brick", turn) for turn in turns]
    side = kernel(
        functools.partial(gather_body, bricks),
        "gather",
        shape((half, total)),
        pieces,
        scalars=[brick],
    )
    other = lax.ppermute(side, "rep", swap)
    grad_weight = kernel(
        functools.partial(join_body, half),
        "join",
        shape((TAPS * share, total), F32),
        [side, other],
        scalars=[rep, chan * share],
        scratch=[pltpu.VMEM((reps * half, total), BF16)],
    )
    grad_features = kernel(
        add_body, "add", shape((share, sites)), [cotangent, own_part, *terms]
    )
    grad_weight = jnp.transpose(grad_weight.reshape(TAPS, share, total), (0, 2, 1))
    return output, grad_features, grad_weight


def solution(mesh):
    return jax.shard_map(
        local,
        mesh=mesh,
        in_specs=(
            P("chan", ("scene", "brick", "rep")),
            P(None, None, "chan"),
            P(None, ("scene", "brick", "rep")),
            P("chan", ("scene", "brick", "rep")),
        ),
        out_specs=(
            P("chan", ("scene", "brick", "rep")),
            P("chan", ("scene", "brick", "rep")),
            P("scene", None, "chan"),
        ),
        check_vma=False,
    )
```

time: 195 us -> 73.3 us (0.38)
  waiting for transfers between devices: 110 us -> 17.5 us
  Pallas kernels: 0 us -> 31 us
  matrix products: 29.9 us -> 0 us
  between operations: 14.2 us -> 0.75 us
  local copies, waits for them, and re-layouts: 10.5 us -> 0.03 us
  other arithmetic: 9.56 us -> 0.69 us
  starting transfers between devices: 20.5 us -> 23.2 us
    psum x1 -> x0, waiting for transfers between devices: 58.4 us -> none  [local(): grad_weight = lax.psum(weight_terms, ('brick', 'rep'))]
    pallas_call x0 -> x11, Pallas kernels: none -> 31 us  [the longest x10 29.1 us: kernel(): pl.pallas_call(body, out_shape=outs, in_specs=[SCALAR] * len(scalars) + [...]
    dot_general x29 -> x0, matrix products: 29.9 us -> none  [the longest x27 17.8 us: local(): lax.dot_general(conv_weight[offset], gathered, (((0,), (0,)), ((), ())),...]
    all_gather x1 -> x0, waiting for transfers between devices: 27.1 us -> none  [local(): full_here = lax.all_gather(features, 'chan', axis=0, tiled=True)]
    reduce_scatter x1 -> x0, waiting for transfers between devices: 19.5 us -> none  [local(): lax.psum_scatter(jnp.dot(weight_stack, stacked, preferred_element_type=jn...]
    ppermute x4 -> x13, waiting for transfers between devices: 4.33 us -> 17.5 us  [the longest x3 5.33 us: local(): pieces = [done] + [lax.ppermute(done, 'brick', turn) for turn in turns]]
    unnamed x12 -> x8, local copies, waits for them, and re-layouts: 8.87 us -> 0.02 us
    unnamed x26 -> x0, other arithmetic: 6.13 us -> none
  transfers between devices with their start and end apart: 7 -> 13, of which waited for: 4 -> 8; matrix products, arithmetic and copies ran while one was open for 9% -> 1% of each run, Pallas kernels for 0% -> 12%
where the time goes in v2:
time: 73.3 us; the launch traced here: 73.2 us
  Pallas kernels  31 us (42%)
  starting transfers between devices  23.2 us (32%)
  waiting for transfers between devices  17.5 us (24%)
  between operations  0.75 us (1%)
    pallas_call x10, Pallas kernels, kernel(): pl.pallas_call(body, out_shape=outs, in_specs=[SCALAR] * len(scalars) + [...  29.1 us
    ppermute x3, starting transfers between devices, local(): pieces = [lax.ppermute(x, 'brick', turn) for x, turn in zip(pieces, turns)]  7.89 us
    ppermute x3, waiting for transfers between devices, local(): pieces = [done] + [lax.ppermute(done, 'brick', turn) for turn in turns]  5.33 us
    ppermute x2, waiting for transfers between devices, around(): lax.ppermute(x, 'chan', [((i + over) % chans, i) for i in range(chans)])  5.08 us
    ppermute x3, starting transfers between devices, local(): pieces = [done] + [lax.ppermute(done, 'brick', turn) for turn in turns]  4.16 us
    ppermute x2, starting transfers between devices, around(): lax.ppermute(x, 'chan', [((i + over) % chans, i) for i in range(chans)])  3.88 us
    ppermute x2, starting transfers between devices, hop(): return lax.ppermute(x, ('brick', 'rep'), pairs)  3.65 us
    ppermute x3, waiting for transfers between devices, local(): pieces = [lax.ppermute(x, 'brick', turn) for x, turn in zip(pieces, turns)]  2.51 us
  transfers between devices with their start and end apart: 13, of which 8 were waited for; matrix products, arithmetic and copies ran while one was open for 1% of the time, Pallas kernels for 12%

profile of v2, /device:TPU:0, one launch (start us, length us, event | category | flops | bytes accessed | tf_op | source)
XLA Modules:
  0.0 73.2 jit_solution(16376062720211670721)
XLA Ops:
  0.6 0.0 copy-start.1
  0.6 0.0 copy-start
  0.7 0.0 copy-start.2
  0.7 0.0 copy-start.3
  0.7 1.9 %pack.1 = (bf16[128,768]{1,0:T(8,128)(2,1)}, bf16[128,768]{1,0:T(8,128)(2,1)}) custom-call(bf16[64,4608]{1,0:T(8,128)(2,1)} %own.1, bf16[64,4608]{1,0:T(8,128)(2,1)} %cotangent.3, s32[27,4608]{1,0:T(8,128)} %neighbours.1, bf16[64,4608]{1,0:T(8,128)(2,1)} %own.1, bf16[64,4608]{1,0:T(8,128)(2,1)} %cotangent.3, s32[27,4608]{1,0:T(8,128)} %neighbours.1), custom_call_target="tpu_custom_call" | custom-call | bytes 1048576 | tf_op jit(solution)/shard_map/pack/pallas_call | solution.py:105
  2.6 2.4 %collective-permute-start = (bf16[128,768]{1,0:T(8,128)(2,1)}, bf16[128,768]{1,0:T(8,128)(2,1)S(1)}, u32[]{:S(2)}, u32[]{:S(2)}) collective-permute-start(bf16[128,768]{1,0:T(8,128)(2,1)} %get-tuple-element.21), channel_id=1, source_target_pairs={{0,1},{1,4},{4,5},{5,8},{8,9},{9,12},{12,13},{2,3},{3,6},{6,7},{7,... | collective-permute-start | bytes 589832 | tf_op jit(solution)/shard_map/ppermute | solution.py:281
  4.9 1.3 %collective-permute-start.1 = (bf16[128,768]{1,0:T(8,128)(2,1)}, bf16[128,768]{1,0:T(8,128)(2,1)S(1)}, u32[]{:S(2)}, u32[]{:S(2)}) collective-permute-start(bf16[128,768]{1,0:T(8,128)(2,1)} %get-tuple-element.22), channel_id=1, source_target_pairs={{1,0},{4,1},{5,4},{8,5},{9,8},{12,9},{13,12},{3,2},{6,3},{7,6},{10... | collective-permute-start | bytes 589832 | tf_op jit(solution)/shard_map/ppermute | solution.py:281
  6.2 2.4 %collective-permute-start.3 = (bf16[64,4608]{1,0:T(8,128)(2,1)}, bf16[64,4608]{1,0:T(8,128)(2,1)S(1)}, u32[]{:S(2)}, u32[]{:S(2)}) collective-permute-start(bf16[64,4608]{1,0:T(8,128)(2,1)} %own.1), channel_id=1, source_target_pairs={{2,0},{0,2},{3,1},{1,3},{6,4},{4,6},{7,5},{5,7},{10,8},{8,10},{11,... | collective-permute-start | bytes 1769480 | tf_op jit(solution)/shard_map/ppermute | solution.py:295
  8.6 0.0 collective-permute-done.left
  8.6 2.0 %collective-permute-done.1.right = bf16[128,768]{1,0:T(8,128)(2,1)S(1)} collective-permute-done((bf16[128,768]{1,0:T(8,128)(2,1)}, bf16[128,768]{1,0:T(8,128)(2,1)S(1)}, u32[]{:S(2)}, u32[]{:S(2)}) %collective-permute-start.1) | collective-permute-done | bytes 196640 | tf_op jit(solution)/shard_map/ppermute | solution.py:281
  10.7 0.7 pad_maximum_fusion
  11.4 1.5 %collective-permute-start.2 = (bf16[64,1536]{1,0:T(8,128)(2,1)}, bf16[64,1536]{1,0:T(8,128)(2,1)S(1)}, u32[]{:S(2)}, u32[]{:S(2)}) collective-permute-start(bf16[64,1536]{1,0:T(8,128)(2,1)} %pad_maximum_fusion), channel_id=1, source_target_pairs={{2,0},{0,2},{3,1},{1,3},{6,4},{4,6},{7,5},{5,7},{10,8},{8,10},{11,... | collective-permute-start | bytes 589832 | tf_op jit(solution)/shard_map/ppermute | solution.py:295
  12.8 0.0 copy-done.3
  12.9 0.8 %weights.1 = (bf16[64,1728]{1,0:T(8,128)(2,1)S(1)}, bf16[64,1728]{1,0:T(8,128)(2,1)S(1)}, bf16[128,1792]{1,0:T(8,128)(2,1)S(1)}) custom-call(s32[1]{0:T(128)} %bitcast.turn, bf16[27,64,128]{2,1,0:T(8,128)(2,1)S(1)} %bitcast.8), custom_call_target="tpu_custom_call" | custom-call | bytes 1048576 | tf_op jit(solution)/shard_map/weights/pallas_call | solution.py:32
  13.6 0.0 copy-done.1
  13.6 0.0 copy-done.2
  13.7 6.6 %forward_own.1 = (f32[64,5376]{1,0:T(8,128)S(1)}, bf16[27,16,5376]{2,1,0:T(8,128)(2,1)S(1)}) custom-call(bf16[128,768]{1,0:T(8,128)(2,1)S(1)} %collective-permute-done.left, bf16[64,4608]{1,0:T(8,128)(2,1)S(1)} %copy-done.1, bf16[128,768]{1,0:T(8,128)(2,1)S(1)} %collective-permute-done.1.right, bf16[64,1728]{1,0:T(8,128)(2,1)S(1)} %get-tuple-element.24.weights, ...), custom_call_target="tpu_custom_call" | custom-call | flops 1019215872 | bytes 1048576 | tf_op jit(solution)/shard_map/forward_own/pallas_call | solution.py:32
  20.2 5.1 %collective-permute-done.2.ends = bf16[64,1536]{1,0:T(8,128)(2,1)S(1)} collective-permute-done((bf16[64,1536]{1,0:T(8,128)(2,1)}, bf16[64,1536]{1,0:T(8,128)(2,1)S(1)}, u32[]{:S(2)}, u32[]{:S(2)}) %collective-permute-start.2) | collective-permute-done | bytes 196640 | tf_op jit(solution)/shard_map/ppermute | solution.py:295
  25.3 0.0 collective-permute-done.3.middle.rest
  25.3 0.0 copy-done
  25.3 7.4 %forward_rest.1 = (bf16[64,4608]{1,0:T(8,128)(2,1)}, bf16[64,5376]{1,0:T(8,128)(2,1)S(1)}) custom-call(bf16[64,1536]{1,0:T(8,128)(2,1)S(1)} %collective-permute-done.2.ends, bf16[64,4608]{1,0:T(8,128)(2,1)S(1)} %collective-permute-done.3.middle.rest, bf16[64,1728]{1,0:T(8,128)(2,1)S(1)} %get-tuple-element.23.weights, ...), custom_call_target="tpu_custom_call" | custom-call | flops 1019215872 | bytes 1048576 | tf_op jit(solution)/shard_map/forward_rest/pallas_call | solution.py:32
  32.7 7.3 %grad_weight.1 = (f32[896,128]{1,0:T(8,128)S(1)}, bf16[896,128]{1,0:T(8,128)(2,1)S(1)}, bf16[9,64,5376]{2,1,0:T(8,128)(2,1)S(1)}) custom-call(s32[1]{0:T(128)} %bitcast.2.rep, bf16[64,5376]{1,0:T(8,128)(2,1)S(1)} %get-tuple-element.28.grad, bf16[27,16,5376]{2,1,0:T(8,128)(2,1)S(1)} %get-tuple-element.25.valid, bf16[64,4608]{1,0:T(8,128)(2,1)S(1)} %copy-done.1, ...), custom_call_target="tpu_custom_call" | custom-call | flops 2038431744 | bytes 1048576 | tf_op jit(solution)/shard_map/grad_weight/pallas_call | solution.py:32
  40.1 4.8 %grad_features.1 = (f32[64,4608]{1,0:T(8,128)S(1)}, bf16[64,4608]{1,0:T(8,128)(2,1)}) custom-call(bf16[9,64,5376]{2,1,0:T(8,128)(2,1)S(1)} %get-tuple-element.29.shifts, bf16[27,16,5376]{2,1,0:T(8,128)(2,1)S(1)} %get-tuple-element.25.valid, bf16[128,1792]{1,0:T(8,128)(2,1)S(1)} %get-tuple-element.30.weights), custom_call_target="tpu_custom_call" | custom-call | flops 2038431744 | bytes 1048576 | tf_op jit(solution)/shard_map/grad_features/pallas_call | solution.py:32
  44.8 2.4 %collective-permute-start.4 = (bf16[64,4608]{1,0:T(8,128)(2,1)}, bf16[64,4608]{1,0:T(8,128)(2,1)S(1)}, u32[]{:S(2)}, u32[]{:S(2)}) collective-permute-start(bf16[64,4608]{1,0:T(8,128)(2,1)} %get-tuple-element.32), channel_id=1, source_target_pairs={{0,2},{2,0},{1,3},{3,1},{4,6},{6,4},{5,7},{7,5},{8,10},{10,8},{9,1... | collective-permute-start | bytes 1769480 | tf_op jit(solution)/shard_map/ppermute | solution.py:362
  47.2 1.1 %collective-permute-start.5 = (bf16[896,128]{1,0:T(8,128)(2,1)S(1)}, bf16[896,128]{1,0:T(8,128)(2,1)S(1)}, u32[]{:S(2)}, u32[]{:S(2)}) collective-permute-start(bf16[896,128]{1,0:T(8,128)(2,1)S(1)} %get-tuple-element.34), channel_id=1, source_target_pairs={{0,1},{1,0},{2,3},{3,2},{4,5},{5,4},{6,7},{7,6},{8,9},{9,8},{10,11... | collective-permute-start | bytes 688136 | tf_op jit(solution)/shard_map/ppermute | solution.py:351
  48.3 1.1 %collective-permute-done.5.arrived = bf16[896,128]{1,0:T(8,128)(2,1)S(1)} collective-permute-done((bf16[896,128]{1,0:T(8,128)(2,1)S(1)}, bf16[896,128]{1,0:T(8,128)(2,1)S(1)}, u32[]{:S(2)}, u32[]{:S(2)}) %collective-permute-start.5) | collective-permute-done | bytes 229408 | tf_op jit(solution)/shard_map/ppermute | solution.py:351
  49.5 4.0 %collective-permute-start.6 = (bf16[224,128]{1,0:T(8,128)(2,1)S(1)}, bf16[224,128]{1,0:T(8,128)(2,1)S(1)}, u32[]{:S(2)}, u32[]{:S(2)}) collective-permute-start(bf16[224,128]{1,0:T(8,128)(2,1)S(1)} %get-tuple-element.36), channel_id=1, source_target_pairs={{0,4},{4,8},{8,12},{12,0},{1,5},{5,9},{9,13},{13,1},{2,6},{6,10},{... | collective-permute-start | bytes 172040 | tf_op jit(solution)/shard_map/ppermute | solution.py:378
  53.5 1.4 %collective-permute-start.7 = (bf16[224,128]{1,0:T(8,128)(2,1)S(1)}, bf16[224,128]{1,0:T(8,128)(2,1)S(1)}, u32[]{:S(2)}, u32[]{:S(2)}) collective-permute-start(bf16[224,128]{1,0:T(8,128)(2,1)S(1)} %get-tuple-element.37), channel_id=1, source_target_pairs={{0,8},{4,12},{8,0},{12,4},{1,9},{5,13},{9,1},{13,5},{2,10},{6,14},... | collective-permute-start | bytes 172040 | tf_op jit(solution)/shard_map/ppermute | solution.py:378
  54.9 2.5 %collective-permute-start.8 = (bf16[224,128]{1,0:T(8,128)(2,1)S(1)}, bf16[224,128]{1,0:T(8,128)(2,1)S(1)}, u32[]{:S(2)}, u32[]{:S(2)}) collective-permute-start(bf16[224,128]{1,0:T(8,128)(2,1)S(1)} %get-tuple-element.38), channel_id=1, source_target_pairs={{0,12},{4,0},{8,4},{12,8},{1,13},{5,1},{9,5},{13,9},{2,14},{6,2},{... | collective-permute-start | bytes 172040 | tf_op jit(solution)/shard_map/ppermute | solution.py:378
  57.4 0.0 collective-permute-done.6.rest_0_
  57.4 2.5 %collective-permute-done.7.rest_1_ = bf16[224,128]{1,0:T(8,128)(2,1)S(1)} collective-permute-done((bf16[224,128]{1,0:T(8,128)(2,1)S(1)}, bf16[224,128]{1,0:T(8,128)(2,1)S(1)}, u32[]{:S(2)}, u32[]{:S(2)}) %collective-permute-start.7) | collective-permute-done | bytes 57376 | tf_op jit(solution)/shard_map/ppermute | solution.py:378
  59.9 0.0 collective-permute-done.8.rest_2_
  60.0 3.5 %collective-permute-start.11 = (bf16[224,128]{1,0:T(8,128)(2,1)S(1)}, bf16[224,128]{1,0:T(8,128)(2,1)S(1)}, u32[]{:S(2)}, u32[]{:S(2)}) collective-permute-start(bf16[224,128]{1,0:T(8,128)(2,1)S(1)} %merge.1.rest_0_), channel_id=1, source_target_pairs={{0,12},{4,0},{8,4},{12,8},{1,13},{5,1},{9,5},{13,9},{2,14},{6,2},{... | collective-permute-start | bytes 172040 | tf_op jit(solution)/shard_map/ppermute | solution.py:380
  63.5 0.0 collective-permute-start.10
  63.5 0.6 collective-permute-start.9
  64.1 1.2 %collective-permute-done.11.rest_3_ = bf16[224,128]{1,0:T(8,128)(2,1)S(1)} collective-permute-done((bf16[224,128]{1,0:T(8,128)(2,1)S(1)}, bf16[224,128]{1,0:T(8,128)(2,1)S(1)}, u32[]{:S(2)}, u32[]{:S(2)}) %collective-permute-start.11) | collective-permute-done | bytes 57376 | tf_op jit(solution)/shard_map/ppermute | solution.py:380
  65.3 3.2 %collective-permute-done.10.rest_2_ = bf16[224,128]{1,0:T(8,128)(2,1)S(1)} collective-permute-done((bf16[224,128]{1,0:T(8,128)(2,1)S(1)}, bf16[224,128]{1,0:T(8,128)(2,1)S(1)}, u32[]{:S(2)}, u32[]{:S(2)}) %collective-permute-start.10) | collective-permute-done | bytes 57376 | tf_op jit(solution)/shard_map/ppermute | solution.py:380
  68.6 0.9 %collective-permute-done.9.rest_1_ = bf16[224,128]{1,0:T(8,128)(2,1)S(1)} collective-permute-done((bf16[224,128]{1,0:T(8,128)(2,1)S(1)}, bf16[224,128]{1,0:T(8,128)(2,1)S(1)}, u32[]{:S(2)}, u32[]{:S(2)}) %collective-permute-start.9) | collective-permute-done | bytes 57376 | tf_op jit(solution)/shard_map/ppermute | solution.py:380
  69.5 0.1 collective-permute-start.12
  69.6 1.5 %collective-permute-done.12.other = bf16[896,128]{1,0:T(8,128)(2,1)S(1)} collective-permute-done((bf16[896,128]{1,0:T(8,128)(2,1)S(1)}, bf16[896,128]{1,0:T(8,128)(2,1)S(1)}, u32[]{:S(2)}, u32[]{:S(2)}) %collective-permute-start.12) | collective-permute-done | bytes 229408 | tf_op jit(solution)/shard_map/ppermute | solution.py:388
  71.0 1.1 %join.1 = f32[1728,128]{1,0:T(8,128)} custom-call(s32[1]{0:T(128)} %bitcast.2.rep, s32[1]{0:T(128)} %bitcast.3.turn, bf16[896,128]{1,0:T(8,128)(2,1)S(1)} %gather.1.side, bf16[896,128]{1,0:T(8,128)(2,1)S(1)} %collective-permute-done.12.other), custom_call_target="tpu_custom_call" | custom-call | bytes 1048576 | tf_op jit(solution)/shard_map/join/pallas_call | solution.py:32
  72.2 0.0 collective-permute-done.4.rest_0_
  72.2 1.0 %add.6 = bf16[64,4608]{1,0:T(8,128)(2,1)} custom-call(bf16[64,4608]{1,0:T(8,128)(2,1)S(1)} %copy-done, f32[64,4608]{1,0:T(8,128)S(1)} %get-tuple-element.31.own, bf16[64,4608]{1,0:T(8,128)(2,1)S(1)} %collective-permute-done.4.rest_0_), custom_call_target="tpu_custom_call" | custom-call | bytes 1048576 | tf_op jit(solution)/shard_map/add/pallas_call | solution.py:32
  (5 shorter events, 0.1 us)
Async XLA Ops:
  0.6 13.0 %copy-start.1 = (bf16[64,4608]{1,0:T(8,128)(2,1)S(1)}, bf16[64,4608]{1,0:T(8,128)(2,1)}, u32[]{:S(2)}) copy-start(bf16[64,4608]{1,0:T(8,128)(2,1)} %own.1) | copy-start | bytes 1769476
  0.6 24.7 %copy-start = (bf16[64,4608]{1,0:T(8,128)(2,1)S(1)}, bf16[64,4608]{1,0:T(8,128)(2,1)}, u32[]{:S(2)}) copy-start(bf16[64,4608]{1,0:T(8,128)(2,1)} %cotangent.3) | copy-start | bytes 1769476
  0.7 13.0 %copy-start.2 = (s32[27,4608]{1,0:T(8,128)S(1)}, s32[27,4608]{1,0:T(8,128)}, u32[]{:S(2)}) copy-start(s32[27,4608]{1,0:T(8,128)} %neighbours.1) | copy-start | bytes 1492996
  0.7 12.2 %copy-start.3 = (bf16[27,128,64]{1,2,0:T(8,128)(2,1)S(1)}, bf16[27,128,64]{1,2,0:T(8,128)(2,1)}, u32[]{:S(2)}) copy-start(bf16[27,128,64]{1,2,0:T(8,128)(2,1)} %param.5) | copy-start | bytes 1327108
  2.6 6.1 %collective-permute-start = (bf16[128,768]{1,0:T(8,128)(2,1)}, bf16[128,768]{1,0:T(8,128)(2,1)S(1)}, u32[]{:S(2)}, u32[]{:S(2)}) collective-permute-start(bf16[128,768]{1,0:T(8,128)(2,1)} %get-tuple-element.21), channel_id=1, source_target_pairs={{0,1},{1,4},{4,5},{5,8},{8,9},{9,12},{12,13},{2,3},{3,6},{6,7},{7,... | collective-permute-start | bytes 589832 | tf_op jit(solution)/shard_map/ppermute | solution.py:281
  4.9 5.7 %collective-permute-start.1 = (bf16[128,768]{1,0:T(8,128)(2,1)}, bf16[128,768]{1,0:T(8,128)(2,1)S(1)}, u32[]{:S(2)}, u32[]{:S(2)}) collective-permute-start(bf16[128,768]{1,0:T(8,128)(2,1)} %get-tuple-element.22), channel_id=1, source_target_pairs={{1,0},{4,1},{5,4},{8,5},{9,8},{12,9},{13,12},{3,2},{6,3},{7,6},{10... | collective-permute-start | bytes 589832 | tf_op jit(solution)/shard_map/ppermute | solution.py:281
  6.2 19.1 %collective-permute-start.3 = (bf16[64,4608]{1,0:T(8,128)(2,1)}, bf16[64,4608]{1,0:T(8,128)(2,1)S(1)}, u32[]{:S(2)}, u32[]{:S(2)}) collective-permute-start(bf16[64,4608]{1,0:T(8,128)(2,1)} %own.1), channel_id=1, source_target_pairs={{2,0},{0,2},{3,1},{1,3},{6,4},{4,6},{7,5},{5,7},{10,8},{8,10},{11,... | collective-permute-start | bytes 1769480 | tf_op jit(solution)/shard_map/ppermute | solution.py:295
  11.4 13.9 %collective-permute-start.2 = (bf16[64,1536]{1,0:T(8,128)(2,1)}, bf16[64,1536]{1,0:T(8,128)(2,1)S(1)}, u32[]{:S(2)}, u32[]{:S(2)}) collective-permute-start(bf16[64,1536]{1,0:T(8,128)(2,1)} %pad_maximum_fusion), channel_id=1, source_target_pairs={{2,0},{0,2},{3,1},{1,3},{6,4},{4,6},{7,5},{5,7},{10,8},{8,10},{11,... | collective-permute-start | bytes 589832 | tf_op jit(solution)/shard_map/ppermute | solution.py:295
  44.8 27.3 %collective-permute-start.4 = (bf16[64,4608]{1,0:T(8,128)(2,1)}, bf16[64,4608]{1,0:T(8,128)(2,1)S(1)}, u32[]{:S(2)}, u32[]{:S(2)}) collective-permute-start(bf16[64,4608]{1,0:T(8,128)(2,1)} %get-tuple-element.32), channel_id=1, source_target_pairs={{0,2},{2,0},{1,3},{3,1},{4,6},{6,4},{5,7},{7,5},{8,10},{10,8},{9,1... | collective-permute-start | bytes 1769480 | tf_op jit(solution)/shard_map/ppermute | solution.py:362
  47.2 2.2 %collective-permute-start.5 = (bf16[896,128]{1,0:T(8,128)(2,1)S(1)}, bf16[896,128]{1,0:T(8,128)(2,1)S(1)}, u32[]{:S(2)}, u32[]{:S(2)}) collective-permute-start(bf16[896,128]{1,0:T(8,128)(2,1)S(1)} %get-tuple-element.34), channel_id=1, source_target_pairs={{0,1},{1,0},{2,3},{3,2},{4,5},{5,4},{6,7},{7,6},{8,9},{9,8},{10,11... | collective-permute-start | bytes 688136 | tf_op jit(solution)/shard_map/ppermute | solution.py:351
  49.5 7.9 %collective-permute-start.6 = (bf16[224,128]{1,0:T(8,128)(2,1)S(1)}, bf16[224,128]{1,0:T(8,128)(2,1)S(1)}, u32[]{:S(2)}, u32[]{:S(2)}) collective-permute-start(bf16[224,128]{1,0:T(8,128)(2,1)S(1)} %get-tuple-element.36), channel_id=1, source_target_pairs={{0,4},{4,8},{8,12},{12,0},{1,5},{5,9},{9,13},{13,1},{2,6},{6,10},{... | collective-permute-start | bytes 172040 | tf_op jit(solution)/shard_map/ppermute | solution.py:378
  53.5 6.4 %collective-permute-start.7 = (bf16[224,128]{1,0:T(8,128)(2,1)S(1)}, bf16[224,128]{1,0:T(8,128)(2,1)S(1)}, u32[]{:S(2)}, u32[]{:S(2)}) collective-permute-start(bf16[224,128]{1,0:T(8,128)(2,1)S(1)} %get-tuple-element.37), channel_id=1, source_target_pairs={{0,8},{4,12},{8,0},{12,4},{1,9},{5,13},{9,1},{13,5},{2,10},{6,14},... | collective-permute-start | bytes 172040 | tf_op jit(solution)/shard_map/ppermute | solution.py:378
  54.9 5.0 %collective-permute-start.8 = (bf16[224,128]{1,0:T(8,128)(2,1)S(1)}, bf16[224,128]{1,0:T(8,128)(2,1)S(1)}, u32[]{:S(2)}, u32[]{:S(2)}) collective-permute-start(bf16[224,128]{1,0:T(8,128)(2,1)S(1)} %get-tuple-element.38), channel_id=1, source_target_pairs={{0,12},{4,0},{8,4},{12,8},{1,13},{5,1},{9,5},{13,9},{2,14},{6,2},{... | collective-permute-start | bytes 172040 | tf_op jit(solution)/shard_map/ppermute | solution.py:378
  60.0 5.3 %collective-permute-start.11 = (bf16[224,128]{1,0:T(8,128)(2,1)S(1)}, bf16[224,128]{1,0:T(8,128)(2,1)S(1)}, u32[]{:S(2)}, u32[]{:S(2)}) collective-permute-start(bf16[224,128]{1,0:T(8,128)(2,1)S(1)} %merge.1.rest_0_), channel_id=1, source_target_pairs={{0,12},{4,0},{8,4},{12,8},{1,13},{5,1},{9,5},{13,9},{2,14},{6,2},{... | collective-permute-start | bytes 172040 | tf_op jit(solution)/shard_map/ppermute | solution.py:380
  63.5 5.1 %collective-permute-start.10 = (bf16[224,128]{1,0:T(8,128)(2,1)S(1)}, bf16[224,128]{1,0:T(8,128)(2,1)S(1)}, u32[]{:S(2)}, u32[]{:S(2)}) collective-permute-start(bf16[224,128]{1,0:T(8,128)(2,1)S(1)} %merge.1.rest_0_), channel_id=1, source_target_pairs={{0,8},{4,12},{8,0},{12,4},{1,9},{5,13},{9,1},{13,5},{2,10},{6,14},... | collective-permute-start | bytes 172040 | tf_op jit(solution)/shard_map/ppermute | solution.py:380
  63.5 6.0 %collective-permute-start.9 = (bf16[224,128]{1,0:T(8,128)(2,1)S(1)}, bf16[224,128]{1,0:T(8,128)(2,1)S(1)}, u32[]{:S(2)}, u32[]{:S(2)}) collective-permute-start(bf16[224,128]{1,0:T(8,128)(2,1)S(1)} %merge.1.rest_0_), channel_id=1, source_target_pairs={{0,4},{4,8},{8,12},{12,0},{1,5},{5,9},{9,13},{13,1},{2,6},{6,10},{... | collective-permute-start | bytes 172040 | tf_op jit(solution)/shard_map/ppermute | solution.py:380
  69.5 1.6 %collective-permute-start.12 = (bf16[896,128]{1,0:T(8,128)(2,1)S(1)}, bf16[896,128]{1,0:T(8,128)(2,1)S(1)}, u32[]{:S(2)}, u32[]{:S(2)}) collective-permute-start(bf16[896,128]{1,0:T(8,128)(2,1)S(1)} %gather.1.side), channel_id=1, source_target_pairs={{0,1},{1,0},{2,3},{3,2},{4,5},{5,4},{6,7},{7,6},{8,9},{9,8},{10,11... | collective-permute-start | bytes 688136 | tf_op jit(solution)/shard_map/ppermute | solution.py:388

commit v3 on v2

v3 whole, which is shorter than its diff:
```python
import functools

import jax
import jax.numpy as jnp
from jax import lax
from jax.experimental import pallas as pl
from jax.experimental.pallas import tpu as pltpu
from jax.sharding import PartitionSpec as P

EDGE = 16
FACE = EDGE * EDGE
TAPS = 27
HALO = 384
FAR = 2 * HALO
ROWS = 16
GROUP = 4
WIDTH = 768
LATER = 25 * 10**7
LINE = ("brick", "chan", "rep")
MIB = 1024 * 1024
F32, BF16 = jnp.float32, jnp.bfloat16

STEPS = [(k // 3 - 1) * EDGE + k % 3 - 1 for k in range(9)]

HERE = pl.BlockSpec(memory_space=pltpu.VMEM)
SCALAR = pl.BlockSpec(memory_space=pltpu.SMEM)


def kernel(body, name, outs, args, scalars=(), scratch=(), aliases={}, limit=8, flops=0):
    single = not isinstance(outs, (tuple, list))
    return pl.pallas_call(
        body,
        out_shape=outs,
        in_specs=[SCALAR] * len(scalars) + [HERE] * len(args),
        out_specs=HERE if single else [HERE] * len(outs),
        scratch_shapes=list(scratch),
        input_output_aliases={len(scalars) + i: o for i, o in aliases.items()},
        compiler_params=pltpu.CompilerParams(vmem_limit_bytes=limit * MIB),
        cost_estimate=pl.CostEstimate(flops=flops, bytes_accessed=MIB, transcendentals=0),
        name=name,
    )(*(x[None] for x in scalars), *args)


def after(body, at):
    def ordered(*refs):
        body(*refs[:at], *refs[at + 1 :])

    return ordered


def shape(dims, kind=BF16):
    return jax.ShapeDtypeStruct(dims, kind)


def shift(shifts, low, high):
    for at in range(0, shifts.shape[1], ROWS):
        rows = pl.ds(at, ROWS)
        for j, step in enumerate(STEPS):
            if j != 4:
                shifts[j, rows, low:high] = shifts[4, rows, low + step : high + step]


def masked(shifts, valid, tap, at_shift, at_valid, width):
    keep = valid[tap, :, pl.ds(at_valid, width)]
    begin = pl.multiple_of(at_shift + (tap // 9 - 1) * FACE, 128)
    return [
        shifts[tap % 9, at : at + ROWS, pl.ds(begin, width)] * keep
        for at in range(0, shifts.shape[1], ROWS)
    ]


def groups():
    return [range(first, min(first + GROUP, TAPS)) for first in range(0, TAPS, GROUP)]


def product(weights, shifts, valid, at_shift, at_valid, width, taps_of):
    channels = shifts.shape[1]
    total = None
    for group in groups():
        rows = []
        for tap in group:
            rows += masked(shifts, valid, taps_of(tap), at_shift, at_valid, width)
        part = jnp.dot(
            weights[:, group[0] * channels : (group[-1] + 1) * channels],
            jnp.concatenate(rows, axis=0),
            preferred_element_type=F32,
        )
        total = part if total is None else total + part
    return total


def pack_body(rep, *refs):
    ends, outs = refs[:6], refs[6:]
    for at, (features, cotangent, neighbours) in enumerate((ends[:3], ends[3:])):
        share = features.shape[0]
        kept = (neighbours[...] >= 0).astype(F32)
        kept = jnp.concatenate([kept, jnp.zeros((32 - TAPS, HALO), F32)], axis=0).astype(BF16)

        def fill(out):
            out[...] = jnp.zeros_like(out)
            out[:share, :] = features[...]
            out[share : 2 * share, :HALO] = cotangent[...]
            out[share : share + 32, HALO:] = kept

        pl.when(rep[0] == at)(functools.partial(fill, outs[0]))
        pl.when(rep[0] != at)(functools.partial(fill, outs[1]))


def pack(rep, features, cotangent, neighbours):
    share, sites = features.shape

    def end(rows, width, at):
        return pl.BlockSpec((rows, width), lambda i: (0, at * (sites // width - 1)))

    rows = share + max(share, 32)
    return pl.pallas_call(
        pack_body,
        grid=(1,),
        out_shape=[shape((rows, FAR))] * 2,
        in_specs=[SCALAR]
        + [
            spec
            for at in (1, 0)
            for spec in (end(share, FAR, at), end(share, HALO, at), end(TAPS, HALO, at))
        ],
        out_specs=[pl.BlockSpec((rows, FAR), lambda i: (0, 0))] * 2,
        cost_estimate=pl.CostEstimate(flops=0, bytes_accessed=MIB, transcendentals=0),
        name="pack",
    )(rep[None], *(features, cotangent, neighbours) * 2)


def ends_body(rep, core, line, before, behind, both):
    share = both.shape[0]

    def fill(first, second):
        before[...] = first[...]
        behind[...] = second[...]
        both[:, :FAR] = first[:share, :]
        both[:, FAR:] = second[:share, :]

    pl.when(rep[0] == 0)(functools.partial(fill, line, core))
    pl.when(rep[0] != 0)(functools.partial(fill, core, line))


def prepare_body(
    turn, by_out, features, neighbours, own, rest, by_in, shifts, valid, flat, kept
):
    total = by_out.shape[2]
    share, sites = features.shape
    flat[...] = jnp.zeros_like(flat)
    for group in groups():
        taps = []
        for tap in group:
            ring = pltpu.roll(by_out[tap].astype(F32), turn[0], 1)
            flat[tap * share : (tap + 1) * share, :] = ring
            taps.append(ring)
        first, last = group[0], group[-1] + 1
        own[:, first * share : last * share] = jnp.concatenate(
            [x[:, :share] for x in taps], axis=1
        ).astype(BF16)
        left = total - share
        rest[:, first * left : last * left] = jnp.concatenate(
            [x[:, share:] for x in taps], axis=1
        ).astype(BF16)
    by_in[...] = flat[...].T.astype(BF16)
    shifts[4, :, FAR : FAR + sites] = features[...]
    shift(shifts, FAR + 128, FAR + sites - 128)
    kept[...] = (neighbours[...] >= 0).astype(F32)
    for tap in range(TAPS):
        valid[tap, :, HALO : HALO + sites] = jnp.broadcast_to(
            kept[tap : tap + 1, :], (ROWS, sites)
        ).astype(BF16)


def own_body(left, right, weights, shifts_in, valid_in, begun, shifts, valid, kept):
    del shifts_in, valid_in
    share = begun.shape[0]
    far = shifts.shape[2] - FAR
    for side, at, start in ((left, 0, 128), (right, 1, far - 128)):
        shifts[4, :, at * far : at * far + FAR] = side[:share, :]
        shift(shifts, start, start + FAR)
        kept[...] = side[share : share + 32, HALO:].astype(F32)
        begin = at * (valid.shape[2] - HALO)
        for tap in range(TAPS):
            valid[tap, :, begin : begin + HALO] = jnp.broadcast_to(
                kept[tap : tap + 1, :], (ROWS, HALO)
            ).astype(BF16)

    def block(j, carry):
        start = pl.multiple_of(j * WIDTH, 128)
        begun[:, pl.ds(start, WIDTH)] = product(
            weights, shifts, valid, start + HALO, start, WIDTH, lambda tap: tap
        )
        return carry

    lax.fori_loop(0, begun.shape[1] // WIDTH, block, 0)


def rest_body(
    ends, middle, weights, valid, begun, left, features, right, cotangent, output, grad, shifts, kept
):
    share, sites = features.shape
    shifts[4, :, :FAR] = ends[:, :FAR]
    shifts[4, :, FAR : FAR + sites] = middle[...]
    shifts[4, :, FAR + sites :] = ends[:, FAR:]
    shift(shifts, 128, shifts.shape[2] - 128)
    grad[:, :HALO] = left[share : 2 * share, :HALO]
    grad[:, HALO : HALO + sites] = cotangent[...]
    grad[:, HALO + sites :] = right[share : 2 * share, :HALO]
    kept[:, HALO : HALO + sites] = features[...]

    def block(j, carry):
        start = pl.multiple_of(j * WIDTH, 128)
        here = pl.ds(start, WIDTH)
        hidden = begun[:, here] + product(
            weights, shifts, valid, start + HALO, start, WIDTH, lambda tap: tap
        )
        sigma = jax.nn.sigmoid(hidden)
        kept[:, here] = (kept[:, here].astype(F32) + hidden * sigma).astype(BF16)
        grad[:, here] = (
            grad[:, here].astype(F32) * sigma * (1.0 + hidden * (1.0 - sigma))
        ).astype(BF16)
        return carry

    lax.fori_loop(0, begun.shape[1] // WIDTH, block, 0)
    output[...] = kept[:, HALO : HALO + sites]


def weight_body(half, rep, grad, valid, own, rest, kept, sent, shifts, total):
    share, sites = own.shape
    shifts[4] = grad[...]
    shift(shifts, 128, shifts.shape[2] - 128)
    total[...] = jnp.zeros_like(total)

    def block(j, carry):
        start = pl.multiple_of(j * WIDTH, 128)
        here = pl.ds(start, WIDTH)
        features = jnp.concatenate([own[:, here], rest[:, here]], axis=0).T
        for group in groups():
            rows = []
            for tap in group:
                rows += masked(shifts, valid, TAPS - 1 - tap, start + HALO, start + HALO, WIDTH)
            total[group[0] * share : (group[-1] + 1) * share, :] += jnp.dot(
                jnp.concatenate(rows, axis=0), features, preferred_element_type=F32
            )
        return carry

    lax.fori_loop(0, sites // WIDTH, block, 0)
    mine = rep[0]
    kept[...] = total[pl.ds(pl.multiple_of(mine * half, ROWS), half), :]
    sent[...] = total[pl.ds(pl.multiple_of((1 - mine) * half, ROWS), half), :].astype(BF16)


def feature_body(part, shifts, valid, weights, *refs):
    own, rest = refs[-2:]
    share, sites = own.shape
    begin = part * sites // 2

    def block(j, carry):
        start = pl.multiple_of(begin + j * WIDTH, 128)
        here = pl.ds(start, WIDTH)
        at = pl.multiple_of(start + HALO, 128)
        total = product(weights, shifts, valid, at, at, WIDTH, lambda tap: TAPS - 1 - tap)
        own[:, here] = total[:share]
        rest[:, here] = total[share:].astype(BF16)
        return carry

    lax.fori_loop(0, sites // 2 // WIDTH, block, 0)


def split_body(brick, kept, arrived, mine, sent):
    size = mine.shape[0]
    at = brick[0] % 2
    mine_rows = pl.ds(pl.multiple_of(at * size, ROWS), size)
    sent_rows = pl.ds(pl.multiple_of((1 - at) * size, ROWS), size)
    mine[...] = kept[mine_rows, :] + arrived[mine_rows, :].astype(F32)
    sent[...] = (kept[sent_rows, :] + arrived[sent_rows, :].astype(F32)).astype(BF16)


def merge_body(mine, other, out):
    out[...] = (mine[...].astype(F32) + other[...].astype(F32)).astype(BF16)


def gather_body(brick, mine, other, side):
    size = mine.shape[0]
    at = brick[0] % 2
    side[pl.ds(pl.multiple_of(at * size, ROWS), size), :] = mine[...]
    side[pl.ds(pl.multiple_of((1 - at) * size, ROWS), size), :] = other[...]


def join_body(half, rep, turn, side, other, out, both):
    mine = rep[0]
    both[pl.ds(pl.multiple_of(mine * half, ROWS), half), :] = side[...]
    both[pl.ds(pl.multiple_of((1 - mine) * half, ROWS), half), :] = other[...]
    out[...] = pltpu.roll(both[: out.shape[0], :].astype(F32), turn[0], 1)


def add_body(cotangent, own, *rest):
    *terms, out = rest
    total = cotangent[...].astype(F32) + own[...]
    for term in terms:
        total += term[...].astype(F32)
    out[...] = total.astype(BF16)


def line_swap(x):
    count = lax.axis_size(("brick", "rep"))
    pairs = [p for i in range(1, count - 1, 2) for p in ((i, i + 1), (i + 1, i))]
    return lax.ppermute(x, ("brick", "rep"), pairs)


def local(features, conv_weight, neighbours, cotangent):
    share, sites = features.shape
    total = conv_weight.shape[1]
    left = total - share
    chans, bricks, reps = (lax.axis_size(axis) for axis in ("chan", "brick", "rep"))
    chan, brick, rep = (lax.axis_index(axis) for axis in ("chan", "brick", "rep"))
    margin = sites + 2 * HALO
    flops = 2 * TAPS * share * sites

    def around(x):
        return [
            lax.ppermute(x, "chan", [((i + over) % chans, i) for i in range(chans)])
            for over in range(1, chans)
        ]

    def stack(parts):
        return parts[0] if len(parts) == 1 else jnp.concatenate(parts, axis=0)

    assert reps == 2
    swap = [(0, 1), (1, 0)]
    rest = stack(around(features))
    to_core, to_line = pack(rep, features, cotangent, neighbours)
    line = line_swap(to_line)
    core = lax.ppermute(to_core, "rep", swap)
    lanes = -(-TAPS * share // 128) * 128
    own_weights, rest_weights, by_in, shifts, valid = kernel(
        prepare_body,
        "prepare",
        [
            shape((share, TAPS * share)),
            shape((share, TAPS * left)),
            shape((total, lanes)),
            shape((9, share, sites + 2 * FAR)),
            shape((TAPS, ROWS, margin)),
        ],
        [jnp.transpose(conv_weight, (0, 2, 1)), features, neighbours],
        scalars=[(total - chan * share) % total],
        scratch=[pltpu.VMEM((lanes, total), F32), pltpu.VMEM((TAPS, sites), F32)],
    )
    before, behind, both = kernel(
        after(ends_body, 1),
        "ends",
        [shape(core.shape), shape(core.shape), shape((share, 2 * FAR))],
        [own_weights, core, line],
        scalars=[rep],
    )
    ends = stack(around(both))

    begun, _, valid = kernel(
        own_body,
        "forward_own",
        [shape((share, margin), F32), shape(shifts.shape), shape(valid.shape)],
        [before, behind, own_weights, shifts, valid],
        scratch=[pltpu.VMEM((32, HALO), F32)],
        aliases={3: 1, 4: 2},
    )
    output, grad = kernel(
        rest_body,
        "forward_rest",
        [shape((share, sites)), shape((share, margin))],
        [ends, rest, rest_weights, valid, begun, before, features, behind, cotangent],
        scratch=[
            pltpu.VMEM((9, left, sites + 2 * FAR), BF16),
            pltpu.VMEM((share, margin), BF16),
        ],
        limit=24,
        flops=flops * left,
    )

    piece = -(-TAPS * share // (reps * bricks * ROWS)) * ROWS
    half = piece * bricks
    kept, sent, shifts = kernel(
        functools.partial(weight_body, half),
        "grad_weight",
        [shape((half, total), F32), shape((half, total)), shape((9, share, margin))],
        [grad, valid, features, rest],
        scalars=[rep],
        scratch=[pltpu.VMEM((reps * half, total), F32)],
        limit=12,
        flops=flops * total,
    )
    arrived = lax.ppermute(sent, "rep", swap)

    def feature_part(part, first, so_far):
        return kernel(
            after(functools.partial(feature_body, part), 0),
            "grad_features_%d" % part,
            [shape((share, sites), F32), shape((left, sites))],
            [first, shifts, valid, by_in, *so_far],
            aliases={4 + i: i for i in range(len(so_far))},
            limit=12,
            flops=flops * total // 2,
        )

    parts = feature_part(0, kept, [])
    size = half // 2
    mine, sent = kernel(
        after(split_body, 1),
        "split",
        [shape((size, total), F32), shape((size, total))],
        [parts[0], kept, arrived],
        scalars=[brick],
        flops=LATER,
    )
    pairs = [(i, i ^ 1) for i in range(bricks)]
    arrived = lax.ppermute(sent, "brick", pairs)
    own, other = feature_part(1, mine, parts)
    terms = [
        lax.ppermute(
            other if left == share else other[(over - 1) * share : over * share],
            "chan",
            [(i, (i + over) % chans) for i in range(chans)],
        )
        for over in range(1, chans)
    ]
    mine = kernel(
        after(merge_body, 0),
        "merge_1",
        shape((size, total)),
        [own, mine, arrived],
        flops=LATER,
    )
    step = 2
    while step < bricks:
        other = lax.ppermute(mine, "brick", [(i, i ^ step) for i in range(bricks)])
        step *= 2
        mine = kernel(
            merge_body, "merge_%d" % step, shape((size, total)), [mine, other], flops=LATER
        )
    other = lax.ppermute(mine, "brick", pairs)
    side = kernel(
        gather_body, "gather", shape((half, total)), [mine, other], scalars=[brick], flops=LATER
    )
    other = lax.ppermute(side, "rep", swap)
    grad_weight = kernel(
        functools.partial(join_body, half),
        "join",
        shape((TAPS * share, total), F32),
        [side, other],
        scalars=[rep, chan * share],
        scratch=[pltpu.VMEM((reps * half, total), BF16)],
        flops=LATER,
    )
    grad_features = kernel(add_body, "add", shape((share, sites)), [cotangent, own, *terms])
    grad_weight = jnp.transpose(grad_weight.reshape(TAPS, share, total), (0, 2, 1))
    return output, grad_features, grad_weight


def solution(mesh):
    return jax.shard_map(
        local,
        mesh=mesh,
        in_specs=(
            P("chan", ("scene", "brick", "rep")),
            P(None, None, "chan"),
            P(None, ("scene", "brick", "rep")),
            P("chan", ("scene", "brick", "rep")),
        ),
        out_specs=(
            P("chan", ("scene", "brick", "rep")),
            P("chan", ("scene", "brick", "rep")),
            P("scene", None, "chan"),
        ),
        check_vma=False,
    )
```

time: 73.3 us -> 68.3 us (0.932)
  starting transfers between devices: 23.2 us -> 11.1 us
  local copies, waits for them, and re-layouts: 0.03 us -> 10.8 us
  waiting for transfers between devices: 17.5 us -> 15.8 us
  Pallas kernels: 31 us -> 29.4 us
    unnamed x8 -> x20, local copies, waits for them, and re-layouts: 0.02 us -> 10.8 us
    ppermute x9 -> x6, starting transfers between devices: 18.1 us -> 7.79 us  [the longest x1 2.84 us: local(): other = lax.ppermute(mine, 'brick', [(i, i ^ step) for i in range(bricks)])]
    pallas_call x10 -> x13, Pallas kernels: 29.1 us -> 27.7 us  [kernel(): pl.pallas_call(body, out_shape=outs, in_specs=[SCALAR] * len(scalars) + [...]
    ppermute x1, waiting for transfers between devices: 1.12 us -> 0.01 us  [local(): arrived = lax.ppermute(sent, 'rep', swap)]
    ppermute x1, starting transfers between devices: 1.13 us -> 0.11 us  [local(): arrived = lax.ppermute(sent, 'rep', swap)]
    ppermute x2, waiting for transfers between devices: 5.08 us -> 4.2 us  [around(): lax.ppermute(x, 'chan', [((i + over) % chans, i) for i in range(chans)])]
    ppermute x2, starting transfers between devices: 3.88 us -> 3.1 us  [around(): lax.ppermute(x, 'chan', [((i + over) % chans, i) for i in range(chans)])]
    ppermute x9 -> x6, waiting for transfers between devices: 9.88 us -> 10.1 us  [the longest x1 5.47 us: local(): other = lax.ppermute(mine, 'brick', [(i, i ^ step) for i in range(bricks)])]
  transfers between devices with their start and end apart: 13 -> 10, of which waited for: 8 -> 5; matrix products, arithmetic and copies ran while one was open for 1% -> 0% of each run, Pallas kernels for 12% -> 21%
where the time goes in v3:
time: 68.3 us; the launch traced here: 68 us
  Pallas kernels  29.4 us (43%)
  waiting for transfers between devices  15.8 us (23%)
  starting transfers between devices  11.1 us (16%)
  local copies, waits for them, and re-layouts  10.8 us (16%)
  between operations  0.79 us (1%)
    pallas_call x13, Pallas kernels, kernel(): pl.pallas_call(body, out_shape=outs, in_specs=[SCALAR] * len(scalars) + [...  27.7 us
    unnamed x20, local copies, waits for them, and re-layouts  10.8 us
    ppermute x1, waiting for transfers between devices, local(): other = lax.ppermute(mine, 'brick', [(i, i ^ step) for i in range(bricks)])  5.47 us
    ppermute x2, waiting for transfers between devices, around(): lax.ppermute(x, 'chan', [((i + over) % chans, i) for i in range(chans)])  4.2 us
    ppermute x1, waiting for transfers between devices, local(): other = lax.ppermute(mine, 'brick', pairs)  4.14 us
    ppermute x2, starting transfers between devices, around(): lax.ppermute(x, 'chan', [((i + over) % chans, i) for i in range(chans)])  3.1 us
    ppermute x1, starting transfers between devices, local(): other = lax.ppermute(mine, 'brick', [(i, i ^ step) for i in range(bricks)])  2.84 us
    ppermute x1, starting transfers between devices, local(): arrived = lax.ppermute(sent, 'brick', pairs)  2.1 us
  transfers between devices with their start and end apart: 10, of which 5 were waited for; matrix products, arithmetic and copies ran while one was open for 0% of the time, Pallas kernels for 21%

profile of v3, /device:TPU:0, one launch (start us, length us, event | category | flops | bytes accessed | tf_op | source)
XLA Modules:
  0.0 68.0 jit_solution(17728810283333579237)
XLA Ops:
  0.6 3.0 %collective-permute-start.3 = (bf16[64,4608]{1,0:T(8,128)(2,1)}, bf16[64,4608]{1,0:T(8,128)(2,1)S(1)}, u32[]{:S(2)}, u32[]{:S(2)}) collective-permute-start(bf16[64,4608]{1,0:T(8,128)(2,1)} %own.1), channel_id=1, source_target_pairs={{2,0},{0,2},{3,1},{1,3},{6,4},{4,6},{7,5},{5,7},{10,8},{8,10},{11,... | collective-permute-start | bytes 1769480 | tf_op jit(solution)/shard_map/ppermute | solution.py:323
  3.6 1.8 %pack.1 = (bf16[128,768]{1,0:T(8,128)(2,1)}, bf16[128,768]{1,0:T(8,128)(2,1)}) custom-call(s32[1]{0:T(128)} %bitcast.rep.refs_0_, bf16[64,4608]{1,0:T(8,128)(2,1)} %own.1, bf16[64,4608]{1,0:T(8,128)(2,1)} %cotangent.3, s32[27,4608]{1,0:T(8,128)} %refs_5_.1, bf16[64,4608]{1,0:T(8,128)(2,1)} %own.1, bf16[64,4608]{1,0:T(8,128)(2,1)} %cotangent.3, ...), custom_call_target="tpu_custom_call" | custom-call | bytes 1048576 | tf_op jit(solution)/shard_map/pack/pallas_call | solution.py:116
  5.4 0.0 collective-permute-start
  5.4 0.7 collective-permute-start.1
  6.1 0.0 copy-start.5
  6.1 1.1 %copy-done.5 = bf16[64,4608]{1,0:T(8,128)(2,1)S(1)} copy-done((bf16[64,4608]{1,0:T(8,128)(2,1)S(1)}, bf16[64,4608]{1,0:T(8,128)(2,1)}, u32[]{:S(2)}) %copy-start.5) | copy-done | bytes 589848
  7.2 0.0 copy-start.8
  7.2 1.1 %copy-done.8 = s32[27,4608]{1,0:T(8,128)S(1)} copy-done((s32[27,4608]{1,0:T(8,128)S(1)}, s32[27,4608]{1,0:T(8,128)}, u32[]{:S(2)}) %copy-start.8) | copy-done | bytes 497688
  8.2 0.0 copy-start.9
  8.2 1.0 %copy-done.9 = bf16[27,128,64]{1,2,0:T(8,128)(2,1)S(1)} copy-done((bf16[27,128,64]{1,2,0:T(8,128)(2,1)S(1)}, bf16[27,128,64]{1,2,0:T(8,128)(2,1)}, u32[]{:S(2)}) %copy-start.9) | copy-done | bytes 442392
  9.2 2.4 %prepare.1 = (bf16[64,1728]{1,0:T(8,128)(2,1)S(1)}, bf16[64,1728]{1,0:T(8,128)(2,1)S(1)}, bf16[128,1792]{1,0:T(8,128)(2,1)S(1)}, bf16[9,64,6144]{2,1,0:T(8,128)(2,1)S(1)}, bf16[27,16,5376]{2,1,0:T(8,128)(2,1)S(1)}) custom-call(s32[1]{0:T(128)} %bitcast.1.turn, bf16[27,64,128]{2,1,0:T(8,128)(2,1)S(1)} %bitcast.8, bf16[64,4608]{1,0:T(8,128)(2,1)S(1)} %copy-done.5, ...), custom_call_target="tpu_custom_call" | custom-call | bytes 1048576 | tf_op jit(solution)/shard_map/prepare/pallas_call | solution.py:31
  11.7 0.0 collective-permute-done.refs_2_
  11.7 0.0 collective-permute-done.1.refs_3_
  11.7 0.1 ends.1
  11.7 0.1 collective-permute-start.2
  11.8 0.0 copy-start.6
  11.8 0.0 copy-start.7
  11.9 5.1 %forward_own.1 = (f32[64,5376]{1,0:T(8,128)S(1)}, bf16[9,64,6144]{2,1,0:T(8,128)(2,1)S(1)}, bf16[27,16,5376]{2,1,0:T(8,128)(2,1)S(1)}) custom-call(bf16[128,768]{1,0:T(8,128)(2,1)S(1)} %get-tuple-element.31.left, bf16[128,768]{1,0:T(8,128)(2,1)S(1)} %get-tuple-element.32.right, ...), custom_call_target="tpu_custom_call", output_to_operand_aliasing={{1}: (3, {}), {2}: (4, {})} | custom-call | bytes 1048576 | tf_op jit(solution)/shard_map/forward_own/pallas_call | solution.py:31
  17.0 0.0 copy-start
  17.0 4.2 %collective-permute-done.2.ends = bf16[64,1536]{1,0:T(8,128)(2,1)S(1)} collective-permute-done((bf16[64,1536]{1,0:T(8,128)(2,1)S(1)}, bf16[64,1536]{1,0:T(8,128)(2,1)S(1)}, u32[]{:S(2)}, u32[]{:S(2)}) %collective-permute-start.2) | collective-permute-done | bytes 196640 | tf_op jit(solution)/shard_map/ppermute | solution.py:323
  21.2 0.0 collective-permute-done.3.middle.rest
  21.2 0.0 copy-done.6
  21.2 0.0 copy-done.7
  21.2 7.5 %forward_rest.1 = (bf16[64,4608]{1,0:T(8,128)(2,1)}, bf16[64,5376]{1,0:T(8,128)(2,1)S(1)}) custom-call(bf16[64,1536]{1,0:T(8,128)(2,1)S(1)} %collective-permute-done.2.ends, bf16[64,4608]{1,0:T(8,128)(2,1)S(1)} %collective-permute-done.3.middle.rest, bf16[64,1728]{1,0:T(8,128)(2,1)S(1)} %get-tuple-element.30.weights, ...), custom_call_target="tpu_custom_call" | custom-call | flops 1019215872 | bytes 1048576 | tf_op jit(solution)/shard_map/forward_rest/pallas_call | solution.py:31
  28.6 6.9 %grad_weight.1 = (f32[896,128]{1,0:T(8,128)S(1)}, bf16[896,128]{1,0:T(8,128)(2,1)S(1)}, bf16[9,64,5376]{2,1,0:T(8,128)(2,1)S(1)}) custom-call(s32[1]{0:T(128)} %bitcast.rep.refs_0_, bf16[64,5376]{1,0:T(8,128)(2,1)S(1)} %get-tuple-element.38.grad, bf16[27,16,5376]{2,1,0:T(8,128)(2,1)S(1)} %get-tuple-element.35.valid.refs_2_, bf16[64,4608]{1,0:T(8,128)(2,1)S(1)} %copy-done.6, ...), custom_call_target="tpu_custom_call" | custom-call | flops 2038431744 | bytes 1048576 | tf_op jit(solution)/shard_map/grad_weight/pallas_call | solution.py:31
  35.6 0.0 copy-done
  35.6 0.0 copy-start.2
  35.6 2.6 %copy-done.2 = bf16[9,64,5376]{2,1,0:T(8,128)(2,1)} copy-done((bf16[9,64,5376]{2,1,0:T(8,128)(2,1)}, bf16[9,64,5376]{2,1,0:T(8,128)(2,1)S(1)}, u32[]{:S(2)}) %copy-start.2) | copy-done | bytes 6193176
  38.2 0.1 collective-permute-start.4
  38.3 2.3 %copy-done.1 = bf16[27,16,5376]{2,1,0:T(8,128)(2,1)S(1)} copy-done((bf16[27,16,5376]{2,1,0:T(8,128)(2,1)S(1)}, bf16[27,16,5376]{2,1,0:T(8,128)(2,1)}, u32[]{:S(2)}) %copy-start.1) | copy-done | bytes 4644888
  40.6 2.8 %copy-done.3 = bf16[9,64,5376]{2,1,0:T(8,128)(2,1)S(1)} copy-done((bf16[9,64,5376]{2,1,0:T(8,128)(2,1)S(1)}, bf16[9,64,5376]{2,1,0:T(8,128)(2,1)}, u32[]{:S(2)}) %copy-start.3) | copy-done | bytes 6193176
  43.4 1.7 %grad_features_0.1 = (f32[64,4608]{1,0:T(8,128)S(1)}, bf16[64,4608]{1,0:T(8,128)(2,1)S(1)}) custom-call(f32[896,128]{1,0:T(8,128)S(1)} %get-tuple-element.39.refs_0_.refs_2_, bf16[9,64,5376]{2,1,0:T(8,128)(2,1)S(1)} %copy-done.3, bf16[27,16,5376]{2,1,0:T(8,128)(2,1)S(1)} %copy-done.1, bf16[128,1792]{1,0:T(8,128)(2,1)S(1)} %get-tuple-element.41.refs_3_), custom_call_target="tpu_custom_call" | custom-call | flops 1019215872 | bytes 1048576 | tf_op jit(solution)/shard_map/grad_features_0/pallas_call | solution.py:31
  45.1 0.0 collective-permute-done.4.refs_3_
  45.1 0.1 split.1
  45.2 2.1 %collective-permute-start.6 = (bf16[448,128]{1,0:T(8,128)(2,1)S(1)}, bf16[448,128]{1,0:T(8,128)(2,1)S(1)}, u32[]{:S(2)}, u32[]{:S(2)}) collective-permute-start(bf16[448,128]{1,0:T(8,128)(2,1)S(1)} %get-tuple-element.48), channel_id=1, source_target_pairs={{0,4},{4,0},{8,12},{12,8},{1,5},{5,1},{9,13},{13,9},{2,6},{6,2},{1... | collective-permute-start | bytes 344072 | tf_op jit(solution)/shard_map/ppermute | solution.py:417
  47.3 0.0 copy-done.4
  47.3 1.7 %grad_features_1.1 = (f32[64,4608]{1,0:T(8,128)S(1)}, bf16[64,4608]{1,0:T(8,128)(2,1)S(1)}) custom-call(f32[448,128]{1,0:T(8,128)S(1)} %get-tuple-element.44.refs_0_.refs_1_, bf16[9,64,5376]{2,1,0:T(8,128)(2,1)S(1)} %copy-done.4, bf16[27,16,5376]{2,1,0:T(8,128)(2,1)S(1)} %copy-done.1, ...), custom_call_target="tpu_custom_call", output_to_operand_aliasing={{0}: (4, {}), {1}: (5, {})} | custom-call | flops 1019215872 | bytes 1048576 | tf_op jit(solution)/shard_map/grad_features_1/pallas_call | solution.py:31
  49.0 1.5 %collective-permute-start.5 = (bf16[64,4608]{1,0:T(8,128)(2,1)S(1)}, bf16[64,4608]{1,0:T(8,128)(2,1)S(1)}, u32[]{:S(2)}, u32[]{:S(2)}) collective-permute-start(bf16[64,4608]{1,0:T(8,128)(2,1)S(1)} %get-tuple-element.47), channel_id=1, source_target_pairs={{0,2},{2,0},{1,3},{3,1},{4,6},{6,4},{5,7},{7,5},{8,10},{10,8},{9,1... | collective-permute-start | bytes 1769480 | tf_op jit(solution)/shard_map/ppermute | solution.py:420
  50.5 0.5 collective-permute-done.6.refs_2_
  51.0 2.8 %collective-permute-start.7 = (bf16[448,128]{1,0:T(8,128)(2,1)S(1)}, bf16[448,128]{1,0:T(8,128)(2,1)S(1)}, u32[]{:S(2)}, u32[]{:S(2)}) collective-permute-start(bf16[448,128]{1,0:T(8,128)(2,1)S(1)} %merge_1.1.mine), channel_id=1, source_target_pairs={{0,8},{4,12},{8,0},{12,4},{1,9},{5,13},{9,1},{13,5},{2,10},{6,14},... | collective-permute-start | bytes 344072 | tf_op jit(solution)/shard_map/ppermute | solution.py:436
  53.9 5.5 %collective-permute-done.7.other = bf16[448,128]{1,0:T(8,128)(2,1)S(1)} collective-permute-done((bf16[448,128]{1,0:T(8,128)(2,1)S(1)}, bf16[448,128]{1,0:T(8,128)(2,1)S(1)}, u32[]{:S(2)}, u32[]{:S(2)}) %collective-permute-start.7) | collective-permute-done | bytes 114720 | tf_op jit(solution)/shard_map/ppermute | solution.py:436
  59.4 0.7 %collective-permute-start.8 = (bf16[448,128]{1,0:T(8,128)(2,1)S(1)}, bf16[448,128]{1,0:T(8,128)(2,1)S(1)}, u32[]{:S(2)}, u32[]{:S(2)}) collective-permute-start(bf16[448,128]{1,0:T(8,128)(2,1)S(1)} %merge_4.1.mine), channel_id=1, source_target_pairs={{0,4},{4,0},{8,12},{12,8},{1,5},{5,1},{9,13},{13,9},{2,6},{6,2},{1... | collective-permute-start | bytes 344072 | tf_op jit(solution)/shard_map/ppermute | solution.py:441
  60.1 4.1 %collective-permute-done.8.other = bf16[448,128]{1,0:T(8,128)(2,1)S(1)} collective-permute-done((bf16[448,128]{1,0:T(8,128)(2,1)S(1)}, bf16[448,128]{1,0:T(8,128)(2,1)S(1)}, u32[]{:S(2)}, u32[]{:S(2)}) %collective-permute-start.8) | collective-permute-done | bytes 114720 | tf_op jit(solution)/shard_map/ppermute | solution.py:441
  64.3 0.1 collective-permute-start.9
  64.3 1.5 %collective-permute-done.9.other = bf16[896,128]{1,0:T(8,128)(2,1)S(1)} collective-permute-done((bf16[896,128]{1,0:T(8,128)(2,1)S(1)}, bf16[896,128]{1,0:T(8,128)(2,1)S(1)}, u32[]{:S(2)}, u32[]{:S(2)}) %collective-permute-start.9) | collective-permute-done | bytes 229408 | tf_op jit(solution)/shard_map/ppermute | solution.py:445
  65.8 1.1 %join.1 = f32[1728,128]{1,0:T(8,128)} custom-call(s32[1]{0:T(128)} %bitcast.rep.refs_0_, s32[1]{0:T(128)} %bitcast.4.turn, bf16[896,128]{1,0:T(8,128)(2,1)S(1)} %gather.1.side, bf16[896,128]{1,0:T(8,128)(2,1)S(1)} %collective-permute-done.9.other), custom_call_target="tpu_custom_call" | custom-call | flops 250000000 | bytes 1048576 | tf_op jit(solution)/shard_map/join/pallas_call | solution.py:31
  66.9 0.0 collective-permute-done.5.rest_0_
  66.9 1.0 %add.6 = bf16[64,4608]{1,0:T(8,128)(2,1)} custom-call(bf16[64,4608]{1,0:T(8,128)(2,1)S(1)} %copy-done.7, f32[64,4608]{1,0:T(8,128)S(1)} %get-tuple-element.46.own.refs_0_, bf16[64,4608]{1,0:T(8,128)(2,1)S(1)} %collective-permute-done.5.rest_0_), custom_call_target="tpu_custom_call" | custom-call | bytes 1048576 | tf_op jit(solution)/shard_map/add/pallas_call | solution.py:31
  (6 shorter events, 0.1 us)
Async XLA Ops:
  0.6 20.5 %collective-permute-start.3 = (bf16[64,4608]{1,0:T(8,128)(2,1)}, bf16[64,4608]{1,0:T(8,128)(2,1)S(1)}, u32[]{:S(2)}, u32[]{:S(2)}) collective-permute-start(bf16[64,4608]{1,0:T(8,128)(2,1)} %own.1), channel_id=1, source_target_pairs={{2,0},{0,2},{3,1},{1,3},{6,4},{4,6},{7,5},{5,7},{10,8},{8,10},{11,... | collective-permute-start | bytes 1769480 | tf_op jit(solution)/shard_map/ppermute | solution.py:323
  5.4 6.3 %collective-permute-start = (bf16[128,768]{1,0:T(8,128)(2,1)}, bf16[128,768]{1,0:T(8,128)(2,1)S(1)}, u32[]{:S(2)}, u32[]{:S(2)}) collective-permute-start(bf16[128,768]{1,0:T(8,128)(2,1)} %get-tuple-element.27), channel_id=1, source_target_pairs={{0,1},{1,0},{2,3},{3,2},{4,5},{5,4},{6,7},{7,6},{8,9},{9,8},{10,11... | collective-permute-start | bytes 589832 | tf_op jit(solution)/shard_map/ppermute | solution.py:335
  5.4 6.3 %collective-permute-start.1 = (bf16[128,768]{1,0:T(8,128)(2,1)}, bf16[128,768]{1,0:T(8,128)(2,1)S(1)}, u32[]{:S(2)}, u32[]{:S(2)}) collective-permute-start(bf16[128,768]{1,0:T(8,128)(2,1)} %get-tuple-element.28), channel_id=1, source_target_pairs={{1,4},{4,1},{5,8},{8,5},{9,12},{12,9},{3,6},{6,3},{7,10},{10,7},{1... | collective-permute-start | bytes 589832 | tf_op jit(solution)/shard_map/ppermute | solution.py:309
  6.1 1.1 %copy-start.5 = (bf16[64,4608]{1,0:T(8,128)(2,1)S(1)}, bf16[64,4608]{1,0:T(8,128)(2,1)}, u32[]{:S(2)}) copy-start(bf16[64,4608]{1,0:T(8,128)(2,1)} %own.1) | copy-start | bytes 1769476
  7.2 1.1 %copy-start.8 = (s32[27,4608]{1,0:T(8,128)S(1)}, s32[27,4608]{1,0:T(8,128)}, u32[]{:S(2)}) copy-start(s32[27,4608]{1,0:T(8,128)} %refs_5_.1) | copy-start | bytes 1492996
  8.2 1.0 %copy-start.9 = (bf16[27,128,64]{1,2,0:T(8,128)(2,1)S(1)}, bf16[27,128,64]{1,2,0:T(8,128)(2,1)}, u32[]{:S(2)}) copy-start(bf16[27,128,64]{1,2,0:T(8,128)(2,1)} %param.5) | copy-start | bytes 1327108
  11.7 9.4 %collective-permute-start.2 = (bf16[64,1536]{1,0:T(8,128)(2,1)S(1)}, bf16[64,1536]{1,0:T(8,128)(2,1)S(1)}, u32[]{:S(2)}, u32[]{:S(2)}) collective-permute-start(bf16[64,1536]{1,0:T(8,128)(2,1)S(1)} %get-tuple-element.29), channel_id=1, source_target_pairs={{2,0},{0,2},{3,1},{1,3},{6,4},{4,6},{7,5},{5,7},{10,8},{8,10},{11,... | collective-permute-start | bytes 589832 | tf_op jit(solution)/shard_map/ppermute | solution.py:323
  11.8 9.3 %copy-start.6 = (bf16[64,4608]{1,0:T(8,128)(2,1)S(1)}, bf16[64,4608]{1,0:T(8,128)(2,1)}, u32[]{:S(2)}) copy-start(bf16[64,4608]{1,0:T(8,128)(2,1)} %own.1) | copy-start | bytes 1769476
  11.8 9.3 %copy-start.7 = (bf16[64,4608]{1,0:T(8,128)(2,1)S(1)}, bf16[64,4608]{1,0:T(8,128)(2,1)}, u32[]{:S(2)}) copy-start(bf16[64,4608]{1,0:T(8,128)(2,1)} %cotangent.3) | copy-start | bytes 1769476
  17.0 18.6 %copy-start = (bf16[27,16,5376]{2,1,0:T(8,128)(2,1)}, bf16[27,16,5376]{2,1,0:T(8,128)(2,1)S(1)}, u32[]{:S(2)}) copy-start(bf16[27,16,5376]{2,1,0:T(8,128)(2,1)S(1)} %get-tuple-element.35.valid.refs_2_) | copy-start | bytes 13934596
  35.6 2.6 %copy-start.2 = (bf16[9,64,5376]{2,1,0:T(8,128)(2,1)}, bf16[9,64,5376]{2,1,0:T(8,128)(2,1)S(1)}, u32[]{:S(2)}) copy-start(bf16[9,64,5376]{2,1,0:T(8,128)(2,1)S(1)} %get-tuple-element.40.refs_1_) | copy-start | bytes 18579460
  38.2 6.9 %collective-permute-start.4 = (bf16[896,128]{1,0:T(8,128)(2,1)S(1)}, bf16[896,128]{1,0:T(8,128)(2,1)S(1)}, u32[]{:S(2)}, u32[]{:S(2)}) collective-permute-start(bf16[896,128]{1,0:T(8,128)(2,1)S(1)} %get-tuple-element.43), channel_id=1, source_target_pairs={{0,1},{1,0},{2,3},{3,2},{4,5},{5,4},{6,7},{7,6},{8,9},{9,8},{10,11... | collective-permute-start | bytes 688136 | tf_op jit(solution)/shard_map/ppermute | solution.py:393
  38.3 2.3 %copy-start.1 = (bf16[27,16,5376]{2,1,0:T(8,128)(2,1)S(1)}, bf16[27,16,5376]{2,1,0:T(8,128)(2,1)}, u32[]{:S(2)}) copy-start(bf16[27,16,5376]{2,1,0:T(8,128)(2,1)} %copy-done) | copy-start | bytes 13934596
  40.6 2.8 %copy-start.3 = (bf16[9,64,5376]{2,1,0:T(8,128)(2,1)S(1)}, bf16[9,64,5376]{2,1,0:T(8,128)(2,1)}, u32[]{:S(2)}) copy-start(bf16[9,64,5376]{2,1,0:T(8,128)(2,1)} %copy-done.2) | copy-start | bytes 18579460
  43.4 3.9 %copy-start.4 = (bf16[9,64,5376]{2,1,0:T(8,128)(2,1)S(1)}, bf16[9,64,5376]{2,1,0:T(8,128)(2,1)}, u32[]{:S(2)}) copy-start(bf16[9,64,5376]{2,1,0:T(8,128)(2,1)} %copy-done.2) | copy-start | bytes 18579460
  45.2 5.8 %collective-permute-start.6 = (bf16[448,128]{1,0:T(8,128)(2,1)S(1)}, bf16[448,128]{1,0:T(8,128)(2,1)S(1)}, u32[]{:S(2)}, u32[]{:S(2)}) collective-permute-start(bf16[448,128]{1,0:T(8,128)(2,1)S(1)} %get-tuple-element.48), channel_id=1, source_target_pairs={{0,4},{4,0},{8,12},{12,8},{1,5},{5,1},{9,13},{13,9},{2,6},{6,2},{1... | collective-permute-start | bytes 344072 | tf_op jit(solution)/shard_map/ppermute | solution.py:417
  49.0 17.9 %collective-permute-start.5 = (bf16[64,4608]{1,0:T(8,128)(2,1)S(1)}, bf16[64,4608]{1,0:T(8,128)(2,1)S(1)}, u32[]{:S(2)}, u32[]{:S(2)}) collective-permute-start(bf16[64,4608]{1,0:T(8,128)(2,1)S(1)} %get-tuple-element.47), channel_id=1, source_target_pairs={{0,2},{2,0},{1,3},{3,1},{4,6},{6,4},{5,7},{7,5},{8,10},{10,8},{9,1... | collective-permute-start | bytes 1769480 | tf_op jit(solution)/shard_map/ppermute | solution.py:420
  51.0 8.3 %collective-permute-start.7 = (bf16[448,128]{1,0:T(8,128)(2,1)S(1)}, bf16[448,128]{1,0:T(8,128)(2,1)S(1)}, u32[]{:S(2)}, u32[]{:S(2)}) collective-permute-start(bf16[448,128]{1,0:T(8,128)(2,1)S(1)} %merge_1.1.mine), channel_id=1, source_target_pairs={{0,8},{4,12},{8,0},{12,4},{1,9},{5,13},{9,1},{13,5},{2,10},{6,14},... | collective-permute-start | bytes 344072 | tf_op jit(solution)/shard_map/ppermute | solution.py:436
  59.4 4.9 %collective-permute-start.8 = (bf16[448,128]{1,0:T(8,128)(2,1)S(1)}, bf16[448,128]{1,0:T(8,128)(2,1)S(1)}, u32[]{:S(2)}, u32[]{:S(2)}) collective-permute-start(bf16[448,128]{1,0:T(8,128)(2,1)S(1)} %merge_4.1.mine), channel_id=1, source_target_pairs={{0,4},{4,0},{8,12},{12,8},{1,5},{5,1},{9,13},{13,9},{2,6},{6,2},{1... | collective-permute-start | bytes 344072 | tf_op jit(solution)/shard_map/ppermute | solution.py:441
  64.3 1.6 %collective-permute-start.9 = (bf16[896,128]{1,0:T(8,128)(2,1)S(1)}, bf16[896,128]{1,0:T(8,128)(2,1)S(1)}, u32[]{:S(2)}, u32[]{:S(2)}) collective-permute-start(bf16[896,128]{1,0:T(8,128)(2,1)S(1)} %gather.1.side), channel_id=1, source_target_pairs={{0,1},{1,0},{2,3},{3,2},{4,5},{5,4},{6,7},{7,6},{8,9},{9,8},{10,11... | collective-permute-start | bytes 688136 | tf_op jit(solution)/shard_map/ppermute | solution.py:445

commit v4 on v3

--- a/solution.py
+++ b/solution.py
@@ -12,6 +12,9 @@
 TAPS = 27
 HALO = 384
 FAR = 2 * HALO
+NEAR = 640
+LEAD = 896
+NINE = 9
 ROWS = 16
 GROUP = 4
 WIDTH = 768
@@ -26,12 +29,12 @@
 SCALAR = pl.BlockSpec(memory_space=pltpu.SMEM)
 
 
-def kernel(body, name, outs, args, scalars=(), scratch=(), aliases={}, limit=8, flops=0):
+def kernel(body, name, outs, args, scalars=(), scratch=(), aliases={}, limit=8, flops=0, space=HERE):
     single = not isinstance(outs, (tuple, list))
     return pl.pallas_call(
         body,
         out_shape=outs,
-        in_specs=[SCALAR] * len(scalars) + [HERE] * len(args),
+        in_specs=[SCALAR] * len(scalars) + [space] * len(args),
         out_specs=HERE if single else [HERE] * len(outs),
         scratch_shapes=list(scratch),
         input_output_aliases={len(scalars) + i: o for i, o in aliases.items()},
@@ -69,8 +72,8 @@
     ]
 
 
-def groups():
-    return [range(first, min(first + GROUP, TAPS)) for first in range(0, TAPS, GROUP)]
+def groups(count=GROUP):
+    return [range(first, min(first + count, TAPS)) for first in range(0, TAPS, count)]
 
 
 def product(weights, shifts, valid, at_shift, at_valid, width, taps_of):
@@ -135,23 +138,36 @@
     def fill(first, second):
         before[...] = first[...]
         behind[...] = second[...]
-        both[:, :FAR] = first[:share, :]
-        both[:, FAR:] = second[:share, :]
+        both[:, :NEAR] = first[:share, FAR - NEAR :]
+        both[:, NEAR:] = second[:share, :NEAR]
 
     pl.when(rep[0] == 0)(functools.partial(fill, line, core))
     pl.when(rep[0] != 0)(functools.partial(fill, core, line))
 
 
 def prepare_body(
-    turn, by_out, features, neighbours, own, rest, by_in, shifts, valid, flat, kept
+    turn, by_out, features, neighbours, own, rest, by_in, shifts, valid, flat, kept, taken, near, done
 ):
     total = by_out.shape[2]
     share, sites = features.shape
+    copies = [
+        pltpu.make_async_copy(source, target, done.at[i])
+        for i, (source, target) in enumerate(
+            [
+                (by_out, taken),
+                (features, shifts.at[4, :, pl.ds(FAR, sites)]),
+                (neighbours, near),
+            ]
+        )
+    ]
+    for copy in copies:
+        copy.start()
+    copies[0].wait()
     flat[...] = jnp.zeros_like(flat)
     for group in groups():
         taps = []
         for tap in group:
-            ring = pltpu.roll(by_out[tap].astype(F32), turn[0], 1)
+            ring = pltpu.roll(taken[tap].astype(F32), turn[0], 1)
             flat[tap * share : (tap + 1) * share, :] = ring
             taps.append(ring)
         first, last = group[0], group[-1] + 1
@@ -163,9 +179,10 @@
             [x[:, share:] for x in taps], axis=1
         ).astype(BF16)
     by_in[...] = flat[...].T.astype(BF16)
-    shifts[4, :, FAR : FAR + sites] = features[...]
+    copies[1].wait()
     shift(shifts, FAR + 128, FAR + sites - 128)
-    kept[...] = (neighbours[...] >= 0).astype(F32)
+    copies[2].wait()
+    kept[...] = (near[...] >= 0).astype(F32)
     for tap in range(TAPS):
         valid[tap, :, HALO : HALO + sites] = jnp.broadcast_to(
             kept[tap : tap + 1, :], (ROWS, sites)
@@ -196,50 +213,97 @@
     lax.fori_loop(0, begun.shape[1] // WIDTH, block, 0)
 
 
-def rest_body(
-    ends, middle, weights, valid, begun, left, features, right, cotangent, output, grad, shifts, kept
-):
-    share, sites = features.shape
-    shifts[4, :, :FAR] = ends[:, :FAR]
-    shifts[4, :, FAR : FAR + sites] = middle[...]
-    shifts[4, :, FAR + sites :] = ends[:, FAR:]
-    shift(shifts, 128, shifts.shape[2] - 128)
-    grad[:, :HALO] = left[share : 2 * share, :HALO]
-    grad[:, HALO : HALO + sites] = cotangent[...]
-    grad[:, HALO + sites :] = right[share : 2 * share, :HALO]
-    kept[:, HALO : HALO + sites] = features[...]
+def arrive_body(rest, own_in, shifts, across, own):
+    del own_in
+    sites = rest.shape[1]
+    shifts[4, :, FAR : FAR + sites] = rest[...]
+    shift(shifts, FAR + 128, FAR + sites - 128)
 
     def block(j, carry):
         start = pl.multiple_of(j * WIDTH, 128)
+        here = pl.ds(pl.multiple_of(start + FAR, 128), WIDTH)
+        across[pl.ds(start, WIDTH), :] = jnp.concatenate(
+            [own[4, :, here], shifts[4, :, here]], axis=0
+        ).T
+        return carry
+
+    lax.fori_loop(0, sites // WIDTH, block, 0)
+
+
+def rest_body(
+    ends,
+    shifts_in,
+    weights,
+    valid_in,
+    begun,
+    left,
+    right,
+    own,
+    cotangent,
+    output,
+    grads,
+    valid,
+    shifts,
+    grad,
+    kept,
+):
+    del shifts_in, valid_in
+    share, sites = cotangent.shape
+    far = shifts.shape[2] - FAR
+    shifts[4, :, : FAR - NEAR] = jnp.zeros((shifts.shape[1], FAR - NEAR), BF16)
+    shifts[4, :, FAR - NEAR : FAR] = ends[:, :NEAR]
+    shifts[4, :, far : far + NEAR] = ends[:, NEAR:]
+    shifts[4, :, far + NEAR :] = jnp.zeros((shifts.shape[1], FAR - NEAR), BF16)
+    shift(shifts, 128, 128 + FAR)
+    shift(shifts, far - 128, far + FAR - 128)
+    lead = LEAD + 128
+    grad[:, lead : lead + HALO] = left[share : 2 * share, :HALO]
+    grad[:, lead + HALO : lead + HALO + sites] = cotangent[...]
+    grad[:, lead + HALO + sites :] = right[share : 2 * share, :HALO]
+
+    def spread(start):
+        for at in range(0, share, ROWS):
+            rows = pl.ds(at, ROWS)
+            window = grad[rows, pl.ds(start, WIDTH + 256)]
+            for j, step in enumerate(STEPS):
+                grads[j, rows, pl.ds(start, WIDTH)] = window[:, 128 + step : 128 + step + WIDTH]
+
+    def block(j, carry):
+        start = pl.multiple_of(j * WIDTH, 128)
+        spread(start)
         here = pl.ds(start, WIDTH)
+        there = pl.ds(pl.multiple_of(start + lead, 128), WIDTH)
         hidden = begun[:, here] + product(
             weights, shifts, valid, start + HALO, start, WIDTH, lambda tap: tap
         )
         sigma = jax.nn.sigmoid(hidden)
-        kept[:, here] = (kept[:, here].astype(F32) + hidden * sigma).astype(BF16)
-        grad[:, here] = (
-            grad[:, here].astype(F32) * sigma * (1.0 + hidden * (1.0 - sigma))
+        features = own[4, :, pl.ds(pl.multiple_of(start + HALO, 128), WIDTH)]
+        kept[:, here] = (features.astype(F32) + hidden * sigma).astype(BF16)
+        grad[:, there] = (
+            grad[:, there].astype(F32) * sigma * (1.0 + hidden * (1.0 - sigma))
         ).astype(BF16)
         return carry
 
-    lax.fori_loop(0, begun.shape[1] // WIDTH, block, 0)
+    count = begun.shape[1] // WIDTH
+    lax.fori_loop(0, count, block, 0)
+    spread(count * WIDTH)
     output[...] = kept[:, HALO : HALO + sites]
 
 
-def weight_body(half, rep, grad, valid, own, rest, kept, sent, shifts, total):
-    share, sites = own.shape
-    shifts[4] = grad[...]
-    shift(shifts, 128, shifts.shape[2] - 128)
+def weight_body(half, rep, across, valid_in, grads_in, kept, sent, valid, grads, total):
+    del valid_in, grads_in
+    share, sites = grads.shape[1], across.shape[0]
     total[...] = jnp.zeros_like(total)
 
     def block(j, carry):
         start = pl.multiple_of(j * WIDTH, 128)
-        here = pl.ds(start, WIDTH)
-        features = jnp.concatenate([own[:, here], rest[:, here]], axis=0).T
-        for group in groups():
+        features = across[pl.ds(start, WIDTH), :]
+        for group in groups(NINE):
             rows = []
             for tap in group:
-                rows += masked(shifts, valid, TAPS - 1 - tap, start + HALO, start + HALO, WIDTH)
+                rows += masked(
+                    grads, valid, TAPS - 1 - tap, start + HALO + LEAD, start + HALO, WIDTH
+                )
             total[group[0] * share : (group[-1] + 1) * share, :] += jnp.dot(
                 jnp.concatenate(rows, axis=0), features, preferred_element_type=F32
             )
@@ -251,7 +315,7 @@
     sent[...] = total[pl.ds(pl.multiple_of((1 - mine) * half, ROWS), half), :].astype(BF16)
 
 
-def feature_body(part, shifts, valid, weights, *refs):
+def feature_body(part, weights, valid, grads, *refs):
     own, rest = refs[-2:]
     share, sites = own.shape
     begin = part * sites // 2
@@ -259,8 +323,15 @@
     def block(j, carry):
         start = pl.multiple_of(begin + j * WIDTH, 128)
         here = pl.ds(start, WIDTH)
-        at = pl.multiple_of(start + HALO, 128)
-        total = product(weights, shifts, valid, at, at, WIDTH, lambda tap: TAPS - 1 - tap)
+        total = product(
+            weights,
+            grads,
+            valid,
+            start + HALO + LEAD,
+            start + HALO,
+            WIDTH,
+            lambda tap: TAPS - 1 - tap,
+        )
         own[:, here] = total[:share]
         rest[:, here] = total[share:].astype(BF16)
         return carry
@@ -346,18 +417,24 @@
         ],
         [jnp.transpose(conv_weight, (0, 2, 1)), features, neighbours],
         scalars=[(total - chan * share) % total],
-        scratch=[pltpu.VMEM((lanes, total), F32), pltpu.VMEM((TAPS, sites), F32)],
+        scratch=[
+            pltpu.VMEM((lanes, total), F32),
+            pltpu.VMEM((TAPS, sites), F32),
+            pltpu.VMEM((TAPS, share, total), BF16),
+            pltpu.VMEM((TAPS, sites), jnp.int32),
+            pltpu.SemaphoreType.DMA((3,)),
+        ],
+        space=pl.BlockSpec(memory_space=pl.ANY),
     )
     before, behind, both = kernel(
         after(ends_body, 1),
         "ends",
-        [shape(core.shape), shape(core.shape), shape((share, 2 * FAR))],
+        [shape(core.shape), shape(core.shape), shape((share, 2 * NEAR))],
         [own_weights, core, line],
         scalars=[rep],
     )
     ends = stack(around(both))
-
-    begun, _, valid = kernel(
+    begun, own_shifts, valid = kernel(
         own_body,
         "forward_own",
         [shape((share, margin), F32), shape(shifts.shape), shape(valid.shape)],
@@ -365,45 +442,61 @@
         scratch=[pltpu.VMEM((32, HALO), F32)],
         aliases={3: 1, 4: 2},
     )
-    output, grad = kernel(
+    rest_shifts, across, own_shifts = kernel(
+        arrive_body,
+        "arrive",
+        [shape((9, left, sites + 2 * FAR)), shape((sites, total)), shape(own_shifts.shape)],
+        [rest, own_shifts],
+        aliases={1: 2},
+    )
+    output, grads, valid, _ = kernel(
         rest_body,
         "forward_rest",
-        [shape((share, sites)), shape((share, margin))],
-        [ends, rest, rest_weights, valid, begun, before, features, behind, cotangent],
+        [
+            shape((share, sites)),
+            shape((9, share, margin + WIDTH)),
+            shape(valid.shape),
+            shape(rest_shifts.shape),
+        ],
+        [ends, rest_shifts, rest_weights, valid, begun, before, behind, own_shifts, cotangent],
         scratch=[
-            pltpu.VMEM((9, left, sites + 2 * FAR), BF16),
+            pltpu.VMEM((share, LEAD + 128 + margin), BF16),
             pltpu.VMEM((share, margin), BF16),
         ],
-        limit=24,
+        aliases={1: 3, 3: 2},
         flops=flops * left,
     )
 
     piece = -(-TAPS * share // (reps * bricks * ROWS)) * ROWS
     half = piece * bricks
-    kept, sent, shifts = kernel(
+    kept, sent, valid, grads = kernel(
         functools.partial(weight_body, half),
         "grad_weight",
-        [shape((half, total), F32), shape((half, total)), shape((9, share, margin))],
-        [grad, valid, features, rest],
+        [shape((half, total), F32), shape((half, total)), shape(valid.shape), shape(grads.shape)],
+        [across, valid, grads],
         scalars=[rep],
         scratch=[pltpu.VMEM((reps * half, total), F32)],
-        limit=12,
+        aliases={1: 2, 2: 3},
         flops=flops * total,
     )
     arrived = lax.ppermute(sent, "rep", swap)
 
-    def feature_part(part, first, so_far):
+    def feature_part(part, body, args, kept):
+        outs = [shape((share, sites), F32), shape((left, sites))]
         return kernel(
-            after(functools.partial(feature_body, part), 0),
+            body,
             "grad_features_%d" % part,
-            [shape((share, sites), F32), shape((left, sites))],
-            [first, shifts, valid, by_in, *so_far],
-            aliases={4 + i: i for i in range(len(so_far))},
-            limit=12,
+            [shape(x.shape) for x in kept] + outs,
+            args,
+            aliases={len(args) - len(kept) + i: i for i in range(len(kept))}
+            if part == 0
+            else {len(args) - 2 + i: i for i in range(2)},
             flops=flops * total // 2,
         )
 
-    parts = feature_part(0, kept, [])
+    valid, grads, *parts = feature_part(
+        0, functools.partial(feature_body, 0), [by_in, valid, grads], [valid, grads]
+    )
     size = half // 2
     mine, sent = kernel(
         after(split_body, 1),
@@ -415,7 +508,9 @@
     )
     pairs = [(i, i ^ 1) for i in range(bricks)]
     arrived = lax.ppermute(sent, "brick", pairs)
-    own, other = feature_part(1, mine, parts)
+    own, other = feature_part(
+        1, after(functools.partial(feature_body, 1), 0), [mine, by_in, valid, grads, *parts], []
+    )
     terms = [
         lax.ppermute(
             other if left == share else other[(over - 1) * share : over * share],

time: 68.3 us -> 73.4 us (1.075)
  local copies, waits for them, and re-layouts: 10.8 us -> 17.9 us
  waiting for transfers between devices: 15.8 us -> 12.9 us
    unnamed x20, local copies, waits for them, and re-layouts: 10.8 us -> 17.9 us
    ppermute x2, waiting for transfers between devices: 4.2 us -> 0.56 us  [around(): lax.ppermute(x, 'chan', [((i + over) % chans, i) for i in range(chans)])]
    ppermute x1, starting transfers between devices: 0.11 us -> 2.61 us  [local(): arrived = lax.ppermute(sent, 'rep', swap)]
    ppermute x1, starting transfers between devices: 2.84 us -> 1.79 us  [local(): other = lax.ppermute(mine, 'brick', [(i, i ^ step) for i in range(bricks)])]
    pallas_call x13 -> x14, Pallas kernels: 27.7 us -> 28.1 us  [kernel(): pl.pallas_call(body, out_shape=outs, in_specs=[SCALAR] * len(scalars) + [...]
  transfers between devices with their start and end apart: 10 -> 10, of which waited for: 5 -> 4; matrix products, arithmetic and copies ran while one was open for 0% -> 0% of each run, Pallas kernels for 21% -> 23%
where the time goes in v4:
time: 73.4 us; the launch traced here: 73 us
  Pallas kernels  29.9 us (41%)
  local copies, waits for them, and re-layouts  17.9 us (24%)
  waiting for transfers between devices  12.9 us (18%)
  starting transfers between devices  11.5 us (16%)
  between operations  0.8 us (1%)
    pallas_call x14, Pallas kernels, kernel(): pl.pallas_call(body, out_shape=outs, in_specs=[SCALAR] * len(scalars) + [...  28.1 us
    unnamed x20, local copies, waits for them, and re-layouts  17.9 us
    ppermute x1, waiting for transfers between devices, local(): other = lax.ppermute(mine, 'brick', [(i, i ^ step) for i in range(bricks)])  6 us
    ppermute x1, waiting for transfers between devices, local(): other = lax.ppermute(mine, 'brick', pairs)  4.85 us
    ppermute x2, starting transfers between devices, around(): lax.ppermute(x, 'chan', [((i + over) % chans, i) for i in range(chans)])  3.1 us
    ppermute x1, starting transfers between devices, local(): arrived = lax.ppermute(sent, 'rep', swap)  2.61 us
    ppermute x1, starting transfers between devices, local(): other = lax.ppermute(mine, 'brick', [(i, i ^ step) for i in range(bricks)])  1.79 us
    pallas_call x1, Pallas kernels, pack(): pl.pallas_call(pack_body, grid=(1,), out_shape=[shape((rows, FAR))] * 2,...  1.77 us
  transfers between devices with their start and end apart: 10, of which 4 were waited for; matrix products, arithmetic and copies ran while one was open for 0% of the time, Pallas kernels for 23%

profile of v4, /device:TPU:0, one launch (start us, length us, event | category | flops | bytes accessed | tf_op | source)
XLA Modules:
  0.0 73.0 jit_solution(1643890255274629618)
XLA Ops:
  0.6 3.0 %collective-permute-start.3 = (bf16[64,4608]{1,0:T(8,128)(2,1)}, bf16[64,4608]{1,0:T(8,128)(2,1)S(1)}, u32[]{:S(2)}, u32[]{:S(2)}) collective-permute-start(bf16[64,4608]{1,0:T(8,128)(2,1)} %refs_3_.1), channel_id=1, source_target_pairs={{2,0},{0,2},{3,1},{1,3},{6,4},{4,6},{7,5},{5,7},{10,8},{8,10},{11,... | collective-permute-start | bytes 1769480 | tf_op jit(solution)/shard_map/ppermute | solution.py:394
  3.6 1.8 %pack.1 = (bf16[128,768]{1,0:T(8,128)(2,1)}, bf16[128,768]{1,0:T(8,128)(2,1)}) custom-call(s32[1]{0:T(128)} %bitcast.rep.refs_0_, bf16[64,4608]{1,0:T(8,128)(2,1)} %refs_3_.1, bf16[64,4608]{1,0:T(8,128)(2,1)} %cotangent.3, s32[27,4608]{1,0:T(8,128)} %refs_5_.1, bf16[64,4608]{1,0:T(8,128)(2,1)} %refs_3_.1, bf16[64,4608]{1,0:T(8,128)(2,1)} %cotangent.3, ...), custom_call_target="tpu_custom_call" | custom-call | bytes 1048576 | tf_op jit(solution)/shard_map/pack/pallas_call | solution.py:119
  5.4 0.0 collective-permute-start
  5.4 0.7 collective-permute-start.1
  6.1 0.0 copy-start.7
  6.1 1.1 %copy-done.7 = s32[27,4608]{1,0:T(8,128)S(1)} copy-done((s32[27,4608]{1,0:T(8,128)S(1)}, s32[27,4608]{1,0:T(8,128)}, u32[]{:S(2)}) %copy-start.7) | copy-done | bytes 497688
  7.2 0.0 copy-start.8
  7.2 1.1 %copy-done.8 = bf16[64,4608]{1,0:T(8,128)(2,1)S(1)} copy-done((bf16[64,4608]{1,0:T(8,128)(2,1)S(1)}, bf16[64,4608]{1,0:T(8,128)(2,1)}, u32[]{:S(2)}) %copy-start.8) | copy-done | bytes 589848
  8.2 0.0 copy-start.9
  8.2 1.0 %copy-done.9 = bf16[27,128,64]{1,2,0:T(8,128)(2,1)S(1)} copy-done((bf16[27,128,64]{1,2,0:T(8,128)(2,1)S(1)}, bf16[27,128,64]{1,2,0:T(8,128)(2,1)}, u32[]{:S(2)}) %copy-start.9) | copy-done | bytes 442392
  9.2 2.9 %prepare.1 = (bf16[64,1728]{1,0:T(8,128)(2,1)S(1)}, bf16[64,1728]{1,0:T(8,128)(2,1)S(1)}, bf16[128,1792]{1,0:T(8,128)(2,1)S(1)}, bf16[9,64,6144]{2,1,0:T(8,128)(2,1)S(1)}, bf16[27,16,5376]{2,1,0:T(8,128)(2,1)S(1)}) custom-call(s32[1]{0:T(128)} %bitcast.1.turn, bf16[27,64,128]{2,1,0:T(8,128)(2,1)S(1)} %bitcast.8, bf16[64,4608]{1,0:T(8,128)(2,1)S(1)} %copy-done.8, ...), custom_call_target="tpu_custom_call" | custom-call | bytes 1048576 | tf_op jit(solution)/shard_map/prepare/pallas_call | solution.py:34
  12.2 0.0 collective-permute-done.refs_2_
  12.2 0.0 collective-permute-done.1.refs_3_
  12.2 0.1 ends.1
  12.3 0.1 collective-permute-start.2
  12.3 5.1 %forward_own.1 = (f32[64,5376]{1,0:T(8,128)S(1)}, bf16[9,64,6144]{2,1,0:T(8,128)(2,1)S(1)}, bf16[27,16,5376]{2,1,0:T(8,128)(2,1)S(1)}) custom-call(bf16[128,768]{1,0:T(8,128)(2,1)S(1)} %get-tuple-element.38.left, bf16[128,768]{1,0:T(8,128)(2,1)S(1)} %get-tuple-element.39.right, ...), custom_call_target="tpu_custom_call", output_to_operand_aliasing={{1}: (3, {}), {2}: (4, {})} | custom-call | bytes 1048576 | tf_op jit(solution)/shard_map/forward_own/pallas_call | solution.py:34
  17.4 0.0 copy-start.6
  17.4 0.0 collective-permute-done.3.rest
  17.5 1.9 %arrive.1 = (bf16[9,64,6144]{2,1,0:T(8,128)(2,1)S(1)}, bf16[4608,128]{1,0:T(8,128)(2,1)S(1)}, bf16[9,64,6144]{2,1,0:T(8,128)(2,1)S(1)}) custom-call(bf16[64,4608]{1,0:T(8,128)(2,1)S(1)} %collective-permute-done.3.rest, bf16[9,64,6144]{2,1,0:T(8,128)(2,1)S(1)} %get-tuple-element.42.own_in), custom_call_target="tpu_custom_call", output_to_operand_aliasing={{2}: (1, {})} | custom-call | bytes 1048576 | tf_op jit(solution)/shard_map/arrive/pallas_call | solution.py:34
  19.4 0.6 collective-permute-done.2.ends
  19.9 0.0 copy-done.6
  20.0 6.8 %forward_rest.1 = (bf16[64,4608]{1,0:T(8,128)(2,1)}, bf16[9,64,6144]{2,1,0:T(8,128)(2,1)S(1)}, bf16[27,16,5376]{2,1,0:T(8,128)(2,1)S(1)}, bf16[9,64,6144]{2,1,0:T(8,128)(2,1)S(1)}) custom-call(bf16[64,1280]{1,0:T(8,128)(2,1)S(1)} %collective-permute-done.2.ends, ...), custom_call_target="tpu_custom_call", output_to_operand_aliasing={{3}: (1, {}), {2}: (3, {})} | custom-call | flops 1019215872 | bytes 1048576 | tf_op jit(solution)/shard_map/forward_rest/pallas_call | solution.py:34
  26.7 5.4 %grad_weight.1 = (f32[896,128]{1,0:T(8,128)S(1)}, bf16[896,128]{1,0:T(8,128)(2,1)S(1)}, bf16[27,16,5376]{2,1,0:T(8,128)(2,1)S(1)}, bf16[9,64,6144]{2,1,0:T(8,128)(2,1)S(1)}) custom-call(s32[1]{0:T(128)} %bitcast.rep.refs_0_, bf16[4608,128]{1,0:T(8,128)(2,1)S(1)} %get-tuple-element.50.across, ...), custom_call_target="tpu_custom_call", output_to_operand_aliasing={{2}: (2, {}), {3}: (3, {})} | custom-call | flops 2038431744 | bytes 1048576 | tf_op jit(solution)/shard_map/grad_weight/pallas_call | solution.py:34
  32.2 0.0 copy-start
  32.2 2.1 %copy-done = bf16[27,16,5376]{2,1,0:T(8,128)(2,1)} copy-done((bf16[27,16,5376]{2,1,0:T(8,128)(2,1)}, bf16[27,16,5376]{2,1,0:T(8,128)(2,1)S(1)}, u32[]{:S(2)}) %copy-start) | copy-done | bytes 4644888
  34.3 0.0 copy-start.4
  34.3 2.9 %copy-done.4 = bf16[9,64,6144]{2,1,0:T(8,128)(2,1)} copy-done((bf16[9,64,6144]{2,1,0:T(8,128)(2,1)}, bf16[9,64,6144]{2,1,0:T(8,128)(2,1)S(1)}, u32[]{:S(2)}) %copy-start.4) | copy-done | bytes 7077912
  37.2 2.6 %collective-permute-start.4 = (bf16[896,128]{1,0:T(8,128)(2,1)S(1)}, bf16[896,128]{1,0:T(8,128)(2,1)S(1)}, u32[]{:S(2)}, u32[]{:S(2)}) collective-permute-start(bf16[896,128]{1,0:T(8,128)(2,1)S(1)} %get-tuple-element.57), channel_id=1, source_target_pairs={{0,1},{1,0},{2,3},{3,2},{4,5},{5,4},{6,7},{7,6},{8,9},{9,8},{10,11... | collective-permute-start | bytes 688136 | tf_op jit(solution)/shard_map/ppermute | solution.py:482
  39.8 2.3 %copy-done.1 = bf16[27,16,5376]{2,1,0:T(8,128)(2,1)S(1)} copy-done((bf16[27,16,5376]{2,1,0:T(8,128)(2,1)S(1)}, bf16[27,16,5376]{2,1,0:T(8,128)(2,1)}, u32[]{:S(2)}) %copy-start.1) | copy-done | bytes 4644888
  42.1 3.0 %copy-done.5 = bf16[9,64,6144]{2,1,0:T(8,128)(2,1)S(1)} copy-done((bf16[9,64,6144]{2,1,0:T(8,128)(2,1)S(1)}, bf16[9,64,6144]{2,1,0:T(8,128)(2,1)}, u32[]{:S(2)}) %copy-start.5) | copy-done | bytes 7077912
  45.1 1.8 %grad_features_0.1 = (bf16[27,16,5376]{2,1,0:T(8,128)(2,1)S(1)}, bf16[9,64,6144]{2,1,0:T(8,128)(2,1)S(1)}, f32[64,4608]{1,0:T(8,128)S(1)}, bf16[64,4608]{1,0:T(8,128)(2,1)S(1)}) custom-call(bf16[128,1792]{1,0:T(8,128)(2,1)S(1)} %get-tuple-element.49.weights.refs_1_, ...), custom_call_target="tpu_custom_call", output_to_operand_aliasing={{0}: (1, {}), {1}: (2, {})} | custom-call | flops 1019215872 | bytes 1048576 | tf_op jit(solution)/shard_map/grad_features_0/pallas_call | solution.py:34
  47.0 0.0 copy-start.2
  47.0 2.1 %copy-done.2 = bf16[27,16,5376]{2,1,0:T(8,128)(2,1)} copy-done((bf16[27,16,5376]{2,1,0:T(8,128)(2,1)}, bf16[27,16,5376]{2,1,0:T(8,128)(2,1)S(1)}, u32[]{:S(2)}) %copy-start.2) | copy-done | bytes 4644888
  49.1 0.0 collective-permute-done.4.refs_3_
  49.1 1.7 %collective-permute-start.6 = (bf16[448,128]{1,0:T(8,128)(2,1)S(1)}, bf16[448,128]{1,0:T(8,128)(2,1)S(1)}, u32[]{:S(2)}, u32[]{:S(2)}) collective-permute-start(bf16[448,128]{1,0:T(8,128)(2,1)S(1)} %get-tuple-element.64), channel_id=1, source_target_pairs={{0,4},{4,0},{8,12},{12,8},{1,5},{5,1},{9,13},{13,9},{2,6},{6,2},{1... | collective-permute-start | bytes 344072 | tf_op jit(solution)/shard_map/ppermute | solution.py:510
  50.8 2.3 %copy-done.3 = bf16[27,16,5376]{2,1,0:T(8,128)(2,1)S(1)} copy-done((bf16[27,16,5376]{2,1,0:T(8,128)(2,1)S(1)}, bf16[27,16,5376]{2,1,0:T(8,128)(2,1)}, u32[]{:S(2)}) %copy-start.3) | copy-done | bytes 4644888
  53.1 1.8 %grad_features_1.1 = (f32[64,4608]{1,0:T(8,128)S(1)}, bf16[64,4608]{1,0:T(8,128)(2,1)S(1)}) custom-call(f32[448,128]{1,0:T(8,128)S(1)} %get-tuple-element.58.refs_0_.refs_1_, bf16[128,1792]{1,0:T(8,128)(2,1)S(1)} %get-tuple-element.49.weights.refs_1_, bf16[27,16,5376]{2,1,0:T(8,128)(2,1)S(1)} %copy-done.3, ...), custom_call_target="tpu_custom_call", output_to_operand_aliasing={{0}: (4, {}), {1}: (5, {})} | custom-call | flops 1019215872 | bytes 1048576 | tf_op jit(solution)/shard_map/grad_features_1/pallas_call | solution.py:34
  54.9 1.6 %collective-permute-start.5 = (bf16[64,4608]{1,0:T(8,128)(2,1)S(1)}, bf16[64,4608]{1,0:T(8,128)(2,1)S(1)}, u32[]{:S(2)}, u32[]{:S(2)}) collective-permute-start(bf16[64,4608]{1,0:T(8,128)(2,1)S(1)} %get-tuple-element.63), channel_id=1, source_target_pairs={{0,2},{2,0},{1,3},{3,1},{4,6},{6,4},{5,7},{7,5},{8,10},{10,8},{9,1... | collective-permute-start | bytes 1769480 | tf_op jit(solution)/shard_map/ppermute | solution.py:515
  56.5 0.0 collective-permute-done.6.refs_2_
  56.5 1.8 %collective-permute-start.7 = (bf16[448,128]{1,0:T(8,128)(2,1)S(1)}, bf16[448,128]{1,0:T(8,128)(2,1)S(1)}, u32[]{:S(2)}, u32[]{:S(2)}) collective-permute-start(bf16[448,128]{1,0:T(8,128)(2,1)S(1)} %merge_1.1.mine), channel_id=1, source_target_pairs={{0,8},{4,12},{8,0},{12,4},{1,9},{5,13},{9,1},{13,5},{2,10},{6,14},... | collective-permute-start | bytes 344072 | tf_op jit(solution)/shard_map/ppermute | solution.py:531
  58.3 6.0 %collective-permute-done.7.other = bf16[448,128]{1,0:T(8,128)(2,1)S(1)} collective-permute-done((bf16[448,128]{1,0:T(8,128)(2,1)S(1)}, bf16[448,128]{1,0:T(8,128)(2,1)S(1)}, u32[]{:S(2)}, u32[]{:S(2)}) %collective-permute-start.7) | collective-permute-done | bytes 114720 | tf_op jit(solution)/shard_map/ppermute | solution.py:531
  64.3 0.1 collective-permute-start.8
  64.4 4.8 %collective-permute-done.8.other = bf16[448,128]{1,0:T(8,128)(2,1)S(1)} collective-permute-done((bf16[448,128]{1,0:T(8,128)(2,1)S(1)}, bf16[448,128]{1,0:T(8,128)(2,1)S(1)}, u32[]{:S(2)}, u32[]{:S(2)}) %collective-permute-start.8) | collective-permute-done | bytes 114720 | tf_op jit(solution)/shard_map/ppermute | solution.py:536
  69.3 0.1 collective-permute-start.9
  69.4 1.5 %collective-permute-done.9.other = bf16[896,128]{1,0:T(8,128)(2,1)S(1)} collective-permute-done((bf16[896,128]{1,0:T(8,128)(2,1)S(1)}, bf16[896,128]{1,0:T(8,128)(2,1)S(1)}, u32[]{:S(2)}, u32[]{:S(2)}) %collective-permute-start.9) | collective-permute-done | bytes 229408 | tf_op jit(solution)/shard_map/ppermute | solution.py:540
  70.8 1.1 %join.1 = f32[1728,128]{1,0:T(8,128)} custom-call(s32[1]{0:T(128)} %bitcast.rep.refs_0_, s32[1]{0:T(128)} %bitcast.4.turn, bf16[896,128]{1,0:T(8,128)(2,1)S(1)} %gather.1.side, bf16[896,128]{1,0:T(8,128)(2,1)S(1)} %collective-permute-done.9.other), custom_call_target="tpu_custom_call" | custom-call | flops 250000000 | bytes 1048576 | tf_op jit(solution)/shard_map/join/pallas_call | solution.py:34
  72.0 0.0 collective-permute-done.5.rest_0_
  72.0 1.0 %add.6 = bf16[64,4608]{1,0:T(8,128)(2,1)} custom-call(bf16[64,4608]{1,0:T(8,128)(2,1)S(1)} %copy-done.6, f32[64,4608]{1,0:T(8,128)S(1)} %get-tuple-element.62.own.refs_0_, bf16[64,4608]{1,0:T(8,128)(2,1)S(1)} %collective-permute-done.5.rest_0_), custom_call_target="tpu_custom_call" | custom-call | bytes 1048576 | tf_op jit(solution)/shard_map/add/pallas_call | solution.py:34
  (7 shorter events, 0.1 us)
Async XLA Ops:
  0.6 16.8 %collective-permute-start.3 = (bf16[64,4608]{1,0:T(8,128)(2,1)}, bf16[64,4608]{1,0:T(8,128)(2,1)S(1)}, u32[]{:S(2)}, u32[]{:S(2)}) collective-permute-start(bf16[64,4608]{1,0:T(8,128)(2,1)} %refs_3_.1), channel_id=1, source_target_pairs={{2,0},{0,2},{3,1},{1,3},{6,4},{4,6},{7,5},{5,7},{10,8},{8,10},{11,... | collective-permute-start | bytes 1769480 | tf_op jit(solution)/shard_map/ppermute | solution.py:394
  5.4 6.8 %collective-permute-start = (bf16[128,768]{1,0:T(8,128)(2,1)}, bf16[128,768]{1,0:T(8,128)(2,1)S(1)}, u32[]{:S(2)}, u32[]{:S(2)}) collective-permute-start(bf16[128,768]{1,0:T(8,128)(2,1)} %get-tuple-element.35), channel_id=1, source_target_pairs={{0,1},{1,0},{2,3},{3,2},{4,5},{5,4},{6,7},{7,6},{8,9},{9,8},{10,11... | collective-permute-start | bytes 589832 | tf_op jit(solution)/shard_map/ppermute | solution.py:406
  5.4 6.8 %collective-permute-start.1 = (bf16[128,768]{1,0:T(8,128)(2,1)}, bf16[128,768]{1,0:T(8,128)(2,1)S(1)}, u32[]{:S(2)}, u32[]{:S(2)}) collective-permute-start(bf16[128,768]{1,0:T(8,128)(2,1)} %get-tuple-element.36), channel_id=1, source_target_pairs={{1,4},{4,1},{5,8},{8,5},{9,12},{12,9},{3,6},{6,3},{7,10},{10,7},{1... | collective-permute-start | bytes 589832 | tf_op jit(solution)/shard_map/ppermute | solution.py:380
  6.1 1.1 %copy-start.7 = (s32[27,4608]{1,0:T(8,128)S(1)}, s32[27,4608]{1,0:T(8,128)}, u32[]{:S(2)}) copy-start(s32[27,4608]{1,0:T(8,128)} %refs_5_.1) | copy-start | bytes 1492996
  7.2 1.1 %copy-start.8 = (bf16[64,4608]{1,0:T(8,128)(2,1)S(1)}, bf16[64,4608]{1,0:T(8,128)(2,1)}, u32[]{:S(2)}) copy-start(bf16[64,4608]{1,0:T(8,128)(2,1)} %refs_3_.1) | copy-start | bytes 1769476
  8.2 1.0 %copy-start.9 = (bf16[27,128,64]{1,2,0:T(8,128)(2,1)S(1)}, bf16[27,128,64]{1,2,0:T(8,128)(2,1)}, u32[]{:S(2)}) copy-start(bf16[27,128,64]{1,2,0:T(8,128)(2,1)} %param.5) | copy-start | bytes 1327108
  12.3 7.7 %collective-permute-start.2 = (bf16[64,1280]{1,0:T(8,128)(2,1)S(1)}, bf16[64,1280]{1,0:T(8,128)(2,1)S(1)}, u32[]{:S(2)}, u32[]{:S(2)}) collective-permute-start(bf16[64,1280]{1,0:T(8,128)(2,1)S(1)} %get-tuple-element.37), channel_id=1, source_target_pairs={{2,0},{0,2},{3,1},{1,3},{6,4},{4,6},{7,5},{5,7},{10,8},{8,10},{11,... | collective-permute-start | bytes 491528 | tf_op jit(solution)/shard_map/ppermute | solution.py:394
  17.4 2.5 %copy-start.6 = (bf16[64,4608]{1,0:T(8,128)(2,1)S(1)}, bf16[64,4608]{1,0:T(8,128)(2,1)}, u32[]{:S(2)}) copy-start(bf16[64,4608]{1,0:T(8,128)(2,1)} %cotangent.3) | copy-start | bytes 1769476
  32.2 2.1 %copy-start = (bf16[27,16,5376]{2,1,0:T(8,128)(2,1)}, bf16[27,16,5376]{2,1,0:T(8,128)(2,1)S(1)}, u32[]{:S(2)}) copy-start(bf16[27,16,5376]{2,1,0:T(8,128)(2,1)S(1)} %get-tuple-element.53.valid) | copy-start | bytes 13934596
  34.3 2.9 %copy-start.4 = (bf16[9,64,6144]{2,1,0:T(8,128)(2,1)}, bf16[9,64,6144]{2,1,0:T(8,128)(2,1)S(1)}, u32[]{:S(2)}) copy-start(bf16[9,64,6144]{2,1,0:T(8,128)(2,1)S(1)} %get-tuple-element.54.grads) | copy-start | bytes 21233668
  37.2 11.9 %collective-permute-start.4 = (bf16[896,128]{1,0:T(8,128)(2,1)S(1)}, bf16[896,128]{1,0:T(8,128)(2,1)S(1)}, u32[]{:S(2)}, u32[]{:S(2)}) collective-permute-start(bf16[896,128]{1,0:T(8,128)(2,1)S(1)} %get-tuple-element.57), channel_id=1, source_target_pairs={{0,1},{1,0},{2,3},{3,2},{4,5},{5,4},{6,7},{7,6},{8,9},{9,8},{10,11... | collective-permute-start | bytes 688136 | tf_op jit(solution)/shard_map/ppermute | solution.py:482
  39.8 2.3 %copy-start.1 = (bf16[27,16,5376]{2,1,0:T(8,128)(2,1)S(1)}, bf16[27,16,5376]{2,1,0:T(8,128)(2,1)}, u32[]{:S(2)}) copy-start(bf16[27,16,5376]{2,1,0:T(8,128)(2,1)} %copy-done) | copy-start | bytes 13934596
  42.1 3.0 %copy-start.5 = (bf16[9,64,6144]{2,1,0:T(8,128)(2,1)S(1)}, bf16[9,64,6144]{2,1,0:T(8,128)(2,1)}, u32[]{:S(2)}) copy-start(bf16[9,64,6144]{2,1,0:T(8,128)(2,1)} %copy-done.4) | copy-start | bytes 21233668
  47.0 2.1 %copy-start.2 = (bf16[27,16,5376]{2,1,0:T(8,128)(2,1)}, bf16[27,16,5376]{2,1,0:T(8,128)(2,1)S(1)}, u32[]{:S(2)}) copy-start(bf16[27,16,5376]{2,1,0:T(8,128)(2,1)S(1)} %get-tuple-element.59.refs_2_) | copy-start | bytes 13934596
  49.1 7.3 %collective-permute-start.6 = (bf16[448,128]{1,0:T(8,128)(2,1)S(1)}, bf16[448,128]{1,0:T(8,128)(2,1)S(1)}, u32[]{:S(2)}, u32[]{:S(2)}) collective-permute-start(bf16[448,128]{1,0:T(8,128)(2,1)S(1)} %get-tuple-element.64), channel_id=1, source_target_pairs={{0,4},{4,0},{8,12},{12,8},{1,5},{5,1},{9,13},{13,9},{2,6},{6,2},{1... | collective-permute-start | bytes 344072 | tf_op jit(solution)/shard_map/ppermute | solution.py:510
  50.8 2.3 %copy-start.3 = (bf16[27,16,5376]{2,1,0:T(8,128)(2,1)S(1)}, bf16[27,16,5376]{2,1,0:T(8,128)(2,1)}, u32[]{:S(2)}) copy-start(bf16[27,16,5376]{2,1,0:T(8,128)(2,1)} %copy-done.2) | copy-start | bytes 13934596
  54.9 17.1 %collective-permute-start.5 = (bf16[64,4608]{1,0:T(8,128)(2,1)S(1)}, bf16[64,4608]{1,0:T(8,128)(2,1)S(1)}, u32[]{:S(2)}, u32[]{:S(2)}) collective-permute-start(bf16[64,4608]{1,0:T(8,128)(2,1)S(1)} %get-tuple-element.63), channel_id=1, source_target_pairs={{0,2},{2,0},{1,3},{3,1},{4,6},{6,4},{5,7},{7,5},{8,10},{10,8},{9,1... | collective-permute-start | bytes 1769480 | tf_op jit(solution)/shard_map/ppermute | solution.py:515
  56.5 7.8 %collective-permute-start.7 = (bf16[448,128]{1,0:T(8,128)(2,1)S(1)}, bf16[448,128]{1,0:T(8,128)(2,1)S(1)}, u32[]{:S(2)}, u32[]{:S(2)}) collective-permute-start(bf16[448,128]{1,0:T(8,128)(2,1)S(1)} %merge_1.1.mine), channel_id=1, source_target_pairs={{0,8},{4,12},{8,0},{12,4},{1,9},{5,13},{9,1},{13,5},{2,10},{6,14},... | collective-permute-start | bytes 344072 | tf_op jit(solution)/shard_map/ppermute | solution.py:531
  64.3 4.9 %collective-permute-start.8 = (bf16[448,128]{1,0:T(8,128)(2,1)S(1)}, bf16[448,128]{1,0:T(8,128)(2,1)S(1)}, u32[]{:S(2)}, u32[]{:S(2)}) collective-permute-start(bf16[448,128]{1,0:T(8,128)(2,1)S(1)} %merge_4.1.mine), channel_id=1, source_target_pairs={{0,4},{4,0},{8,12},{12,8},{1,5},{5,1},{9,13},{13,9},{2,6},{6,2},{1... | collective-permute-start | bytes 344072 | tf_op jit(solution)/shard_map/ppermute | solution.py:536
  69.3 1.6 %collective-permute-start.9 = (bf16[896,128]{1,0:T(8,128)(2,1)S(1)}, bf16[896,128]{1,0:T(8,128)(2,1)S(1)}, u32[]{:S(2)}, u32[]{:S(2)}) collective-permute-start(bf16[896,128]{1,0:T(8,128)(2,1)S(1)} %gather.1.side), channel_id=1, source_target_pairs={{0,1},{1,0},{2,3},{3,2},{4,5},{5,4},{6,7},{7,6},{8,9},{9,8},{10,11... | collective-permute-start | bytes 688136 | tf_op jit(solution)/shard_map/ppermute | solution.py:540

commit v5 on v4

--- a/solution.py
+++ b/solution.py
@@ -26,6 +26,7 @@
 STEPS = [(k // 3 - 1) * EDGE + k % 3 - 1 for k in range(9)]
 
 HERE = pl.BlockSpec(memory_space=pltpu.VMEM)
+FAR_OFF = pl.BlockSpec(memory_space=pltpu.HBM)
 SCALAR = pl.BlockSpec(memory_space=pltpu.SMEM)
 
 
@@ -41,7 +42,7 @@
         compiler_params=pltpu.CompilerParams(vmem_limit_bytes=limit * MIB),
         cost_estimate=pl.CostEstimate(flops=flops, bytes_accessed=MIB, transcendentals=0),
         name=name,
-    )(*(x[None] for x in scalars), *args)
+    )(*scalars, *args)
 
 
 def after(body, at):
@@ -92,47 +93,34 @@
     return total
 
 
-def pack_body(rep, *refs):
-    ends, outs = refs[:6], refs[6:]
-    for at, (features, cotangent, neighbours) in enumerate((ends[:3], ends[3:])):
-        share = features.shape[0]
-        kept = (neighbours[...] >= 0).astype(F32)
-        kept = jnp.concatenate([kept, jnp.zeros((32 - TAPS, HALO), F32)], axis=0).astype(BF16)
-
-        def fill(out):
-            out[...] = jnp.zeros_like(out)
-            out[:share, :] = features[...]
-            out[share : 2 * share, :HALO] = cotangent[...]
-            out[share : share + 32, HALO:] = kept
-
-        pl.when(rep[0] == at)(functools.partial(fill, outs[0]))
-        pl.when(rep[0] != at)(functools.partial(fill, outs[1]))
-
-
-def pack(rep, features, cotangent, neighbours):
+def pack_body(brick, chan, rep, features, cotangent, neighbours, to_core, to_line, near, done):
     share, sites = features.shape
-
-    def end(rows, width, at):
-        return pl.BlockSpec((rows, width), lambda i: (0, at * (sites // width - 1)))
-
-    rows = share + max(share, 32)
-    return pl.pallas_call(
-        pack_body,
-        grid=(1,),
-        out_shape=[shape((rows, FAR))] * 2,
-        in_specs=[SCALAR]
-        + [
-            spec
-            for at in (1, 0)
-            for spec in (end(share, FAR, at), end(share, HALO, at), end(TAPS, HALO, at))
-        ],
-        out_specs=[pl.BlockSpec((rows, FAR), lambda i: (0, 0))] * 2,
-        cost_estimate=pl.CostEstimate(flops=0, bytes_accessed=MIB, transcendentals=0),
-        name="pack",
-    )(rep[None], *(features, cotangent, neighbours) * 2)
-
-
-def ends_body(rep, core, line, before, behind, both):
+    copies = []
+    for i, (out, last) in enumerate(((to_core, 1 - rep[0]), (to_line, rep[0]))):
+        far = pl.ds(pl.multiple_of(last * (sites - FAR), 128), FAR)
+        close = pl.ds(pl.multiple_of(last * (sites - HALO), 128), HALO)
+        copies += [
+            pltpu.make_async_copy(source, target, done.at[3 * i + j])
+            for j, (source, target) in enumerate(
+                [
+                    (neighbours.at[:, close], near.at[i]),
+                    (features.at[:, far], out.at[pl.ds(0, share), :]),
+                    (cotangent.at[:, close], out.at[pl.ds(share, share), pl.ds(0, HALO)]),
+                ]
+            )
+        ]
+    for copy in copies:
+        copy.start()
+    for i, out in enumerate((to_core, to_line)):
+        copies[3 * i].wait()
+        kept = (near[i] >= 0).astype(F32)
+        kept = jnp.concatenate([kept, jnp.zeros((32 - TAPS, HALO), F32)], axis=0)
+        out[share : share + 32, HALO:] = kept.astype(BF16)
+        copies[3 * i + 1].wait()
+        copies[3 * i + 2].wait()
+
+
+def ends_body(brick, chan, rep, core, line, before, behind, both):
     share = both.shape[0]
 
     def fill(first, second):
@@ -146,10 +134,11 @@
 
 
 def prepare_body(
-    turn, by_out, features, neighbours, own, rest, by_in, shifts, valid, flat, kept, taken, near, done
+    brick, chan, rep, by_out, features, neighbours, own, rest, by_in, shifts, valid, flat, kept, taken, near, done
 ):
     total = by_out.shape[2]
     share, sites = features.shape
+    turn = lax.rem(total - chan[0] * share, total)
     copies = [
         pltpu.make_async_copy(source, target, done.at[i])
         for i, (source, target) in enumerate(
@@ -167,7 +156,7 @@
     for group in groups():
         taps = []
         for tap in group:
-            ring = pltpu.roll(taken[tap].astype(F32), turn[0], 1)
+            ring = pltpu.roll(taken[tap].astype(F32), turn, 1)
             flat[tap * share : (tap + 1) * share, :] = ring
             taps.append(ring)
         first, last = group[0], group[-1] + 1
@@ -290,7 +279,7 @@
     output[...] = kept[:, HALO : HALO + sites]
 
 
-def weight_body(half, rep, across, valid_in, grads_in, kept, sent, valid, grads, total):
+def weight_body(half, brick, chan, rep, across, valid_in, grads_in, kept, sent, valid, grads, total):
     del valid_in, grads_in
     share, sites = grads.shape[1], across.shape[0]
     total[...] = jnp.zeros_like(total)
@@ -339,7 +328,7 @@
     lax.fori_loop(0, sites // 2 // WIDTH, block, 0)
 
 
-def split_body(brick, kept, arrived, mine, sent):
+def split_body(brick, chan, rep, kept, arrived, mine, sent):
     size = mine.shape[0]
     at = brick[0] % 2
     mine_rows = pl.ds(pl.multiple_of(at * size, ROWS), size)
@@ -352,18 +341,18 @@
     out[...] = (mine[...].astype(F32) + other[...].astype(F32)).astype(BF16)
 
 
-def gather_body(brick, mine, other, side):
+def gather_body(brick, chan, rep, mine, other, side):
     size = mine.shape[0]
     at = brick[0] % 2
     side[pl.ds(pl.multiple_of(at * size, ROWS), size), :] = mine[...]
     side[pl.ds(pl.multiple_of((1 - at) * size, ROWS), size), :] = other[...]
 
 
-def join_body(half, rep, turn, side, other, out, both):
+def join_body(half, share, brick, chan, rep, side, other, out, both):
     mine = rep[0]
     both[pl.ds(pl.multiple_of(mine * half, ROWS), half), :] = side[...]
     both[pl.ds(pl.multiple_of((1 - mine) * half, ROWS), half), :] = other[...]
-    out[...] = pltpu.roll(both[: out.shape[0], :].astype(F32), turn[0], 1)
+    out[...] = pltpu.roll(both[: out.shape[0], :].astype(F32), chan[0] * share, 1)
 
 
 def add_body(cotangent, own, *rest):
@@ -385,7 +374,7 @@
     total = conv_weight.shape[1]
     left = total - share
     chans, bricks, reps = (lax.axis_size(axis) for axis in ("chan", "brick", "rep"))
-    chan, brick, rep = (lax.axis_index(axis) for axis in ("chan", "brick", "rep"))
+    place = [lax.axis_index(axis)[None] for axis in LINE]
     margin = sites + 2 * HALO
     flops = 2 * TAPS * share * sites
 
@@ -401,7 +390,16 @@
     assert reps == 2
     swap = [(0, 1), (1, 0)]
     rest = stack(around(features))
-    to_core, to_line = pack(rep, features, cotangent, neighbours)
+    to_core, to_line = kernel(
+        pack_body,
+        "pack",
+        [shape((share + max(share, 32), FAR))] * 2,
+        [features, cotangent, neighbours],
+        scalars=place,
+        scratch=[pltpu.VMEM((2, TAPS, HALO), jnp.int32), pltpu.SemaphoreType.DMA((6,))],
+        limit=58,
+        space=FAR_OFF,
+    )
     line = line_swap(to_line)
     core = lax.ppermute(to_core, "rep", swap)
     lanes = -(-TAPS * share // 128) * 128
@@ -416,7 +414,7 @@
             shape((TAPS, ROWS, margin)),
         ],
         [jnp.transpose(conv_weight, (0, 2, 1)), features, neighbours],
-        scalars=[(total - chan * share) % total],
+        scalars=place,
         scratch=[
             pltpu.VMEM((lanes, total), F32),
             pltpu.VMEM((TAPS, sites), F32),
@@ -424,14 +422,14 @@
             pltpu.VMEM((TAPS, sites), jnp.int32),
             pltpu.SemaphoreType.DMA((3,)),
         ],
-        space=pl.BlockSpec(memory_space=pl.ANY),
+        space=FAR_OFF,
     )
     before, behind, both = kernel(
-        after(ends_body, 1),
+        after(ends_body, 3),
         "ends",
         [shape(core.shape), shape(core.shape), shape((share, 2 * NEAR))],
         [own_weights, core, line],
-        scalars=[rep],
+        scalars=place,
     )
     ends = stack(around(both))
     begun, own_shifts, valid = kernel(
@@ -474,7 +472,7 @@
         "grad_weight",
         [shape((half, total), F32), shape((half, total)), shape(valid.shape), shape(grads.shape)],
         [across, valid, grads],
-        scalars=[rep],
+        scalars=place,
         scratch=[pltpu.VMEM((reps * half, total), F32)],
         aliases={1: 2, 2: 3},
         flops=flops * total,
@@ -499,11 +497,11 @@
     )
     size = half // 2
     mine, sent = kernel(
-        after(split_body, 1),
+        after(split_body, 3),
         "split",
         [shape((size, total), F32), shape((size, total))],
         [parts[0], kept, arrived],
-        scalars=[brick],
+        scalars=place,
         flops=LATER,
     )
     pairs = [(i, i ^ 1) for i in range(bricks)]
@@ -535,15 +533,15 @@
         )
     other = lax.ppermute(mine, "brick", pairs)
     side = kernel(
-        gather_body, "gather", shape((half, total)), [mine, other], scalars=[brick], flops=LATER
+        gather_body, "gather", shape((half, total)), [mine, other], scalars=place, flops=LATER
     )
     other = lax.ppermute(side, "rep", swap)
     grad_weight = kernel(
-        functools.partial(join_body, half),
+        functools.partial(join_body, half, share),
         "join",
         shape((TAPS * share, total), F32),
         [side, other],
-        scalars=[rep, chan * share],
+        scalars=place,
         scratch=[pltpu.VMEM((reps * half, total), BF16)],
         flops=LATER,
     )

time: 73.4 us -> 58.8 us (0.80)
  local copies, waits for them, and re-layouts: 17.9 us -> 3.14 us
  starting transfers between devices: 11.5 us -> 13.1 us
  waiting for transfers between devices: 12.9 us -> 11.5 us
    unnamed x20 -> x8, local copies, waits for them, and re-layouts: 17.9 us -> 3.14 us
    pallas_call x14 -> x15, Pallas kernels: 28.1 us -> 29.9 us  [kernel(): pl.pallas_call(body, out_shape=outs, in_specs=[SCALAR] * len(scalars) + [...]
    pallas_call x1 -> x0, Pallas kernels: 1.77 us -> none  [pack(): pl.pallas_call(pack_body, grid=(1,), out_shape=[shape((rows, FAR))] * 2,...]
    ppermute x1, starting transfers between devices: 1.79 us -> 2.66 us  [local(): other = lax.ppermute(mine, 'brick', [(i, i ^ step) for i in range(bricks)])]
    ppermute x1, waiting for transfers between devices: 6 us -> 5.16 us  [local(): other = lax.ppermute(mine, 'brick', [(i, i ^ step) for i in range(bricks)])]
  transfers between devices with their start and end apart: 10 -> 10, of which waited for: 4 -> 5; matrix products, arithmetic and copies ran while one was open for 0% -> 0% of each run, Pallas kernels for 23% -> 28%
where the time goes in v5:
time: 58.8 us; the launch traced here: 58.5 us
  Pallas kernels  29.9 us (51%)
  starting transfers between devices  13.1 us (22%)
  waiting for transfers between devices  11.5 us (20%)
  local copies, waits for them, and re-layouts  3.14 us (5%)
  between operations  0.78 us (1%)
    pallas_call x15, Pallas kernels, kernel(): pl.pallas_call(body, out_shape=outs, in_specs=[SCALAR] * len(scalars) + [...  29.9 us
    ppermute x1, waiting for transfers between devices, local(): other = lax.ppermute(mine, 'brick', [(i, i ^ step) for i in range(bricks)])  5.16 us
    ppermute x1, waiting for transfers between devices, local(): other = lax.ppermute(mine, 'brick', pairs)  4.29 us
    unnamed x8, local copies, waits for them, and re-layouts  3.14 us
    ppermute x2, starting transfers between devices, around(): lax.ppermute(x, 'chan', [((i + over) % chans, i) for i in range(chans)])  3.1 us
    ppermute x1, starting transfers between devices, local(): arrived = lax.ppermute(sent, 'rep', swap)  2.82 us
    ppermute x1, starting transfers between devices, local(): other = lax.ppermute(mine, 'brick', [(i, i ^ step) for i in range(bricks)])  2.66 us
    ppermute x1, starting transfers between devices, local(): arrived = lax.ppermute(sent, 'brick', pairs)  1.64 us
  transfers between devices with their start and end apart: 10, of which 5 were waited for; matrix products, arithmetic and copies ran while one was open for 0% of the time, Pallas kernels for 28%

profile of v5, /device:TPU:0, one launch (start us, length us, event | category | flops | bytes accessed | tf_op | source)
XLA Modules:
  0.0 58.5 jit_solution(15646104336669218559)
XLA Ops:
  0.6 3.0 %collective-permute-start.3 = (bf16[64,4608]{1,0:T(8,128)(2,1)}, bf16[64,4608]{1,0:T(8,128)(2,1)S(1)}, u32[]{:S(2)}, u32[]{:S(2)}) collective-permute-start(bf16[64,4608]{1,0:T(8,128)(2,1)} %features.3), channel_id=1, source_target_pairs={{2,0},{0,2},{3,1},{1,3},{6,4},{4,6},{7,5},{5,7},{10,8},{8,10},{11,... | collective-permute-start | bytes 1769480 | tf_op jit(solution)/shard_map/ppermute | solution.py:383
  3.6 1.8 %pack.1 = (bf16[128,768]{1,0:T(8,128)(2,1)}, bf16[128,768]{1,0:T(8,128)(2,1)}) custom-call(s32[1]{0:T(128)} %bitcast.brick.refs_0_, s32[1]{0:T(128)} %bitcast.1.chan.refs_1_, s32[1]{0:T(128)} %bitcast.2.rep.refs_2_, bf16[64,4608]{1,0:T(8,128)(2,1)} %features.3, bf16[64,4608]{1,0:T(8,128)(2,1)} %cotangent.5, s32[27,4608]{1,0:T(8,128)} %neighbours.3), custom_call_target="tpu_custom_call" | custom-call | bytes 1048576 | tf_op jit(solution)/shard_map/pack/pallas_call | solution.py:35
  5.5 0.1 collective-permute-start
  5.5 0.7 %collective-permute-start.1 = (bf16[128,768]{1,0:T(8,128)(2,1)}, bf16[128,768]{1,0:T(8,128)(2,1)S(1)}, u32[]{:S(2)}, u32[]{:S(2)}) collective-permute-start(bf16[128,768]{1,0:T(8,128)(2,1)} %get-tuple-element.36), channel_id=1, source_target_pairs={{1,4},{4,1},{5,8},{8,5},{9,12},{12,9},{3,6},{6,3},{7,10},{10,7},{1... | collective-permute-start | bytes 589832 | tf_op jit(solution)/shard_map/ppermute | solution.py:369
  6.2 0.0 copy-start.1
  6.2 1.1 %copy-done.1 = s32[27,4608]{1,0:T(8,128)S(1)} copy-done((s32[27,4608]{1,0:T(8,128)S(1)}, s32[27,4608]{1,0:T(8,128)}, u32[]{:S(2)}) %copy-start.1) | copy-done | bytes 497688
  7.3 0.0 copy-start.2
  7.3 1.1 %copy-done.2 = bf16[64,4608]{1,0:T(8,128)(2,1)S(1)} copy-done((bf16[64,4608]{1,0:T(8,128)(2,1)S(1)}, bf16[64,4608]{1,0:T(8,128)(2,1)}, u32[]{:S(2)}) %copy-start.2) | copy-done | bytes 589848
  8.3 0.0 copy-start.3
  8.3 1.0 %copy-done.3 = bf16[27,128,64]{1,2,0:T(8,128)(2,1)S(1)} copy-done((bf16[27,128,64]{1,2,0:T(8,128)(2,1)S(1)}, bf16[27,128,64]{1,2,0:T(8,128)(2,1)}, u32[]{:S(2)}) %copy-start.3) | copy-done | bytes 442392
  9.4 2.9 %prepare.1 = (bf16[64,1728]{1,0:T(8,128)(2,1)S(1)}, bf16[64,1728]{1,0:T(8,128)(2,1)S(1)}, bf16[128,1792]{1,0:T(8,128)(2,1)S(1)}, bf16[9,64,6144]{2,1,0:T(8,128)(2,1)S(1)}, bf16[27,16,5376]{2,1,0:T(8,128)(2,1)S(1)}) custom-call(s32[1]{0:T(128)} %bitcast.brick.refs_0_, s32[1]{0:T(128)} %bitcast.1.chan.refs_1_, s32[1]{0:T(128)} %bitcast.2.rep.refs_2_, ...), custom_call_target="tpu_custom_call" | custom-call | bytes 1048576 | tf_op jit(solution)/shard_map/prepare/pallas_call | solution.py:35
  12.3 0.0 collective-permute-done.refs_4_
  12.3 0.0 collective-permute-done.1.refs_5_
  12.3 0.1 ends.1
  12.4 0.1 collective-permute-start.2
  12.5 5.1 %forward_own.1 = (f32[64,5376]{1,0:T(8,128)S(1)}, bf16[9,64,6144]{2,1,0:T(8,128)(2,1)S(1)}, bf16[27,16,5376]{2,1,0:T(8,128)(2,1)S(1)}) custom-call(bf16[128,768]{1,0:T(8,128)(2,1)S(1)} %get-tuple-element.38.left, bf16[128,768]{1,0:T(8,128)(2,1)S(1)} %get-tuple-element.39.right, ...), custom_call_target="tpu_custom_call", output_to_operand_aliasing={{1}: (3, {}), {2}: (4, {})} | custom-call | bytes 1048576 | tf_op jit(solution)/shard_map/forward_own/pallas_call | solution.py:35
  17.6 0.0 copy-start
  17.6 0.0 collective-permute-done.3.rest
  17.6 1.9 %arrive.1 = (bf16[9,64,6144]{2,1,0:T(8,128)(2,1)S(1)}, bf16[4608,128]{1,0:T(8,128)(2,1)S(1)}, bf16[9,64,6144]{2,1,0:T(8,128)(2,1)S(1)}) custom-call(bf16[64,4608]{1,0:T(8,128)(2,1)S(1)} %collective-permute-done.3.rest, bf16[9,64,6144]{2,1,0:T(8,128)(2,1)S(1)} %get-tuple-element.42.own_in), custom_call_target="tpu_custom_call", output_to_operand_aliasing={{2}: (1, {})} | custom-call | bytes 1048576 | tf_op jit(solution)/shard_map/arrive/pallas_call | solution.py:35
  19.5 0.4 collective-permute-done.2.ends
  19.9 0.0 copy-done
  19.9 6.8 %forward_rest.1 = (bf16[64,4608]{1,0:T(8,128)(2,1)}, bf16[9,64,6144]{2,1,0:T(8,128)(2,1)S(1)}, bf16[27,16,5376]{2,1,0:T(8,128)(2,1)S(1)}, bf16[9,64,6144]{2,1,0:T(8,128)(2,1)S(1)}) custom-call(bf16[64,1280]{1,0:T(8,128)(2,1)S(1)} %collective-permute-done.2.ends, ...), custom_call_target="tpu_custom_call", output_to_operand_aliasing={{3}: (1, {}), {2}: (3, {})} | custom-call | flops 1019215872 | bytes 1048576 | tf_op jit(solution)/shard_map/forward_rest/pallas_call | solution.py:35
  26.7 5.4 %grad_weight.1 = (f32[896,128]{1,0:T(8,128)S(1)}, bf16[896,128]{1,0:T(8,128)(2,1)S(1)}, bf16[27,16,5376]{2,1,0:T(8,128)(2,1)S(1)}, bf16[9,64,6144]{2,1,0:T(8,128)(2,1)S(1)}) custom-call(s32[1]{0:T(128)} %bitcast.brick.refs_0_, s32[1]{0:T(128)} %bitcast.1.chan.refs_1_, s32[1]{0:T(128)} %bitcast.2.rep.refs_2_, ...), custom_call_target="tpu_custom_call", output_to_operand_aliasing={{2}: (4, {}), {3}: (5, {})} | custom-call | flops 2038431744 | bytes 1048576 | tf_op jit(solution)/shard_map/grad_weight/pallas_call | solution.py:35
  32.2 2.8 %collective-permute-start.4 = (bf16[896,128]{1,0:T(8,128)(2,1)S(1)}, bf16[896,128]{1,0:T(8,128)(2,1)S(1)}, u32[]{:S(2)}, u32[]{:S(2)}) collective-permute-start(bf16[896,128]{1,0:T(8,128)(2,1)S(1)} %get-tuple-element.57), channel_id=1, source_target_pairs={{0,1},{1,0},{2,3},{3,2},{4,5},{5,4},{6,7},{7,6},{8,9},{9,8},{10,11... | collective-permute-start | bytes 688136 | tf_op jit(solution)/shard_map/ppermute | solution.py:480
  35.0 1.8 %grad_features_0.1 = (bf16[27,16,5376]{2,1,0:T(8,128)(2,1)S(1)}, bf16[9,64,6144]{2,1,0:T(8,128)(2,1)S(1)}, f32[64,4608]{1,0:T(8,128)S(1)}, bf16[64,4608]{1,0:T(8,128)(2,1)S(1)}) custom-call(bf16[128,1792]{1,0:T(8,128)(2,1)S(1)} %get-tuple-element.49.weights.refs_1_, ...), custom_call_target="tpu_custom_call", output_to_operand_aliasing={{0}: (1, {}), {1}: (2, {})} | custom-call | flops 1019215872 | bytes 1048576 | tf_op jit(solution)/shard_map/grad_features_0/pallas_call | solution.py:35
  36.8 0.0 collective-permute-done.4.refs_5_
  36.8 0.1 split.1
  36.9 1.6 %collective-permute-start.6 = (bf16[448,128]{1,0:T(8,128)(2,1)S(1)}, bf16[448,128]{1,0:T(8,128)(2,1)S(1)}, u32[]{:S(2)}, u32[]{:S(2)}) collective-permute-start(bf16[448,128]{1,0:T(8,128)(2,1)S(1)} %get-tuple-element.64), channel_id=1, source_target_pairs={{0,4},{4,0},{8,12},{12,8},{1,5},{5,1},{9,13},{13,9},{2,6},{6,2},{1... | collective-permute-start | bytes 344072 | tf_op jit(solution)/shard_map/ppermute | solution.py:508
  38.5 1.8 %grad_features_1.1 = (f32[64,4608]{1,0:T(8,128)S(1)}, bf16[64,4608]{1,0:T(8,128)(2,1)S(1)}) custom-call(f32[448,128]{1,0:T(8,128)S(1)} %get-tuple-element.58.refs_0_.refs_1_, bf16[128,1792]{1,0:T(8,128)(2,1)S(1)} %get-tuple-element.49.weights.refs_1_, ...), custom_call_target="tpu_custom_call", output_to_operand_aliasing={{0}: (4, {}), {1}: (5, {})} | custom-call | flops 1019215872 | bytes 1048576 | tf_op jit(solution)/shard_map/grad_features_1/pallas_call | solution.py:35
  40.3 1.5 %collective-permute-start.5 = (bf16[64,4608]{1,0:T(8,128)(2,1)S(1)}, bf16[64,4608]{1,0:T(8,128)(2,1)S(1)}, u32[]{:S(2)}, u32[]{:S(2)}) collective-permute-start(bf16[64,4608]{1,0:T(8,128)(2,1)S(1)} %get-tuple-element.63), channel_id=1, source_target_pairs={{0,2},{2,0},{1,3},{3,1},{4,6},{6,4},{5,7},{7,5},{8,10},{10,8},{9,1... | collective-permute-start | bytes 1769480 | tf_op jit(solution)/shard_map/ppermute | solution.py:513
  41.9 0.1 collective-permute-done.6.refs_2_
  42.0 2.7 %collective-permute-start.7 = (bf16[448,128]{1,0:T(8,128)(2,1)S(1)}, bf16[448,128]{1,0:T(8,128)(2,1)S(1)}, u32[]{:S(2)}, u32[]{:S(2)}) collective-permute-start(bf16[448,128]{1,0:T(8,128)(2,1)S(1)} %merge_1.1.mine), channel_id=1, source_target_pairs={{0,8},{4,12},{8,0},{12,4},{1,9},{5,13},{9,1},{13,5},{2,10},{6,14},... | collective-permute-start | bytes 344072 | tf_op jit(solution)/shard_map/ppermute | solution.py:529
  44.7 5.2 %collective-permute-done.7.other = bf16[448,128]{1,0:T(8,128)(2,1)S(1)} collective-permute-done((bf16[448,128]{1,0:T(8,128)(2,1)S(1)}, bf16[448,128]{1,0:T(8,128)(2,1)S(1)}, u32[]{:S(2)}, u32[]{:S(2)}) %collective-permute-start.7) | collective-permute-done | bytes 114720 | tf_op jit(solution)/shard_map/ppermute | solution.py:529
  49.9 0.6 collective-permute-start.8
  50.4 4.3 %collective-permute-done.8.other = bf16[448,128]{1,0:T(8,128)(2,1)S(1)} collective-permute-done((bf16[448,128]{1,0:T(8,128)(2,1)S(1)}, bf16[448,128]{1,0:T(8,128)(2,1)S(1)}, u32[]{:S(2)}, u32[]{:S(2)}) %collective-permute-start.8) | collective-permute-done | bytes 114720 | tf_op jit(solution)/shard_map/ppermute | solution.py:534
  54.8 0.1 collective-permute-start.9
  54.8 1.5 %collective-permute-done.9.other = bf16[896,128]{1,0:T(8,128)(2,1)S(1)} collective-permute-done((bf16[896,128]{1,0:T(8,128)(2,1)S(1)}, bf16[896,128]{1,0:T(8,128)(2,1)S(1)}, u32[]{:S(2)}, u32[]{:S(2)}) %collective-permute-start.9) | collective-permute-done | bytes 229408 | tf_op jit(solution)/shard_map/ppermute | solution.py:538
  56.3 1.1 %join.1 = f32[1728,128]{1,0:T(8,128)} custom-call(s32[1]{0:T(128)} %bitcast.brick.refs_0_, s32[1]{0:T(128)} %bitcast.1.chan.refs_1_, s32[1]{0:T(128)} %bitcast.2.rep.refs_2_, bf16[896,128]{1,0:T(8,128)(2,1)S(1)} %gather.1.side, bf16[896,128]{1,0:T(8,128)(2,1)S(1)} %collective-permute-done.9.other), custom_call_target="tpu_custom_call" | custom-call | flops 250000000 | bytes 1048576 | tf_op jit(solution)/shard_map/join/pallas_call | solution.py:35
  57.4 0.0 collective-permute-done.5.rest_0_
  57.4 1.0 %add.1 = bf16[64,4608]{1,0:T(8,128)(2,1)} custom-call(bf16[64,4608]{1,0:T(8,128)(2,1)S(1)} %copy-done, f32[64,4608]{1,0:T(8,128)S(1)} %get-tuple-element.62.own.refs_0_, bf16[64,4608]{1,0:T(8,128)(2,1)S(1)} %collective-permute-done.5.rest_0_), custom_call_target="tpu_custom_call" | custom-call | bytes 1048576 | tf_op jit(solution)/shard_map/add/pallas_call | solution.py:35
  (3 shorter events, 0.1 us)
Async XLA Ops:
  0.6 16.9 %collective-permute-start.3 = (bf16[64,4608]{1,0:T(8,128)(2,1)}, bf16[64,4608]{1,0:T(8,128)(2,1)S(1)}, u32[]{:S(2)}, u32[]{:S(2)}) collective-permute-start(bf16[64,4608]{1,0:T(8,128)(2,1)} %features.3), channel_id=1, source_target_pairs={{2,0},{0,2},{3,1},{1,3},{6,4},{4,6},{7,5},{5,7},{10,8},{8,10},{11,... | collective-permute-start | bytes 1769480 | tf_op jit(solution)/shard_map/ppermute | solution.py:383
  5.5 6.8 %collective-permute-start = (bf16[128,768]{1,0:T(8,128)(2,1)}, bf16[128,768]{1,0:T(8,128)(2,1)S(1)}, u32[]{:S(2)}, u32[]{:S(2)}) collective-permute-start(bf16[128,768]{1,0:T(8,128)(2,1)} %get-tuple-element.35), channel_id=1, source_target_pairs={{0,1},{1,0},{2,3},{3,2},{4,5},{5,4},{6,7},{7,6},{8,9},{9,8},{10,11... | collective-permute-start | bytes 589832 | tf_op jit(solution)/shard_map/ppermute | solution.py:404
  5.5 6.8 %collective-permute-start.1 = (bf16[128,768]{1,0:T(8,128)(2,1)}, bf16[128,768]{1,0:T(8,128)(2,1)S(1)}, u32[]{:S(2)}, u32[]{:S(2)}) collective-permute-start(bf16[128,768]{1,0:T(8,128)(2,1)} %get-tuple-element.36), channel_id=1, source_target_pairs={{1,4},{4,1},{5,8},{8,5},{9,12},{12,9},{3,6},{6,3},{7,10},{10,7},{1... | collective-permute-start | bytes 589832 | tf_op jit(solution)/shard_map/ppermute | solution.py:369
  6.2 1.1 %copy-start.1 = (s32[27,4608]{1,0:T(8,128)S(1)}, s32[27,4608]{1,0:T(8,128)}, u32[]{:S(2)}) copy-start(s32[27,4608]{1,0:T(8,128)} %neighbours.3) | copy-start | bytes 1492996
  7.3 1.1 %copy-start.2 = (bf16[64,4608]{1,0:T(8,128)(2,1)S(1)}, bf16[64,4608]{1,0:T(8,128)(2,1)}, u32[]{:S(2)}) copy-start(bf16[64,4608]{1,0:T(8,128)(2,1)} %features.3) | copy-start | bytes 1769476
  8.3 1.0 %copy-start.3 = (bf16[27,128,64]{1,2,0:T(8,128)(2,1)S(1)}, bf16[27,128,64]{1,2,0:T(8,128)(2,1)}, u32[]{:S(2)}) copy-start(bf16[27,128,64]{1,2,0:T(8,128)(2,1)} %param.5) | copy-start | bytes 1327108
  12.4 7.6 %collective-permute-start.2 = (bf16[64,1280]{1,0:T(8,128)(2,1)S(1)}, bf16[64,1280]{1,0:T(8,128)(2,1)S(1)}, u32[]{:S(2)}, u32[]{:S(2)}) collective-permute-start(bf16[64,1280]{1,0:T(8,128)(2,1)S(1)} %get-tuple-element.37), channel_id=1, source_target_pairs={{2,0},{0,2},{3,1},{1,3},{6,4},{4,6},{7,5},{5,7},{10,8},{8,10},{11,... | collective-permute-start | bytes 491528 | tf_op jit(solution)/shard_map/ppermute | solution.py:383
  17.6 2.4 %copy-start = (bf16[64,4608]{1,0:T(8,128)(2,1)S(1)}, bf16[64,4608]{1,0:T(8,128)(2,1)}, u32[]{:S(2)}) copy-start(bf16[64,4608]{1,0:T(8,128)(2,1)} %cotangent.5) | copy-start | bytes 1769476
  32.2 4.6 %collective-permute-start.4 = (bf16[896,128]{1,0:T(8,128)(2,1)S(1)}, bf16[896,128]{1,0:T(8,128)(2,1)S(1)}, u32[]{:S(2)}, u32[]{:S(2)}) collective-permute-start(bf16[896,128]{1,0:T(8,128)(2,1)S(1)} %get-tuple-element.57), channel_id=1, source_target_pairs={{0,1},{1,0},{2,3},{3,2},{4,5},{5,4},{6,7},{7,6},{8,9},{9,8},{10,11... | collective-permute-start | bytes 688136 | tf_op jit(solution)/shard_map/ppermute | solution.py:480
  36.9 5.1 %collective-permute-start.6 = (bf16[448,128]{1,0:T(8,128)(2,1)S(1)}, bf16[448,128]{1,0:T(8,128)(2,1)S(1)}, u32[]{:S(2)}, u32[]{:S(2)}) collective-permute-start(bf16[448,128]{1,0:T(8,128)(2,1)S(1)} %get-tuple-element.64), channel_id=1, source_target_pairs={{0,4},{4,0},{8,12},{12,8},{1,5},{5,1},{9,13},{13,9},{2,6},{6,2},{1... | collective-permute-start | bytes 344072 | tf_op jit(solution)/shard_map/ppermute | solution.py:508
  40.3 17.1 %collective-permute-start.5 = (bf16[64,4608]{1,0:T(8,128)(2,1)S(1)}, bf16[64,4608]{1,0:T(8,128)(2,1)S(1)}, u32[]{:S(2)}, u32[]{:S(2)}) collective-permute-start(bf16[64,4608]{1,0:T(8,128)(2,1)S(1)} %get-tuple-element.63), channel_id=1, source_target_pairs={{0,2},{2,0},{1,3},{3,1},{4,6},{6,4},{5,7},{7,5},{8,10},{10,8},{9,1... | collective-permute-start | bytes 1769480 | tf_op jit(solution)/shard_map/ppermute | solution.py:513
  42.0 7.8 %collective-permute-start.7 = (bf16[448,128]{1,0:T(8,128)(2,1)S(1)}, bf16[448,128]{1,0:T(8,128)(2,1)S(1)}, u32[]{:S(2)}, u32[]{:S(2)}) collective-permute-start(bf16[448,128]{1,0:T(8,128)(2,1)S(1)} %merge_1.1.mine), channel_id=1, source_target_pairs={{0,8},{4,12},{8,0},{12,4},{1,9},{5,13},{9,1},{13,5},{2,10},{6,14},... | collective-permute-start | bytes 344072 | tf_op jit(solution)/shard_map/ppermute | solution.py:529
  49.9 4.9 %collective-permute-start.8 = (bf16[448,128]{1,0:T(8,128)(2,1)S(1)}, bf16[448,128]{1,0:T(8,128)(2,1)S(1)}, u32[]{:S(2)}, u32[]{:S(2)}) collective-permute-start(bf16[448,128]{1,0:T(8,128)(2,1)S(1)} %merge_4.1.mine), channel_id=1, source_target_pairs={{0,4},{4,0},{8,12},{12,8},{1,5},{5,1},{9,13},{13,9},{2,6},{6,2},{1... | collective-permute-start | bytes 344072 | tf_op jit(solution)/shard_map/ppermute | solution.py:534
  54.8 1.6 %collective-permute-start.9 = (bf16[896,128]{1,0:T(8,128)(2,1)S(1)}, bf16[896,128]{1,0:T(8,128)(2,1)S(1)}, u32[]{:S(2)}, u32[]{:S(2)}) collective-permute-start(bf16[896,128]{1,0:T(8,128)(2,1)S(1)} %gather.1.side), channel_id=1, source_target_pairs={{0,1},{1,0},{2,3},{3,2},{4,5},{5,4},{6,7},{7,6},{8,9},{9,8},{10,11... | collective-permute-start | bytes 688136 | tf_op jit(solution)/shard_map/ppermute | solution.py:538

commit v6 on v5

--- a/solution.py
+++ b/solution.py
@@ -304,13 +304,9 @@
     sent[...] = total[pl.ds(pl.multiple_of((1 - mine) * half, ROWS), half), :].astype(BF16)
 
 
-def feature_body(part, weights, valid, grads, *refs):
-    own, rest = refs[-2:]
-    share, sites = own.shape
-    begin = part * sites // 2
-
+def feature_body(weights, valid, grads, own, rest):
     def block(j, carry):
-        start = pl.multiple_of(begin + j * WIDTH, 128)
+        start = pl.multiple_of(j * WIDTH, 128)
         here = pl.ds(start, WIDTH)
         total = product(
             weights,
@@ -321,31 +317,29 @@
             WIDTH,
             lambda tap: TAPS - 1 - tap,
         )
-        own[:, here] = total[:share]
-        rest[:, here] = total[share:].astype(BF16)
+        own[:, here] = total[: own.shape[0]]
+        rest[:, here] = total[own.shape[0] :].astype(BF16)
         return carry
 
-    lax.fori_loop(0, sites // 2 // WIDTH, block, 0)
+    lax.fori_loop(0, own.shape[1] // WIDTH, block, 0)
 
 
 def split_body(brick, chan, rep, kept, arrived, mine, sent):
     size = mine.shape[0]
-    at = brick[0] % 2
-    mine_rows = pl.ds(pl.multiple_of(at * size, ROWS), size)
-    sent_rows = pl.ds(pl.multiple_of((1 - at) * size, ROWS), size)
-    mine[...] = kept[mine_rows, :] + arrived[mine_rows, :].astype(F32)
-    sent[...] = (kept[sent_rows, :] + arrived[sent_rows, :].astype(F32)).astype(BF16)
-
-
-def merge_body(mine, other, out):
-    out[...] = (mine[...].astype(F32) + other[...].astype(F32)).astype(BF16)
-
-
-def gather_body(brick, chan, rep, mine, other, side):
+    rows = pl.ds(pl.multiple_of(brick[0] * size, ROWS), size)
+    mine[...] = kept[rows, :] + arrived[rows, :].astype(F32)
+    sent[...] = (kept[...] + arrived[...].astype(F32)).astype(BF16)
+
+
+def merge_body(brick, chan, rep, mine, others, out):
     size = mine.shape[0]
-    at = brick[0] % 2
-    side[pl.ds(pl.multiple_of(at * size, ROWS), size), :] = mine[...]
-    side[pl.ds(pl.multiple_of((1 - at) * size, ROWS), size), :] = other[...]
+    count = others.shape[0] // size
+    total = mine[...]
+    for at in range(count):
+        part = others[at * size : (at + 1) * size, :].astype(F32)
+        total += jnp.where(brick[0] == at, 0.0, part)
+    for at in range(count):
+        out[at * size : (at + 1) * size, :] = total.astype(BF16)
 
 
 def join_body(half, share, brick, chan, rep, side, other, out, both):
@@ -479,35 +473,12 @@
     )
     arrived = lax.ppermute(sent, "rep", swap)
 
-    def feature_part(part, body, args, kept):
-        outs = [shape((share, sites), F32), shape((left, sites))]
-        return kernel(
-            body,
-            "grad_features_%d" % part,
-            [shape(x.shape) for x in kept] + outs,
-            args,
-            aliases={len(args) - len(kept) + i: i for i in range(len(kept))}
-            if part == 0
-            else {len(args) - 2 + i: i for i in range(2)},
-            flops=flops * total // 2,
-        )
-
-    valid, grads, *parts = feature_part(
-        0, functools.partial(feature_body, 0), [by_in, valid, grads], [valid, grads]
-    )
-    size = half // 2
-    mine, sent = kernel(
-        after(split_body, 3),
-        "split",
-        [shape((size, total), F32), shape((size, total))],
-        [parts[0], kept, arrived],
-        scalars=place,
-        flops=LATER,
-    )
-    pairs = [(i, i ^ 1) for i in range(bricks)]
-    arrived = lax.ppermute(sent, "brick", pairs)
-    own, other = feature_part(
-        1, after(functools.partial(feature_body, 1), 0), [mine, by_in, valid, grads, *parts], []
+    own, other = kernel(
+        feature_body,
+        "grad_features",
+        [shape((share, sites), F32), shape((left, sites))],
+        [by_in, valid, grads],
+        flops=flops * total,
     )
     terms = [
         lax.ppermute(
@@ -517,24 +488,29 @@
         )
         for over in range(1, chans)
     ]
-    mine = kernel(
-        after(merge_body, 0),
-        "merge_1",
-        shape((size, total)),
-        [own, mine, arrived],
+
+    mine, sent = kernel(
+        after(split_body, 3),
+        "split",
+        [shape((piece, total), F32), shape((half, total))],
+        [own, kept, arrived],
+        scalars=place,
         flops=LATER,
     )
-    step = 2
-    while step < bricks:
-        other = lax.ppermute(mine, "brick", [(i, i ^ step) for i in range(bricks)])
-        step *= 2
-        mine = kernel(
-            merge_body, "merge_%d" % step, shape((size, total)), [mine, other], flops=LATER
-        )
-    other = lax.ppermute(mine, "brick", pairs)
-    side = kernel(
-        gather_body, "gather", shape((half, total)), [mine, other], scalars=place, flops=LATER
-    )
+
+    def across_bricks(x):
+        return lax.all_to_all(x, "brick", split_axis=0, concat_axis=0, tiled=True)
+
+    arrived = across_bricks(sent)
+    done = kernel(
+        merge_body,
+        "merge",
+        shape((half, total)),
+        [mine, arrived],
+        scalars=place,
+        flops=LATER,
+    )
+    side = across_bricks(done)
     other = lax.ppermute(side, "rep", swap)
     grad_weight = kernel(
         functools.partial(join_body, half, share),

time: 58.8 us -> 65.4 us (1.11)
  blocking collectives: 0 us -> 10.1 us
  waiting for transfers between devices: 11.5 us -> 8.29 us
  starting transfers between devices: 13.1 us -> 12.2 us
  Pallas kernels: 29.9 us -> 30.6 us
    all_to_all x0 -> x1, blocking collectives: none -> 10.1 us  [across_bricks(): return lax.all_to_all(x, 'brick', split_axis=0, concat_axis=0, tiled=True)]
    ppermute x3 -> x0, waiting for transfers between devices: 9.57 us -> none  [the longest x1 5.16 us: local(): other = lax.ppermute(mine, 'brick', [(i, i ^ step) for i in range(bricks)])]
    all_to_all x0 -> x1, waiting for transfers between devices: none -> 7.35 us  [across_bricks(): return lax.all_to_all(x, 'brick', split_axis=0, concat_axis=0, tiled=True)]
    ppermute x3 -> x0, starting transfers between devices: 4.87 us -> none  [the longest x1 2.66 us: local(): other = lax.ppermute(mine, 'brick', [(i, i ^ step) for i in range(bricks)])]
    all_to_all x0 -> x1, starting transfers between devices: none -> 4.03 us  [across_bricks(): return lax.all_to_all(x, 'brick', split_axis=0, concat_axis=0, tiled=True)]
    ppermute x1, waiting for transfers between devices: 1.48 us -> 0.49 us  [local(): other = lax.ppermute(side, 'rep', swap)]
    pallas_call x15 -> x12, Pallas kernels: 29.9 us -> 30.6 us  [kernel(): pl.pallas_call(body, out_shape=outs, in_specs=[SCALAR] * len(scalars) + [...]
  transfers between devices with their start and end apart: 10 -> 8, of which waited for: 5 -> 3; matrix products, arithmetic and copies ran while one was open for 0% -> 0% of each run, Pallas kernels for 28% -> 25%
where the time goes in v6:
time: 65.4 us; the launch traced here: 65 us
  Pallas kernels  30.6 us (47%)
  starting transfers between devices  12.2 us (19%)
  blocking collectives  10.1 us (15%)
  waiting for transfers between devices  8.29 us (13%)
  local copies, waits for them, and re-layouts  3.14 us (5%)
  between operations  0.75 us (1%)
    pallas_call x12, Pallas kernels, kernel(): pl.pallas_call(body, out_shape=outs, in_specs=[SCALAR] * len(scalars) + [...  30.6 us
    all_to_all x1, blocking collectives, across_bricks(): return lax.all_to_all(x, 'brick', split_axis=0, concat_axis=0, tiled=True)  10.1 us
    all_to_all x1, waiting for transfers between devices, across_bricks(): return lax.all_to_all(x, 'brick', split_axis=0, concat_axis=0, tiled=True)  7.35 us
    all_to_all x1, starting transfers between devices, across_bricks(): return lax.all_to_all(x, 'brick', split_axis=0, concat_axis=0, tiled=True)  4.03 us
    unnamed x8, local copies, waits for them, and re-layouts  3.14 us
    ppermute x2, starting transfers between devices, around(): lax.ppermute(x, 'chan', [((i + over) % chans, i) for i in range(chans)])  3.1 us
    ppermute x1, starting transfers between devices, local(): arrived = lax.ppermute(sent, 'rep', swap)  2.8 us
    ppermute x1, starting transfers between devices, local(): lax.ppermute(other if left == share else other[(over - 1) * share:over *...  1.48 us
  transfers between devices with their start and end apart: 8, of which 3 were waited for; matrix products, arithmetic and copies ran while one was open for 0% of the time, Pallas kernels for 25%

profile of v6, /device:TPU:0, one launch (start us, length us, event | category | flops | bytes accessed | tf_op | source)
XLA Modules:
  0.0 65.0 jit_solution(16577012450432280951)
XLA Ops:
  0.6 3.0 %collective-permute-start.3 = (bf16[64,4608]{1,0:T(8,128)(2,1)}, bf16[64,4608]{1,0:T(8,128)(2,1)S(1)}, u32[]{:S(2)}, u32[]{:S(2)}) collective-permute-start(bf16[64,4608]{1,0:T(8,128)(2,1)} %features.3), channel_id=1, source_target_pairs={{2,0},{0,2},{3,1},{1,3},{6,4},{4,6},{7,5},{5,7},{10,8},{8,10},{11,... | collective-permute-start | bytes 1769480 | tf_op jit(solution)/shard_map/ppermute | solution.py:377
  3.6 1.8 %pack.1 = (bf16[128,768]{1,0:T(8,128)(2,1)}, bf16[128,768]{1,0:T(8,128)(2,1)}) custom-call(s32[1]{0:T(128)} %bitcast.brick.refs_0_, s32[1]{0:T(128)} %bitcast.1.chan.refs_1_, s32[1]{0:T(128)} %bitcast.2.rep.refs_2_, bf16[64,4608]{1,0:T(8,128)(2,1)} %features.3, bf16[64,4608]{1,0:T(8,128)(2,1)} %cotangent.5, s32[27,4608]{1,0:T(8,128)} %neighbours.3), custom_call_target="tpu_custom_call" | custom-call | bytes 1048576 | tf_op jit(solution)/shard_map/pack/pallas_call | solution.py:35
  5.5 0.1 collective-permute-start
  5.5 0.7 %collective-permute-start.1 = (bf16[128,768]{1,0:T(8,128)(2,1)}, bf16[128,768]{1,0:T(8,128)(2,1)S(1)}, u32[]{:S(2)}, u32[]{:S(2)}) collective-permute-start(bf16[128,768]{1,0:T(8,128)(2,1)} %get-tuple-element.32), channel_id=1, source_target_pairs={{1,4},{4,1},{5,8},{8,5},{9,12},{12,9},{3,6},{6,3},{7,10},{10,7},{1... | collective-permute-start | bytes 589832 | tf_op jit(solution)/shard_map/ppermute | solution.py:363
  6.2 0.0 copy-start.1
  6.2 1.1 %copy-done.1 = s32[27,4608]{1,0:T(8,128)S(1)} copy-done((s32[27,4608]{1,0:T(8,128)S(1)}, s32[27,4608]{1,0:T(8,128)}, u32[]{:S(2)}) %copy-start.1) | copy-done | bytes 497688
  7.3 0.0 copy-start.2
  7.3 1.1 %copy-done.2 = bf16[64,4608]{1,0:T(8,128)(2,1)S(1)} copy-done((bf16[64,4608]{1,0:T(8,128)(2,1)S(1)}, bf16[64,4608]{1,0:T(8,128)(2,1)}, u32[]{:S(2)}) %copy-start.2) | copy-done | bytes 589848
  8.3 0.0 copy-start.3
  8.3 1.0 %copy-done.3 = bf16[27,128,64]{1,2,0:T(8,128)(2,1)S(1)} copy-done((bf16[27,128,64]{1,2,0:T(8,128)(2,1)S(1)}, bf16[27,128,64]{1,2,0:T(8,128)(2,1)}, u32[]{:S(2)}) %copy-start.3) | copy-done | bytes 442392
  9.4 2.9 %prepare.1 = (bf16[64,1728]{1,0:T(8,128)(2,1)S(1)}, bf16[64,1728]{1,0:T(8,128)(2,1)S(1)}, bf16[128,1792]{1,0:T(8,128)(2,1)S(1)}, bf16[9,64,6144]{2,1,0:T(8,128)(2,1)S(1)}, bf16[27,16,5376]{2,1,0:T(8,128)(2,1)S(1)}) custom-call(s32[1]{0:T(128)} %bitcast.brick.refs_0_, s32[1]{0:T(128)} %bitcast.1.chan.refs_1_, s32[1]{0:T(128)} %bitcast.2.rep.refs_2_, ...), custom_call_target="tpu_custom_call" | custom-call | bytes 1048576 | tf_op jit(solution)/shard_map/prepare/pallas_call | solution.py:35
  12.3 0.0 collective-permute-done.refs_4_
  12.3 0.0 collective-permute-done.1.refs_5_
  12.3 0.1 ends.1
  12.4 0.1 collective-permute-start.2
  12.5 0.0 copy-start
  12.5 5.1 %forward_own.1 = (f32[64,5376]{1,0:T(8,128)S(1)}, bf16[9,64,6144]{2,1,0:T(8,128)(2,1)S(1)}, bf16[27,16,5376]{2,1,0:T(8,128)(2,1)S(1)}) custom-call(bf16[128,768]{1,0:T(8,128)(2,1)S(1)} %get-tuple-element.34.left, bf16[128,768]{1,0:T(8,128)(2,1)S(1)} %get-tuple-element.35.right, ...), custom_call_target="tpu_custom_call", output_to_operand_aliasing={{1}: (3, {}), {2}: (4, {})} | custom-call | bytes 1048576 | tf_op jit(solution)/shard_map/forward_own/pallas_call | solution.py:35
  17.6 0.0 collective-permute-done.3.rest
  17.6 1.9 %arrive.1 = (bf16[9,64,6144]{2,1,0:T(8,128)(2,1)S(1)}, bf16[4608,128]{1,0:T(8,128)(2,1)S(1)}, bf16[9,64,6144]{2,1,0:T(8,128)(2,1)S(1)}) custom-call(bf16[64,4608]{1,0:T(8,128)(2,1)S(1)} %collective-permute-done.3.rest, bf16[9,64,6144]{2,1,0:T(8,128)(2,1)S(1)} %get-tuple-element.38.own_in), custom_call_target="tpu_custom_call", output_to_operand_aliasing={{2}: (1, {})} | custom-call | bytes 1048576 | tf_op jit(solution)/shard_map/arrive/pallas_call | solution.py:35
  19.5 0.4 collective-permute-done.2.ends
  19.9 0.0 copy-done
  19.9 6.8 %forward_rest.1 = (bf16[64,4608]{1,0:T(8,128)(2,1)}, bf16[9,64,6144]{2,1,0:T(8,128)(2,1)S(1)}, bf16[27,16,5376]{2,1,0:T(8,128)(2,1)S(1)}, bf16[9,64,6144]{2,1,0:T(8,128)(2,1)S(1)}) custom-call(bf16[64,1280]{1,0:T(8,128)(2,1)S(1)} %collective-permute-done.2.ends, ...), custom_call_target="tpu_custom_call", output_to_operand_aliasing={{3}: (1, {}), {2}: (3, {})} | custom-call | flops 1019215872 | bytes 1048576 | tf_op jit(solution)/shard_map/forward_rest/pallas_call | solution.py:35
  26.7 5.4 %grad_weight.1 = (f32[896,128]{1,0:T(8,128)S(1)}, bf16[896,128]{1,0:T(8,128)(2,1)S(1)}, bf16[27,16,5376]{2,1,0:T(8,128)(2,1)S(1)}, bf16[9,64,6144]{2,1,0:T(8,128)(2,1)S(1)}) custom-call(s32[1]{0:T(128)} %bitcast.brick.refs_0_, s32[1]{0:T(128)} %bitcast.1.chan.refs_1_, s32[1]{0:T(128)} %bitcast.2.rep.refs_2_, ...), custom_call_target="tpu_custom_call", output_to_operand_aliasing={{2}: (4, {}), {3}: (5, {})} | custom-call | flops 2038431744 | bytes 1048576 | tf_op jit(solution)/shard_map/grad_weight/pallas_call | solution.py:35
  32.2 2.8 %collective-permute-start.5 = (bf16[896,128]{1,0:T(8,128)(2,1)S(1)}, bf16[896,128]{1,0:T(8,128)(2,1)S(1)}, u32[]{:S(2)}, u32[]{:S(2)}) collective-permute-start(bf16[896,128]{1,0:T(8,128)(2,1)S(1)} %get-tuple-element.54), channel_id=1, source_target_pairs={{0,1},{1,0},{2,3},{3,2},{4,5},{5,4},{6,7},{7,6},{8,9},{9,8},{10,11... | collective-permute-start | bytes 688136 | tf_op jit(solution)/shard_map/ppermute | solution.py:474
  35.0 3.6 %grad_features.1 = (f32[64,4608]{1,0:T(8,128)S(1)}, bf16[64,4608]{1,0:T(8,128)(2,1)S(1)}) custom-call(bf16[128,1792]{1,0:T(8,128)(2,1)S(1)} %get-tuple-element.45.weights, bf16[27,16,5376]{2,1,0:T(8,128)(2,1)S(1)} %get-tuple-element.49.valid, bf16[9,64,6144]{2,1,0:T(8,128)(2,1)S(1)} %get-tuple-element.50.grads), custom_call_target="tpu_custom_call" | custom-call | flops 2038431744 | bytes 1048576 | tf_op jit(solution)/shard_map/grad_features/pallas_call | solution.py:35
  38.6 0.0 collective-permute-done.5.refs_5_
  38.6 0.7 %split.1 = (f32[224,128]{1,0:T(8,128)S(1)}, bf16[896,128]{1,0:T(8,128)(2,1)}) custom-call(s32[1]{0:T(128)} %bitcast.brick.refs_0_, s32[1]{0:T(128)} %bitcast.1.chan.refs_1_, s32[1]{0:T(128)} %bitcast.2.rep.refs_2_, f32[64,4608]{1,0:T(8,128)S(1)} %get-tuple-element.51.own.refs_3_, f32[896,128]{1,0:T(8,128)S(1)} %get-tuple-element.53.refs_4_, ...), custom_call_target="tpu_custom_call" | custom-call | flops 250000000 | bytes 1048576 | tf_op jit(solution)/shard_map/split/pallas_call | solution.py:35
  39.4 4.0 %all-to-all-start = ((bf16[4,224,128]{2,1,0:T(8,128)(2,1)}), bf16[4,224,128]{2,1,0:T(8,128)(2,1)S(1)}, u32[]{:S(2)}, u32[]{:S(2)}) async-start(bf16[4,224,128]{2,1,0:T(8,128)(2,1)} %bitcast.4), calls=%async_computation | async-start | bytes 458752 | tf_op jit(solution)/shard_map/all_to_all | solution.py:502
  43.4 1.5 %collective-permute-start.4 = (bf16[64,4608]{1,0:T(8,128)(2,1)S(1)}, bf16[64,4608]{1,0:T(8,128)(2,1)S(1)}, u32[]{:S(2)}, u32[]{:S(2)}) collective-permute-start(bf16[64,4608]{1,0:T(8,128)(2,1)S(1)} %get-tuple-element.52), channel_id=1, source_target_pairs={{0,2},{2,0},{1,3},{3,1},{4,6},{6,4},{5,7},{7,5},{8,10},{10,8},{9,1... | collective-permute-start | bytes 1769480 | tf_op jit(solution)/shard_map/ppermute | solution.py:484
  44.9 7.4 %all-to-all-done = bf16[4,224,128]{2,1,0:T(8,128)(2,1)S(1)} async-done(((bf16[4,224,128]{2,1,0:T(8,128)(2,1)}), bf16[4,224,128]{2,1,0:T(8,128)(2,1)S(1)}, u32[]{:S(2)}, u32[]{:S(2)}) %all-to-all-start) | async-done | bytes 229408 | tf_op jit(solution)/shard_map/all_to_all | solution.py:502
  52.2 0.1 merge.1
  52.3 10.1 %all_to_all.22 = bf16[4,224,128]{2,1,0:T(8,128)(2,1)S(1)} all-to-all(bf16[4,224,128]{2,1,0:T(8,128)(2,1)S(1)} %bitcast.15), channel_id=1, replica_groups=mesh['scene'=2,'brick'=4,'chan'=2,'rep'=2] {'brick'}, dimensions={0} | all-to-all | bytes 458752 | tf_op jit(solution)/shard_map/all_to_all | solution.py:502
  62.4 0.0 collective-permute-start.6
  62.4 0.0 collective-permute-done.4.rest_0_
  62.4 1.0 %add.1 = bf16[64,4608]{1,0:T(8,128)(2,1)} custom-call(bf16[64,4608]{1,0:T(8,128)(2,1)S(1)} %copy-done, f32[64,4608]{1,0:T(8,128)S(1)} %get-tuple-element.51.own.refs_3_, bf16[64,4608]{1,0:T(8,128)(2,1)S(1)} %collective-permute-done.4.rest_0_), custom_call_target="tpu_custom_call" | custom-call | bytes 1048576 | tf_op jit(solution)/shard_map/add/pallas_call | solution.py:35
  63.4 0.5 collective-permute-done.6.other
  63.9 1.1 %join.1 = f32[1728,128]{1,0:T(8,128)} custom-call(s32[1]{0:T(128)} %bitcast.brick.refs_0_, s32[1]{0:T(128)} %bitcast.1.chan.refs_1_, s32[1]{0:T(128)} %bitcast.2.rep.refs_2_, bf16[896,128]{1,0:T(8,128)(2,1)S(1)} %bitcast.12, bf16[896,128]{1,0:T(8,128)(2,1)S(1)} %collective-permute-done.6.other), custom_call_target="tpu_custom_call" | custom-call | flops 250000000 | bytes 1048576 | tf_op jit(solution)/shard_map/join/pallas_call | solution.py:35
Async XLA Ops:
  0.6 16.9 %collective-permute-start.3 = (bf16[64,4608]{1,0:T(8,128)(2,1)}, bf16[64,4608]{1,0:T(8,128)(2,1)S(1)}, u32[]{:S(2)}, u32[]{:S(2)}) collective-permute-start(bf16[64,4608]{1,0:T(8,128)(2,1)} %features.3), channel_id=1, source_target_pairs={{2,0},{0,2},{3,1},{1,3},{6,4},{4,6},{7,5},{5,7},{10,8},{8,10},{11,... | collective-permute-start | bytes 1769480 | tf_op jit(solution)/shard_map/ppermute | solution.py:377
  5.5 6.8 %collective-permute-start = (bf16[128,768]{1,0:T(8,128)(2,1)}, bf16[128,768]{1,0:T(8,128)(2,1)S(1)}, u32[]{:S(2)}, u32[]{:S(2)}) collective-permute-start(bf16[128,768]{1,0:T(8,128)(2,1)} %get-tuple-element.31), channel_id=1, source_target_pairs={{0,1},{1,0},{2,3},{3,2},{4,5},{5,4},{6,7},{7,6},{8,9},{9,8},{10,11... | collective-permute-start | bytes 589832 | tf_op jit(solution)/shard_map/ppermute | solution.py:398
  5.5 6.8 %collective-permute-start.1 = (bf16[128,768]{1,0:T(8,128)(2,1)}, bf16[128,768]{1,0:T(8,128)(2,1)S(1)}, u32[]{:S(2)}, u32[]{:S(2)}) collective-permute-start(bf16[128,768]{1,0:T(8,128)(2,1)} %get-tuple-element.32), channel_id=1, source_target_pairs={{1,4},{4,1},{5,8},{8,5},{9,12},{12,9},{3,6},{6,3},{7,10},{10,7},{1... | collective-permute-start | bytes 589832 | tf_op jit(solution)/shard_map/ppermute | solution.py:363
  6.2 1.1 %copy-start.1 = (s32[27,4608]{1,0:T(8,128)S(1)}, s32[27,4608]{1,0:T(8,128)}, u32[]{:S(2)}) copy-start(s32[27,4608]{1,0:T(8,128)} %neighbours.3) | copy-start | bytes 1492996
  7.3 1.1 %copy-start.2 = (bf16[64,4608]{1,0:T(8,128)(2,1)S(1)}, bf16[64,4608]{1,0:T(8,128)(2,1)}, u32[]{:S(2)}) copy-start(bf16[64,4608]{1,0:T(8,128)(2,1)} %features.3) | copy-start | bytes 1769476
  8.3 1.0 %copy-start.3 = (bf16[27,128,64]{1,2,0:T(8,128)(2,1)S(1)}, bf16[27,128,64]{1,2,0:T(8,128)(2,1)}, u32[]{:S(2)}) copy-start(bf16[27,128,64]{1,2,0:T(8,128)(2,1)} %param.5) | copy-start | bytes 1327108
  12.4 7.6 %collective-permute-start.2 = (bf16[64,1280]{1,0:T(8,128)(2,1)S(1)}, bf16[64,1280]{1,0:T(8,128)(2,1)S(1)}, u32[]{:S(2)}, u32[]{:S(2)}) collective-permute-start(bf16[64,1280]{1,0:T(8,128)(2,1)S(1)} %get-tuple-element.33), channel_id=1, source_target_pairs={{2,0},{0,2},{3,1},{1,3},{6,4},{4,6},{7,5},{5,7},{10,8},{8,10},{11,... | collective-permute-start | bytes 491528 | tf_op jit(solution)/shard_map/ppermute | solution.py:377
  12.5 7.5 %copy-start = (bf16[64,4608]{1,0:T(8,128)(2,1)S(1)}, bf16[64,4608]{1,0:T(8,128)(2,1)}, u32[]{:S(2)}) copy-start(bf16[64,4608]{1,0:T(8,128)(2,1)} %cotangent.5) | copy-start | bytes 1769476
  32.2 6.4 %collective-permute-start.5 = (bf16[896,128]{1,0:T(8,128)(2,1)S(1)}, bf16[896,128]{1,0:T(8,128)(2,1)S(1)}, u32[]{:S(2)}, u32[]{:S(2)}) collective-permute-start(bf16[896,128]{1,0:T(8,128)(2,1)S(1)} %get-tuple-element.54), channel_id=1, source_target_pairs={{0,1},{1,0},{2,3},{3,2},{4,5},{5,4},{6,7},{7,6},{8,9},{9,8},{10,11... | collective-permute-start | bytes 688136 | tf_op jit(solution)/shard_map/ppermute | solution.py:474
  39.4 12.9 %all-to-all-start = ((bf16[4,224,128]{2,1,0:T(8,128)(2,1)}), bf16[4,224,128]{2,1,0:T(8,128)(2,1)S(1)}, u32[]{:S(2)}, u32[]{:S(2)}) async-start(bf16[4,224,128]{2,1,0:T(8,128)(2,1)} %bitcast.4), calls=%async_computation | async-start | bytes 458752 | tf_op jit(solution)/shard_map/all_to_all | solution.py:502
  43.4 19.0 %collective-permute-start.4 = (bf16[64,4608]{1,0:T(8,128)(2,1)S(1)}, bf16[64,4608]{1,0:T(8,128)(2,1)S(1)}, u32[]{:S(2)}, u32[]{:S(2)}) collective-permute-start(bf16[64,4608]{1,0:T(8,128)(2,1)S(1)} %get-tuple-element.52), channel_id=1, source_target_pairs={{0,2},{2,0},{1,3},{3,1},{4,6},{6,4},{5,7},{7,5},{8,10},{10,8},{9,1... | collective-permute-start | bytes 1769480 | tf_op jit(solution)/shard_map/ppermute | solution.py:484
  62.4 1.5 %collective-permute-start.6 = (bf16[896,128]{1,0:T(8,128)(2,1)S(1)}, bf16[896,128]{1,0:T(8,128)(2,1)S(1)}, u32[]{:S(2)}, u32[]{:S(2)}) collective-permute-start(bf16[896,128]{1,0:T(8,128)(2,1)S(1)} %bitcast.11), channel_id=1, source_target_pairs={{0,1},{1,0},{2,3},{3,2},{4,5},{5,4},{6,7},{7,6},{8,9},{9,8},{10,11... | collective-permute-start | bytes 688136 | tf_op jit(solution)/shard_map/ppermute | solution.py:514

commit v7 on v5

--- a/solution.py
+++ b/solution.py
@@ -14,7 +14,7 @@
 FAR = 2 * HALO
 NEAR = 640
 LEAD = 896
-NINE = 9
+MANY = 14
 ROWS = 16
 GROUP = 4
 WIDTH = 768
@@ -30,12 +30,14 @@
 SCALAR = pl.BlockSpec(memory_space=pltpu.SMEM)
 
 
-def kernel(body, name, outs, args, scalars=(), scratch=(), aliases={}, limit=8, flops=0, space=HERE):
+def kernel(body, name, outs, args, scalars=(), scratch=(), aliases={}, limit=8, flops=0, held=False):
+    if held:
+        args = [pltpu.with_memory_space_constraint(x, pltpu.HBM) for x in args]
     single = not isinstance(outs, (tuple, list))
     return pl.pallas_call(
         body,
         out_shape=outs,
-        in_specs=[SCALAR] * len(scalars) + [space] * len(args),
+        in_specs=[SCALAR] * len(scalars) + [FAR_OFF if held else HERE] * len(args),
         out_specs=HERE if single else [HERE] * len(outs),
         scratch_shapes=list(scratch),
         input_output_aliases={len(scalars) + i: o for i, o in aliases.items()},
@@ -265,7 +267,7 @@
         hidden = begun[:, here] + product(
             weights, shifts, valid, start + HALO, start, WIDTH, lambda tap: tap
         )
-        sigma = jax.nn.sigmoid(hidden)
+        sigma = 0.5 * jnp.tanh(0.5 * hidden) + 0.5
         features = own[4, :, pl.ds(pl.multiple_of(start + HALO, 128), WIDTH)]
         kept[:, here] = (features.astype(F32) + hidden * sigma).astype(BF16)
         grad[:, there] = (
@@ -287,7 +289,7 @@
     def block(j, carry):
         start = pl.multiple_of(j * WIDTH, 128)
         features = across[pl.ds(start, WIDTH), :]
-        for group in groups(NINE):
+        for group in groups(MANY):
             rows = []
             for tap in group:
                 rows += masked(
@@ -356,7 +358,8 @@
 
 
 def add_body(cotangent, own, *rest):
-    *terms, out = rest
+    *terms, out, token = rest
+    token[...] = jnp.zeros_like(token)
     total = cotangent[...].astype(F32) + own[...]
     for term in terms:
         total += term[...].astype(F32)
@@ -397,8 +400,7 @@
         [features, cotangent, neighbours],
         scalars=place,
         scratch=[pltpu.VMEM((2, TAPS, HALO), jnp.int32), pltpu.SemaphoreType.DMA((6,))],
-        limit=58,
-        space=FAR_OFF,
+        held=True,
     )
     line = line_swap(to_line)
     core = lax.ppermute(to_core, "rep", swap)
@@ -422,7 +424,7 @@
             pltpu.VMEM((TAPS, sites), jnp.int32),
             pltpu.SemaphoreType.DMA((3,)),
         ],
-        space=FAR_OFF,
+        held=True,
     )
     before, behind, both = kernel(
         after(ends_body, 3),
@@ -536,16 +538,21 @@
         gather_body, "gather", shape((half, total)), [mine, other], scalars=place, flops=LATER
     )
     other = lax.ppermute(side, "rep", swap)
+    grad_features, token = kernel(
+        add_body,
+        "add",
+        [shape((share, sites)), shape((8, 128), F32)],
+        [cotangent, own, *terms],
+    )
     grad_weight = kernel(
-        functools.partial(join_body, half, share),
+        after(functools.partial(join_body, half, share), 3),
         "join",
         shape((TAPS * share, total), F32),
-        [side, other],
+        [token, side, other],
         scalars=place,
         scratch=[pltpu.VMEM((reps * half, total), BF16)],
         flops=LATER,
     )
-    grad_features = kernel(add_body, "add", shape((share, sites)), [cotangent, own, *terms])
     grad_weight = jnp.transpose(grad_weight.reshape(TAPS, share, total), (0, 2, 1))
     return output, grad_features, grad_weight
 

time: 58.8 us -> 56.9 us (0.968)
  waiting for transfers between devices: 11.5 us -> 14.9 us
  local copies, waits for them, and re-layouts: 3.14 us -> 0.01 us
  starting transfers between devices: 13.1 us -> 11 us
    ppermute x2, waiting for transfers between devices: 0.44 us -> 4.46 us  [around(): lax.ppermute(x, 'chan', [((i + over) % chans, i) for i in range(chans)])]
    unnamed x8 -> x2, local copies, waits for them, and re-layouts: 3.14 us -> 0.01 us
    ppermute x1, starting transfers between devices: 2.82 us -> 0.07 us  [local(): arrived = lax.ppermute(sent, 'rep', swap)]
    ppermute x1, waiting for transfers between devices: 1.48 us -> 0.24 us  [local(): other = lax.ppermute(side, 'rep', swap)]
  transfers between devices with their start and end apart: 10 -> 10, of which waited for: 5 -> 7; matrix products, arithmetic and copies ran while one was open for 0% -> 0% of each run, Pallas kernels for 28% -> 29%
where the time goes in v7:
time: 56.9 us; the launch traced here: 56.7 us
  Pallas kernels  30 us (53%)
  waiting for transfers between devices  14.9 us (26%)
  starting transfers between devices  11 us (19%)
  between operations  0.77 us (1%)
    pallas_call x15, Pallas kernels, kernel(): pl.pallas_call(body, out_shape=outs, in_specs=[SCALAR] * len(scalars) + [...  30 us
    ppermute x1, waiting for transfers between devices, local(): other = lax.ppermute(mine, 'brick', [(i, i ^ step) for i in range(bricks)])  5.48 us
    ppermute x2, waiting for transfers between devices, around(): lax.ppermute(x, 'chan', [((i + over) % chans, i) for i in range(chans)])  4.46 us
    ppermute x1, waiting for transfers between devices, local(): other = lax.ppermute(mine, 'brick', pairs)  4.07 us
    ppermute x2, starting transfers between devices, around(): lax.ppermute(x, 'chan', [((i + over) % chans, i) for i in range(chans)])  3.1 us
    ppermute x1, starting transfers between devices, local(): other = lax.ppermute(mine, 'brick', [(i, i ^ step) for i in range(bricks)])  2.81 us
    ppermute x1, starting transfers between devices, local(): arrived = lax.ppermute(sent, 'brick', pairs)  1.9 us
    ppermute x1, starting transfers between devices, local(): lax.ppermute(other if left == share else other[(over - 1) * share:over *...  1.55 us
  transfers between devices with their start and end apart: 10, of which 7 were waited for; matrix products, arithmetic and copies ran while one was open for 0% of the time, Pallas kernels for 29%

profile of v7, /device:TPU:0, one launch (start us, length us, event | category | flops | bytes accessed | tf_op | source)
XLA Modules:
  0.0 56.7 jit_solution(15956280134674154380)
XLA Ops:
  0.6 3.0 %collective-permute-start.3 = (bf16[64,4608]{1,0:T(8,128)(2,1)}, bf16[64,4608]{1,0:T(8,128)(2,1)S(1)}, u32[]{:S(2)}, u32[]{:S(2)}) collective-permute-start(bf16[64,4608]{1,0:T(8,128)(2,1)} %features.3), channel_id=1, source_target_pairs={{2,0},{0,2},{3,1},{1,3},{6,4},{4,6},{7,5},{5,7},{10,8},{8,10},{11,... | collective-permute-start | bytes 1769480 | tf_op jit(solution)/shard_map/ppermute | solution.py:386
  3.6 1.1 %pack.1 = (bf16[128,768]{1,0:T(8,128)(2,1)S(1)}, bf16[128,768]{1,0:T(8,128)(2,1)S(1)}) custom-call(s32[1]{0:T(128)} %bitcast.brick.refs_0_, s32[1]{0:T(128)} %bitcast.1.chan.refs_1_, s32[1]{0:T(128)} %bitcast.2.rep.refs_2_, bf16[64,4608]{1,0:T(8,128)(2,1)} %features.3, bf16[64,4608]{1,0:T(8,128)(2,1)} %cotangent.5, s32[27,4608]{1,0:T(8,128)} %neighbours.3), custom_call_target="tpu_custom_call" | custom-call | bytes 1048576 | tf_op jit(solution)/shard_map/pack/pallas_call | solution.py:37
  4.7 0.1 collective-permute-start
  4.8 0.7 %collective-permute-start.1 = (bf16[128,768]{1,0:T(8,128)(2,1)S(1)}, bf16[128,768]{1,0:T(8,128)(2,1)S(1)}, u32[]{:S(2)}, u32[]{:S(2)}) collective-permute-start(bf16[128,768]{1,0:T(8,128)(2,1)S(1)} %get-tuple-element.38), channel_id=1, source_target_pairs={{1,4},{4,1},{5,8},{8,5},{9,12},{12,9},{3,6},{6,3},{7,10},{10,7},{1... | collective-permute-start | bytes 589832 | tf_op jit(solution)/shard_map/ppermute | solution.py:372
  5.5 3.5 %prepare.1 = (bf16[64,1728]{1,0:T(8,128)(2,1)S(1)}, bf16[64,1728]{1,0:T(8,128)(2,1)S(1)}, bf16[128,1792]{1,0:T(8,128)(2,1)S(1)}, bf16[9,64,6144]{2,1,0:T(8,128)(2,1)S(1)}, bf16[27,16,5376]{2,1,0:T(8,128)(2,1)S(1)}) custom-call(s32[1]{0:T(128)} %bitcast.brick.refs_0_, s32[1]{0:T(128)} %bitcast.1.chan.refs_1_, s32[1]{0:T(128)} %bitcast.2.rep.refs_2_, ...), custom_call_target="tpu_custom_call" | custom-call | bytes 1048576 | tf_op jit(solution)/shard_map/prepare/pallas_call | solution.py:37
  9.0 0.0 collective-permute-done.refs_4_
  9.0 0.0 collective-permute-done.1.refs_5_
  9.0 0.1 ends.1
  9.1 0.1 collective-permute-start.2
  9.2 5.1 %forward_own.1 = (f32[64,5376]{1,0:T(8,128)S(1)}, bf16[9,64,6144]{2,1,0:T(8,128)(2,1)S(1)}, bf16[27,16,5376]{2,1,0:T(8,128)(2,1)S(1)}) custom-call(bf16[128,768]{1,0:T(8,128)(2,1)S(1)} %get-tuple-element.40.left, bf16[128,768]{1,0:T(8,128)(2,1)S(1)} %get-tuple-element.41.right, ...), custom_call_target="tpu_custom_call", output_to_operand_aliasing={{1}: (3, {}), {2}: (4, {})} | custom-call | bytes 1048576 | tf_op jit(solution)/shard_map/forward_own/pallas_call | solution.py:37
  14.3 0.0 copy-start
  14.3 3.7 %collective-permute-done.3.rest = bf16[64,4608]{1,0:T(8,128)(2,1)S(1)} collective-permute-done((bf16[64,4608]{1,0:T(8,128)(2,1)}, bf16[64,4608]{1,0:T(8,128)(2,1)S(1)}, u32[]{:S(2)}, u32[]{:S(2)}) %collective-permute-start.3) | collective-permute-done | bytes 589856 | tf_op jit(solution)/shard_map/ppermute | solution.py:386
  18.0 1.9 %arrive.1 = (bf16[9,64,6144]{2,1,0:T(8,128)(2,1)S(1)}, bf16[4608,128]{1,0:T(8,128)(2,1)S(1)}, bf16[9,64,6144]{2,1,0:T(8,128)(2,1)S(1)}) custom-call(bf16[64,4608]{1,0:T(8,128)(2,1)S(1)} %collective-permute-done.3.rest, bf16[9,64,6144]{2,1,0:T(8,128)(2,1)S(1)} %get-tuple-element.44.own_in), custom_call_target="tpu_custom_call", output_to_operand_aliasing={{2}: (1, {})} | custom-call | bytes 1048576 | tf_op jit(solution)/shard_map/arrive/pallas_call | solution.py:37
  19.9 0.8 %collective-permute-done.2.ends = bf16[64,1280]{1,0:T(8,128)(2,1)S(1)} collective-permute-done((bf16[64,1280]{1,0:T(8,128)(2,1)S(1)}, bf16[64,1280]{1,0:T(8,128)(2,1)S(1)}, u32[]{:S(2)}, u32[]{:S(2)}) %collective-permute-start.2) | collective-permute-done | bytes 163872 | tf_op jit(solution)/shard_map/ppermute | solution.py:386
  20.7 0.0 copy-done
  20.7 6.9 %forward_rest.1 = (bf16[64,4608]{1,0:T(8,128)(2,1)}, bf16[9,64,6144]{2,1,0:T(8,128)(2,1)S(1)}, bf16[27,16,5376]{2,1,0:T(8,128)(2,1)S(1)}, bf16[9,64,6144]{2,1,0:T(8,128)(2,1)S(1)}) custom-call(bf16[64,1280]{1,0:T(8,128)(2,1)S(1)} %collective-permute-done.2.ends, ...), custom_call_target="tpu_custom_call", output_to_operand_aliasing={{3}: (1, {}), {2}: (3, {})} | custom-call | flops 1019215872 | bytes 1048576 | tf_op jit(solution)/shard_map/forward_rest/pallas_call | solution.py:37
  27.6 5.5 %grad_weight.1 = (f32[896,128]{1,0:T(8,128)S(1)}, bf16[896,128]{1,0:T(8,128)(2,1)S(1)}, bf16[27,16,5376]{2,1,0:T(8,128)(2,1)S(1)}, bf16[9,64,6144]{2,1,0:T(8,128)(2,1)S(1)}) custom-call(s32[1]{0:T(128)} %bitcast.brick.refs_0_, s32[1]{0:T(128)} %bitcast.1.chan.refs_1_, s32[1]{0:T(128)} %bitcast.2.rep.refs_2_, ...), custom_call_target="tpu_custom_call", output_to_operand_aliasing={{2}: (4, {}), {3}: (5, {})} | custom-call | flops 2038431744 | bytes 1048576 | tf_op jit(solution)/shard_map/grad_weight/pallas_call | solution.py:37
  33.1 0.1 collective-permute-start.4
  33.2 1.8 %grad_features_0.1 = (bf16[27,16,5376]{2,1,0:T(8,128)(2,1)S(1)}, bf16[9,64,6144]{2,1,0:T(8,128)(2,1)S(1)}, f32[64,4608]{1,0:T(8,128)S(1)}, bf16[64,4608]{1,0:T(8,128)(2,1)S(1)}) custom-call(bf16[128,1792]{1,0:T(8,128)(2,1)S(1)} %get-tuple-element.51.weights.refs_1_, ...), custom_call_target="tpu_custom_call", output_to_operand_aliasing={{0}: (1, {}), {1}: (2, {})} | custom-call | flops 1019215872 | bytes 1048576 | tf_op jit(solution)/shard_map/grad_features_0/pallas_call | solution.py:37
  35.0 0.0 collective-permute-done.4.refs_5_
  35.0 0.1 split.1
  35.1 1.9 %collective-permute-start.6 = (bf16[448,128]{1,0:T(8,128)(2,1)S(1)}, bf16[448,128]{1,0:T(8,128)(2,1)S(1)}, u32[]{:S(2)}, u32[]{:S(2)}) collective-permute-start(bf16[448,128]{1,0:T(8,128)(2,1)S(1)} %get-tuple-element.68), channel_id=1, source_target_pairs={{0,4},{4,0},{8,12},{12,8},{1,5},{5,1},{9,13},{13,9},{2,6},{6,2},{1... | collective-permute-start | bytes 344072 | tf_op jit(solution)/shard_map/ppermute | solution.py:510
  37.0 1.8 %grad_features_1.1 = (f32[64,4608]{1,0:T(8,128)S(1)}, bf16[64,4608]{1,0:T(8,128)(2,1)S(1)}) custom-call(f32[448,128]{1,0:T(8,128)S(1)} %get-tuple-element.60.refs_0_.refs_1_, bf16[128,1792]{1,0:T(8,128)(2,1)S(1)} %get-tuple-element.51.weights.refs_1_, ...), custom_call_target="tpu_custom_call", output_to_operand_aliasing={{0}: (4, {}), {1}: (5, {})} | custom-call | flops 1019215872 | bytes 1048576 | tf_op jit(solution)/shard_map/grad_features_1/pallas_call | solution.py:37
  38.8 1.6 %collective-permute-start.5 = (bf16[64,4608]{1,0:T(8,128)(2,1)S(1)}, bf16[64,4608]{1,0:T(8,128)(2,1)S(1)}, u32[]{:S(2)}, u32[]{:S(2)}) collective-permute-start(bf16[64,4608]{1,0:T(8,128)(2,1)S(1)} %get-tuple-element.65), channel_id=1, source_target_pairs={{0,2},{2,0},{1,3},{3,1},{4,6},{6,4},{5,7},{7,5},{8,10},{10,8},{9,1... | collective-permute-start | bytes 1769480 | tf_op jit(solution)/shard_map/ppermute | solution.py:515
  40.3 0.4 collective-permute-done.6.refs_2_
  40.8 2.8 %collective-permute-start.7 = (bf16[448,128]{1,0:T(8,128)(2,1)S(1)}, bf16[448,128]{1,0:T(8,128)(2,1)S(1)}, u32[]{:S(2)}, u32[]{:S(2)}) collective-permute-start(bf16[448,128]{1,0:T(8,128)(2,1)S(1)} %merge_1.1.mine), channel_id=1, source_target_pairs={{0,8},{4,12},{8,0},{12,4},{1,9},{5,13},{9,1},{13,5},{2,10},{6,14},... | collective-permute-start | bytes 344072 | tf_op jit(solution)/shard_map/ppermute | solution.py:531
  43.6 5.5 %collective-permute-done.7.other = bf16[448,128]{1,0:T(8,128)(2,1)S(1)} collective-permute-done((bf16[448,128]{1,0:T(8,128)(2,1)S(1)}, bf16[448,128]{1,0:T(8,128)(2,1)S(1)}, u32[]{:S(2)}, u32[]{:S(2)}) %collective-permute-start.7) | collective-permute-done | bytes 114720 | tf_op jit(solution)/shard_map/ppermute | solution.py:531
  49.1 0.8 %collective-permute-start.8 = (bf16[448,128]{1,0:T(8,128)(2,1)S(1)}, bf16[448,128]{1,0:T(8,128)(2,1)S(1)}, u32[]{:S(2)}, u32[]{:S(2)}) collective-permute-start(bf16[448,128]{1,0:T(8,128)(2,1)S(1)} %merge_4.1.mine), channel_id=1, source_target_pairs={{0,4},{4,0},{8,12},{12,8},{1,5},{5,1},{9,13},{13,9},{2,6},{6,2},{1... | collective-permute-start | bytes 344072 | tf_op jit(solution)/shard_map/ppermute | solution.py:536
  49.9 4.1 %collective-permute-done.8.other = bf16[448,128]{1,0:T(8,128)(2,1)S(1)} collective-permute-done((bf16[448,128]{1,0:T(8,128)(2,1)S(1)}, bf16[448,128]{1,0:T(8,128)(2,1)S(1)}, u32[]{:S(2)}, u32[]{:S(2)}) %collective-permute-start.8) | collective-permute-done | bytes 114720 | tf_op jit(solution)/shard_map/ppermute | solution.py:536
  54.0 0.1 collective-permute-start.9
  54.1 0.2 collective-permute-done.5.rest_0_
  54.3 1.0 %add.1 = (bf16[64,4608]{1,0:T(8,128)(2,1)}, f32[8,128]{1,0:T(8,128)S(1)}) custom-call(bf16[64,4608]{1,0:T(8,128)(2,1)S(1)} %copy-done, f32[64,4608]{1,0:T(8,128)S(1)} %get-tuple-element.64.own.refs_0_, bf16[64,4608]{1,0:T(8,128)(2,1)S(1)} %collective-permute-done.5.rest_0_), custom_call_target="tpu_custom_call" | custom-call | bytes 1048576 | tf_op jit(solution)/shard_map/add/pallas_call | solution.py:37
  55.3 0.2 collective-permute-done.9.refs_5_
  55.6 1.1 %join.1 = f32[1728,128]{1,0:T(8,128)} custom-call(s32[1]{0:T(128)} %bitcast.brick.refs_0_, s32[1]{0:T(128)} %bitcast.1.chan.refs_1_, s32[1]{0:T(128)} %bitcast.2.rep.refs_2_, f32[8,128]{1,0:T(8,128)S(1)} %get-tuple-element.67.refs_3_, bf16[896,128]{1,0:T(8,128)(2,1)S(1)} %gather.1.refs_4_, bf16[896,128]{1,0:T(8,128)(2,1)S(1)} %collective-permute-done.9.refs_5_), custom_call_target="tpu_custom_call" | custom-call | flops 250000000 | bytes 1048576 | tf_op jit(solution)/shard_map/join/pallas_call | solution.py:37
  (3 shorter events, 0.1 us)
Async XLA Ops:
  0.6 17.4 %collective-permute-start.3 = (bf16[64,4608]{1,0:T(8,128)(2,1)}, bf16[64,4608]{1,0:T(8,128)(2,1)S(1)}, u32[]{:S(2)}, u32[]{:S(2)}) collective-permute-start(bf16[64,4608]{1,0:T(8,128)(2,1)} %features.3), channel_id=1, source_target_pairs={{2,0},{0,2},{3,1},{1,3},{6,4},{4,6},{7,5},{5,7},{10,8},{8,10},{11,... | collective-permute-start | bytes 1769480 | tf_op jit(solution)/shard_map/ppermute | solution.py:386
  4.7 4.3 %collective-permute-start = (bf16[128,768]{1,0:T(8,128)(2,1)S(1)}, bf16[128,768]{1,0:T(8,128)(2,1)S(1)}, u32[]{:S(2)}, u32[]{:S(2)}) collective-permute-start(bf16[128,768]{1,0:T(8,128)(2,1)S(1)} %get-tuple-element.37), channel_id=1, source_target_pairs={{0,1},{1,0},{2,3},{3,2},{4,5},{5,4},{6,7},{7,6},{8,9},{9,8},{10,11... | collective-permute-start | bytes 589832 | tf_op jit(solution)/shard_map/ppermute | solution.py:406
  4.8 4.2 %collective-permute-start.1 = (bf16[128,768]{1,0:T(8,128)(2,1)S(1)}, bf16[128,768]{1,0:T(8,128)(2,1)S(1)}, u32[]{:S(2)}, u32[]{:S(2)}) collective-permute-start(bf16[128,768]{1,0:T(8,128)(2,1)S(1)} %get-tuple-element.38), channel_id=1, source_target_pairs={{1,4},{4,1},{5,8},{8,5},{9,12},{12,9},{3,6},{6,3},{7,10},{10,7},{1... | collective-permute-start | bytes 589832 | tf_op jit(solution)/shard_map/ppermute | solution.py:372
  9.1 11.6 %collective-permute-start.2 = (bf16[64,1280]{1,0:T(8,128)(2,1)S(1)}, bf16[64,1280]{1,0:T(8,128)(2,1)S(1)}, u32[]{:S(2)}, u32[]{:S(2)}) collective-permute-start(bf16[64,1280]{1,0:T(8,128)(2,1)S(1)} %get-tuple-element.39), channel_id=1, source_target_pairs={{2,0},{0,2},{3,1},{1,3},{6,4},{4,6},{7,5},{5,7},{10,8},{8,10},{11,... | collective-permute-start | bytes 491528 | tf_op jit(solution)/shard_map/ppermute | solution.py:386
  14.3 6.4 %copy-start = (bf16[64,4608]{1,0:T(8,128)(2,1)S(1)}, bf16[64,4608]{1,0:T(8,128)(2,1)}, u32[]{:S(2)}) copy-start(bf16[64,4608]{1,0:T(8,128)(2,1)} %cotangent.5) | copy-start | bytes 1769476
  33.1 1.9 %collective-permute-start.4 = (bf16[896,128]{1,0:T(8,128)(2,1)S(1)}, bf16[896,128]{1,0:T(8,128)(2,1)S(1)}, u32[]{:S(2)}, u32[]{:S(2)}) collective-permute-start(bf16[896,128]{1,0:T(8,128)(2,1)S(1)} %get-tuple-element.59), channel_id=1, source_target_pairs={{0,1},{1,0},{2,3},{3,2},{4,5},{5,4},{6,7},{7,6},{8,9},{9,8},{10,11... | collective-permute-start | bytes 688136 | tf_op jit(solution)/shard_map/ppermute | solution.py:482
  35.1 5.7 %collective-permute-start.6 = (bf16[448,128]{1,0:T(8,128)(2,1)S(1)}, bf16[448,128]{1,0:T(8,128)(2,1)S(1)}, u32[]{:S(2)}, u32[]{:S(2)}) collective-permute-start(bf16[448,128]{1,0:T(8,128)(2,1)S(1)} %get-tuple-element.68), channel_id=1, source_target_pairs={{0,4},{4,0},{8,12},{12,8},{1,5},{5,1},{9,13},{13,9},{2,6},{6,2},{1... | collective-permute-start | bytes 344072 | tf_op jit(solution)/shard_map/ppermute | solution.py:510
  38.8 15.5 %collective-permute-start.5 = (bf16[64,4608]{1,0:T(8,128)(2,1)S(1)}, bf16[64,4608]{1,0:T(8,128)(2,1)S(1)}, u32[]{:S(2)}, u32[]{:S(2)}) collective-permute-start(bf16[64,4608]{1,0:T(8,128)(2,1)S(1)} %get-tuple-element.65), channel_id=1, source_target_pairs={{0,2},{2,0},{1,3},{3,1},{4,6},{6,4},{5,7},{7,5},{8,10},{10,8},{9,1... | collective-permute-start | bytes 1769480 | tf_op jit(solution)/shard_map/ppermute | solution.py:515
  40.8 8.3 %collective-permute-start.7 = (bf16[448,128]{1,0:T(8,128)(2,1)S(1)}, bf16[448,128]{1,0:T(8,128)(2,1)S(1)}, u32[]{:S(2)}, u32[]{:S(2)}) collective-permute-start(bf16[448,128]{1,0:T(8,128)(2,1)S(1)} %merge_1.1.mine), channel_id=1, source_target_pairs={{0,8},{4,12},{8,0},{12,4},{1,9},{5,13},{9,1},{13,5},{2,10},{6,14},... | collective-permute-start | bytes 344072 | tf_op jit(solution)/shard_map/ppermute | solution.py:531
  49.1 4.9 %collective-permute-start.8 = (bf16[448,128]{1,0:T(8,128)(2,1)S(1)}, bf16[448,128]{1,0:T(8,128)(2,1)S(1)}, u32[]{:S(2)}, u32[]{:S(2)}) collective-permute-start(bf16[448,128]{1,0:T(8,128)(2,1)S(1)} %merge_4.1.mine), channel_id=1, source_target_pairs={{0,4},{4,0},{8,12},{12,8},{1,5},{5,1},{9,13},{13,9},{2,6},{6,2},{1... | collective-permute-start | bytes 344072 | tf_op jit(solution)/shard_map/ppermute | solution.py:536
  54.0 1.6 %collective-permute-start.9 = (bf16[896,128]{1,0:T(8,128)(2,1)S(1)}, bf16[896,128]{1,0:T(8,128)(2,1)S(1)}, u32[]{:S(2)}, u32[]{:S(2)}) collective-permute-start(bf16[896,128]{1,0:T(8,128)(2,1)S(1)} %gather.1.refs_4_), channel_id=1, source_target_pairs={{0,1},{1,0},{2,3},{3,2},{4,5},{5,4},{6,7},{7,6},{8,9},{9,8},{10,11... | collective-permute-start | bytes 688136 | tf_op jit(solution)/shard_map/ppermute | solution.py:540

commit v8 on v7

--- a/solution.py
+++ b/solution.py
@@ -58,12 +58,17 @@
     return jax.ShapeDtypeStruct(dims, kind)
 
 
+def spread(window, target, rows, lanes):
+    width = window.shape[1]
+    for j, step in enumerate(STEPS):
+        moved = pltpu.roll(window, -step % width, 1) if step else window
+        target[j, rows, lanes] = moved[:, 128 : width - 128]
+
+
 def shift(shifts, low, high):
     for at in range(0, shifts.shape[1], ROWS):
         rows = pl.ds(at, ROWS)
-        for j, step in enumerate(STEPS):
-            if j != 4:
-                shifts[j, rows, low:high] = shifts[4, rows, low + step : high + step]
+        spread(shifts[4, rows, low - 128 : high + 128], shifts, rows, slice(low, high))
 
 
 def masked(shifts, valid, tap, at_shift, at_valid, width):
@@ -159,7 +164,7 @@
         taps = []
         for tap in group:
             ring = pltpu.roll(taken[tap].astype(F32), turn, 1)
-            flat[tap * share : (tap + 1) * share, :] = ring
+            flat[tap * share : (tap + 1) * share, :] = ring.astype(BF16)
             taps.append(ring)
         first, last = group[0], group[-1] + 1
         own[:, first * share : last * share] = jnp.concatenate(
@@ -169,7 +174,7 @@
         rest[:, first * left : last * left] = jnp.concatenate(
             [x[:, share:] for x in taps], axis=1
         ).astype(BF16)
-    by_in[...] = flat[...].T.astype(BF16)
+    by_in[...] = flat[...].T
     copies[1].wait()
     shift(shifts, FAR + 128, FAR + sites - 128)
     copies[2].wait()
@@ -237,6 +242,7 @@
     shifts,
     grad,
     kept,
+    hidden,
 ):
     del shifts_in, valid_in
     share, sites = cotangent.shape
@@ -252,33 +258,33 @@
     grad[:, lead + HALO : lead + HALO + sites] = cotangent[...]
     grad[:, lead + HALO + sites :] = right[share : 2 * share, :HALO]
 
-    def spread(start):
+    def finish(before, start):
+        previous = pl.multiple_of(jnp.maximum(start - WIDTH, 0) + HALO, 128)
+        there = pl.ds(pl.multiple_of(start - WIDTH + lead, 128), WIDTH)
+        value = hidden[before]
+        sigma = 0.5 * jnp.tanh(0.5 * value) + 0.5
+        features = own[4, :, pl.ds(previous, WIDTH)]
+        kept[:, pl.ds(start, WIDTH)] = (features.astype(F32) + value * sigma).astype(BF16)
+        grad[:, there] = (
+            grad[:, there].astype(F32) * sigma * (1.0 + value * (1.0 - sigma))
+        ).astype(BF16)
         for at in range(0, share, ROWS):
             rows = pl.ds(at, ROWS)
             window = grad[rows, pl.ds(start, WIDTH + 256)]
-            for j, step in enumerate(STEPS):
-                grads[j, rows, pl.ds(start, WIDTH)] = window[:, 128 + step : 128 + step + WIDTH]
+            spread(window, grads, rows, pl.ds(start, WIDTH))
 
     def block(j, carry):
         start = pl.multiple_of(j * WIDTH, 128)
-        spread(start)
-        here = pl.ds(start, WIDTH)
-        there = pl.ds(pl.multiple_of(start + lead, 128), WIDTH)
-        hidden = begun[:, here] + product(
+        finish((j + 1) % 2, start)
+        hidden[j % 2] = begun[:, pl.ds(start, WIDTH)] + product(
             weights, shifts, valid, start + HALO, start, WIDTH, lambda tap: tap
         )
-        sigma = 0.5 * jnp.tanh(0.5 * hidden) + 0.5
-        features = own[4, :, pl.ds(pl.multiple_of(start + HALO, 128), WIDTH)]
-        kept[:, here] = (features.astype(F32) + hidden * sigma).astype(BF16)
-        grad[:, there] = (
-            grad[:, there].astype(F32) * sigma * (1.0 + hidden * (1.0 - sigma))
-        ).astype(BF16)
         return carry
 
     count = begun.shape[1] // WIDTH
     lax.fori_loop(0, count, block, 0)
-    spread(count * WIDTH)
-    output[...] = kept[:, HALO : HALO + sites]
+    finish((count + 1) % 2, count * WIDTH)
+    output[...] = kept[:, WIDTH + HALO : WIDTH + HALO + sites]
 
 
 def weight_body(half, brick, chan, rep, across, valid_in, grads_in, kept, sent, valid, grads, total):
@@ -418,7 +424,7 @@
         [jnp.transpose(conv_weight, (0, 2, 1)), features, neighbours],
         scalars=place,
         scratch=[
-            pltpu.VMEM((lanes, total), F32),
+            pltpu.VMEM((lanes, total), BF16),
             pltpu.VMEM((TAPS, sites), F32),
             pltpu.VMEM((TAPS, share, total), BF16),
             pltpu.VMEM((TAPS, sites), jnp.int32),
@@ -461,7 +467,8 @@
         [ends, rest_shifts, rest_weights, valid, begun, before, behind, own_shifts, cotangent],
         scratch=[
             pltpu.VMEM((share, LEAD + 128 + margin), BF16),
-            pltpu.VMEM((share, margin), BF16),
+            pltpu.VMEM((share, WIDTH + margin), BF16),
+            pltpu.VMEM((2, share, WIDTH), F32),
         ],
         aliases={1: 3, 3: 2},
         flops=flops * left,

time: 56.9 us -> 57 us (level)
  no operation moved by 1% of the time
where the time goes in v8:
time: 57 us; the launch traced here: 56.8 us
  Pallas kernels  30 us (53%)
  waiting for transfers between devices  15 us (26%)
  starting transfers between devices  11 us (19%)
  between operations  0.77 us (1%)
    pallas_call x15, Pallas kernels, kernel(): pl.pallas_call(body, out_shape=outs, in_specs=[SCALAR] * len(scalars) + [...  30 us
    ppermute x1, waiting for transfers between devices, local(): other = lax.ppermute(mine, 'brick', [(i, i ^ step) for i in range(bricks)])  5.48 us
    ppermute x2, waiting for transfers between devices, around(): lax.ppermute(x, 'chan', [((i + over) % chans, i) for i in range(chans)])  4.58 us
    ppermute x1, waiting for transfers between devices, local(): other = lax.ppermute(mine, 'brick', pairs)  4.07 us
    ppermute x2, starting transfers between devices, around(): lax.ppermute(x, 'chan', [((i + over) % chans, i) for i in range(chans)])  3.1 us
    ppermute x1, starting transfers between devices, local(): other = lax.ppermute(mine, 'brick', [(i, i ^ step) for i in range(bricks)])  2.82 us
    ppermute x1, starting transfers between devices, local(): arrived = lax.ppermute(sent, 'brick', pairs)  1.89 us
    ppermute x1, starting transfers between devices, local(): lax.ppermute(other if left == share else other[(over - 1) * share:over *...  1.55 us
  transfers between devices with their start and end apart: 10, of which 7 were waited for; matrix products, arithmetic and copies ran while one was open for 0% of the time, Pallas kernels for 29%

profile of v8, /device:TPU:0, one launch (start us, length us, event | category | flops | bytes accessed | tf_op | source)
XLA Modules:
  0.0 56.8 jit_solution(13306097206424511415)
XLA Ops:
  0.6 3.0 %collective-permute-start.3 = (bf16[64,4608]{1,0:T(8,128)(2,1)}, bf16[64,4608]{1,0:T(8,128)(2,1)S(1)}, u32[]{:S(2)}, u32[]{:S(2)}) collective-permute-start(bf16[64,4608]{1,0:T(8,128)(2,1)} %features.3), channel_id=1, source_target_pairs={{2,0},{0,2},{3,1},{1,3},{6,4},{4,6},{7,5},{5,7},{10,8},{8,10},{11,... | collective-permute-start | bytes 1769480 | tf_op jit(solution)/shard_map/ppermute | solution.py:392
  3.6 1.1 %pack.1 = (bf16[128,768]{1,0:T(8,128)(2,1)S(1)}, bf16[128,768]{1,0:T(8,128)(2,1)S(1)}) custom-call(s32[1]{0:T(128)} %bitcast.brick.refs_0_, s32[1]{0:T(128)} %bitcast.1.chan.refs_1_, s32[1]{0:T(128)} %bitcast.2.rep.refs_2_, bf16[64,4608]{1,0:T(8,128)(2,1)} %features.3, bf16[64,4608]{1,0:T(8,128)(2,1)} %cotangent.5, s32[27,4608]{1,0:T(8,128)} %neighbours.3), custom_call_target="tpu_custom_call" | custom-call | bytes 1048576 | tf_op jit(solution)/shard_map/pack/pallas_call | solution.py:37
  4.7 0.1 collective-permute-start
  4.8 0.7 %collective-permute-start.1 = (bf16[128,768]{1,0:T(8,128)(2,1)S(1)}, bf16[128,768]{1,0:T(8,128)(2,1)S(1)}, u32[]{:S(2)}, u32[]{:S(2)}) collective-permute-start(bf16[128,768]{1,0:T(8,128)(2,1)S(1)} %get-tuple-element.38), channel_id=1, source_target_pairs={{1,4},{4,1},{5,8},{8,5},{9,12},{12,9},{3,6},{6,3},{7,10},{10,7},{1... | collective-permute-start | bytes 589832 | tf_op jit(solution)/shard_map/ppermute | solution.py:378
  5.5 3.5 %prepare.1 = (bf16[64,1728]{1,0:T(8,128)(2,1)S(1)}, bf16[64,1728]{1,0:T(8,128)(2,1)S(1)}, bf16[128,1792]{1,0:T(8,128)(2,1)S(1)}, bf16[9,64,6144]{2,1,0:T(8,128)(2,1)S(1)}, bf16[27,16,5376]{2,1,0:T(8,128)(2,1)S(1)}) custom-call(s32[1]{0:T(128)} %bitcast.brick.refs_0_, s32[1]{0:T(128)} %bitcast.1.chan.refs_1_, s32[1]{0:T(128)} %bitcast.2.rep.refs_2_, ...), custom_call_target="tpu_custom_call" | custom-call | bytes 1048576 | tf_op jit(solution)/shard_map/prepare/pallas_call | solution.py:37
  9.0 0.0 collective-permute-done.refs_4_
  9.0 0.0 collective-permute-done.1.refs_5_
  9.0 0.1 ends.1
  9.1 0.1 collective-permute-start.2
  9.2 5.0 %forward_own.1 = (f32[64,5376]{1,0:T(8,128)S(1)}, bf16[9,64,6144]{2,1,0:T(8,128)(2,1)S(1)}, bf16[27,16,5376]{2,1,0:T(8,128)(2,1)S(1)}) custom-call(bf16[128,768]{1,0:T(8,128)(2,1)S(1)} %get-tuple-element.40.left, bf16[128,768]{1,0:T(8,128)(2,1)S(1)} %get-tuple-element.41.right, ...), custom_call_target="tpu_custom_call", output_to_operand_aliasing={{1}: (3, {}), {2}: (4, {})} | custom-call | bytes 1048576 | tf_op jit(solution)/shard_map/forward_own/pallas_call | solution.py:37
  14.2 0.0 copy-start
  14.2 3.8 %collective-permute-done.3.rest = bf16[64,4608]{1,0:T(8,128)(2,1)S(1)} collective-permute-done((bf16[64,4608]{1,0:T(8,128)(2,1)}, bf16[64,4608]{1,0:T(8,128)(2,1)S(1)}, u32[]{:S(2)}, u32[]{:S(2)}) %collective-permute-start.3) | collective-permute-done | bytes 589856 | tf_op jit(solution)/shard_map/ppermute | solution.py:392
  18.0 1.9 %arrive.1 = (bf16[9,64,6144]{2,1,0:T(8,128)(2,1)S(1)}, bf16[4608,128]{1,0:T(8,128)(2,1)S(1)}, bf16[9,64,6144]{2,1,0:T(8,128)(2,1)S(1)}) custom-call(bf16[64,4608]{1,0:T(8,128)(2,1)S(1)} %collective-permute-done.3.rest, bf16[9,64,6144]{2,1,0:T(8,128)(2,1)S(1)} %get-tuple-element.44.own_in), custom_call_target="tpu_custom_call", output_to_operand_aliasing={{2}: (1, {})} | custom-call | bytes 1048576 | tf_op jit(solution)/shard_map/arrive/pallas_call | solution.py:37
  19.9 0.8 %collective-permute-done.2.ends = bf16[64,1280]{1,0:T(8,128)(2,1)S(1)} collective-permute-done((bf16[64,1280]{1,0:T(8,128)(2,1)S(1)}, bf16[64,1280]{1,0:T(8,128)(2,1)S(1)}, u32[]{:S(2)}, u32[]{:S(2)}) %collective-permute-start.2) | collective-permute-done | bytes 163872 | tf_op jit(solution)/shard_map/ppermute | solution.py:392
  20.7 0.0 copy-done
  20.7 7.0 %forward_rest.1 = (bf16[64,4608]{1,0:T(8,128)(2,1)}, bf16[9,64,6144]{2,1,0:T(8,128)(2,1)S(1)}, bf16[27,16,5376]{2,1,0:T(8,128)(2,1)S(1)}, bf16[9,64,6144]{2,1,0:T(8,128)(2,1)S(1)}) custom-call(bf16[64,1280]{1,0:T(8,128)(2,1)S(1)} %collective-permute-done.2.ends, ...), custom_call_target="tpu_custom_call", output_to_operand_aliasing={{3}: (1, {}), {2}: (3, {})} | custom-call | flops 1019215872 | bytes 1048576 | tf_op jit(solution)/shard_map/forward_rest/pallas_call | solution.py:37
  27.7 5.5 %grad_weight.1 = (f32[896,128]{1,0:T(8,128)S(1)}, bf16[896,128]{1,0:T(8,128)(2,1)S(1)}, bf16[27,16,5376]{2,1,0:T(8,128)(2,1)S(1)}, bf16[9,64,6144]{2,1,0:T(8,128)(2,1)S(1)}) custom-call(s32[1]{0:T(128)} %bitcast.brick.refs_0_, s32[1]{0:T(128)} %bitcast.1.chan.refs_1_, s32[1]{0:T(128)} %bitcast.2.rep.refs_2_, ...), custom_call_target="tpu_custom_call", output_to_operand_aliasing={{2}: (4, {}), {3}: (5, {})} | custom-call | flops 2038431744 | bytes 1048576 | tf_op jit(solution)/shard_map/grad_weight/pallas_call | solution.py:37
  33.2 0.1 collective-permute-start.4
  33.3 1.8 %grad_features_0.1 = (bf16[27,16,5376]{2,1,0:T(8,128)(2,1)S(1)}, bf16[9,64,6144]{2,1,0:T(8,128)(2,1)S(1)}, f32[64,4608]{1,0:T(8,128)S(1)}, bf16[64,4608]{1,0:T(8,128)(2,1)S(1)}) custom-call(bf16[128,1792]{1,0:T(8,128)(2,1)S(1)} %get-tuple-element.51.weights.refs_1_, ...), custom_call_target="tpu_custom_call", output_to_operand_aliasing={{0}: (1, {}), {1}: (2, {})} | custom-call | flops 1019215872 | bytes 1048576 | tf_op jit(solution)/shard_map/grad_features_0/pallas_call | solution.py:37
  35.1 0.0 collective-permute-done.4.refs_5_
  35.1 0.1 split.1
  35.2 1.9 %collective-permute-start.6 = (bf16[448,128]{1,0:T(8,128)(2,1)S(1)}, bf16[448,128]{1,0:T(8,128)(2,1)S(1)}, u32[]{:S(2)}, u32[]{:S(2)}) collective-permute-start(bf16[448,128]{1,0:T(8,128)(2,1)S(1)} %get-tuple-element.68), channel_id=1, source_target_pairs={{0,4},{4,0},{8,12},{12,8},{1,5},{5,1},{9,13},{13,9},{2,6},{6,2},{1... | collective-permute-start | bytes 344072 | tf_op jit(solution)/shard_map/ppermute | solution.py:517
  37.1 1.8 %grad_features_1.1 = (f32[64,4608]{1,0:T(8,128)S(1)}, bf16[64,4608]{1,0:T(8,128)(2,1)S(1)}) custom-call(f32[448,128]{1,0:T(8,128)S(1)} %get-tuple-element.60.refs_0_.refs_1_, bf16[128,1792]{1,0:T(8,128)(2,1)S(1)} %get-tuple-element.51.weights.refs_1_, ...), custom_call_target="tpu_custom_call", output_to_operand_aliasing={{0}: (4, {}), {1}: (5, {})} | custom-call | flops 1019215872 | bytes 1048576 | tf_op jit(solution)/shard_map/grad_features_1/pallas_call | solution.py:37
  38.9 1.6 %collective-permute-start.5 = (bf16[64,4608]{1,0:T(8,128)(2,1)S(1)}, bf16[64,4608]{1,0:T(8,128)(2,1)S(1)}, u32[]{:S(2)}, u32[]{:S(2)}) collective-permute-start(bf16[64,4608]{1,0:T(8,128)(2,1)S(1)} %get-tuple-element.65), channel_id=1, source_target_pairs={{0,2},{2,0},{1,3},{3,1},{4,6},{6,4},{5,7},{7,5},{8,10},{10,8},{9,1... | collective-permute-start | bytes 1769480 | tf_op jit(solution)/shard_map/ppermute | solution.py:522
  40.5 0.4 collective-permute-done.6.refs_2_
  40.9 2.8 %collective-permute-start.7 = (bf16[448,128]{1,0:T(8,128)(2,1)S(1)}, bf16[448,128]{1,0:T(8,128)(2,1)S(1)}, u32[]{:S(2)}, u32[]{:S(2)}) collective-permute-start(bf16[448,128]{1,0:T(8,128)(2,1)S(1)} %merge_1.1.mine), channel_id=1, source_target_pairs={{0,8},{4,12},{8,0},{12,4},{1,9},{5,13},{9,1},{13,5},{2,10},{6,14},... | collective-permute-start | bytes 344072 | tf_op jit(solution)/shard_map/ppermute | solution.py:538
  43.7 5.5 %collective-permute-done.7.other = bf16[448,128]{1,0:T(8,128)(2,1)S(1)} collective-permute-done((bf16[448,128]{1,0:T(8,128)(2,1)S(1)}, bf16[448,128]{1,0:T(8,128)(2,1)S(1)}, u32[]{:S(2)}, u32[]{:S(2)}) %collective-permute-start.7) | collective-permute-done | bytes 114720 | tf_op jit(solution)/shard_map/ppermute | solution.py:538
  49.3 0.8 %collective-permute-start.8 = (bf16[448,128]{1,0:T(8,128)(2,1)S(1)}, bf16[448,128]{1,0:T(8,128)(2,1)S(1)}, u32[]{:S(2)}, u32[]{:S(2)}) collective-permute-start(bf16[448,128]{1,0:T(8,128)(2,1)S(1)} %merge_4.1.mine), channel_id=1, source_target_pairs={{0,4},{4,0},{8,12},{12,8},{1,5},{5,1},{9,13},{13,9},{2,6},{6,2},{1... | collective-permute-start | bytes 344072 | tf_op jit(solution)/shard_map/ppermute | solution.py:543
  50.1 4.1 %collective-permute-done.8.other = bf16[448,128]{1,0:T(8,128)(2,1)S(1)} collective-permute-done((bf16[448,128]{1,0:T(8,128)(2,1)S(1)}, bf16[448,128]{1,0:T(8,128)(2,1)S(1)}, u32[]{:S(2)}, u32[]{:S(2)}) %collective-permute-start.8) | collective-permute-done | bytes 114720 | tf_op jit(solution)/shard_map/ppermute | solution.py:543
  54.1 0.1 collective-permute-start.9
  54.2 0.2 collective-permute-done.5.rest_0_
  54.4 1.0 %add.1 = (bf16[64,4608]{1,0:T(8,128)(2,1)}, f32[8,128]{1,0:T(8,128)S(1)}) custom-call(bf16[64,4608]{1,0:T(8,128)(2,1)S(1)} %copy-done, f32[64,4608]{1,0:T(8,128)S(1)} %get-tuple-element.64.own.refs_0_, bf16[64,4608]{1,0:T(8,128)(2,1)S(1)} %collective-permute-done.5.rest_0_), custom_call_target="tpu_custom_call" | custom-call | bytes 1048576 | tf_op jit(solution)/shard_map/add/pallas_call | solution.py:37
  55.5 0.2 collective-permute-done.9.refs_5_
  55.7 1.1 %join.1 = f32[1728,128]{1,0:T(8,128)} custom-call(s32[1]{0:T(128)} %bitcast.brick.refs_0_, s32[1]{0:T(128)} %bitcast.1.chan.refs_1_, s32[1]{0:T(128)} %bitcast.2.rep.refs_2_, f32[8,128]{1,0:T(8,128)S(1)} %get-tuple-element.67.refs_3_, bf16[896,128]{1,0:T(8,128)(2,1)S(1)} %gather.1.refs_4_, bf16[896,128]{1,0:T(8,128)(2,1)S(1)} %collective-permute-done.9.refs_5_), custom_call_target="tpu_custom_call" | custom-call | flops 250000000 | bytes 1048576 | tf_op jit(solution)/shard_map/join/pallas_call | solution.py:37
  (3 shorter events, 0.1 us)
Async XLA Ops:
  0.6 17.4 %collective-permute-start.3 = (bf16[64,4608]{1,0:T(8,128)(2,1)}, bf16[64,4608]{1,0:T(8,128)(2,1)S(1)}, u32[]{:S(2)}, u32[]{:S(2)}) collective-permute-start(bf16[64,4608]{1,0:T(8,128)(2,1)} %features.3), channel_id=1, source_target_pairs={{2,0},{0,2},{3,1},{1,3},{6,4},{4,6},{7,5},{5,7},{10,8},{8,10},{11,... | collective-permute-start | bytes 1769480 | tf_op jit(solution)/shard_map/ppermute | solution.py:392
  4.7 4.3 %collective-permute-start = (bf16[128,768]{1,0:T(8,128)(2,1)S(1)}, bf16[128,768]{1,0:T(8,128)(2,1)S(1)}, u32[]{:S(2)}, u32[]{:S(2)}) collective-permute-start(bf16[128,768]{1,0:T(8,128)(2,1)S(1)} %get-tuple-element.37), channel_id=1, source_target_pairs={{0,1},{1,0},{2,3},{3,2},{4,5},{5,4},{6,7},{7,6},{8,9},{9,8},{10,11... | collective-permute-start | bytes 589832 | tf_op jit(solution)/shard_map/ppermute | solution.py:412
  4.8 4.2 %collective-permute-start.1 = (bf16[128,768]{1,0:T(8,128)(2,1)S(1)}, bf16[128,768]{1,0:T(8,128)(2,1)S(1)}, u32[]{:S(2)}, u32[]{:S(2)}) collective-permute-start(bf16[128,768]{1,0:T(8,128)(2,1)S(1)} %get-tuple-element.38), channel_id=1, source_target_pairs={{1,4},{4,1},{5,8},{8,5},{9,12},{12,9},{3,6},{6,3},{7,10},{10,7},{1... | collective-permute-start | bytes 589832 | tf_op jit(solution)/shard_map/ppermute | solution.py:378
  9.1 11.6 %collective-permute-start.2 = (bf16[64,1280]{1,0:T(8,128)(2,1)S(1)}, bf16[64,1280]{1,0:T(8,128)(2,1)S(1)}, u32[]{:S(2)}, u32[]{:S(2)}) collective-permute-start(bf16[64,1280]{1,0:T(8,128)(2,1)S(1)} %get-tuple-element.39), channel_id=1, source_target_pairs={{2,0},{0,2},{3,1},{1,3},{6,4},{4,6},{7,5},{5,7},{10,8},{8,10},{11,... | collective-permute-start | bytes 491528 | tf_op jit(solution)/shard_map/ppermute | solution.py:392
  14.2 6.5 %copy-start = (bf16[64,4608]{1,0:T(8,128)(2,1)S(1)}, bf16[64,4608]{1,0:T(8,128)(2,1)}, u32[]{:S(2)}) copy-start(bf16[64,4608]{1,0:T(8,128)(2,1)} %cotangent.5) | copy-start | bytes 1769476
  33.2 1.9 %collective-permute-start.4 = (bf16[896,128]{1,0:T(8,128)(2,1)S(1)}, bf16[896,128]{1,0:T(8,128)(2,1)S(1)}, u32[]{:S(2)}, u32[]{:S(2)}) collective-permute-start(bf16[896,128]{1,0:T(8,128)(2,1)S(1)} %get-tuple-element.59), channel_id=1, source_target_pairs={{0,1},{1,0},{2,3},{3,2},{4,5},{5,4},{6,7},{7,6},{8,9},{9,8},{10,11... | collective-permute-start | bytes 688136 | tf_op jit(solution)/shard_map/ppermute | solution.py:489
  35.2 5.7 %collective-permute-start.6 = (bf16[448,128]{1,0:T(8,128)(2,1)S(1)}, bf16[448,128]{1,0:T(8,128)(2,1)S(1)}, u32[]{:S(2)}, u32[]{:S(2)}) collective-permute-start(bf16[448,128]{1,0:T(8,128)(2,1)S(1)} %get-tuple-element.68), channel_id=1, source_target_pairs={{0,4},{4,0},{8,12},{12,8},{1,5},{5,1},{9,13},{13,9},{2,6},{6,2},{1... | collective-permute-start | bytes 344072 | tf_op jit(solution)/shard_map/ppermute | solution.py:517
  38.9 15.5 %collective-permute-start.5 = (bf16[64,4608]{1,0:T(8,128)(2,1)S(1)}, bf16[64,4608]{1,0:T(8,128)(2,1)S(1)}, u32[]{:S(2)}, u32[]{:S(2)}) collective-permute-start(bf16[64,4608]{1,0:T(8,128)(2,1)S(1)} %get-tuple-element.65), channel_id=1, source_target_pairs={{0,2},{2,0},{1,3},{3,1},{4,6},{6,4},{5,7},{7,5},{8,10},{10,8},{9,1... | collective-permute-start | bytes 1769480 | tf_op jit(solution)/shard_map/ppermute | solution.py:522
  40.9 8.3 %collective-permute-start.7 = (bf16[448,128]{1,0:T(8,128)(2,1)S(1)}, bf16[448,128]{1,0:T(8,128)(2,1)S(1)}, u32[]{:S(2)}, u32[]{:S(2)}) collective-permute-start(bf16[448,128]{1,0:T(8,128)(2,1)S(1)} %merge_1.1.mine), channel_id=1, source_target_pairs={{0,8},{4,12},{8,0},{12,4},{1,9},{5,13},{9,1},{13,5},{2,10},{6,14},... | collective-permute-start | bytes 344072 | tf_op jit(solution)/shard_map/ppermute | solution.py:538
  49.3 4.9 %collective-permute-start.8 = (bf16[448,128]{1,0:T(8,128)(2,1)S(1)}, bf16[448,128]{1,0:T(8,128)(2,1)S(1)}, u32[]{:S(2)}, u32[]{:S(2)}) collective-permute-start(bf16[448,128]{1,0:T(8,128)(2,1)S(1)} %merge_4.1.mine), channel_id=1, source_target_pairs={{0,4},{4,0},{8,12},{12,8},{1,5},{5,1},{9,13},{13,9},{2,6},{6,2},{1... | collective-permute-start | bytes 344072 | tf_op jit(solution)/shard_map/ppermute | solution.py:543
  54.1 1.6 %collective-permute-start.9 = (bf16[896,128]{1,0:T(8,128)(2,1)S(1)}, bf16[896,128]{1,0:T(8,128)(2,1)S(1)}, u32[]{:S(2)}, u32[]{:S(2)}) collective-permute-start(bf16[896,128]{1,0:T(8,128)(2,1)S(1)} %gather.1.refs_4_), channel_id=1, source_target_pairs={{0,1},{1,0},{2,3},{3,2},{4,5},{5,4},{6,7},{7,6},{8,9},{9,8},{10,11... | collective-permute-start | bytes 688136 | tf_op jit(solution)/shard_map/ppermute | solution.py:547

commit v9 on v8

--- a/solution.py
+++ b/solution.py
@@ -84,10 +84,12 @@
     return [range(first, min(first + count, TAPS)) for first in range(0, TAPS, count)]
 
 
-def product(weights, shifts, valid, at_shift, at_valid, width, taps_of):
+def product(weights, shifts, valid, at_shift, at_valid, width, taps_of, between=()):
     channels = shifts.shape[1]
     total = None
-    for group in groups():
+    for at, group in enumerate(groups()):
+        for piece in between[at :: len(groups())]:
+            piece()
         rows = []
         for tap in group:
             rows += masked(shifts, valid, taps_of(tap), at_shift, at_valid, width)
@@ -258,32 +260,41 @@
     grad[:, lead + HALO : lead + HALO + sites] = cotangent[...]
     grad[:, lead + HALO + sites :] = right[share : 2 * share, :HALO]
 
-    def finish(before, start):
+    def finish(before, start, at):
+        rows = pl.ds(at, ROWS)
         previous = pl.multiple_of(jnp.maximum(start - WIDTH, 0) + HALO, 128)
         there = pl.ds(pl.multiple_of(start - WIDTH + lead, 128), WIDTH)
-        value = hidden[before]
+        value = hidden[before, rows, :]
         sigma = 0.5 * jnp.tanh(0.5 * value) + 0.5
-        features = own[4, :, pl.ds(previous, WIDTH)]
-        kept[:, pl.ds(start, WIDTH)] = (features.astype(F32) + value * sigma).astype(BF16)
-        grad[:, there] = (
-            grad[:, there].astype(F32) * sigma * (1.0 + value * (1.0 - sigma))
+        features = own[4, rows, pl.ds(previous, WIDTH)]
+        kept[rows, pl.ds(start, WIDTH)] = (features.astype(F32) + value * sigma).astype(BF16)
+        grad[rows, there] = (
+            grad[rows, there].astype(F32) * sigma * (1.0 + value * (1.0 - sigma))
         ).astype(BF16)
-        for at in range(0, share, ROWS):
-            rows = pl.ds(at, ROWS)
-            window = grad[rows, pl.ds(start, WIDTH + 256)]
-            spread(window, grads, rows, pl.ds(start, WIDTH))
+        window = grad[rows, pl.ds(start, WIDTH + 256)]
+        spread(window, grads, rows, pl.ds(start, WIDTH))
+
+    def finishes(before, start):
+        return [functools.partial(finish, before, start, at) for at in range(0, share, ROWS)]
 
     def block(j, carry):
         start = pl.multiple_of(j * WIDTH, 128)
-        finish((j + 1) % 2, start)
         hidden[j % 2] = begun[:, pl.ds(start, WIDTH)] + product(
-            weights, shifts, valid, start + HALO, start, WIDTH, lambda tap: tap
+            weights,
+            shifts,
+            valid,
+            start + HALO,
+            start,
+            WIDTH,
+            lambda tap: tap,
+            [lambda: None, *finishes((j + 1) % 2, start)],
         )
         return carry
 
     count = begun.shape[1] // WIDTH
     lax.fori_loop(0, count, block, 0)
-    finish((count + 1) % 2, count * WIDTH)
+    for piece in finishes((count + 1) % 2, count * WIDTH):
+        piece()
     output[...] = kept[:, WIDTH + HALO : WIDTH + HALO + sites]
 
 

time: 57 us -> 57.1 us (level)
  no operation moved by 1% of the time
where the time goes in v9:
time: 57.1 us; the launch traced here: 56.9 us
  Pallas kernels  30.1 us (53%)
  waiting for transfers between devices  15 us (26%)
  starting transfers between devices  11 us (19%)
  between operations  0.77 us (1%)
    pallas_call x15, Pallas kernels, kernel(): pl.pallas_call(body, out_shape=outs, in_specs=[SCALAR] * len(scalars) + [...  30.1 us
    ppermute x1, waiting for transfers between devices, local(): other = lax.ppermute(mine, 'brick', [(i, i ^ step) for i in range(bricks)])  5.48 us
    ppermute x2, waiting for transfers between devices, around(): lax.ppermute(x, 'chan', [((i + over) % chans, i) for i in range(chans)])  4.58 us
    ppermute x1, waiting for transfers between devices, local(): other = lax.ppermute(mine, 'brick', pairs)  4.07 us
    ppermute x2, starting transfers between devices, around(): lax.ppermute(x, 'chan', [((i + over) % chans, i) for i in range(chans)])  3.1 us
    ppermute x1, starting transfers between devices, local(): other = lax.ppermute(mine, 'brick', [(i, i ^ step) for i in range(bricks)])  2.82 us
    ppermute x1, starting transfers between devices, local(): arrived = lax.ppermute(sent, 'brick', pairs)  1.88 us
    ppermute x1, starting transfers between devices, local(): lax.ppermute(other if left == share else other[(over - 1) * share:over *...  1.55 us
  transfers between devices with their start and end apart: 10, of which 7 were waited for; matrix products, arithmetic and copies ran while one was open for 0% of the time, Pallas kernels for 29%

profile of v9, /device:TPU:0, one launch (start us, length us, event | category | flops | bytes accessed | tf_op | source)
XLA Modules:
  0.0 56.9 jit_solution(710290701682222872)
XLA Ops:
  0.6 3.0 %collective-permute-start.3 = (bf16[64,4608]{1,0:T(8,128)(2,1)}, bf16[64,4608]{1,0:T(8,128)(2,1)S(1)}, u32[]{:S(2)}, u32[]{:S(2)}) collective-permute-start(bf16[64,4608]{1,0:T(8,128)(2,1)} %features.3), channel_id=1, source_target_pairs={{2,0},{0,2},{3,1},{1,3},{6,4},{4,6},{7,5},{5,7},{10,8},{8,10},{11,... | collective-permute-start | bytes 1769480 | tf_op jit(solution)/shard_map/ppermute | solution.py:403
  3.6 1.1 %pack.1 = (bf16[128,768]{1,0:T(8,128)(2,1)S(1)}, bf16[128,768]{1,0:T(8,128)(2,1)S(1)}) custom-call(s32[1]{0:T(128)} %bitcast.brick.refs_0_, s32[1]{0:T(128)} %bitcast.1.chan.refs_1_, s32[1]{0:T(128)} %bitcast.2.rep.refs_2_, bf16[64,4608]{1,0:T(8,128)(2,1)} %features.3, bf16[64,4608]{1,0:T(8,128)(2,1)} %cotangent.5, s32[27,4608]{1,0:T(8,128)} %neighbours.3), custom_call_target="tpu_custom_call" | custom-call | bytes 1048576 | tf_op jit(solution)/shard_map/pack/pallas_call | solution.py:37
  4.7 0.1 collective-permute-start
  4.8 0.7 %collective-permute-start.1 = (bf16[128,768]{1,0:T(8,128)(2,1)S(1)}, bf16[128,768]{1,0:T(8,128)(2,1)S(1)}, u32[]{:S(2)}, u32[]{:S(2)}) collective-permute-start(bf16[128,768]{1,0:T(8,128)(2,1)S(1)} %get-tuple-element.38), channel_id=1, source_target_pairs={{1,4},{4,1},{5,8},{8,5},{9,12},{12,9},{3,6},{6,3},{7,10},{10,7},{1... | collective-permute-start | bytes 589832 | tf_op jit(solution)/shard_map/ppermute | solution.py:389
  5.5 3.5 %prepare.1 = (bf16[64,1728]{1,0:T(8,128)(2,1)S(1)}, bf16[64,1728]{1,0:T(8,128)(2,1)S(1)}, bf16[128,1792]{1,0:T(8,128)(2,1)S(1)}, bf16[9,64,6144]{2,1,0:T(8,128)(2,1)S(1)}, bf16[27,16,5376]{2,1,0:T(8,128)(2,1)S(1)}) custom-call(s32[1]{0:T(128)} %bitcast.brick.refs_0_, s32[1]{0:T(128)} %bitcast.1.chan.refs_1_, s32[1]{0:T(128)} %bitcast.2.rep.refs_2_, ...), custom_call_target="tpu_custom_call" | custom-call | bytes 1048576 | tf_op jit(solution)/shard_map/prepare/pallas_call | solution.py:37
  9.0 0.0 collective-permute-done.refs_4_
  9.0 0.0 collective-permute-done.1.refs_5_
  9.0 0.1 ends.1
  9.1 0.1 collective-permute-start.2
  9.2 5.0 %forward_own.1 = (f32[64,5376]{1,0:T(8,128)S(1)}, bf16[9,64,6144]{2,1,0:T(8,128)(2,1)S(1)}, bf16[27,16,5376]{2,1,0:T(8,128)(2,1)S(1)}) custom-call(bf16[128,768]{1,0:T(8,128)(2,1)S(1)} %get-tuple-element.40.left, bf16[128,768]{1,0:T(8,128)(2,1)S(1)} %get-tuple-element.41.right, ...), custom_call_target="tpu_custom_call", output_to_operand_aliasing={{1}: (3, {}), {2}: (4, {})} | custom-call | bytes 1048576 | tf_op jit(solution)/shard_map/forward_own/pallas_call | solution.py:37
  14.2 0.0 copy-start
  14.2 3.8 %collective-permute-done.3.rest = bf16[64,4608]{1,0:T(8,128)(2,1)S(1)} collective-permute-done((bf16[64,4608]{1,0:T(8,128)(2,1)}, bf16[64,4608]{1,0:T(8,128)(2,1)S(1)}, u32[]{:S(2)}, u32[]{:S(2)}) %collective-permute-start.3) | collective-permute-done | bytes 589856 | tf_op jit(solution)/shard_map/ppermute | solution.py:403
  18.0 1.9 %arrive.1 = (bf16[9,64,6144]{2,1,0:T(8,128)(2,1)S(1)}, bf16[4608,128]{1,0:T(8,128)(2,1)S(1)}, bf16[9,64,6144]{2,1,0:T(8,128)(2,1)S(1)}) custom-call(bf16[64,4608]{1,0:T(8,128)(2,1)S(1)} %collective-permute-done.3.rest, bf16[9,64,6144]{2,1,0:T(8,128)(2,1)S(1)} %get-tuple-element.44.own_in), custom_call_target="tpu_custom_call", output_to_operand_aliasing={{2}: (1, {})} | custom-call | bytes 1048576 | tf_op jit(solution)/shard_map/arrive/pallas_call | solution.py:37
  19.9 0.8 %collective-permute-done.2.ends = bf16[64,1280]{1,0:T(8,128)(2,1)S(1)} collective-permute-done((bf16[64,1280]{1,0:T(8,128)(2,1)S(1)}, bf16[64,1280]{1,0:T(8,128)(2,1)S(1)}, u32[]{:S(2)}, u32[]{:S(2)}) %collective-permute-start.2) | collective-permute-done | bytes 163872 | tf_op jit(solution)/shard_map/ppermute | solution.py:403
  20.7 0.0 copy-done
  20.7 7.2 %forward_rest.1 = (bf16[64,4608]{1,0:T(8,128)(2,1)}, bf16[9,64,6144]{2,1,0:T(8,128)(2,1)S(1)}, bf16[27,16,5376]{2,1,0:T(8,128)(2,1)S(1)}, bf16[9,64,6144]{2,1,0:T(8,128)(2,1)S(1)}) custom-call(bf16[64,1280]{1,0:T(8,128)(2,1)S(1)} %collective-permute-done.2.ends, ...), custom_call_target="tpu_custom_call", output_to_operand_aliasing={{3}: (1, {}), {2}: (3, {})} | custom-call | flops 1019215872 | bytes 1048576 | tf_op jit(solution)/shard_map/forward_rest/pallas_call | solution.py:37
  27.9 5.5 %grad_weight.1 = (f32[896,128]{1,0:T(8,128)S(1)}, bf16[896,128]{1,0:T(8,128)(2,1)S(1)}, bf16[27,16,5376]{2,1,0:T(8,128)(2,1)S(1)}, bf16[9,64,6144]{2,1,0:T(8,128)(2,1)S(1)}) custom-call(s32[1]{0:T(128)} %bitcast.brick.refs_0_, s32[1]{0:T(128)} %bitcast.1.chan.refs_1_, s32[1]{0:T(128)} %bitcast.2.rep.refs_2_, ...), custom_call_target="tpu_custom_call", output_to_operand_aliasing={{2}: (4, {}), {3}: (5, {})} | custom-call | flops 2038431744 | bytes 1048576 | tf_op jit(solution)/shard_map/grad_weight/pallas_call | solution.py:37
  33.4 0.1 collective-permute-start.4
  33.4 1.8 %grad_features_0.1 = (bf16[27,16,5376]{2,1,0:T(8,128)(2,1)S(1)}, bf16[9,64,6144]{2,1,0:T(8,128)(2,1)S(1)}, f32[64,4608]{1,0:T(8,128)S(1)}, bf16[64,4608]{1,0:T(8,128)(2,1)S(1)}) custom-call(bf16[128,1792]{1,0:T(8,128)(2,1)S(1)} %get-tuple-element.51.weights.refs_1_, ...), custom_call_target="tpu_custom_call", output_to_operand_aliasing={{0}: (1, {}), {1}: (2, {})} | custom-call | flops 1019215872 | bytes 1048576 | tf_op jit(solution)/shard_map/grad_features_0/pallas_call | solution.py:37
  35.3 0.0 collective-permute-done.4.refs_5_
  35.3 0.1 split.1
  35.3 1.9 %collective-permute-start.6 = (bf16[448,128]{1,0:T(8,128)(2,1)S(1)}, bf16[448,128]{1,0:T(8,128)(2,1)S(1)}, u32[]{:S(2)}, u32[]{:S(2)}) collective-permute-start(bf16[448,128]{1,0:T(8,128)(2,1)S(1)} %get-tuple-element.68), channel_id=1, source_target_pairs={{0,4},{4,0},{8,12},{12,8},{1,5},{5,1},{9,13},{13,9},{2,6},{6,2},{1... | collective-permute-start | bytes 344072 | tf_op jit(solution)/shard_map/ppermute | solution.py:528
  37.2 1.8 %grad_features_1.1 = (f32[64,4608]{1,0:T(8,128)S(1)}, bf16[64,4608]{1,0:T(8,128)(2,1)S(1)}) custom-call(f32[448,128]{1,0:T(8,128)S(1)} %get-tuple-element.60.refs_0_.refs_1_, bf16[128,1792]{1,0:T(8,128)(2,1)S(1)} %get-tuple-element.51.weights.refs_1_, ...), custom_call_target="tpu_custom_call", output_to_operand_aliasing={{0}: (4, {}), {1}: (5, {})} | custom-call | flops 1019215872 | bytes 1048576 | tf_op jit(solution)/shard_map/grad_features_1/pallas_call | solution.py:37
  39.0 1.6 %collective-permute-start.5 = (bf16[64,4608]{1,0:T(8,128)(2,1)S(1)}, bf16[64,4608]{1,0:T(8,128)(2,1)S(1)}, u32[]{:S(2)}, u32[]{:S(2)}) collective-permute-start(bf16[64,4608]{1,0:T(8,128)(2,1)S(1)} %get-tuple-element.65), channel_id=1, source_target_pairs={{0,2},{2,0},{1,3},{3,1},{4,6},{6,4},{5,7},{7,5},{8,10},{10,8},{9,1... | collective-permute-start | bytes 1769480 | tf_op jit(solution)/shard_map/ppermute | solution.py:533
  40.6 0.4 collective-permute-done.6.refs_2_
  41.0 2.8 %collective-permute-start.7 = (bf16[448,128]{1,0:T(8,128)(2,1)S(1)}, bf16[448,128]{1,0:T(8,128)(2,1)S(1)}, u32[]{:S(2)}, u32[]{:S(2)}) collective-permute-start(bf16[448,128]{1,0:T(8,128)(2,1)S(1)} %merge_1.1.mine), channel_id=1, source_target_pairs={{0,8},{4,12},{8,0},{12,4},{1,9},{5,13},{9,1},{13,5},{2,10},{6,14},... | collective-permute-start | bytes 344072 | tf_op jit(solution)/shard_map/ppermute | solution.py:549
  43.9 5.5 %collective-permute-done.7.other = bf16[448,128]{1,0:T(8,128)(2,1)S(1)} collective-permute-done((bf16[448,128]{1,0:T(8,128)(2,1)S(1)}, bf16[448,128]{1,0:T(8,128)(2,1)S(1)}, u32[]{:S(2)}, u32[]{:S(2)}) %collective-permute-start.7) | collective-permute-done | bytes 114720 | tf_op jit(solution)/shard_map/ppermute | solution.py:549
  49.4 0.8 %collective-permute-start.8 = (bf16[448,128]{1,0:T(8,128)(2,1)S(1)}, bf16[448,128]{1,0:T(8,128)(2,1)S(1)}, u32[]{:S(2)}, u32[]{:S(2)}) collective-permute-start(bf16[448,128]{1,0:T(8,128)(2,1)S(1)} %merge_4.1.mine), channel_id=1, source_target_pairs={{0,4},{4,0},{8,12},{12,8},{1,5},{5,1},{9,13},{13,9},{2,6},{6,2},{1... | collective-permute-start | bytes 344072 | tf_op jit(solution)/shard_map/ppermute | solution.py:554
  50.2 4.1 %collective-permute-done.8.other = bf16[448,128]{1,0:T(8,128)(2,1)S(1)} collective-permute-done((bf16[448,128]{1,0:T(8,128)(2,1)S(1)}, bf16[448,128]{1,0:T(8,128)(2,1)S(1)}, u32[]{:S(2)}, u32[]{:S(2)}) %collective-permute-start.8) | collective-permute-done | bytes 114720 | tf_op jit(solution)/shard_map/ppermute | solution.py:554
  54.3 0.1 collective-permute-start.9
  54.3 0.2 collective-permute-done.5.rest_0_
  54.5 1.0 %add.1 = (bf16[64,4608]{1,0:T(8,128)(2,1)}, f32[8,128]{1,0:T(8,128)S(1)}) custom-call(bf16[64,4608]{1,0:T(8,128)(2,1)S(1)} %copy-done, f32[64,4608]{1,0:T(8,128)S(1)} %get-tuple-element.64.own.refs_0_, bf16[64,4608]{1,0:T(8,128)(2,1)S(1)} %collective-permute-done.5.rest_0_), custom_call_target="tpu_custom_call" | custom-call | bytes 1048576 | tf_op jit(solution)/shard_map/add/pallas_call | solution.py:37
  55.6 0.2 collective-permute-done.9.refs_5_
  55.8 1.1 %join.1 = f32[1728,128]{1,0:T(8,128)} custom-call(s32[1]{0:T(128)} %bitcast.brick.refs_0_, s32[1]{0:T(128)} %bitcast.1.chan.refs_1_, s32[1]{0:T(128)} %bitcast.2.rep.refs_2_, f32[8,128]{1,0:T(8,128)S(1)} %get-tuple-element.67.refs_3_, bf16[896,128]{1,0:T(8,128)(2,1)S(1)} %gather.1.refs_4_, bf16[896,128]{1,0:T(8,128)(2,1)S(1)} %collective-permute-done.9.refs_5_), custom_call_target="tpu_custom_call" | custom-call | flops 250000000 | bytes 1048576 | tf_op jit(solution)/shard_map/join/pallas_call | solution.py:37
  (3 shorter events, 0.1 us)
Async XLA Ops:
  0.6 17.4 %collective-permute-start.3 = (bf16[64,4608]{1,0:T(8,128)(2,1)}, bf16[64,4608]{1,0:T(8,128)(2,1)S(1)}, u32[]{:S(2)}, u32[]{:S(2)}) collective-permute-start(bf16[64,4608]{1,0:T(8,128)(2,1)} %features.3), channel_id=1, source_target_pairs={{2,0},{0,2},{3,1},{1,3},{6,4},{4,6},{7,5},{5,7},{10,8},{8,10},{11,... | collective-permute-start | bytes 1769480 | tf_op jit(solution)/shard_map/ppermute | solution.py:403
  4.7 4.3 %collective-permute-start = (bf16[128,768]{1,0:T(8,128)(2,1)S(1)}, bf16[128,768]{1,0:T(8,128)(2,1)S(1)}, u32[]{:S(2)}, u32[]{:S(2)}) collective-permute-start(bf16[128,768]{1,0:T(8,128)(2,1)S(1)} %get-tuple-element.37), channel_id=1, source_target_pairs={{0,1},{1,0},{2,3},{3,2},{4,5},{5,4},{6,7},{7,6},{8,9},{9,8},{10,11... | collective-permute-start | bytes 589832 | tf_op jit(solution)/shard_map/ppermute | solution.py:423
  4.8 4.2 %collective-permute-start.1 = (bf16[128,768]{1,0:T(8,128)(2,1)S(1)}, bf16[128,768]{1,0:T(8,128)(2,1)S(1)}, u32[]{:S(2)}, u32[]{:S(2)}) collective-permute-start(bf16[128,768]{1,0:T(8,128)(2,1)S(1)} %get-tuple-element.38), channel_id=1, source_target_pairs={{1,4},{4,1},{5,8},{8,5},{9,12},{12,9},{3,6},{6,3},{7,10},{10,7},{1... | collective-permute-start | bytes 589832 | tf_op jit(solution)/shard_map/ppermute | solution.py:389
  9.1 11.6 %collective-permute-start.2 = (bf16[64,1280]{1,0:T(8,128)(2,1)S(1)}, bf16[64,1280]{1,0:T(8,128)(2,1)S(1)}, u32[]{:S(2)}, u32[]{:S(2)}) collective-permute-start(bf16[64,1280]{1,0:T(8,128)(2,1)S(1)} %get-tuple-element.39), channel_id=1, source_target_pairs={{2,0},{0,2},{3,1},{1,3},{6,4},{4,6},{7,5},{5,7},{10,8},{8,10},{11,... | collective-permute-start | bytes 491528 | tf_op jit(solution)/shard_map/ppermute | solution.py:403
  14.2 6.5 %copy-start = (bf16[64,4608]{1,0:T(8,128)(2,1)S(1)}, bf16[64,4608]{1,0:T(8,128)(2,1)}, u32[]{:S(2)}) copy-start(bf16[64,4608]{1,0:T(8,128)(2,1)} %cotangent.5) | copy-start | bytes 1769476
  33.4 1.9 %collective-permute-start.4 = (bf16[896,128]{1,0:T(8,128)(2,1)S(1)}, bf16[896,128]{1,0:T(8,128)(2,1)S(1)}, u32[]{:S(2)}, u32[]{:S(2)}) collective-permute-start(bf16[896,128]{1,0:T(8,128)(2,1)S(1)} %get-tuple-element.59), channel_id=1, source_target_pairs={{0,1},{1,0},{2,3},{3,2},{4,5},{5,4},{6,7},{7,6},{8,9},{9,8},{10,11... | collective-permute-start | bytes 688136 | tf_op jit(solution)/shard_map/ppermute | solution.py:500
  35.3 5.7 %collective-permute-start.6 = (bf16[448,128]{1,0:T(8,128)(2,1)S(1)}, bf16[448,128]{1,0:T(8,128)(2,1)S(1)}, u32[]{:S(2)}, u32[]{:S(2)}) collective-permute-start(bf16[448,128]{1,0:T(8,128)(2,1)S(1)} %get-tuple-element.68), channel_id=1, source_target_pairs={{0,4},{4,0},{8,12},{12,8},{1,5},{5,1},{9,13},{13,9},{2,6},{6,2},{1... | collective-permute-start | bytes 344072 | tf_op jit(solution)/shard_map/ppermute | solution.py:528
  39.0 15.5 %collective-permute-start.5 = (bf16[64,4608]{1,0:T(8,128)(2,1)S(1)}, bf16[64,4608]{1,0:T(8,128)(2,1)S(1)}, u32[]{:S(2)}, u32[]{:S(2)}) collective-permute-start(bf16[64,4608]{1,0:T(8,128)(2,1)S(1)} %get-tuple-element.65), channel_id=1, source_target_pairs={{0,2},{2,0},{1,3},{3,1},{4,6},{6,4},{5,7},{7,5},{8,10},{10,8},{9,1... | collective-permute-start | bytes 1769480 | tf_op jit(solution)/shard_map/ppermute | solution.py:533
  41.0 8.3 %collective-permute-start.7 = (bf16[448,128]{1,0:T(8,128)(2,1)S(1)}, bf16[448,128]{1,0:T(8,128)(2,1)S(1)}, u32[]{:S(2)}, u32[]{:S(2)}) collective-permute-start(bf16[448,128]{1,0:T(8,128)(2,1)S(1)} %merge_1.1.mine), channel_id=1, source_target_pairs={{0,8},{4,12},{8,0},{12,4},{1,9},{5,13},{9,1},{13,5},{2,10},{6,14},... | collective-permute-start | bytes 344072 | tf_op jit(solution)/shard_map/ppermute | solution.py:549
  49.4 4.9 %collective-permute-start.8 = (bf16[448,128]{1,0:T(8,128)(2,1)S(1)}, bf16[448,128]{1,0:T(8,128)(2,1)S(1)}, u32[]{:S(2)}, u32[]{:S(2)}) collective-permute-start(bf16[448,128]{1,0:T(8,128)(2,1)S(1)} %merge_4.1.mine), channel_id=1, source_target_pairs={{0,4},{4,0},{8,12},{12,8},{1,5},{5,1},{9,13},{13,9},{2,6},{6,2},{1... | collective-permute-start | bytes 344072 | tf_op jit(solution)/shard_map/ppermute | solution.py:554
  54.3 1.6 %collective-permute-start.9 = (bf16[896,128]{1,0:T(8,128)(2,1)S(1)}, bf16[896,128]{1,0:T(8,128)(2,1)S(1)}, u32[]{:S(2)}, u32[]{:S(2)}) collective-permute-start(bf16[896,128]{1,0:T(8,128)(2,1)S(1)} %gather.1.refs_4_), channel_id=1, source_target_pairs={{0,1},{1,0},{2,3},{3,2},{4,5},{5,4},{6,7},{7,6},{8,9},{9,8},{10,11... | collective-permute-start | bytes 688136 | tf_op jit(solution)/shard_map/ppermute | solution.py:558

commit v10 on v9

--- a/solution.py
+++ b/solution.py
@@ -16,8 +16,10 @@
 LEAD = 896
 MANY = 14
 ROWS = 16
+LANES = 128
 GROUP = 4
-WIDTH = 768
+TILES = 6
+WIDTH = TILES * LANES
 LATER = 25 * 10**7
 LINE = ("brick", "chan", "rep")
 MIB = 1024 * 1024
@@ -58,25 +60,34 @@
     return jax.ShapeDtypeStruct(dims, kind)
 
 
-def spread(window, target, rows, lanes):
+def wide(ref, first, count, *rows):
+    return jnp.concatenate([ref[(first + i, *rows)] for i in range(count)], axis=1)
+
+
+def lay(ref, first, value, *rows):
+    for i in range(value.shape[1] // LANES):
+        ref[(first + i, *rows)] = value[:, i * LANES : (i + 1) * LANES]
+
+
+def spread(window, target, rows, first):
     width = window.shape[1]
     for j, step in enumerate(STEPS):
         moved = pltpu.roll(window, -step % width, 1) if step else window
-        target[j, rows, lanes] = moved[:, 128 : width - 128]
+        lay(target.at[j], first, moved[:, LANES : width - LANES], rows)
 
 
 def shift(shifts, low, high):
-    for at in range(0, shifts.shape[1], ROWS):
+    for at in range(0, shifts.shape[2], ROWS):
         rows = pl.ds(at, ROWS)
-        spread(shifts[4, rows, low - 128 : high + 128], shifts, rows, slice(low, high))
-
-
-def masked(shifts, valid, tap, at_shift, at_valid, width):
-    keep = valid[tap, :, pl.ds(at_valid, width)]
-    begin = pl.multiple_of(at_shift + (tap // 9 - 1) * FACE, 128)
+        spread(wide(shifts.at[4], low - 1, high - low + 2, rows), shifts, rows, low)
+
+
+def masked(shifts, valid, tap, at_shift, at_valid):
+    keep = wide(valid.at[tap], at_valid, TILES)
+    begin = at_shift + (tap // 9 - 1) * FACE // LANES
     return [
-        shifts[tap % 9, at : at + ROWS, pl.ds(begin, width)] * keep
-        for at in range(0, shifts.shape[1], ROWS)
+        wide(shifts.at[tap % 9], begin, TILES, pl.ds(at, ROWS)) * keep
+        for at in range(0, shifts.shape[2], ROWS)
     ]
 
 
@@ -84,15 +95,15 @@
     return [range(first, min(first + count, TAPS)) for first in range(0, TAPS, count)]
 
 
-def product(weights, shifts, valid, at_shift, at_valid, width, taps_of, between=()):
-    channels = shifts.shape[1]
+def product(weights, shifts, valid, at_shift, at_valid, taps_of, between=()):
+    channels = shifts.shape[2]
     total = None
     for at, group in enumerate(groups()):
         for piece in between[at :: len(groups())]:
             piece()
         rows = []
         for tap in group:
-            rows += masked(shifts, valid, taps_of(tap), at_shift, at_valid, width)
+            rows += masked(shifts, valid, taps_of(tap), at_shift, at_valid)
         part = jnp.dot(
             weights[:, group[0] * channels : (group[-1] + 1) * channels],
             jnp.concatenate(rows, axis=0),
@@ -142,8 +153,14 @@
     pl.when(rep[0] != 0)(functools.partial(fill, core, line))
 
 
+def expand(kept, valid, first):
+    for tap in range(TAPS):
+        row = jnp.broadcast_to(kept[tap : tap + 1, :], (ROWS, kept.shape[1]))
+        lay(valid.at[tap], first, row.astype(BF16))
+
+
 def prepare_body(
-    brick, chan, rep, by_out, features, neighbours, own, rest, by_in, shifts, valid, flat, kept, taken, near, done
+    brick, chan, rep, by_out, features, neighbours, own, rest, by_in, shifts, valid, flat, kept, taken, staged, near, done
 ):
     total = by_out.shape[2]
     share, sites = features.shape
@@ -153,7 +170,7 @@
         for i, (source, target) in enumerate(
             [
                 (by_out, taken),
-                (features, shifts.at[4, :, pl.ds(FAR, sites)]),
+                (features, staged),
                 (neighbours, near),
             ]
         )
@@ -178,33 +195,27 @@
         ).astype(BF16)
     by_in[...] = flat[...].T
     copies[1].wait()
-    shift(shifts, FAR + 128, FAR + sites - 128)
+    lay(shifts.at[4], FAR // LANES, staged[...])
+    shift(shifts, FAR // LANES + 1, (FAR + sites) // LANES - 1)
     copies[2].wait()
     kept[...] = (near[...] >= 0).astype(F32)
-    for tap in range(TAPS):
-        valid[tap, :, HALO : HALO + sites] = jnp.broadcast_to(
-            kept[tap : tap + 1, :], (ROWS, sites)
-        ).astype(BF16)
+    expand(kept, valid, HALO // LANES)
 
 
 def own_body(left, right, weights, shifts_in, valid_in, begun, shifts, valid, kept):
     del shifts_in, valid_in
     share = begun.shape[0]
-    far = shifts.shape[2] - FAR
-    for side, at, start in ((left, 0, 128), (right, 1, far - 128)):
-        shifts[4, :, at * far : at * far + FAR] = side[:share, :]
-        shift(shifts, start, start + FAR)
+    edge = FAR // LANES
+    far = shifts.shape[1] - edge
+    for side, at, start in ((left, 0, 1), (right, 1, far - 1)):
+        lay(shifts.at[4], at * far, side[:share, :])
+        shift(shifts, start, start + edge)
         kept[...] = side[share : share + 32, HALO:].astype(F32)
-        begin = at * (valid.shape[2] - HALO)
-        for tap in range(TAPS):
-            valid[tap, :, begin : begin + HALO] = jnp.broadcast_to(
-                kept[tap : tap + 1, :], (ROWS, HALO)
-            ).astype(BF16)
+        expand(kept, valid, at * (valid.shape[1] - HALO // LANES))
 
     def block(j, carry):
-        start = pl.multiple_of(j * WIDTH, 128)
-        begun[:, pl.ds(start, WIDTH)] = product(
-            weights, shifts, valid, start + HALO, start, WIDTH, lambda tap: tap
+        begun[:, pl.ds(pl.multiple_of(j * WIDTH, LANES), WIDTH)] = product(
+            weights, shifts, valid, j * TILES + HALO // LANES, j * TILES, lambda tap: tap
         )
         return carry
 
@@ -214,14 +225,14 @@
 def arrive_body(rest, own_in, shifts, across, own):
     del own_in
     sites = rest.shape[1]
-    shifts[4, :, FAR : FAR + sites] = rest[...]
-    shift(shifts, FAR + 128, FAR + sites - 128)
+    edge = FAR // LANES
+    lay(shifts.at[4], edge, rest[...])
+    shift(shifts, edge + 1, edge + sites // LANES - 1)
 
     def block(j, carry):
-        start = pl.multiple_of(j * WIDTH, 128)
-        here = pl.ds(pl.multiple_of(start + FAR, 128), WIDTH)
-        across[pl.ds(start, WIDTH), :] = jnp.concatenate(
-            [own[4, :, here], shifts[4, :, here]], axis=0
+        at = j * TILES + edge
+        across[pl.ds(pl.multiple_of(j * WIDTH, LANES), WIDTH), :] = jnp.concatenate(
+            [wide(own.at[4], at, TILES), wide(shifts.at[4], at, TILES)], axis=0
         ).T
         return carry
 
@@ -248,44 +259,45 @@
 ):
     del shifts_in, valid_in
     share, sites = cotangent.shape
-    far = shifts.shape[2] - FAR
-    shifts[4, :, : FAR - NEAR] = jnp.zeros((shifts.shape[1], FAR - NEAR), BF16)
-    shifts[4, :, FAR - NEAR : FAR] = ends[:, :NEAR]
-    shifts[4, :, far : far + NEAR] = ends[:, NEAR:]
-    shifts[4, :, far + NEAR :] = jnp.zeros((shifts.shape[1], FAR - NEAR), BF16)
-    shift(shifts, 128, 128 + FAR)
-    shift(shifts, far - 128, far + FAR - 128)
-    lead = LEAD + 128
-    grad[:, lead : lead + HALO] = left[share : 2 * share, :HALO]
-    grad[:, lead + HALO : lead + HALO + sites] = cotangent[...]
-    grad[:, lead + HALO + sites :] = right[share : 2 * share, :HALO]
+    edge, near, halo, lead = (n // LANES for n in (FAR, NEAR, HALO, LEAD + LANES))
+    far = shifts.shape[1] - edge
+    lay(shifts.at[4], 0, jnp.zeros((shifts.shape[2], FAR - NEAR), BF16))
+    lay(shifts.at[4], edge - near, ends[:, :NEAR])
+    lay(shifts.at[4], far, ends[:, NEAR:])
+    lay(shifts.at[4], far + near, jnp.zeros((shifts.shape[2], FAR - NEAR), BF16))
+    shift(shifts, 1, 1 + edge)
+    shift(shifts, far - 1, far - 1 + edge)
+    lay(grad, lead, left[share : 2 * share, :HALO])
+    lay(grad, lead + halo, cotangent[...])
+    lay(grad, lead + halo + sites // LANES, right[share : 2 * share, :HALO])
 
     def finish(before, start, at):
         rows = pl.ds(at, ROWS)
-        previous = pl.multiple_of(jnp.maximum(start - WIDTH, 0) + HALO, 128)
-        there = pl.ds(pl.multiple_of(start - WIDTH + lead, 128), WIDTH)
         value = hidden[before, rows, :]
         sigma = 0.5 * jnp.tanh(0.5 * value) + 0.5
-        features = own[4, rows, pl.ds(previous, WIDTH)]
-        kept[rows, pl.ds(start, WIDTH)] = (features.astype(F32) + value * sigma).astype(BF16)
-        grad[rows, there] = (
-            grad[rows, there].astype(F32) * sigma * (1.0 + value * (1.0 - sigma))
+        features = wide(own.at[4], jnp.maximum(start - TILES, 0) + halo, TILES, rows)
+        kept[rows, pl.ds(pl.multiple_of(start * LANES, LANES), WIDTH)] = (
+            features.astype(F32) + value * sigma
         ).astype(BF16)
-        window = grad[rows, pl.ds(start, WIDTH + 256)]
-        spread(window, grads, rows, pl.ds(start, WIDTH))
+        there = start - TILES + lead
+        ready = (
+            wide(grad, there, TILES, rows).astype(F32) * sigma * (1.0 + value * (1.0 - sigma))
+        ).astype(BF16)
+        lay(grad, there, ready, rows)
+        spread(wide(grad, start, TILES + 2, rows), grads, rows, start)
 
     def finishes(before, start):
         return [functools.partial(finish, before, start, at) for at in range(0, share, ROWS)]
 
     def block(j, carry):
-        start = pl.multiple_of(j * WIDTH, 128)
-        hidden[j % 2] = begun[:, pl.ds(start, WIDTH)] + product(
+        start = j * TILES
+        here = pl.ds(pl.multiple_of(j * WIDTH, LANES), WIDTH)
+        hidden[j % 2] = begun[:, here] + product(
             weights,
             shifts,
             valid,
-            start + HALO,
+            start + halo,
             start,
-            WIDTH,
             lambda tap: tap,
             [lambda: None, *finishes((j + 1) % 2, start)],
         )
@@ -293,25 +305,24 @@
 
     count = begun.shape[1] // WIDTH
     lax.fori_loop(0, count, block, 0)
-    for piece in finishes((count + 1) % 2, count * WIDTH):
+    for piece in finishes((count + 1) % 2, count * TILES):
         piece()
     output[...] = kept[:, WIDTH + HALO : WIDTH + HALO + sites]
 
 
 def weight_body(half, brick, chan, rep, across, valid_in, grads_in, kept, sent, valid, grads, total):
     del valid_in, grads_in
-    share, sites = grads.shape[1], across.shape[0]
+    share, sites = grads.shape[2], across.shape[0]
+    halo, lead = HALO // LANES, LEAD // LANES
     total[...] = jnp.zeros_like(total)
 
     def block(j, carry):
-        start = pl.multiple_of(j * WIDTH, 128)
-        features = across[pl.ds(start, WIDTH), :]
+        start = j * TILES + halo
+        features = across[pl.ds(pl.multiple_of(j * WIDTH, LANES), WIDTH), :]
         for group in groups(MANY):
             rows = []
             for tap in group:
-                rows += masked(
-                    grads, valid, TAPS - 1 - tap, start + HALO + LEAD, start + HALO, WIDTH
-                )
+                rows += masked(grads, valid, TAPS - 1 - tap, start + lead, start)
             total[group[0] * share : (group[-1] + 1) * share, :] += jnp.dot(
                 jnp.concatenate(rows, axis=0), features, preferred_element_type=F32
             )
@@ -326,25 +337,20 @@
 def feature_body(part, weights, valid, grads, *refs):
     own, rest = refs[-2:]
     share, sites = own.shape
-    begin = part * sites // 2
+    blocks = sites // 2 // WIDTH
 
     def block(j, carry):
-        start = pl.multiple_of(begin + j * WIDTH, 128)
-        here = pl.ds(start, WIDTH)
+        at = part * blocks + j
+        here = pl.ds(pl.multiple_of(at * WIDTH, LANES), WIDTH)
+        start = at * TILES + HALO // LANES
         total = product(
-            weights,
-            grads,
-            valid,
-            start + HALO + LEAD,
-            start + HALO,
-            WIDTH,
-            lambda tap: TAPS - 1 - tap,
+            weights, grads, valid, start + LEAD // LANES, start, lambda tap: TAPS - 1 - tap
         )
         own[:, here] = total[:share]
         rest[:, here] = total[share:].astype(BF16)
         return carry
 
-    lax.fori_loop(0, sites // 2 // WIDTH, block, 0)
+    lax.fori_loop(0, blocks, block, 0)
 
 
 def split_body(brick, chan, rep, kept, arrived, mine, sent):
@@ -429,8 +435,8 @@
             shape((share, TAPS * share)),
             shape((share, TAPS * left)),
             shape((total, lanes)),
-            shape((9, share, sites + 2 * FAR)),
-            shape((TAPS, ROWS, margin)),
+            shape((9, (sites + 2 * FAR) // LANES, share, LANES)),
+            shape((TAPS, margin // LANES, ROWS, LANES)),
         ],
         [jnp.transpose(conv_weight, (0, 2, 1)), features, neighbours],
         scalars=place,
@@ -438,6 +444,7 @@
             pltpu.VMEM((lanes, total), BF16),
             pltpu.VMEM((TAPS, sites), F32),
             pltpu.VMEM((TAPS, share, total), BF16),
+            pltpu.VMEM((share, sites), BF16),
             pltpu.VMEM((TAPS, sites), jnp.int32),
             pltpu.SemaphoreType.DMA((3,)),
         ],
@@ -462,7 +469,7 @@
     rest_shifts, across, own_shifts = kernel(
         arrive_body,
         "arrive",
-        [shape((9, left, sites + 2 * FAR)), shape((sites, total)), shape(own_shifts.shape)],
+        [shape((9, (sites + 2 * FAR) // LANES, left, LANES)), shape((sites, total)), shape(own_shifts.shape)],
         [rest, own_shifts],
         aliases={1: 2},
     )
@@ -471,13 +478,13 @@
         "forward_rest",
         [
             shape((share, sites)),
-            shape((9, share, margin + WIDTH)),
+            shape((9, (margin + WIDTH) // LANES, share, LANES)),
             shape(valid.shape),
             shape(rest_shifts.shape),
         ],
         [ends, rest_shifts, rest_weights, valid, begun, before, behind, own_shifts, cotangent],
         scratch=[
-            pltpu.VMEM((share, LEAD + 128 + margin), BF16),
+            pltpu.VMEM(((LEAD + LANES + margin) // LANES, share, LANES), BF16),
             pltpu.VMEM((share, WIDTH + margin), BF16),
             pltpu.VMEM((2, share, WIDTH), F32),
         ],

time: 57.1 us -> 56.5 us (0.989)
  Pallas kernels: 30.1 us -> 29.4 us
    pallas_call x15, Pallas kernels: 30.1 us -> 29.4 us  [kernel(): pl.pallas_call(body, out_shape=outs, in_specs=[SCALAR] * len(scalars) + [...]
where the time goes in v10:
time: 56.5 us; the launch traced here: 56.3 us
  Pallas kernels  29.4 us (52%)
  waiting for transfers between devices  15.1 us (27%)
  starting transfers between devices  11 us (19%)
  between operations  0.77 us (1%)
    pallas_call x15, Pallas kernels, kernel(): pl.pallas_call(body, out_shape=outs, in_specs=[SCALAR] * len(scalars) + [...  29.4 us
    ppermute x1, waiting for transfers between devices, local(): other = lax.ppermute(mine, 'brick', [(i, i ^ step) for i in range(bricks)])  5.48 us
    ppermute x2, waiting for transfers between devices, around(): lax.ppermute(x, 'chan', [((i + over) % chans, i) for i in range(chans)])  4.59 us
    ppermute x1, waiting for transfers between devices, local(): other = lax.ppermute(mine, 'brick', pairs)  4.07 us
    ppermute x2, starting transfers between devices, around(): lax.ppermute(x, 'chan', [((i + over) % chans, i) for i in range(chans)])  3.1 us
    ppermute x1, starting transfers between devices, local(): other = lax.ppermute(mine, 'brick', [(i, i ^ step) for i in range(bricks)])  2.82 us
    ppermute x1, starting transfers between devices, local(): arrived = lax.ppermute(sent, 'brick', pairs)  1.89 us
    ppermute x1, starting transfers between devices, local(): lax.ppermute(other if left == share else other[(over - 1) * share:over *...  1.55 us
  transfers between devices with their start and end apart: 10, of which 7 were waited for; matrix products, arithmetic and copies ran while one was open for 0% of the time, Pallas kernels for 29%

profile of v10, /device:TPU:0, one launch (start us, length us, event | category | flops | bytes accessed | tf_op | source)
XLA Modules:
  0.0 56.3 jit_solution(7821025877957084961)
XLA Ops:
  0.6 3.0 %collective-permute-start.3 = (bf16[64,4608]{1,0:T(8,128)(2,1)}, bf16[64,4608]{1,0:T(8,128)(2,1)S(1)}, u32[]{:S(2)}, u32[]{:S(2)}) collective-permute-start(bf16[64,4608]{1,0:T(8,128)(2,1)} %features.3), channel_id=1, source_target_pairs={{2,0},{0,2},{3,1},{1,3},{6,4},{4,6},{7,5},{5,7},{10,8},{8,10},{11,... | collective-permute-start | bytes 1769480 | tf_op jit(solution)/shard_map/ppermute | solution.py:409
  3.6 1.1 %pack.1 = (bf16[128,768]{1,0:T(8,128)(2,1)S(1)}, bf16[128,768]{1,0:T(8,128)(2,1)S(1)}) custom-call(s32[1]{0:T(128)} %bitcast.brick.refs_0_, s32[1]{0:T(128)} %bitcast.1.chan.refs_1_, s32[1]{0:T(128)} %bitcast.2.rep.refs_2_, bf16[64,4608]{1,0:T(8,128)(2,1)} %features.3, bf16[64,4608]{1,0:T(8,128)(2,1)} %cotangent.5, s32[27,4608]{1,0:T(8,128)} %neighbours.3), custom_call_target="tpu_custom_call" | custom-call | bytes 1048576 | tf_op jit(solution)/shard_map/pack/pallas_call | solution.py:39
  4.7 0.1 collective-permute-start
  4.8 0.7 %collective-permute-start.1 = (bf16[128,768]{1,0:T(8,128)(2,1)S(1)}, bf16[128,768]{1,0:T(8,128)(2,1)S(1)}, u32[]{:S(2)}, u32[]{:S(2)}) collective-permute-start(bf16[128,768]{1,0:T(8,128)(2,1)S(1)} %get-tuple-element.38), channel_id=1, source_target_pairs={{1,4},{4,1},{5,8},{8,5},{9,12},{12,9},{3,6},{6,3},{7,10},{10,7},{1... | collective-permute-start | bytes 589832 | tf_op jit(solution)/shard_map/ppermute | solution.py:395
  5.5 3.6 %prepare.1 = (bf16[64,1728]{1,0:T(8,128)(2,1)S(1)}, bf16[64,1728]{1,0:T(8,128)(2,1)S(1)}, bf16[128,1792]{1,0:T(8,128)(2,1)S(1)}, bf16[9,48,64,128]{3,2,1,0:T(8,128)(2,1)S(1)}, bf16[27,42,16,128]{3,2,1,0:T(8,128)(2,1)S(1)}) custom-call(s32[1]{0:T(128)} %bitcast.brick.refs_0_, s32[1]{0:T(128)} %bitcast.1.chan.refs_1_, s32[1]{0:T(128)} %bitcast.2.rep.refs_2_, ...), custom_call_target="tpu_custom_call" | custom-call | bytes 1048576 | tf_op jit(solution)/shard_map/prepare/pallas_call | solution.py:39
  9.1 0.0 collective-permute-done.refs_4_
  9.1 0.0 collective-permute-done.1.refs_5_
  9.1 0.1 ends.1
  9.2 0.1 collective-permute-start.2
  9.3 4.8 %forward_own.1 = (f32[64,5376]{1,0:T(8,128)S(1)}, bf16[9,48,64,128]{3,2,1,0:T(8,128)(2,1)S(1)}, bf16[27,42,16,128]{3,2,1,0:T(8,128)(2,1)S(1)}) custom-call(bf16[128,768]{1,0:T(8,128)(2,1)S(1)} %get-tuple-element.40.left, bf16[128,768]{1,0:T(8,128)(2,1)S(1)} %get-tuple-element.41.right, ...), custom_call_target="tpu_custom_call", output_to_operand_aliasing={{1}: (3, {}), {2}: (4, {})} | custom-call | bytes 1048576 | tf_op jit(solution)/shard_map/forward_own/pallas_call | solution.py:39
  14.1 0.0 copy-start
  14.1 3.9 %collective-permute-done.3.rest = bf16[64,4608]{1,0:T(8,128)(2,1)S(1)} collective-permute-done((bf16[64,4608]{1,0:T(8,128)(2,1)}, bf16[64,4608]{1,0:T(8,128)(2,1)S(1)}, u32[]{:S(2)}, u32[]{:S(2)}) %collective-permute-start.3) | collective-permute-done | bytes 589856 | tf_op jit(solution)/shard_map/ppermute | solution.py:409
  18.0 2.0 %arrive.1 = (bf16[9,48,64,128]{3,2,1,0:T(8,128)(2,1)S(1)}, bf16[4608,128]{1,0:T(8,128)(2,1)S(1)}, bf16[9,48,64,128]{3,2,1,0:T(8,128)(2,1)S(1)}) custom-call(bf16[64,4608]{1,0:T(8,128)(2,1)S(1)} %collective-permute-done.3.rest, bf16[9,48,64,128]{3,2,1,0:T(8,128)(2,1)S(1)} %get-tuple-element.44.own_in), custom_call_target="tpu_custom_call", output_to_operand_aliasing={{2}: (1, {})} | custom-call | bytes 1048576 | tf_op jit(solution)/shard_map/arrive/pallas_call | solution.py:39
  20.0 0.7 %collective-permute-done.2.ends = bf16[64,1280]{1,0:T(8,128)(2,1)S(1)} collective-permute-done((bf16[64,1280]{1,0:T(8,128)(2,1)S(1)}, bf16[64,1280]{1,0:T(8,128)(2,1)S(1)}, u32[]{:S(2)}, u32[]{:S(2)}) %collective-permute-start.2) | collective-permute-done | bytes 163872 | tf_op jit(solution)/shard_map/ppermute | solution.py:409
  20.7 0.0 copy-done
  20.7 6.6 %forward_rest.1 = (bf16[64,4608]{1,0:T(8,128)(2,1)}, bf16[9,48,64,128]{3,2,1,0:T(8,128)(2,1)S(1)}, bf16[27,42,16,128]{3,2,1,0:T(8,128)(2,1)S(1)}, bf16[9,48,64,128]{3,2,1,0:T(8,128)(2,1)S(1)}) custom-call(bf16[64,1280]{1,0:T(8,128)(2,1)S(1)} %collective-permute-done.2.ends, ...), custom_call_target="tpu_custom_call", output_to_operand_aliasing={{3}: (1, {}), {2}: (3, {})} | custom-call | flops 1019215872 | bytes 1048576 | tf_op jit(solution)/shard_map/forward_rest/pallas_call | solution.py:39
  27.3 5.5 %grad_weight.1 = (f32[896,128]{1,0:T(8,128)S(1)}, bf16[896,128]{1,0:T(8,128)(2,1)S(1)}, bf16[27,42,16,128]{3,2,1,0:T(8,128)(2,1)S(1)}, bf16[9,48,64,128]{3,2,1,0:T(8,128)(2,1)S(1)}) custom-call(s32[1]{0:T(128)} %bitcast.brick.refs_0_, s32[1]{0:T(128)} %bitcast.1.chan.refs_1_, s32[1]{0:T(128)} %bitcast.2.rep.refs_2_, ...), custom_call_target="tpu_custom_call", output_to_operand_aliasing={{2}: (4, {}), {3}: (5, {})} | custom-call | flops 2038431744 | bytes 1048576 | tf_op jit(solution)/shard_map/grad_weight/pallas_call | solution.py:39
  32.8 0.1 collective-permute-start.4
  32.9 1.7 %grad_features_0.1 = (bf16[27,42,16,128]{3,2,1,0:T(8,128)(2,1)S(1)}, bf16[9,48,64,128]{3,2,1,0:T(8,128)(2,1)S(1)}, f32[64,4608]{1,0:T(8,128)S(1)}, bf16[64,4608]{1,0:T(8,128)(2,1)S(1)}) custom-call(bf16[128,1792]{1,0:T(8,128)(2,1)S(1)} %get-tuple-element.51.weights.refs_1_, ...), custom_call_target="tpu_custom_call", output_to_operand_aliasing={{0}: (1, {}), {1}: (2, {})} | custom-call | flops 1019215872 | bytes 1048576 | tf_op jit(solution)/shard_map/grad_features_0/pallas_call | solution.py:39
  34.6 0.0 collective-permute-done.4.refs_5_
  34.6 0.1 split.1
  34.7 1.9 %collective-permute-start.6 = (bf16[448,128]{1,0:T(8,128)(2,1)S(1)}, bf16[448,128]{1,0:T(8,128)(2,1)S(1)}, u32[]{:S(2)}, u32[]{:S(2)}) collective-permute-start(bf16[448,128]{1,0:T(8,128)(2,1)S(1)} %get-tuple-element.68), channel_id=1, source_target_pairs={{0,4},{4,0},{8,12},{12,8},{1,5},{5,1},{9,13},{13,9},{2,6},{6,2},{1... | collective-permute-start | bytes 344072 | tf_op jit(solution)/shard_map/ppermute | solution.py:535
  36.6 1.7 %grad_features_1.1 = (f32[64,4608]{1,0:T(8,128)S(1)}, bf16[64,4608]{1,0:T(8,128)(2,1)S(1)}) custom-call(f32[448,128]{1,0:T(8,128)S(1)} %get-tuple-element.60.refs_0_.refs_1_, bf16[128,1792]{1,0:T(8,128)(2,1)S(1)} %get-tuple-element.51.weights.refs_1_, ...), custom_call_target="tpu_custom_call", output_to_operand_aliasing={{0}: (4, {}), {1}: (5, {})} | custom-call | flops 1019215872 | bytes 1048576 | tf_op jit(solution)/shard_map/grad_features_1/pallas_call | solution.py:39
  38.3 1.6 %collective-permute-start.5 = (bf16[64,4608]{1,0:T(8,128)(2,1)S(1)}, bf16[64,4608]{1,0:T(8,128)(2,1)S(1)}, u32[]{:S(2)}, u32[]{:S(2)}) collective-permute-start(bf16[64,4608]{1,0:T(8,128)(2,1)S(1)} %get-tuple-element.65), channel_id=1, source_target_pairs={{0,2},{2,0},{1,3},{3,1},{4,6},{6,4},{5,7},{7,5},{8,10},{10,8},{9,1... | collective-permute-start | bytes 1769480 | tf_op jit(solution)/shard_map/ppermute | solution.py:540
  39.8 0.5 collective-permute-done.6.refs_2_
  40.4 2.8 %collective-permute-start.7 = (bf16[448,128]{1,0:T(8,128)(2,1)S(1)}, bf16[448,128]{1,0:T(8,128)(2,1)S(1)}, u32[]{:S(2)}, u32[]{:S(2)}) collective-permute-start(bf16[448,128]{1,0:T(8,128)(2,1)S(1)} %merge_1.1.mine), channel_id=1, source_target_pairs={{0,8},{4,12},{8,0},{12,4},{1,9},{5,13},{9,1},{13,5},{2,10},{6,14},... | collective-permute-start | bytes 344072 | tf_op jit(solution)/shard_map/ppermute | solution.py:556
  43.2 5.5 %collective-permute-done.7.other = bf16[448,128]{1,0:T(8,128)(2,1)S(1)} collective-permute-done((bf16[448,128]{1,0:T(8,128)(2,1)S(1)}, bf16[448,128]{1,0:T(8,128)(2,1)S(1)}, u32[]{:S(2)}, u32[]{:S(2)}) %collective-permute-start.7) | collective-permute-done | bytes 114720 | tf_op jit(solution)/shard_map/ppermute | solution.py:556
  48.8 0.8 %collective-permute-start.8 = (bf16[448,128]{1,0:T(8,128)(2,1)S(1)}, bf16[448,128]{1,0:T(8,128)(2,1)S(1)}, u32[]{:S(2)}, u32[]{:S(2)}) collective-permute-start(bf16[448,128]{1,0:T(8,128)(2,1)S(1)} %merge_4.1.mine), channel_id=1, source_target_pairs={{0,4},{4,0},{8,12},{12,8},{1,5},{5,1},{9,13},{13,9},{2,6},{6,2},{1... | collective-permute-start | bytes 344072 | tf_op jit(solution)/shard_map/ppermute | solution.py:561
  49.5 4.1 %collective-permute-done.8.other = bf16[448,128]{1,0:T(8,128)(2,1)S(1)} collective-permute-done((bf16[448,128]{1,0:T(8,128)(2,1)S(1)}, bf16[448,128]{1,0:T(8,128)(2,1)S(1)}, u32[]{:S(2)}, u32[]{:S(2)}) %collective-permute-start.8) | collective-permute-done | bytes 114720 | tf_op jit(solution)/shard_map/ppermute | solution.py:561
  53.6 0.1 collective-permute-start.9
  53.7 0.1 collective-permute-done.5.rest_0_
  53.8 1.0 %add.1 = (bf16[64,4608]{1,0:T(8,128)(2,1)}, f32[8,128]{1,0:T(8,128)S(1)}) custom-call(bf16[64,4608]{1,0:T(8,128)(2,1)S(1)} %copy-done, f32[64,4608]{1,0:T(8,128)S(1)} %get-tuple-element.64.own.refs_0_, bf16[64,4608]{1,0:T(8,128)(2,1)S(1)} %collective-permute-done.5.rest_0_), custom_call_target="tpu_custom_call" | custom-call | bytes 1048576 | tf_op jit(solution)/shard_map/add/pallas_call | solution.py:39
  54.8 0.4 collective-permute-done.9.refs_5_
  55.2 1.1 %join.1 = f32[1728,128]{1,0:T(8,128)} custom-call(s32[1]{0:T(128)} %bitcast.brick.refs_0_, s32[1]{0:T(128)} %bitcast.1.chan.refs_1_, s32[1]{0:T(128)} %bitcast.2.rep.refs_2_, f32[8,128]{1,0:T(8,128)S(1)} %get-tuple-element.67.refs_3_, bf16[896,128]{1,0:T(8,128)(2,1)S(1)} %gather.1.refs_4_, bf16[896,128]{1,0:T(8,128)(2,1)S(1)} %collective-permute-done.9.refs_5_), custom_call_target="tpu_custom_call" | custom-call | flops 250000000 | bytes 1048576 | tf_op jit(solution)/shard_map/join/pallas_call | solution.py:39
  (3 shorter events, 0.1 us)
Async XLA Ops:
  0.6 17.4 %collective-permute-start.3 = (bf16[64,4608]{1,0:T(8,128)(2,1)}, bf16[64,4608]{1,0:T(8,128)(2,1)S(1)}, u32[]{:S(2)}, u32[]{:S(2)}) collective-permute-start(bf16[64,4608]{1,0:T(8,128)(2,1)} %features.3), channel_id=1, source_target_pairs={{2,0},{0,2},{3,1},{1,3},{6,4},{4,6},{7,5},{5,7},{10,8},{8,10},{11,... | collective-permute-start | bytes 1769480 | tf_op jit(solution)/shard_map/ppermute | solution.py:409
  4.7 4.4 %collective-permute-start = (bf16[128,768]{1,0:T(8,128)(2,1)S(1)}, bf16[128,768]{1,0:T(8,128)(2,1)S(1)}, u32[]{:S(2)}, u32[]{:S(2)}) collective-permute-start(bf16[128,768]{1,0:T(8,128)(2,1)S(1)} %get-tuple-element.37), channel_id=1, source_target_pairs={{0,1},{1,0},{2,3},{3,2},{4,5},{5,4},{6,7},{7,6},{8,9},{9,8},{10,11... | collective-permute-start | bytes 589832 | tf_op jit(solution)/shard_map/ppermute | solution.py:429
  4.8 4.3 %collective-permute-start.1 = (bf16[128,768]{1,0:T(8,128)(2,1)S(1)}, bf16[128,768]{1,0:T(8,128)(2,1)S(1)}, u32[]{:S(2)}, u32[]{:S(2)}) collective-permute-start(bf16[128,768]{1,0:T(8,128)(2,1)S(1)} %get-tuple-element.38), channel_id=1, source_target_pairs={{1,4},{4,1},{5,8},{8,5},{9,12},{12,9},{3,6},{6,3},{7,10},{10,7},{1... | collective-permute-start | bytes 589832 | tf_op jit(solution)/shard_map/ppermute | solution.py:395
  9.2 11.5 %collective-permute-start.2 = (bf16[64,1280]{1,0:T(8,128)(2,1)S(1)}, bf16[64,1280]{1,0:T(8,128)(2,1)S(1)}, u32[]{:S(2)}, u32[]{:S(2)}) collective-permute-start(bf16[64,1280]{1,0:T(8,128)(2,1)S(1)} %get-tuple-element.39), channel_id=1, source_target_pairs={{2,0},{0,2},{3,1},{1,3},{6,4},{4,6},{7,5},{5,7},{10,8},{8,10},{11,... | collective-permute-start | bytes 491528 | tf_op jit(solution)/shard_map/ppermute | solution.py:409
  14.1 6.6 %copy-start = (bf16[64,4608]{1,0:T(8,128)(2,1)S(1)}, bf16[64,4608]{1,0:T(8,128)(2,1)}, u32[]{:S(2)}) copy-start(bf16[64,4608]{1,0:T(8,128)(2,1)} %cotangent.5) | copy-start | bytes 1769476
  32.8 1.8 %collective-permute-start.4 = (bf16[896,128]{1,0:T(8,128)(2,1)S(1)}, bf16[896,128]{1,0:T(8,128)(2,1)S(1)}, u32[]{:S(2)}, u32[]{:S(2)}) collective-permute-start(bf16[896,128]{1,0:T(8,128)(2,1)S(1)} %get-tuple-element.59), channel_id=1, source_target_pairs={{0,1},{1,0},{2,3},{3,2},{4,5},{5,4},{6,7},{7,6},{8,9},{9,8},{10,11... | collective-permute-start | bytes 688136 | tf_op jit(solution)/shard_map/ppermute | solution.py:507
  34.7 5.7 %collective-permute-start.6 = (bf16[448,128]{1,0:T(8,128)(2,1)S(1)}, bf16[448,128]{1,0:T(8,128)(2,1)S(1)}, u32[]{:S(2)}, u32[]{:S(2)}) collective-permute-start(bf16[448,128]{1,0:T(8,128)(2,1)S(1)} %get-tuple-element.68), channel_id=1, source_target_pairs={{0,4},{4,0},{8,12},{12,8},{1,5},{5,1},{9,13},{13,9},{2,6},{6,2},{1... | collective-permute-start | bytes 344072 | tf_op jit(solution)/shard_map/ppermute | solution.py:535
  38.3 15.5 %collective-permute-start.5 = (bf16[64,4608]{1,0:T(8,128)(2,1)S(1)}, bf16[64,4608]{1,0:T(8,128)(2,1)S(1)}, u32[]{:S(2)}, u32[]{:S(2)}) collective-permute-start(bf16[64,4608]{1,0:T(8,128)(2,1)S(1)} %get-tuple-element.65), channel_id=1, source_target_pairs={{0,2},{2,0},{1,3},{3,1},{4,6},{6,4},{5,7},{7,5},{8,10},{10,8},{9,1... | collective-permute-start | bytes 1769480 | tf_op jit(solution)/shard_map/ppermute | solution.py:540
  40.4 8.3 %collective-permute-start.7 = (bf16[448,128]{1,0:T(8,128)(2,1)S(1)}, bf16[448,128]{1,0:T(8,128)(2,1)S(1)}, u32[]{:S(2)}, u32[]{:S(2)}) collective-permute-start(bf16[448,128]{1,0:T(8,128)(2,1)S(1)} %merge_1.1.mine), channel_id=1, source_target_pairs={{0,8},{4,12},{8,0},{12,4},{1,9},{5,13},{9,1},{13,5},{2,10},{6,14},... | collective-permute-start | bytes 344072 | tf_op jit(solution)/shard_map/ppermute | solution.py:556
  48.8 4.9 %collective-permute-start.8 = (bf16[448,128]{1,0:T(8,128)(2,1)S(1)}, bf16[448,128]{1,0:T(8,128)(2,1)S(1)}, u32[]{:S(2)}, u32[]{:S(2)}) collective-permute-start(bf16[448,128]{1,0:T(8,128)(2,1)S(1)} %merge_4.1.mine), channel_id=1, source_target_pairs={{0,4},{4,0},{8,12},{12,8},{1,5},{5,1},{9,13},{13,9},{2,6},{6,2},{1... | collective-permute-start | bytes 344072 | tf_op jit(solution)/shard_map/ppermute | solution.py:561
  53.6 1.6 %collective-permute-start.9 = (bf16[896,128]{1,0:T(8,128)(2,1)S(1)}, bf16[896,128]{1,0:T(8,128)(2,1)S(1)}, u32[]{:S(2)}, u32[]{:S(2)}) collective-permute-start(bf16[896,128]{1,0:T(8,128)(2,1)S(1)} %gather.1.refs_4_), channel_id=1, source_target_pairs={{0,1},{1,0},{2,3},{3,2},{4,5},{5,4},{6,7},{7,6},{8,9},{9,8},{10,11... | collective-permute-start | bytes 688136 | tf_op jit(solution)/shard_map/ppermute | solution.py:565

commit v11 on v10

--- a/solution.py
+++ b/solution.py
@@ -15,9 +15,10 @@
 NEAR = 640
 LEAD = 896
 MANY = 14
+DEEP = 18
 ROWS = 16
 LANES = 128
-GROUP = 4
+GROUP = 8
 TILES = 6
 WIDTH = TILES * LANES
 LATER = 25 * 10**7
@@ -82,11 +83,11 @@
         spread(wide(shifts.at[4], low - 1, high - low + 2, rows), shifts, rows, low)
 
 
-def masked(shifts, valid, tap, at_shift, at_valid):
-    keep = wide(valid.at[tap], at_valid, TILES)
+def masked(shifts, valid, tap, at_shift, at_valid, tiles=TILES):
+    keep = wide(valid.at[tap], at_valid, tiles)
     begin = at_shift + (tap // 9 - 1) * FACE // LANES
     return [
-        wide(shifts.at[tap % 9], begin, TILES, pl.ds(at, ROWS)) * keep
+        wide(shifts.at[tap % 9], begin, tiles, pl.ds(at, ROWS)) * keep
         for at in range(0, shifts.shape[2], ROWS)
     ]
 
@@ -95,11 +96,13 @@
     return [range(first, min(first + count, TAPS)) for first in range(0, TAPS, count)]
 
 
-def product(weights, shifts, valid, at_shift, at_valid, taps_of, between=()):
+def product(
+    weights, shifts, valid, at_shift, at_valid, taps_of, between=(), count=GROUP
+):
     channels = shifts.shape[2]
     total = None
-    for at, group in enumerate(groups()):
-        for piece in between[at :: len(groups())]:
+    for at, group in enumerate(groups(count)):
+        for piece in between[at :: len(groups(count))]:
             piece()
         rows = []
         for tap in group:
@@ -299,7 +302,7 @@
             start + halo,
             start,
             lambda tap: tap,
-            [lambda: None, *finishes((j + 1) % 2, start)],
+            finishes((j + 1) % 2, start),
         )
         return carry
 
@@ -317,18 +320,19 @@
     total[...] = jnp.zeros_like(total)
 
     def block(j, carry):
-        start = j * TILES + halo
-        features = across[pl.ds(pl.multiple_of(j * WIDTH, LANES), WIDTH), :]
+        start = j * DEEP + halo
+        here = pl.ds(pl.multiple_of(j * DEEP * LANES, LANES), DEEP * LANES)
+        features = across[here, :]
         for group in groups(MANY):
             rows = []
             for tap in group:
-                rows += masked(grads, valid, TAPS - 1 - tap, start + lead, start)
+                rows += masked(grads, valid, TAPS - 1 - tap, start + lead, start, DEEP)
             total[group[0] * share : (group[-1] + 1) * share, :] += jnp.dot(
                 jnp.concatenate(rows, axis=0), features, preferred_element_type=F32
             )
         return carry
 
-    lax.fori_loop(0, sites // WIDTH, block, 0)
+    lax.fori_loop(0, sites // (DEEP * LANES), block, 0)
     mine = rep[0]
     kept[...] = total[pl.ds(pl.multiple_of(mine * half, ROWS), half), :]
     sent[...] = total[pl.ds(pl.multiple_of((1 - mine) * half, ROWS), half), :].astype(BF16)
@@ -344,7 +348,13 @@
         here = pl.ds(pl.multiple_of(at * WIDTH, LANES), WIDTH)
         start = at * TILES + HALO // LANES
         total = product(
-            weights, grads, valid, start + LEAD // LANES, start, lambda tap: TAPS - 1 - tap
+            weights,
+            grads,
+            valid,
+            start + LEAD // LANES,
+            start,
+            lambda tap: TAPS - 1 - tap,
+            count=TAPS if part else GROUP,
         )
         own[:, here] = total[:share]
         rest[:, here] = total[share:].astype(BF16)
@@ -492,8 +502,8 @@
         flops=flops * left,
     )
 
-    piece = -(-TAPS * share // (reps * bricks * ROWS)) * ROWS
-    half = piece * bricks
+    size = -(-TAPS * share // (reps * 2 * ROWS)) * ROWS
+    half = 2 * size
     kept, sent, valid, grads = kernel(
         functools.partial(weight_body, half),
         "grad_weight",
@@ -522,7 +532,6 @@
     valid, grads, *parts = feature_part(
         0, functools.partial(feature_body, 0), [by_in, valid, grads], [valid, grads]
     )
-    size = half // 2
     mine, sent = kernel(
         after(split_body, 3),
         "split",

time: 56.5 us -> 55.4 us (0.981)
  Pallas kernels: 29.4 us -> 28.6 us
    pallas_call x15, Pallas kernels: 29.4 us -> 28.6 us  [kernel(): pl.pallas_call(body, out_shape=outs, in_specs=[SCALAR] * len(scalars) + [...]
  transfers between devices with their start and end apart: 10 -> 10, of which waited for: 7 -> 6; matrix products, arithmetic and copies ran while one was open for 0% -> 0% of each run, Pallas kernels for 29% -> 29%
where the time goes in v11:
time: 55.4 us; the launch traced here: 55.3 us
  Pallas kernels  28.6 us (52%)
  waiting for transfers between devices  14.9 us (27%)
  starting transfers between devices  11 us (20%)
  between operations  0.77 us (1%)
    pallas_call x15, Pallas kernels, kernel(): pl.pallas_call(body, out_shape=outs, in_specs=[SCALAR] * len(scalars) + [...  28.6 us
    ppermute x1, waiting for transfers between devices, local(): other = lax.ppermute(mine, 'brick', [(i, i ^ step) for i in range(bricks)])  5.31 us
    ppermute x2, waiting for transfers between devices, around(): lax.ppermute(x, 'chan', [((i + over) % chans, i) for i in range(chans)])  4.71 us
    ppermute x1, waiting for transfers between devices, local(): other = lax.ppermute(mine, 'brick', pairs)  4.03 us
    ppermute x2, starting transfers between devices, around(): lax.ppermute(x, 'chan', [((i + over) % chans, i) for i in range(chans)])  3.1 us
    ppermute x1, starting transfers between devices, local(): other = lax.ppermute(mine, 'brick', [(i, i ^ step) for i in range(bricks)])  2.82 us
    ppermute x1, starting transfers between devices, local(): arrived = lax.ppermute(sent, 'brick', pairs)  1.88 us
    ppermute x1, starting transfers between devices, local(): lax.ppermute(other if left == share else other[(over - 1) * share:over *...  1.55 us
  transfers between devices with their start and end apart: 10, of which 6 were waited for; matrix products, arithmetic and copies ran while one was open for 0% of the time, Pallas kernels for 29%

profile of v11, /device:TPU:0, one launch (start us, length us, event | category | flops | bytes accessed | tf_op | source)
XLA Modules:
  0.0 55.3 jit_solution(8701549588805949091)
XLA Ops:
  0.6 3.0 %collective-permute-start.3 = (bf16[64,4608]{1,0:T(8,128)(2,1)}, bf16[64,4608]{1,0:T(8,128)(2,1)S(1)}, u32[]{:S(2)}, u32[]{:S(2)}) collective-permute-start(bf16[64,4608]{1,0:T(8,128)(2,1)} %features.3), channel_id=1, source_target_pairs={{2,0},{0,2},{3,1},{1,3},{6,4},{4,6},{7,5},{5,7},{10,8},{8,10},{11,... | collective-permute-start | bytes 1769480 | tf_op jit(solution)/shard_map/ppermute | solution.py:419
  3.6 1.1 %pack.1 = (bf16[128,768]{1,0:T(8,128)(2,1)S(1)}, bf16[128,768]{1,0:T(8,128)(2,1)S(1)}) custom-call(s32[1]{0:T(128)} %bitcast.brick.refs_0_, s32[1]{0:T(128)} %bitcast.1.chan.refs_1_, s32[1]{0:T(128)} %bitcast.2.rep.refs_2_, bf16[64,4608]{1,0:T(8,128)(2,1)} %features.3, bf16[64,4608]{1,0:T(8,128)(2,1)} %cotangent.5, s32[27,4608]{1,0:T(8,128)} %neighbours.3), custom_call_target="tpu_custom_call" | custom-call | bytes 1048576 | tf_op jit(solution)/shard_map/pack/pallas_call | solution.py:40
  4.7 0.1 collective-permute-start
  4.8 0.7 %collective-permute-start.1 = (bf16[128,768]{1,0:T(8,128)(2,1)S(1)}, bf16[128,768]{1,0:T(8,128)(2,1)S(1)}, u32[]{:S(2)}, u32[]{:S(2)}) collective-permute-start(bf16[128,768]{1,0:T(8,128)(2,1)S(1)} %get-tuple-element.38), channel_id=1, source_target_pairs={{1,4},{4,1},{5,8},{8,5},{9,12},{12,9},{3,6},{6,3},{7,10},{10,7},{1... | collective-permute-start | bytes 589832 | tf_op jit(solution)/shard_map/ppermute | solution.py:405
  5.5 3.5 %prepare.1 = (bf16[64,1728]{1,0:T(8,128)(2,1)S(1)}, bf16[64,1728]{1,0:T(8,128)(2,1)S(1)}, bf16[128,1792]{1,0:T(8,128)(2,1)S(1)}, bf16[9,48,64,128]{3,2,1,0:T(8,128)(2,1)S(1)}, bf16[27,42,16,128]{3,2,1,0:T(8,128)(2,1)S(1)}) custom-call(s32[1]{0:T(128)} %bitcast.brick.refs_0_, s32[1]{0:T(128)} %bitcast.1.chan.refs_1_, s32[1]{0:T(128)} %bitcast.2.rep.refs_2_, ...), custom_call_target="tpu_custom_call" | custom-call | bytes 1048576 | tf_op jit(solution)/shard_map/prepare/pallas_call | solution.py:40
  9.0 0.0 collective-permute-done.refs_4_
  9.0 0.0 collective-permute-done.1.refs_5_
  9.0 0.1 ends.1
  9.1 0.1 collective-permute-start.2
  9.2 4.8 %forward_own.1 = (f32[64,5376]{1,0:T(8,128)S(1)}, bf16[9,48,64,128]{3,2,1,0:T(8,128)(2,1)S(1)}, bf16[27,42,16,128]{3,2,1,0:T(8,128)(2,1)S(1)}) custom-call(bf16[128,768]{1,0:T(8,128)(2,1)S(1)} %get-tuple-element.40.left, bf16[128,768]{1,0:T(8,128)(2,1)S(1)} %get-tuple-element.41.right, ...), custom_call_target="tpu_custom_call", output_to_operand_aliasing={{1}: (3, {}), {2}: (4, {})} | custom-call | bytes 1048576 | tf_op jit(solution)/shard_map/forward_own/pallas_call | solution.py:40
  14.0 0.0 copy-start
  14.0 4.0 %collective-permute-done.3.rest = bf16[64,4608]{1,0:T(8,128)(2,1)S(1)} collective-permute-done((bf16[64,4608]{1,0:T(8,128)(2,1)}, bf16[64,4608]{1,0:T(8,128)(2,1)S(1)}, u32[]{:S(2)}, u32[]{:S(2)}) %collective-permute-start.3) | collective-permute-done | bytes 589856 | tf_op jit(solution)/shard_map/ppermute | solution.py:419
  18.0 2.0 %arrive.1 = (bf16[9,48,64,128]{3,2,1,0:T(8,128)(2,1)S(1)}, bf16[4608,128]{1,0:T(8,128)(2,1)S(1)}, bf16[9,48,64,128]{3,2,1,0:T(8,128)(2,1)S(1)}) custom-call(bf16[64,4608]{1,0:T(8,128)(2,1)S(1)} %collective-permute-done.3.rest, bf16[9,48,64,128]{3,2,1,0:T(8,128)(2,1)S(1)} %get-tuple-element.44.own_in), custom_call_target="tpu_custom_call", output_to_operand_aliasing={{2}: (1, {})} | custom-call | bytes 1048576 | tf_op jit(solution)/shard_map/arrive/pallas_call | solution.py:40
  20.0 0.7 %collective-permute-done.2.ends = bf16[64,1280]{1,0:T(8,128)(2,1)S(1)} collective-permute-done((bf16[64,1280]{1,0:T(8,128)(2,1)S(1)}, bf16[64,1280]{1,0:T(8,128)(2,1)S(1)}, u32[]{:S(2)}, u32[]{:S(2)}) %collective-permute-start.2) | collective-permute-done | bytes 163872 | tf_op jit(solution)/shard_map/ppermute | solution.py:419
  20.7 0.0 copy-done
  20.7 6.7 %forward_rest.1 = (bf16[64,4608]{1,0:T(8,128)(2,1)}, bf16[9,48,64,128]{3,2,1,0:T(8,128)(2,1)S(1)}, bf16[27,42,16,128]{3,2,1,0:T(8,128)(2,1)S(1)}, bf16[9,48,64,128]{3,2,1,0:T(8,128)(2,1)S(1)}) custom-call(bf16[64,1280]{1,0:T(8,128)(2,1)S(1)} %collective-permute-done.2.ends, ...), custom_call_target="tpu_custom_call", output_to_operand_aliasing={{3}: (1, {}), {2}: (3, {})} | custom-call | flops 1019215872 | bytes 1048576 | tf_op jit(solution)/shard_map/forward_rest/pallas_call | solution.py:40
  27.4 4.7 %grad_weight.1 = (f32[864,128]{1,0:T(8,128)S(1)}, bf16[864,128]{1,0:T(8,128)(2,1)S(1)}, bf16[27,42,16,128]{3,2,1,0:T(8,128)(2,1)S(1)}, bf16[9,48,64,128]{3,2,1,0:T(8,128)(2,1)S(1)}) custom-call(s32[1]{0:T(128)} %bitcast.brick.refs_0_, s32[1]{0:T(128)} %bitcast.1.chan.refs_1_, s32[1]{0:T(128)} %bitcast.2.rep.refs_2_, ...), custom_call_target="tpu_custom_call", output_to_operand_aliasing={{2}: (4, {}), {3}: (5, {})} | custom-call | flops 2038431744 | bytes 1048576 | tf_op jit(solution)/shard_map/grad_weight/pallas_call | solution.py:40
  32.1 0.1 collective-permute-start.4
  32.2 1.7 %grad_features_0.1 = (bf16[27,42,16,128]{3,2,1,0:T(8,128)(2,1)S(1)}, bf16[9,48,64,128]{3,2,1,0:T(8,128)(2,1)S(1)}, f32[64,4608]{1,0:T(8,128)S(1)}, bf16[64,4608]{1,0:T(8,128)(2,1)S(1)}) custom-call(bf16[128,1792]{1,0:T(8,128)(2,1)S(1)} %get-tuple-element.51.weights.refs_1_, ...), custom_call_target="tpu_custom_call", output_to_operand_aliasing={{0}: (1, {}), {1}: (2, {})} | custom-call | flops 1019215872 | bytes 1048576 | tf_op jit(solution)/shard_map/grad_features_0/pallas_call | solution.py:40
  33.9 0.0 collective-permute-done.4.refs_5_
  33.9 0.1 split.1
  34.0 1.9 %collective-permute-start.6 = (bf16[432,128]{1,0:T(8,128)(2,1)S(1)}, bf16[432,128]{1,0:T(8,128)(2,1)S(1)}, u32[]{:S(2)}, u32[]{:S(2)}) collective-permute-start(bf16[432,128]{1,0:T(8,128)(2,1)S(1)} %get-tuple-element.68), channel_id=1, source_target_pairs={{0,4},{4,0},{8,12},{12,8},{1,5},{5,1},{9,13},{13,9},{2,6},{6,2},{1... | collective-permute-start | bytes 331784 | tf_op jit(solution)/shard_map/ppermute | solution.py:544
  35.8 1.7 %grad_features_1.1 = (f32[64,4608]{1,0:T(8,128)S(1)}, bf16[64,4608]{1,0:T(8,128)(2,1)S(1)}) custom-call(f32[432,128]{1,0:T(8,128)S(1)} %get-tuple-element.60.refs_0_.refs_1_, bf16[128,1792]{1,0:T(8,128)(2,1)S(1)} %get-tuple-element.51.weights.refs_1_, ...), custom_call_target="tpu_custom_call", output_to_operand_aliasing={{0}: (4, {}), {1}: (5, {})} | custom-call | flops 1019215872 | bytes 1048576 | tf_op jit(solution)/shard_map/grad_features_1/pallas_call | solution.py:40
  37.6 1.6 %collective-permute-start.5 = (bf16[64,4608]{1,0:T(8,128)(2,1)S(1)}, bf16[64,4608]{1,0:T(8,128)(2,1)S(1)}, u32[]{:S(2)}, u32[]{:S(2)}) collective-permute-start(bf16[64,4608]{1,0:T(8,128)(2,1)S(1)} %get-tuple-element.65), channel_id=1, source_target_pairs={{0,2},{2,0},{1,3},{3,1},{4,6},{6,4},{5,7},{7,5},{8,10},{10,8},{9,1... | collective-permute-start | bytes 1769480 | tf_op jit(solution)/shard_map/ppermute | solution.py:549
  39.1 0.4 collective-permute-done.6.refs_2_
  39.6 2.8 %collective-permute-start.7 = (bf16[432,128]{1,0:T(8,128)(2,1)S(1)}, bf16[432,128]{1,0:T(8,128)(2,1)S(1)}, u32[]{:S(2)}, u32[]{:S(2)}) collective-permute-start(bf16[432,128]{1,0:T(8,128)(2,1)S(1)} %merge_1.1.mine), channel_id=1, source_target_pairs={{0,8},{4,12},{8,0},{12,4},{1,9},{5,13},{9,1},{13,5},{2,10},{6,14},... | collective-permute-start | bytes 331784 | tf_op jit(solution)/shard_map/ppermute | solution.py:565
  42.4 5.3 %collective-permute-done.7.other = bf16[432,128]{1,0:T(8,128)(2,1)S(1)} collective-permute-done((bf16[432,128]{1,0:T(8,128)(2,1)S(1)}, bf16[432,128]{1,0:T(8,128)(2,1)S(1)}, u32[]{:S(2)}, u32[]{:S(2)}) %collective-permute-start.7) | collective-permute-done | bytes 110624 | tf_op jit(solution)/shard_map/ppermute | solution.py:565
  47.8 0.8 %collective-permute-start.8 = (bf16[432,128]{1,0:T(8,128)(2,1)S(1)}, bf16[432,128]{1,0:T(8,128)(2,1)S(1)}, u32[]{:S(2)}, u32[]{:S(2)}) collective-permute-start(bf16[432,128]{1,0:T(8,128)(2,1)S(1)} %merge_4.1.mine), channel_id=1, source_target_pairs={{0,4},{4,0},{8,12},{12,8},{1,5},{5,1},{9,13},{13,9},{2,6},{6,2},{1... | collective-permute-start | bytes 331784 | tf_op jit(solution)/shard_map/ppermute | solution.py:570
  48.5 4.0 %collective-permute-done.8.other = bf16[432,128]{1,0:T(8,128)(2,1)S(1)} collective-permute-done((bf16[432,128]{1,0:T(8,128)(2,1)S(1)}, bf16[432,128]{1,0:T(8,128)(2,1)S(1)}, u32[]{:S(2)}, u32[]{:S(2)}) %collective-permute-start.8) | collective-permute-done | bytes 110624 | tf_op jit(solution)/shard_map/ppermute | solution.py:570
  52.6 0.1 collective-permute-start.9
  52.7 0.4 collective-permute-done.5.rest_0_
  53.1 1.0 %add.1 = (bf16[64,4608]{1,0:T(8,128)(2,1)}, f32[8,128]{1,0:T(8,128)S(1)}) custom-call(bf16[64,4608]{1,0:T(8,128)(2,1)S(1)} %copy-done, f32[64,4608]{1,0:T(8,128)S(1)} %get-tuple-element.64.own.refs_0_, bf16[64,4608]{1,0:T(8,128)(2,1)S(1)} %collective-permute-done.5.rest_0_), custom_call_target="tpu_custom_call" | custom-call | bytes 1048576 | tf_op jit(solution)/shard_map/add/pallas_call | solution.py:40
  54.1 0.0 collective-permute-done.9.refs_5_
  54.1 1.1 %join.1 = f32[1728,128]{1,0:T(8,128)} custom-call(s32[1]{0:T(128)} %bitcast.brick.refs_0_, s32[1]{0:T(128)} %bitcast.1.chan.refs_1_, s32[1]{0:T(128)} %bitcast.2.rep.refs_2_, f32[8,128]{1,0:T(8,128)S(1)} %get-tuple-element.67.refs_3_, bf16[864,128]{1,0:T(8,128)(2,1)S(1)} %gather.1.refs_4_, bf16[864,128]{1,0:T(8,128)(2,1)S(1)} %collective-permute-done.9.refs_5_), custom_call_target="tpu_custom_call" | custom-call | flops 250000000 | bytes 1048576 | tf_op jit(solution)/shard_map/join/pallas_call | solution.py:40
  (3 shorter events, 0.1 us)
Async XLA Ops:
  0.6 17.4 %collective-permute-start.3 = (bf16[64,4608]{1,0:T(8,128)(2,1)}, bf16[64,4608]{1,0:T(8,128)(2,1)S(1)}, u32[]{:S(2)}, u32[]{:S(2)}) collective-permute-start(bf16[64,4608]{1,0:T(8,128)(2,1)} %features.3), channel_id=1, source_target_pairs={{2,0},{0,2},{3,1},{1,3},{6,4},{4,6},{7,5},{5,7},{10,8},{8,10},{11,... | collective-permute-start | bytes 1769480 | tf_op jit(solution)/shard_map/ppermute | solution.py:419
  4.7 4.3 %collective-permute-start = (bf16[128,768]{1,0:T(8,128)(2,1)S(1)}, bf16[128,768]{1,0:T(8,128)(2,1)S(1)}, u32[]{:S(2)}, u32[]{:S(2)}) collective-permute-start(bf16[128,768]{1,0:T(8,128)(2,1)S(1)} %get-tuple-element.37), channel_id=1, source_target_pairs={{0,1},{1,0},{2,3},{3,2},{4,5},{5,4},{6,7},{7,6},{8,9},{9,8},{10,11... | collective-permute-start | bytes 589832 | tf_op jit(solution)/shard_map/ppermute | solution.py:439
  4.8 4.2 %collective-permute-start.1 = (bf16[128,768]{1,0:T(8,128)(2,1)S(1)}, bf16[128,768]{1,0:T(8,128)(2,1)S(1)}, u32[]{:S(2)}, u32[]{:S(2)}) collective-permute-start(bf16[128,768]{1,0:T(8,128)(2,1)S(1)} %get-tuple-element.38), channel_id=1, source_target_pairs={{1,4},{4,1},{5,8},{8,5},{9,12},{12,9},{3,6},{6,3},{7,10},{10,7},{1... | collective-permute-start | bytes 589832 | tf_op jit(solution)/shard_map/ppermute | solution.py:405
  9.1 11.6 %collective-permute-start.2 = (bf16[64,1280]{1,0:T(8,128)(2,1)S(1)}, bf16[64,1280]{1,0:T(8,128)(2,1)S(1)}, u32[]{:S(2)}, u32[]{:S(2)}) collective-permute-start(bf16[64,1280]{1,0:T(8,128)(2,1)S(1)} %get-tuple-element.39), channel_id=1, source_target_pairs={{2,0},{0,2},{3,1},{1,3},{6,4},{4,6},{7,5},{5,7},{10,8},{8,10},{11,... | collective-permute-start | bytes 491528 | tf_op jit(solution)/shard_map/ppermute | solution.py:419
  14.0 6.7 %copy-start = (bf16[64,4608]{1,0:T(8,128)(2,1)S(1)}, bf16[64,4608]{1,0:T(8,128)(2,1)}, u32[]{:S(2)}) copy-start(bf16[64,4608]{1,0:T(8,128)(2,1)} %cotangent.5) | copy-start | bytes 1769476
  32.1 1.8 %collective-permute-start.4 = (bf16[864,128]{1,0:T(8,128)(2,1)S(1)}, bf16[864,128]{1,0:T(8,128)(2,1)S(1)}, u32[]{:S(2)}, u32[]{:S(2)}) collective-permute-start(bf16[864,128]{1,0:T(8,128)(2,1)S(1)} %get-tuple-element.59), channel_id=1, source_target_pairs={{0,1},{1,0},{2,3},{3,2},{4,5},{5,4},{6,7},{7,6},{8,9},{9,8},{10,11... | collective-permute-start | bytes 663560 | tf_op jit(solution)/shard_map/ppermute | solution.py:517
  34.0 5.6 %collective-permute-start.6 = (bf16[432,128]{1,0:T(8,128)(2,1)S(1)}, bf16[432,128]{1,0:T(8,128)(2,1)S(1)}, u32[]{:S(2)}, u32[]{:S(2)}) collective-permute-start(bf16[432,128]{1,0:T(8,128)(2,1)S(1)} %get-tuple-element.68), channel_id=1, source_target_pairs={{0,4},{4,0},{8,12},{12,8},{1,5},{5,1},{9,13},{13,9},{2,6},{6,2},{1... | collective-permute-start | bytes 331784 | tf_op jit(solution)/shard_map/ppermute | solution.py:544
  37.6 15.5 %collective-permute-start.5 = (bf16[64,4608]{1,0:T(8,128)(2,1)S(1)}, bf16[64,4608]{1,0:T(8,128)(2,1)S(1)}, u32[]{:S(2)}, u32[]{:S(2)}) collective-permute-start(bf16[64,4608]{1,0:T(8,128)(2,1)S(1)} %get-tuple-element.65), channel_id=1, source_target_pairs={{0,2},{2,0},{1,3},{3,1},{4,6},{6,4},{5,7},{7,5},{8,10},{10,8},{9,1... | collective-permute-start | bytes 1769480 | tf_op jit(solution)/shard_map/ppermute | solution.py:549
  39.6 8.1 %collective-permute-start.7 = (bf16[432,128]{1,0:T(8,128)(2,1)S(1)}, bf16[432,128]{1,0:T(8,128)(2,1)S(1)}, u32[]{:S(2)}, u32[]{:S(2)}) collective-permute-start(bf16[432,128]{1,0:T(8,128)(2,1)S(1)} %merge_1.1.mine), channel_id=1, source_target_pairs={{0,8},{4,12},{8,0},{12,4},{1,9},{5,13},{9,1},{13,5},{2,10},{6,14},... | collective-permute-start | bytes 331784 | tf_op jit(solution)/shard_map/ppermute | solution.py:565
  47.8 4.8 %collective-permute-start.8 = (bf16[432,128]{1,0:T(8,128)(2,1)S(1)}, bf16[432,128]{1,0:T(8,128)(2,1)S(1)}, u32[]{:S(2)}, u32[]{:S(2)}) collective-permute-start(bf16[432,128]{1,0:T(8,128)(2,1)S(1)} %merge_4.1.mine), channel_id=1, source_target_pairs={{0,4},{4,0},{8,12},{12,8},{1,5},{5,1},{9,13},{13,9},{2,6},{6,2},{1... | collective-permute-start | bytes 331784 | tf_op jit(solution)/shard_map/ppermute | solution.py:570
  52.6 1.5 %collective-permute-start.9 = (bf16[864,128]{1,0:T(8,128)(2,1)S(1)}, bf16[864,128]{1,0:T(8,128)(2,1)S(1)}, u32[]{:S(2)}, u32[]{:S(2)}) collective-permute-start(bf16[864,128]{1,0:T(8,128)(2,1)S(1)} %gather.1.refs_4_), channel_id=1, source_target_pairs={{0,1},{1,0},{2,3},{3,2},{4,5},{5,4},{6,7},{7,6},{8,9},{9,8},{10,11... | collective-permute-start | bytes 663560 | tf_op jit(solution)/shard_map/ppermute | solution.py:574

commit v12 on v11

--- a/solution.py
+++ b/solution.py
@@ -14,7 +14,7 @@
 FAR = 2 * HALO
 NEAR = 640
 LEAD = 896
-MANY = 14
+MANY = 27
 DEEP = 18
 ROWS = 16
 LANES = 128
@@ -205,7 +205,20 @@
     expand(kept, valid, HALO // LANES)
 
 
-def own_body(left, right, weights, shifts_in, valid_in, begun, shifts, valid, kept):
+def turn_over(shifts, across, column):
+    channels = shifts.shape[2]
+
+    def block(j, carry):
+        rows = pl.ds(pl.multiple_of(j * WIDTH, LANES), WIDTH)
+        across[rows, column : column + channels] = wide(
+            shifts.at[4], j * TILES + FAR // LANES, TILES
+        ).T
+        return carry
+
+    lax.fori_loop(0, across.shape[0] // WIDTH, block, 0)
+
+
+def own_body(left, right, weights, shifts_in, valid_in, begun, shifts, valid, across, kept):
     del shifts_in, valid_in
     share = begun.shape[0]
     edge = FAR // LANES
@@ -223,23 +236,16 @@
         return carry
 
     lax.fori_loop(0, begun.shape[1] // WIDTH, block, 0)
-
-
-def arrive_body(rest, own_in, shifts, across, own):
-    del own_in
+    turn_over(shifts, across, across.shape[1] - share)
+
+
+def arrive_body(rest, across_in, shifts, across):
+    del across_in
     sites = rest.shape[1]
     edge = FAR // LANES
     lay(shifts.at[4], edge, rest[...])
     shift(shifts, edge + 1, edge + sites // LANES - 1)
-
-    def block(j, carry):
-        at = j * TILES + edge
-        across[pl.ds(pl.multiple_of(j * WIDTH, LANES), WIDTH), :] = jnp.concatenate(
-            [wide(own.at[4], at, TILES), wide(shifts.at[4], at, TILES)], axis=0
-        ).T
-        return carry
-
-    lax.fori_loop(0, sites // WIDTH, block, 0)
+    turn_over(shifts, across, 0)
 
 
 def rest_body(
@@ -252,12 +258,11 @@
     right,
     own,
     cotangent,
-    output,
+    kept,
     grads,
     valid,
     shifts,
     grad,
-    kept,
     hidden,
 ):
     del shifts_in, valid_in
@@ -310,7 +315,6 @@
     lax.fori_loop(0, count, block, 0)
     for piece in finishes((count + 1) % 2, count * TILES):
         piece()
-    output[...] = kept[:, WIDTH + HALO : WIDTH + HALO + sites]
 
 
 def weight_body(half, brick, chan, rep, across, valid_in, grads_in, kept, sent, valid, grads, total):
@@ -385,9 +389,15 @@
 
 def join_body(half, share, brick, chan, rep, side, other, out, both):
     mine = rep[0]
+    turn = lax.rem((chan[0] + 1) * share, out.shape[1])
     both[pl.ds(pl.multiple_of(mine * half, ROWS), half), :] = side[...]
     both[pl.ds(pl.multiple_of((1 - mine) * half, ROWS), half), :] = other[...]
-    out[...] = pltpu.roll(both[: out.shape[0], :].astype(F32), chan[0] * share, 1)
+    out[...] = pltpu.roll(both[: out.shape[0], :].astype(F32), turn, 1)
+
+
+def emit_body(held, out, token):
+    token[...] = jnp.zeros_like(token)
+    out[...] = held[:, WIDTH + HALO : WIDTH + HALO + out.shape[1]]
 
 
 def add_body(cotangent, own, *rest):
@@ -468,26 +478,31 @@
         scalars=place,
     )
     ends = stack(around(both))
-    begun, own_shifts, valid = kernel(
+    begun, own_shifts, valid, across = kernel(
         own_body,
         "forward_own",
-        [shape((share, margin), F32), shape(shifts.shape), shape(valid.shape)],
+        [
+            shape((share, margin), F32),
+            shape(shifts.shape),
+            shape(valid.shape),
+            shape((sites, total)),
+        ],
         [before, behind, own_weights, shifts, valid],
         scratch=[pltpu.VMEM((32, HALO), F32)],
         aliases={3: 1, 4: 2},
     )
-    rest_shifts, across, own_shifts = kernel(
+    rest_shifts, across = kernel(
         arrive_body,
         "arrive",
-        [shape((9, (sites + 2 * FAR) // LANES, left, LANES)), shape((sites, total)), shape(own_shifts.shape)],
-        [rest, own_shifts],
-        aliases={1: 2},
-    )
-    output, grads, valid, _ = kernel(
+        [shape((9, (sites + 2 * FAR) // LANES, left, LANES)), shape(across.shape)],
+        [rest, across],
+        aliases={1: 1},
+    )
+    held, grads, valid, _ = kernel(
         rest_body,
         "forward_rest",
         [
-            shape((share, sites)),
+            shape((share, WIDTH + margin)),
             shape((9, (margin + WIDTH) // LANES, share, LANES)),
             shape(valid.shape),
             shape(rest_shifts.shape),
@@ -495,7 +510,6 @@
         [ends, rest_shifts, rest_weights, valid, begun, before, behind, own_shifts, cotangent],
         scratch=[
             pltpu.VMEM(((LEAD + LANES + margin) // LANES, share, LANES), BF16),
-            pltpu.VMEM((share, WIDTH + margin), BF16),
             pltpu.VMEM((2, share, WIDTH), F32),
         ],
         aliases={1: 3, 3: 2},
@@ -560,12 +574,22 @@
         [own, mine, arrived],
         flops=LATER,
     )
+    output, token = kernel(
+        after(emit_body, 0),
+        "emit",
+        [shape((share, sites)), shape((8, LANES), F32)],
+        [mine, held],
+    )
     step = 2
     while step < bricks:
         other = lax.ppermute(mine, "brick", [(i, i ^ step) for i in range(bricks)])
         step *= 2
         mine = kernel(
-            merge_body, "merge_%d" % step, shape((size, total)), [mine, other], flops=LATER
+            after(merge_body, 0),
+            "merge_%d" % step,
+            shape((size, total)),
+            [token, mine, other],
+            flops=LATER,
         )
     other = lax.ppermute(mine, "brick", pairs)
     side = kernel(

time: 55.4 us -> 54.6 us (0.986)
  waiting for transfers between devices: 14.9 us -> 12.6 us
  Pallas kernels: 28.6 us -> 29.9 us
    pallas_call x15 -> x16, Pallas kernels: 28.6 us -> 29.9 us  [kernel(): pl.pallas_call(body, out_shape=outs, in_specs=[SCALAR] * len(scalars) + [...]
    ppermute x2, waiting for transfers between devices: 4.71 us -> 3.37 us  [around(): lax.ppermute(x, 'chan', [((i + over) % chans, i) for i in range(chans)])]
    ppermute x1, waiting for transfers between devices: 5.31 us -> 4.28 us  [local(): other = lax.ppermute(mine, 'brick', [(i, i ^ step) for i in range(bricks)])]
  transfers between devices with their start and end apart: 10 -> 10, of which waited for: 6 -> 6; matrix products, arithmetic and copies ran while one was open for 0% -> 0% of each run, Pallas kernels for 29% -> 33%
where the time goes in v12:
time: 54.6 us; the launch traced here: 54.5 us
  Pallas kernels  29.9 us (55%)
  waiting for transfers between devices  12.6 us (23%)
  starting transfers between devices  11.2 us (21%)
  between operations  0.77 us (1%)
    pallas_call x16, Pallas kernels, kernel(): pl.pallas_call(body, out_shape=outs, in_specs=[SCALAR] * len(scalars) + [...  29.9 us
    ppermute x1, waiting for transfers between devices, local(): other = lax.ppermute(mine, 'brick', [(i, i ^ step) for i in range(bricks)])  4.28 us
    ppermute x1, waiting for transfers between devices, local(): other = lax.ppermute(mine, 'brick', pairs)  4.03 us
    ppermute x2, waiting for transfers between devices, around(): lax.ppermute(x, 'chan', [((i + over) % chans, i) for i in range(chans)])  3.37 us
    ppermute x2, starting transfers between devices, around(): lax.ppermute(x, 'chan', [((i + over) % chans, i) for i in range(chans)])  3.1 us
    ppermute x1, starting transfers between devices, local(): other = lax.ppermute(mine, 'brick', [(i, i ^ step) for i in range(bricks)])  2.81 us
    ppermute x1, starting transfers between devices, local(): arrived = lax.ppermute(sent, 'brick', pairs)  1.87 us
    ppermute x1, starting transfers between devices, local(): lax.ppermute(other if left == share else other[(over - 1) * share:over *...  1.55 us
  transfers between devices with their start and end apart: 10, of which 6 were waited for; matrix products, arithmetic and copies ran while one was open for 0% of the time, Pallas kernels for 33%

profile of v12, /device:TPU:0, one launch (start us, length us, event | category | flops | bytes accessed | tf_op | source)
XLA Modules:
  0.0 54.5 jit_solution(14494205568873591296)
XLA Ops:
  0.6 3.0 %collective-permute-start = (bf16[64,4608]{1,0:T(8,128)(2,1)}, bf16[64,4608]{1,0:T(8,128)(2,1)S(1)}, u32[]{:S(2)}, u32[]{:S(2)}) collective-permute-start(bf16[64,4608]{1,0:T(8,128)(2,1)} %features.3), channel_id=1, source_target_pairs={{2,0},{0,2},{3,1},{1,3},{6,4},{4,6},{7,5},{5,7},{10,8},{8,10},{11,... | collective-permute-start | bytes 1769480 | tf_op jit(solution)/shard_map/ppermute | solution.py:429
  3.6 1.1 %pack.1 = (bf16[128,768]{1,0:T(8,128)(2,1)S(1)}, bf16[128,768]{1,0:T(8,128)(2,1)S(1)}) custom-call(s32[1]{0:T(128)} %bitcast.brick.refs_0_, s32[1]{0:T(128)} %bitcast.1.chan.refs_1_, s32[1]{0:T(128)} %bitcast.2.rep.refs_2_, bf16[64,4608]{1,0:T(8,128)(2,1)} %features.3, bf16[64,4608]{1,0:T(8,128)(2,1)} %cotangent.5, s32[27,4608]{1,0:T(8,128)} %neighbours.3), custom_call_target="tpu_custom_call" | custom-call | bytes 1048576 | tf_op jit(solution)/shard_map/pack/pallas_call | solution.py:40
  4.7 0.1 collective-permute-start.1
  4.8 0.7 %collective-permute-start.2 = (bf16[128,768]{1,0:T(8,128)(2,1)S(1)}, bf16[128,768]{1,0:T(8,128)(2,1)S(1)}, u32[]{:S(2)}, u32[]{:S(2)}) collective-permute-start(bf16[128,768]{1,0:T(8,128)(2,1)S(1)} %get-tuple-element.41), channel_id=1, source_target_pairs={{1,4},{4,1},{5,8},{8,5},{9,12},{12,9},{3,6},{6,3},{7,10},{10,7},{1... | collective-permute-start | bytes 589832 | tf_op jit(solution)/shard_map/ppermute | solution.py:415
  5.5 3.5 %prepare.1 = (bf16[64,1728]{1,0:T(8,128)(2,1)S(1)}, bf16[64,1728]{1,0:T(8,128)(2,1)S(1)}, bf16[128,1792]{1,0:T(8,128)(2,1)S(1)}, bf16[9,48,64,128]{3,2,1,0:T(8,128)(2,1)S(1)}, bf16[27,42,16,128]{3,2,1,0:T(8,128)(2,1)S(1)}) custom-call(s32[1]{0:T(128)} %bitcast.brick.refs_0_, s32[1]{0:T(128)} %bitcast.1.chan.refs_1_, s32[1]{0:T(128)} %bitcast.2.rep.refs_2_, ...), custom_call_target="tpu_custom_call" | custom-call | bytes 1048576 | tf_op jit(solution)/shard_map/prepare/pallas_call | solution.py:40
  9.0 0.0 collective-permute-done.1.refs_4_
  9.0 0.0 collective-permute-done.2.refs_5_
  9.0 0.1 ends.1
  9.1 0.1 collective-permute-start.3
  9.2 0.0 copy-start
  9.2 6.1 %forward_own.1 = (f32[64,5376]{1,0:T(8,128)S(1)}, bf16[9,48,64,128]{3,2,1,0:T(8,128)(2,1)S(1)}, bf16[27,42,16,128]{3,2,1,0:T(8,128)(2,1)S(1)}, bf16[4608,128]{1,0:T(8,128)(2,1)S(1)}) custom-call(bf16[128,768]{1,0:T(8,128)(2,1)S(1)} %get-tuple-element.42.left, ...), custom_call_target="tpu_custom_call", output_to_operand_aliasing={{1}: (3, {}), {2}: (4, {})} | custom-call | bytes 1048576 | tf_op jit(solution)/shard_map/forward_own/pallas_call | solution.py:40
  15.3 2.7 %collective-permute-done.rest = bf16[64,4608]{1,0:T(8,128)(2,1)S(1)} collective-permute-done((bf16[64,4608]{1,0:T(8,128)(2,1)}, bf16[64,4608]{1,0:T(8,128)(2,1)S(1)}, u32[]{:S(2)}, u32[]{:S(2)}) %collective-permute-start) | collective-permute-done | bytes 589856 | tf_op jit(solution)/shard_map/ppermute | solution.py:429
  18.0 2.0 %arrive.1 = (bf16[9,48,64,128]{3,2,1,0:T(8,128)(2,1)S(1)}, bf16[4608,128]{1,0:T(8,128)(2,1)S(1)}) custom-call(bf16[64,4608]{1,0:T(8,128)(2,1)S(1)} %collective-permute-done.rest, bf16[4608,128]{1,0:T(8,128)(2,1)S(1)} %get-tuple-element.46.across_in), custom_call_target="tpu_custom_call", output_to_operand_aliasing={{1}: (1, {})} | custom-call | bytes 1048576 | tf_op jit(solution)/shard_map/arrive/pallas_call | solution.py:40
  20.0 0.7 %collective-permute-done.3.ends = bf16[64,1280]{1,0:T(8,128)(2,1)S(1)} collective-permute-done((bf16[64,1280]{1,0:T(8,128)(2,1)S(1)}, bf16[64,1280]{1,0:T(8,128)(2,1)S(1)}, u32[]{:S(2)}, u32[]{:S(2)}) %collective-permute-start.3) | collective-permute-done | bytes 163872 | tf_op jit(solution)/shard_map/ppermute | solution.py:429
  20.7 0.0 copy-done
  20.7 5.9 %forward_rest.1 = (bf16[64,6144]{1,0:T(8,128)(2,1)S(1)}, bf16[9,48,64,128]{3,2,1,0:T(8,128)(2,1)S(1)}, bf16[27,42,16,128]{3,2,1,0:T(8,128)(2,1)S(1)}, bf16[9,48,64,128]{3,2,1,0:T(8,128)(2,1)S(1)}) custom-call(bf16[64,1280]{1,0:T(8,128)(2,1)S(1)} %collective-permute-done.3.ends, ...), custom_call_target="tpu_custom_call", output_to_operand_aliasing={{3}: (1, {}), {2}: (3, {})} | custom-call | flops 1019215872 | bytes 1048576 | tf_op jit(solution)/shard_map/forward_rest/pallas_call | solution.py:40
  26.6 4.7 %grad_weight.1 = (f32[864,128]{1,0:T(8,128)S(1)}, bf16[864,128]{1,0:T(8,128)(2,1)S(1)}, bf16[27,42,16,128]{3,2,1,0:T(8,128)(2,1)S(1)}, bf16[9,48,64,128]{3,2,1,0:T(8,128)(2,1)S(1)}) custom-call(s32[1]{0:T(128)} %bitcast.brick.refs_0_, s32[1]{0:T(128)} %bitcast.1.chan.refs_1_, s32[1]{0:T(128)} %bitcast.2.rep.refs_2_, ...), custom_call_target="tpu_custom_call", output_to_operand_aliasing={{2}: (4, {}), {3}: (5, {})} | custom-call | flops 2038431744 | bytes 1048576 | tf_op jit(solution)/shard_map/grad_weight/pallas_call | solution.py:40
  31.3 0.3 collective-permute-start.4
  31.6 1.7 %grad_features_0.1 = (bf16[27,42,16,128]{3,2,1,0:T(8,128)(2,1)S(1)}, bf16[9,48,64,128]{3,2,1,0:T(8,128)(2,1)S(1)}, f32[64,4608]{1,0:T(8,128)S(1)}, bf16[64,4608]{1,0:T(8,128)(2,1)S(1)}) custom-call(bf16[128,1792]{1,0:T(8,128)(2,1)S(1)} %get-tuple-element.38.weights.refs_1_, ...), custom_call_target="tpu_custom_call", output_to_operand_aliasing={{0}: (1, {}), {1}: (2, {})} | custom-call | flops 1019215872 | bytes 1048576 | tf_op jit(solution)/shard_map/grad_features_0/pallas_call | solution.py:40
  33.3 0.0 collective-permute-done.4.refs_5_
  33.3 0.1 split.1
  33.3 1.9 %collective-permute-start.5 = (bf16[432,128]{1,0:T(8,128)(2,1)S(1)}, bf16[432,128]{1,0:T(8,128)(2,1)S(1)}, u32[]{:S(2)}, u32[]{:S(2)}) collective-permute-start(bf16[432,128]{1,0:T(8,128)(2,1)S(1)} %get-tuple-element.66), channel_id=1, source_target_pairs={{0,4},{4,0},{8,12},{12,8},{1,5},{5,1},{9,13},{13,9},{2,6},{6,2},{1... | collective-permute-start | bytes 331784 | tf_op jit(solution)/shard_map/ppermute | solution.py:558
  35.2 1.7 %grad_features_1.1 = (f32[64,4608]{1,0:T(8,128)S(1)}, bf16[64,4608]{1,0:T(8,128)(2,1)S(1)}) custom-call(f32[432,128]{1,0:T(8,128)S(1)} %get-tuple-element.61.refs_0_.refs_1_, bf16[128,1792]{1,0:T(8,128)(2,1)S(1)} %get-tuple-element.38.weights.refs_1_, ...), custom_call_target="tpu_custom_call", output_to_operand_aliasing={{0}: (4, {}), {1}: (5, {})} | custom-call | flops 1019215872 | bytes 1048576 | tf_op jit(solution)/shard_map/grad_features_1/pallas_call | solution.py:40
  37.0 1.6 %collective-permute-start.6 = (bf16[64,4608]{1,0:T(8,128)(2,1)S(1)}, bf16[64,4608]{1,0:T(8,128)(2,1)S(1)}, u32[]{:S(2)}, u32[]{:S(2)}) collective-permute-start(bf16[64,4608]{1,0:T(8,128)(2,1)S(1)} %get-tuple-element.69), channel_id=1, source_target_pairs={{0,2},{2,0},{1,3},{3,1},{4,6},{6,4},{5,7},{7,5},{8,10},{10,8},{9,1... | collective-permute-start | bytes 1769480 | tf_op jit(solution)/shard_map/ppermute | solution.py:563
  38.5 0.3 collective-permute-done.5.refs_2_
  38.8 2.8 %collective-permute-start.7 = (bf16[432,128]{1,0:T(8,128)(2,1)S(1)}, bf16[432,128]{1,0:T(8,128)(2,1)S(1)}, u32[]{:S(2)}, u32[]{:S(2)}) collective-permute-start(bf16[432,128]{1,0:T(8,128)(2,1)S(1)} %merge_1.1.refs_0_.refs_1_), channel_id=1, source_target_pairs={{0,8},{4,12},{8,0},{12,4},{1,9},{5,13},{9,1},{13,5},{2,10},{6,14},... | collective-permute-start | bytes 331784 | tf_op jit(solution)/shard_map/ppermute | solution.py:585
  41.6 0.9 %emit.1 = (bf16[64,4608]{1,0:T(8,128)(2,1)}, f32[8,128]{1,0:T(8,128)S(1)}) custom-call(bf16[432,128]{1,0:T(8,128)(2,1)S(1)} %merge_1.1.refs_0_.refs_1_, bf16[64,6144]{1,0:T(8,128)(2,1)S(1)} %get-tuple-element.67.refs_1_), custom_call_target="tpu_custom_call" | custom-call | bytes 1048576 | tf_op jit(solution)/shard_map/emit/pallas_call | solution.py:40
  42.5 4.3 %collective-permute-done.7.refs_2_ = bf16[432,128]{1,0:T(8,128)(2,1)S(1)} collective-permute-done((bf16[432,128]{1,0:T(8,128)(2,1)S(1)}, bf16[432,128]{1,0:T(8,128)(2,1)S(1)}, u32[]{:S(2)}, u32[]{:S(2)}) %collective-permute-start.7) | collective-permute-done | bytes 110624 | tf_op jit(solution)/shard_map/ppermute | solution.py:585
  46.8 0.8 %collective-permute-start.8 = (bf16[432,128]{1,0:T(8,128)(2,1)S(1)}, bf16[432,128]{1,0:T(8,128)(2,1)S(1)}, u32[]{:S(2)}, u32[]{:S(2)}) collective-permute-start(bf16[432,128]{1,0:T(8,128)(2,1)S(1)} %merge_4.1.mine), channel_id=1, source_target_pairs={{0,4},{4,0},{8,12},{12,8},{1,5},{5,1},{9,13},{13,9},{2,6},{6,2},{1... | collective-permute-start | bytes 331784 | tf_op jit(solution)/shard_map/ppermute | solution.py:594
  47.6 4.0 %collective-permute-done.8.other = bf16[432,128]{1,0:T(8,128)(2,1)S(1)} collective-permute-done((bf16[432,128]{1,0:T(8,128)(2,1)S(1)}, bf16[432,128]{1,0:T(8,128)(2,1)S(1)}, u32[]{:S(2)}, u32[]{:S(2)}) %collective-permute-start.8) | collective-permute-done | bytes 110624 | tf_op jit(solution)/shard_map/ppermute | solution.py:594
  51.6 0.1 collective-permute-start.9
  51.7 0.6 %collective-permute-done.6.rest_0_ = bf16[64,4608]{1,0:T(8,128)(2,1)S(1)} collective-permute-done((bf16[64,4608]{1,0:T(8,128)(2,1)S(1)}, bf16[64,4608]{1,0:T(8,128)(2,1)S(1)}, u32[]{:S(2)}, u32[]{:S(2)}) %collective-permute-start.6) | collective-permute-done | bytes 589856 | tf_op jit(solution)/shard_map/ppermute | solution.py:563
  52.3 1.0 %add.1 = (bf16[64,4608]{1,0:T(8,128)(2,1)}, f32[8,128]{1,0:T(8,128)S(1)}) custom-call(bf16[64,4608]{1,0:T(8,128)(2,1)S(1)} %copy-done, f32[64,4608]{1,0:T(8,128)S(1)} %get-tuple-element.65.refs_0_.own, bf16[64,4608]{1,0:T(8,128)(2,1)S(1)} %collective-permute-done.6.rest_0_), custom_call_target="tpu_custom_call" | custom-call | bytes 1048576 | tf_op jit(solution)/shard_map/add/pallas_call | solution.py:40
  53.3 0.0 collective-permute-done.9.refs_5_
  53.3 1.1 %join.1 = f32[1728,128]{1,0:T(8,128)} custom-call(s32[1]{0:T(128)} %bitcast.brick.refs_0_, s32[1]{0:T(128)} %bitcast.1.chan.refs_1_, s32[1]{0:T(128)} %bitcast.2.rep.refs_2_, f32[8,128]{1,0:T(8,128)S(1)} %get-tuple-element.71.refs_3_, bf16[864,128]{1,0:T(8,128)(2,1)S(1)} %gather.1.refs_4_, bf16[864,128]{1,0:T(8,128)(2,1)S(1)} %collective-permute-done.9.refs_5_), custom_call_target="tpu_custom_call" | custom-call | flops 250000000 | bytes 1048576 | tf_op jit(solution)/shard_map/join/pallas_call | solution.py:40
  (3 shorter events, 0.1 us)
Async XLA Ops:
  0.6 17.4 %collective-permute-start = (bf16[64,4608]{1,0:T(8,128)(2,1)}, bf16[64,4608]{1,0:T(8,128)(2,1)S(1)}, u32[]{:S(2)}, u32[]{:S(2)}) collective-permute-start(bf16[64,4608]{1,0:T(8,128)(2,1)} %features.3), channel_id=1, source_target_pairs={{2,0},{0,2},{3,1},{1,3},{6,4},{4,6},{7,5},{5,7},{10,8},{8,10},{11,... | collective-permute-start | bytes 1769480 | tf_op jit(solution)/shard_map/ppermute | solution.py:429
  4.7 4.3 %collective-permute-start.1 = (bf16[128,768]{1,0:T(8,128)(2,1)S(1)}, bf16[128,768]{1,0:T(8,128)(2,1)S(1)}, u32[]{:S(2)}, u32[]{:S(2)}) collective-permute-start(bf16[128,768]{1,0:T(8,128)(2,1)S(1)} %get-tuple-element.40), channel_id=1, source_target_pairs={{0,1},{1,0},{2,3},{3,2},{4,5},{5,4},{6,7},{7,6},{8,9},{9,8},{10,11... | collective-permute-start | bytes 589832 | tf_op jit(solution)/shard_map/ppermute | solution.py:449
  4.8 4.2 %collective-permute-start.2 = (bf16[128,768]{1,0:T(8,128)(2,1)S(1)}, bf16[128,768]{1,0:T(8,128)(2,1)S(1)}, u32[]{:S(2)}, u32[]{:S(2)}) collective-permute-start(bf16[128,768]{1,0:T(8,128)(2,1)S(1)} %get-tuple-element.41), channel_id=1, source_target_pairs={{1,4},{4,1},{5,8},{8,5},{9,12},{12,9},{3,6},{6,3},{7,10},{10,7},{1... | collective-permute-start | bytes 589832 | tf_op jit(solution)/shard_map/ppermute | solution.py:415
  9.1 11.6 %collective-permute-start.3 = (bf16[64,1280]{1,0:T(8,128)(2,1)S(1)}, bf16[64,1280]{1,0:T(8,128)(2,1)S(1)}, u32[]{:S(2)}, u32[]{:S(2)}) collective-permute-start(bf16[64,1280]{1,0:T(8,128)(2,1)S(1)} %get-tuple-element.48), channel_id=1, source_target_pairs={{2,0},{0,2},{3,1},{1,3},{6,4},{4,6},{7,5},{5,7},{10,8},{8,10},{11,... | collective-permute-start | bytes 491528 | tf_op jit(solution)/shard_map/ppermute | solution.py:429
  9.2 11.5 %copy-start = (bf16[64,4608]{1,0:T(8,128)(2,1)S(1)}, bf16[64,4608]{1,0:T(8,128)(2,1)}, u32[]{:S(2)}) copy-start(bf16[64,4608]{1,0:T(8,128)(2,1)} %cotangent.5) | copy-start | bytes 1769476
  31.3 2.0 %collective-permute-start.4 = (bf16[864,128]{1,0:T(8,128)(2,1)S(1)}, bf16[864,128]{1,0:T(8,128)(2,1)S(1)}, u32[]{:S(2)}, u32[]{:S(2)}) collective-permute-start(bf16[864,128]{1,0:T(8,128)(2,1)S(1)} %get-tuple-element.60), channel_id=1, source_target_pairs={{0,1},{1,0},{2,3},{3,2},{4,5},{5,4},{6,7},{7,6},{8,9},{9,8},{10,11... | collective-permute-start | bytes 663560 | tf_op jit(solution)/shard_map/ppermute | solution.py:531
  33.3 5.4 %collective-permute-start.5 = (bf16[432,128]{1,0:T(8,128)(2,1)S(1)}, bf16[432,128]{1,0:T(8,128)(2,1)S(1)}, u32[]{:S(2)}, u32[]{:S(2)}) collective-permute-start(bf16[432,128]{1,0:T(8,128)(2,1)S(1)} %get-tuple-element.66), channel_id=1, source_target_pairs={{0,4},{4,0},{8,12},{12,8},{1,5},{5,1},{9,13},{13,9},{2,6},{6,2},{1... | collective-permute-start | bytes 331784 | tf_op jit(solution)/shard_map/ppermute | solution.py:558
  37.0 15.4 %collective-permute-start.6 = (bf16[64,4608]{1,0:T(8,128)(2,1)S(1)}, bf16[64,4608]{1,0:T(8,128)(2,1)S(1)}, u32[]{:S(2)}, u32[]{:S(2)}) collective-permute-start(bf16[64,4608]{1,0:T(8,128)(2,1)S(1)} %get-tuple-element.69), channel_id=1, source_target_pairs={{0,2},{2,0},{1,3},{3,1},{4,6},{6,4},{5,7},{7,5},{8,10},{10,8},{9,1... | collective-permute-start | bytes 1769480 | tf_op jit(solution)/shard_map/ppermute | solution.py:563
  38.8 7.9 %collective-permute-start.7 = (bf16[432,128]{1,0:T(8,128)(2,1)S(1)}, bf16[432,128]{1,0:T(8,128)(2,1)S(1)}, u32[]{:S(2)}, u32[]{:S(2)}) collective-permute-start(bf16[432,128]{1,0:T(8,128)(2,1)S(1)} %merge_1.1.refs_0_.refs_1_), channel_id=1, source_target_pairs={{0,8},{4,12},{8,0},{12,4},{1,9},{5,13},{9,1},{13,5},{2,10},{6,14},... | collective-permute-start | bytes 331784 | tf_op jit(solution)/shard_map/ppermute | solution.py:585
  46.8 4.8 %collective-permute-start.8 = (bf16[432,128]{1,0:T(8,128)(2,1)S(1)}, bf16[432,128]{1,0:T(8,128)(2,1)S(1)}, u32[]{:S(2)}, u32[]{:S(2)}) collective-permute-start(bf16[432,128]{1,0:T(8,128)(2,1)S(1)} %merge_4.1.mine), channel_id=1, source_target_pairs={{0,4},{4,0},{8,12},{12,8},{1,5},{5,1},{9,13},{13,9},{2,6},{6,2},{1... | collective-permute-start | bytes 331784 | tf_op jit(solution)/shard_map/ppermute | solution.py:594
  51.6 1.7 %collective-permute-start.9 = (bf16[864,128]{1,0:T(8,128)(2,1)S(1)}, bf16[864,128]{1,0:T(8,128)(2,1)S(1)}, u32[]{:S(2)}, u32[]{:S(2)}) collective-permute-start(bf16[864,128]{1,0:T(8,128)(2,1)S(1)} %gather.1.refs_4_), channel_id=1, source_target_pairs={{0,1},{1,0},{2,3},{3,2},{4,5},{5,4},{6,7},{7,6},{8,9},{9,8},{10,11... | collective-permute-start | bytes 663560 | tf_op jit(solution)/shard_map/ppermute | solution.py:598

commit v13 on v11

--- a/solution.py
+++ b/solution.py
@@ -14,14 +14,14 @@
 FAR = 2 * HALO
 NEAR = 640
 LEAD = 896
-MANY = 14
+MANY = 27
 DEEP = 18
 ROWS = 16
 LANES = 128
 GROUP = 8
 TILES = 6
 WIDTH = TILES * LANES
-LATER = 25 * 10**7
+LATER = 12 * 10**8
 LINE = ("brick", "chan", "rep")
 MIB = 1024 * 1024
 F32, BF16 = jnp.float32, jnp.bfloat16
@@ -252,12 +252,11 @@
     right,
     own,
     cotangent,
-    output,
+    kept,
     grads,
     valid,
     shifts,
     grad,
-    kept,
     hidden,
 ):
     del shifts_in, valid_in
@@ -310,7 +309,6 @@
     lax.fori_loop(0, count, block, 0)
     for piece in finishes((count + 1) % 2, count * TILES):
         piece()
-    output[...] = kept[:, WIDTH + HALO : WIDTH + HALO + sites]
 
 
 def weight_body(half, brick, chan, rep, across, valid_in, grads_in, kept, sent, valid, grads, total):
@@ -338,23 +336,15 @@
     sent[...] = total[pl.ds(pl.multiple_of((1 - mine) * half, ROWS), half), :].astype(BF16)
 
 
-def feature_body(part, weights, valid, grads, *refs):
-    own, rest = refs[-2:]
+def feature_body(part, weights, valid, grads, own, rest):
     share, sites = own.shape
-    blocks = sites // 2 // WIDTH
+    blocks = sites // WIDTH
 
     def block(j, carry):
-        at = part * blocks + j
-        here = pl.ds(pl.multiple_of(at * WIDTH, LANES), WIDTH)
-        start = at * TILES + HALO // LANES
+        here = pl.ds(pl.multiple_of(j * WIDTH, LANES), WIDTH)
+        start = (part * blocks + j) * TILES + HALO // LANES
         total = product(
-            weights,
-            grads,
-            valid,
-            start + LEAD // LANES,
-            start,
-            lambda tap: TAPS - 1 - tap,
-            count=TAPS if part else GROUP,
+            weights, grads, valid, start + LEAD // LANES, start, lambda tap: TAPS - 1 - tap
         )
         own[:, here] = total[:share]
         rest[:, here] = total[share:].astype(BF16)
@@ -385,18 +375,29 @@
 
 def join_body(half, share, brick, chan, rep, side, other, out, both):
     mine = rep[0]
+    turn = chan[0] * share
     both[pl.ds(pl.multiple_of(mine * half, ROWS), half), :] = side[...]
     both[pl.ds(pl.multiple_of((1 - mine) * half, ROWS), half), :] = other[...]
-    out[...] = pltpu.roll(both[: out.shape[0], :].astype(F32), chan[0] * share, 1)
-
-
-def add_body(cotangent, own, *rest):
+    out[...] = pltpu.roll(both[: out.shape[0], :].astype(F32), turn, 1)
+
+
+def emit_body(held, out, token):
+    token[...] = jnp.zeros_like(token)
+    out[...] = held[:, WIDTH + HALO : WIDTH + HALO + out.shape[1]]
+
+
+def add_body(part, done, cotangent, own, *rest):
     *terms, out, token = rest
     token[...] = jnp.zeros_like(token)
-    total = cotangent[...].astype(F32) + own[...]
+    sites = own.shape[1]
+    total = cotangent[:, part * sites : (part + 1) * sites].astype(F32) + own[...]
     for term in terms:
         total += term[...].astype(F32)
-    out[...] = total.astype(BF16)
+    if part == 0:
+        out[...] = total.astype(BF16)
+    else:
+        out[:, :sites] = done[...]
+        out[:, sites:] = total.astype(BF16)
 
 
 def line_swap(x):
@@ -483,11 +484,11 @@
         [rest, own_shifts],
         aliases={1: 2},
     )
-    output, grads, valid, _ = kernel(
+    held, grads, valid, _ = kernel(
         rest_body,
         "forward_rest",
         [
-            shape((share, sites)),
+            shape((share, WIDTH + margin)),
             shape((9, (margin + WIDTH) // LANES, share, LANES)),
             shape(valid.shape),
             shape(rest_shifts.shape),
@@ -495,7 +496,6 @@
         [ends, rest_shifts, rest_weights, valid, begun, before, behind, own_shifts, cotangent],
         scratch=[
             pltpu.VMEM(((LEAD + LANES + margin) // LANES, share, LANES), BF16),
-            pltpu.VMEM((share, WIDTH + margin), BF16),
             pltpu.VMEM((2, share, WIDTH), F32),
         ],
         aliases={1: 3, 3: 2},
@@ -516,67 +516,80 @@
     )
     arrived = lax.ppermute(sent, "rep", swap)
 
-    def feature_part(part, body, args, kept):
-        outs = [shape((share, sites), F32), shape((left, sites))]
-        return kernel(
-            body,
+    def feature_part(part, first):
+        own, other = kernel(
+            after(functools.partial(feature_body, part), 0),
             "grad_features_%d" % part,
-            [shape(x.shape) for x in kept] + outs,
-            args,
-            aliases={len(args) - len(kept) + i: i for i in range(len(kept))}
-            if part == 0
-            else {len(args) - 2 + i: i for i in range(2)},
+            [shape((share, sites // 2), F32), shape((left, sites // 2))],
+            [first, by_in, valid, grads],
             flops=flops * total // 2,
         )
-
-    valid, grads, *parts = feature_part(
-        0, functools.partial(feature_body, 0), [by_in, valid, grads], [valid, grads]
-    )
+        return [own] + [
+            lax.ppermute(
+                other if left == share else other[(over - 1) * share : over * share],
+                "chan",
+                [(i, (i + over) % chans) for i in range(chans)],
+            )
+            for over in range(1, chans)
+        ]
+
     mine, sent = kernel(
-        after(split_body, 3),
+        split_body,
         "split",
         [shape((size, total), F32), shape((size, total))],
-        [parts[0], kept, arrived],
+        [kept, arrived],
         scalars=place,
         flops=LATER,
     )
     pairs = [(i, i ^ 1) for i in range(bricks)]
     arrived = lax.ppermute(sent, "brick", pairs)
-    own, other = feature_part(
-        1, after(functools.partial(feature_body, 1), 0), [mine, by_in, valid, grads, *parts], []
-    )
-    terms = [
-        lax.ppermute(
-            other if left == share else other[(over - 1) * share : over * share],
-            "chan",
-            [(i, (i + over) % chans) for i in range(chans)],
-        )
-        for over in range(1, chans)
-    ]
+    first = feature_part(0, mine)
     mine = kernel(
         after(merge_body, 0),
         "merge_1",
         shape((size, total)),
-        [own, mine, arrived],
+        [first[0], mine, arrived],
         flops=LATER,
+    )
+    second = feature_part(1, mine)
+    output, token = kernel(
+        after(emit_body, 0),
+        "emit",
+        [shape((share, sites)), shape((8, LANES), F32)],
+        [second[0], held],
     )
     step = 2
     while step < bricks:
         other = lax.ppermute(mine, "brick", [(i, i ^ step) for i in range(bricks)])
         step *= 2
         mine = kernel(
-            merge_body, "merge_%d" % step, shape((size, total)), [mine, other], flops=LATER
+            after(merge_body, 0),
+            "merge_%d" % step,
+            shape((size, total)),
+            [token, mine, other],
+            flops=LATER,
         )
     other = lax.ppermute(mine, "brick", pairs)
+    begun, token = kernel(
+        functools.partial(add_body, 0),
+        "add_0",
+        [shape((share, sites // 2)), shape((8, LANES), F32)],
+        [mine, cotangent, *first],
+    )
     side = kernel(
-        gather_body, "gather", shape((half, total)), [mine, other], scalars=place, flops=LATER
+        after(after(gather_body, 3), 3),
+        "gather",
+        shape((half, total)),
+        [token, second[1], mine, other],
+        scalars=place,
+        flops=LATER,
     )
     other = lax.ppermute(side, "rep", swap)
     grad_features, token = kernel(
-        add_body,
-        "add",
-        [shape((share, sites)), shape((8, 128), F32)],
-        [cotangent, own, *terms],
+        functools.partial(add_body, 1),
+        "add_1",
+        [shape((share, sites)), shape((8, LANES), F32)],
+        [begun, cotangent, *second],
     )
     grad_weight = kernel(
         after(functools.partial(join_body, half, share), 3),

time: 55.4 us -> 54.5 us (0.984)
  waiting for transfers between devices: 14.9 us -> 12.4 us
  starting transfers between devices: 11 us -> 12.6 us
    ppermute x1, waiting for transfers between devices: 5.31 us -> 0.86 us  [local(): other = lax.ppermute(mine, 'brick', [(i, i ^ step) for i in range(bricks)])]
    ppermute x1 -> x2, starting transfers between devices: 1.55 us -> 3.13 us  [feature_part(): lax.ppermute(other if left == share else other[(over - 1) * share:over *...]
    ppermute x1, waiting for transfers between devices: 0.01 us -> 1.46 us  [local(): arrived = lax.ppermute(sent, 'rep', swap)]
    pallas_call x15 -> x17, Pallas kernels: 28.6 us -> 28.5 us  [kernel(): pl.pallas_call(body, out_shape=outs, in_specs=[SCALAR] * len(scalars) + [...]
  transfers between devices with their start and end apart: 10 -> 11, of which waited for: 6 -> 8; matrix products, arithmetic and copies ran while one was open for 0% -> 0% of each run, Pallas kernels for 29% -> 31%
where the time goes in v13:
time: 54.5 us; the launch traced here: 54.3 us
  Pallas kernels  28.5 us (52%)
  starting transfers between devices  12.6 us (23%)
  waiting for transfers between devices  12.4 us (23%)
  between operations  0.76 us (1%)
    pallas_call x17, Pallas kernels, kernel(): pl.pallas_call(body, out_shape=outs, in_specs=[SCALAR] * len(scalars) + [...  28.5 us
    ppermute x2, waiting for transfers between devices, around(): lax.ppermute(x, 'chan', [((i + over) % chans, i) for i in range(chans)])  4.72 us
    ppermute x1, waiting for transfers between devices, local(): other = lax.ppermute(mine, 'brick', pairs)  3.92 us
    ppermute x2, starting transfers between devices, feature_part(): lax.ppermute(other if left == share else other[(over - 1) * share:over *...  3.13 us
    ppermute x2, starting transfers between devices, around(): lax.ppermute(x, 'chan', [((i + over) % chans, i) for i in range(chans)])  3.1 us
    ppermute x1, starting transfers between devices, local(): other = lax.ppermute(mine, 'brick', [(i, i ^ step) for i in range(bricks)])  2.81 us
    ppermute x1, starting transfers between devices, local(): arrived = lax.ppermute(sent, 'brick', pairs)  1.89 us
    ppermute x1, waiting for transfers between devices, local(): arrived = lax.ppermute(sent, 'rep', swap)  1.46 us
  transfers between devices with their start and end apart: 11, of which 8 were waited for; matrix products, arithmetic and copies ran while one was open for 0% of the time, Pallas kernels for 31%

profile of v13, /device:TPU:0, one launch (start us, length us, event | category | flops | bytes accessed | tf_op | source)
XLA Modules:
  0.0 54.3 jit_solution(5827140423102014836)
XLA Ops:
  0.6 3.0 %collective-permute-start = (bf16[64,4608]{1,0:T(8,128)(2,1)}, bf16[64,4608]{1,0:T(8,128)(2,1)S(1)}, u32[]{:S(2)}, u32[]{:S(2)}) collective-permute-start(bf16[64,4608]{1,0:T(8,128)(2,1)} %features.3), channel_id=1, source_target_pairs={{2,0},{0,2},{3,1},{1,3},{6,4},{4,6},{7,5},{5,7},{10,8},{8,10},{11,... | collective-permute-start | bytes 1769480 | tf_op jit(solution)/shard_map/ppermute | solution.py:420
  3.6 1.1 %pack.1 = (bf16[128,768]{1,0:T(8,128)(2,1)S(1)}, bf16[128,768]{1,0:T(8,128)(2,1)S(1)}) custom-call(s32[1]{0:T(128)} %bitcast.brick.refs_0_, s32[1]{0:T(128)} %bitcast.1.chan.refs_1_, s32[1]{0:T(128)} %bitcast.2.rep.refs_2_, bf16[64,4608]{1,0:T(8,128)(2,1)} %features.3, bf16[64,4608]{1,0:T(8,128)(2,1)} %cotangent.7, s32[27,4608]{1,0:T(8,128)} %neighbours.3), custom_call_target="tpu_custom_call" | custom-call | bytes 1048576 | tf_op jit(solution)/shard_map/pack/pallas_call | solution.py:40
  4.7 0.1 collective-permute-start.1
  4.8 0.7 %collective-permute-start.2 = (bf16[128,768]{1,0:T(8,128)(2,1)S(1)}, bf16[128,768]{1,0:T(8,128)(2,1)S(1)}, u32[]{:S(2)}, u32[]{:S(2)}) collective-permute-start(bf16[128,768]{1,0:T(8,128)(2,1)S(1)} %get-tuple-element.40), channel_id=1, source_target_pairs={{1,4},{4,1},{5,8},{8,5},{9,12},{12,9},{3,6},{6,3},{7,10},{10,7},{1... | collective-permute-start | bytes 589832 | tf_op jit(solution)/shard_map/ppermute | solution.py:406
  5.5 3.5 %prepare.1 = (bf16[64,1728]{1,0:T(8,128)(2,1)S(1)}, bf16[64,1728]{1,0:T(8,128)(2,1)S(1)}, bf16[128,1792]{1,0:T(8,128)(2,1)S(1)}, bf16[9,48,64,128]{3,2,1,0:T(8,128)(2,1)S(1)}, bf16[27,42,16,128]{3,2,1,0:T(8,128)(2,1)S(1)}) custom-call(s32[1]{0:T(128)} %bitcast.brick.refs_0_, s32[1]{0:T(128)} %bitcast.1.chan.refs_1_, s32[1]{0:T(128)} %bitcast.2.rep.refs_2_, ...), custom_call_target="tpu_custom_call" | custom-call | bytes 1048576 | tf_op jit(solution)/shard_map/prepare/pallas_call | solution.py:40
  9.0 0.0 collective-permute-done.1.refs_4_
  9.0 0.0 collective-permute-done.2.refs_5_
  9.0 0.1 ends.1
  9.1 0.1 collective-permute-start.3
  9.2 0.0 copy-start
  9.2 4.8 %forward_own.1 = (f32[64,5376]{1,0:T(8,128)S(1)}, bf16[9,48,64,128]{3,2,1,0:T(8,128)(2,1)S(1)}, bf16[27,42,16,128]{3,2,1,0:T(8,128)(2,1)S(1)}) custom-call(bf16[128,768]{1,0:T(8,128)(2,1)S(1)} %get-tuple-element.41.left, bf16[128,768]{1,0:T(8,128)(2,1)S(1)} %get-tuple-element.42.right, ...), custom_call_target="tpu_custom_call", output_to_operand_aliasing={{1}: (3, {}), {2}: (4, {})} | custom-call | bytes 1048576 | tf_op jit(solution)/shard_map/forward_own/pallas_call | solution.py:40
  14.0 4.0 %collective-permute-done.rest = bf16[64,4608]{1,0:T(8,128)(2,1)S(1)} collective-permute-done((bf16[64,4608]{1,0:T(8,128)(2,1)}, bf16[64,4608]{1,0:T(8,128)(2,1)S(1)}, u32[]{:S(2)}, u32[]{:S(2)}) %collective-permute-start) | collective-permute-done | bytes 589856 | tf_op jit(solution)/shard_map/ppermute | solution.py:420
  18.0 2.0 %arrive.1 = (bf16[9,48,64,128]{3,2,1,0:T(8,128)(2,1)S(1)}, bf16[4608,128]{1,0:T(8,128)(2,1)S(1)}, bf16[9,48,64,128]{3,2,1,0:T(8,128)(2,1)S(1)}) custom-call(bf16[64,4608]{1,0:T(8,128)(2,1)S(1)} %collective-permute-done.rest, bf16[9,48,64,128]{3,2,1,0:T(8,128)(2,1)S(1)} %get-tuple-element.45.own_in), custom_call_target="tpu_custom_call", output_to_operand_aliasing={{2}: (1, {})} | custom-call | bytes 1048576 | tf_op jit(solution)/shard_map/arrive/pallas_call | solution.py:40
  20.0 0.7 %collective-permute-done.3.ends = bf16[64,1280]{1,0:T(8,128)(2,1)S(1)} collective-permute-done((bf16[64,1280]{1,0:T(8,128)(2,1)S(1)}, bf16[64,1280]{1,0:T(8,128)(2,1)S(1)}, u32[]{:S(2)}, u32[]{:S(2)}) %collective-permute-start.3) | collective-permute-done | bytes 163872 | tf_op jit(solution)/shard_map/ppermute | solution.py:420
  20.7 0.0 copy-done
  20.7 5.9 %forward_rest.1 = (bf16[64,6144]{1,0:T(8,128)(2,1)S(1)}, bf16[9,48,64,128]{3,2,1,0:T(8,128)(2,1)S(1)}, bf16[27,42,16,128]{3,2,1,0:T(8,128)(2,1)S(1)}, bf16[9,48,64,128]{3,2,1,0:T(8,128)(2,1)S(1)}) custom-call(bf16[64,1280]{1,0:T(8,128)(2,1)S(1)} %collective-permute-done.3.ends, ...), custom_call_target="tpu_custom_call", output_to_operand_aliasing={{3}: (1, {}), {2}: (3, {})} | custom-call | flops 1019215872 | bytes 1048576 | tf_op jit(solution)/shard_map/forward_rest/pallas_call | solution.py:40
  26.6 4.7 %grad_weight.1 = (f32[864,128]{1,0:T(8,128)S(1)}, bf16[864,128]{1,0:T(8,128)(2,1)S(1)}, bf16[27,42,16,128]{3,2,1,0:T(8,128)(2,1)S(1)}, bf16[9,48,64,128]{3,2,1,0:T(8,128)(2,1)S(1)}) custom-call(s32[1]{0:T(128)} %bitcast.brick.refs_0_, s32[1]{0:T(128)} %bitcast.1.chan.refs_1_, s32[1]{0:T(128)} %bitcast.2.rep.refs_2_, ...), custom_call_target="tpu_custom_call", output_to_operand_aliasing={{2}: (4, {}), {3}: (5, {})} | custom-call | flops 2038431744 | bytes 1048576 | tf_op jit(solution)/shard_map/grad_weight/pallas_call | solution.py:40
  31.3 0.1 collective-permute-start.4
  31.4 1.5 %collective-permute-done.4.arrived = bf16[864,128]{1,0:T(8,128)(2,1)S(1)} collective-permute-done((bf16[864,128]{1,0:T(8,128)(2,1)S(1)}, bf16[864,128]{1,0:T(8,128)(2,1)S(1)}, u32[]{:S(2)}, u32[]{:S(2)}) %collective-permute-start.4) | collective-permute-done | bytes 221216 | tf_op jit(solution)/shard_map/ppermute | solution.py:517
  32.9 1.9 %collective-permute-start.5 = (bf16[432,128]{1,0:T(8,128)(2,1)S(1)}, bf16[432,128]{1,0:T(8,128)(2,1)S(1)}, u32[]{:S(2)}, u32[]{:S(2)}) collective-permute-start(bf16[432,128]{1,0:T(8,128)(2,1)S(1)} %get-tuple-element.62), channel_id=1, source_target_pairs={{0,4},{4,0},{8,12},{12,8},{1,5},{5,1},{9,13},{13,9},{2,6},{6,2},{1... | collective-permute-start | bytes 331784 | tf_op jit(solution)/shard_map/ppermute | solution.py:545
  34.8 1.7 %grad_features_0.1 = (f32[64,2304]{1,0:T(8,128)S(1)}, bf16[64,2304]{1,0:T(8,128)(2,1)S(1)}) custom-call(f32[432,128]{1,0:T(8,128)S(1)} %get-tuple-element.57.refs_0_.refs_1_, bf16[128,1792]{1,0:T(8,128)(2,1)S(1)} %get-tuple-element.58.refs_1_, bf16[27,42,16,128]{3,2,1,0:T(8,128)(2,1)S(1)} %get-tuple-element.59.refs_2_, ...), custom_call_target="tpu_custom_call" | custom-call | flops 1019215872 | bytes 1048576 | tf_op jit(solution)/shard_map/grad_features_0/pallas_call | solution.py:40
  36.5 1.6 %collective-permute-start.7 = (bf16[64,2304]{1,0:T(8,128)(2,1)S(1)}, bf16[64,2304]{1,0:T(8,128)(2,1)S(1)}, u32[]{:S(2)}, u32[]{:S(2)}) collective-permute-start(bf16[64,2304]{1,0:T(8,128)(2,1)S(1)} %get-tuple-element.67), channel_id=1, source_target_pairs={{0,2},{2,0},{1,3},{3,1},{4,6},{6,4},{5,7},{7,5},{8,10},{10,8},{9,1... | collective-permute-start | bytes 884744 | tf_op jit(solution)/shard_map/ppermute | solution.py:528
  38.0 0.1 collective-permute-done.5.refs_2_
  38.2 2.8 %collective-permute-start.6 = (bf16[432,128]{1,0:T(8,128)(2,1)S(1)}, bf16[432,128]{1,0:T(8,128)(2,1)S(1)}, u32[]{:S(2)}, u32[]{:S(2)}) collective-permute-start(bf16[432,128]{1,0:T(8,128)(2,1)S(1)} %merge_1.1.refs_0_.refs_1_), channel_id=1, source_target_pairs={{0,8},{4,12},{8,0},{12,4},{1,9},{5,13},{9,1},{13,5},{2,10},{6,14},... | collective-permute-start | bytes 331784 | tf_op jit(solution)/shard_map/ppermute | solution.py:563
  41.0 1.7 %grad_features_1.1 = (f32[64,2304]{1,0:T(8,128)S(1)}, bf16[64,2304]{1,0:T(8,128)(2,1)S(1)}) custom-call(bf16[432,128]{1,0:T(8,128)(2,1)S(1)} %merge_1.1.refs_0_.refs_1_, bf16[128,1792]{1,0:T(8,128)(2,1)S(1)} %get-tuple-element.58.refs_1_, bf16[27,42,16,128]{3,2,1,0:T(8,128)(2,1)S(1)} %get-tuple-element.59.refs_2_, ...), custom_call_target="tpu_custom_call" | custom-call | flops 1019215872 | bytes 1048576 | tf_op jit(solution)/shard_map/grad_features_1/pallas_call | solution.py:40
  42.7 1.6 %collective-permute-start.8 = (bf16[64,2304]{1,0:T(8,128)(2,1)S(1)}, bf16[64,2304]{1,0:T(8,128)(2,1)S(1)}, u32[]{:S(2)}, u32[]{:S(2)}) collective-permute-start(bf16[64,2304]{1,0:T(8,128)(2,1)S(1)} %get-tuple-element.69), channel_id=1, source_target_pairs={{0,2},{2,0},{1,3},{3,1},{4,6},{6,4},{5,7},{7,5},{8,10},{10,8},{9,1... | collective-permute-start | bytes 884744 | tf_op jit(solution)/shard_map/ppermute | solution.py:528
  44.2 0.9 %emit.1 = (bf16[64,4608]{1,0:T(8,128)(2,1)}, f32[8,128]{1,0:T(8,128)S(1)}) custom-call(f32[64,2304]{1,0:T(8,128)S(1)} %get-tuple-element.63.refs_0_.own, bf16[64,6144]{1,0:T(8,128)(2,1)S(1)} %get-tuple-element.64.refs_1_), custom_call_target="tpu_custom_call" | custom-call | bytes 1048576 | tf_op jit(solution)/shard_map/emit/pallas_call | solution.py:40
  45.1 0.9 %collective-permute-done.6.refs_2_ = bf16[432,128]{1,0:T(8,128)(2,1)S(1)} collective-permute-done((bf16[432,128]{1,0:T(8,128)(2,1)S(1)}, bf16[432,128]{1,0:T(8,128)(2,1)S(1)}, u32[]{:S(2)}, u32[]{:S(2)}) %collective-permute-start.6) | collective-permute-done | bytes 110624 | tf_op jit(solution)/shard_map/ppermute | solution.py:563
  46.0 0.8 %collective-permute-start.9 = (bf16[432,128]{1,0:T(8,128)(2,1)S(1)}, bf16[432,128]{1,0:T(8,128)(2,1)S(1)}, u32[]{:S(2)}, u32[]{:S(2)}) collective-permute-start(bf16[432,128]{1,0:T(8,128)(2,1)S(1)} %merge_4.1.done.refs_5_), channel_id=1, source_target_pairs={{0,4},{4,0},{8,12},{12,8},{1,5},{5,1},{9,13},{13,9},{2,6},{6,2},{1... | collective-permute-start | bytes 331784 | tf_op jit(solution)/shard_map/ppermute | solution.py:572
  46.8 0.0 collective-permute-done.7.rest_0_
  46.8 0.1 add_0.1
  46.9 3.9 %collective-permute-done.9.refs_6_ = bf16[432,128]{1,0:T(8,128)(2,1)S(1)} collective-permute-done((bf16[432,128]{1,0:T(8,128)(2,1)S(1)}, bf16[432,128]{1,0:T(8,128)(2,1)S(1)}, u32[]{:S(2)}, u32[]{:S(2)}) %collective-permute-start.9) | collective-permute-done | bytes 110624 | tf_op jit(solution)/shard_map/ppermute | solution.py:572
  50.8 0.8 %collective-permute-done.8.rest_0_.refs_4_ = bf16[64,2304]{1,0:T(8,128)(2,1)S(1)} collective-permute-done((bf16[64,2304]{1,0:T(8,128)(2,1)S(1)}, bf16[64,2304]{1,0:T(8,128)(2,1)S(1)}, u32[]{:S(2)}, u32[]{:S(2)}) %collective-permute-start.8) | collective-permute-done | bytes 294944 | tf_op jit(solution)/shard_map/ppermute | solution.py:528
  51.7 0.1 collective-permute-start.10
  51.7 0.9 %add_1.1 = (bf16[64,4608]{1,0:T(8,128)(2,1)}, f32[8,128]{1,0:T(8,128)S(1)}) custom-call(bf16[64,2304]{1,0:T(8,128)(2,1)S(1)} %get-tuple-element.68.done, bf16[64,4608]{1,0:T(8,128)(2,1)S(1)} %copy-done, f32[64,2304]{1,0:T(8,128)S(1)} %get-tuple-element.63.refs_0_.own, bf16[64,2304]{1,0:T(8,128)(2,1)S(1)} %collective-permute-done.8.rest_0_.refs_4_), custom_call_target="tpu_custom_call" | custom-call | bytes 1048576 | tf_op jit(solution)/shard_map/add_1/pallas_call | solution.py:40
  52.7 0.5 collective-permute-done.10.refs_5_
  53.2 1.1 %join.1 = f32[1728,128]{1,0:T(8,128)} custom-call(s32[1]{0:T(128)} %bitcast.brick.refs_0_, s32[1]{0:T(128)} %bitcast.1.chan.refs_1_, s32[1]{0:T(128)} %bitcast.2.rep.refs_2_, f32[8,128]{1,0:T(8,128)S(1)} %get-tuple-element.71.refs_3_, bf16[864,128]{1,0:T(8,128)(2,1)S(1)} %gather.1.refs_4_, bf16[864,128]{1,0:T(8,128)(2,1)S(1)} %collective-permute-done.10.refs_5_), custom_call_target="tpu_custom_call" | custom-call | flops 1200000000 | bytes 1048576 | tf_op jit(solution)/shard_map/join/pallas_call | solution.py:40
  (4 shorter events, 0.1 us)
Async XLA Ops:
  0.6 17.4 %collective-permute-start = (bf16[64,4608]{1,0:T(8,128)(2,1)}, bf16[64,4608]{1,0:T(8,128)(2,1)S(1)}, u32[]{:S(2)}, u32[]{:S(2)}) collective-permute-start(bf16[64,4608]{1,0:T(8,128)(2,1)} %features.3), channel_id=1, source_target_pairs={{2,0},{0,2},{3,1},{1,3},{6,4},{4,6},{7,5},{5,7},{10,8},{8,10},{11,... | collective-permute-start | bytes 1769480 | tf_op jit(solution)/shard_map/ppermute | solution.py:420
  4.7 4.3 %collective-permute-start.1 = (bf16[128,768]{1,0:T(8,128)(2,1)S(1)}, bf16[128,768]{1,0:T(8,128)(2,1)S(1)}, u32[]{:S(2)}, u32[]{:S(2)}) collective-permute-start(bf16[128,768]{1,0:T(8,128)(2,1)S(1)} %get-tuple-element.39), channel_id=1, source_target_pairs={{0,1},{1,0},{2,3},{3,2},{4,5},{5,4},{6,7},{7,6},{8,9},{9,8},{10,11... | collective-permute-start | bytes 589832 | tf_op jit(solution)/shard_map/ppermute | solution.py:440
  4.8 4.2 %collective-permute-start.2 = (bf16[128,768]{1,0:T(8,128)(2,1)S(1)}, bf16[128,768]{1,0:T(8,128)(2,1)S(1)}, u32[]{:S(2)}, u32[]{:S(2)}) collective-permute-start(bf16[128,768]{1,0:T(8,128)(2,1)S(1)} %get-tuple-element.40), channel_id=1, source_target_pairs={{1,4},{4,1},{5,8},{8,5},{9,12},{12,9},{3,6},{6,3},{7,10},{10,7},{1... | collective-permute-start | bytes 589832 | tf_op jit(solution)/shard_map/ppermute | solution.py:406
  9.1 11.6 %collective-permute-start.3 = (bf16[64,1280]{1,0:T(8,128)(2,1)S(1)}, bf16[64,1280]{1,0:T(8,128)(2,1)S(1)}, u32[]{:S(2)}, u32[]{:S(2)}) collective-permute-start(bf16[64,1280]{1,0:T(8,128)(2,1)S(1)} %get-tuple-element.47), channel_id=1, source_target_pairs={{2,0},{0,2},{3,1},{1,3},{6,4},{4,6},{7,5},{5,7},{10,8},{8,10},{11,... | collective-permute-start | bytes 491528 | tf_op jit(solution)/shard_map/ppermute | solution.py:420
  9.2 11.5 %copy-start = (bf16[64,4608]{1,0:T(8,128)(2,1)S(1)}, bf16[64,4608]{1,0:T(8,128)(2,1)}, u32[]{:S(2)}) copy-start(bf16[64,4608]{1,0:T(8,128)(2,1)} %cotangent.7) | copy-start | bytes 1769476
  31.3 1.5 %collective-permute-start.4 = (bf16[864,128]{1,0:T(8,128)(2,1)S(1)}, bf16[864,128]{1,0:T(8,128)(2,1)S(1)}, u32[]{:S(2)}, u32[]{:S(2)}) collective-permute-start(bf16[864,128]{1,0:T(8,128)(2,1)S(1)} %get-tuple-element.56), channel_id=1, source_target_pairs={{0,1},{1,0},{2,3},{3,2},{4,5},{5,4},{6,7},{7,6},{8,9},{9,8},{10,11... | collective-permute-start | bytes 663560 | tf_op jit(solution)/shard_map/ppermute | solution.py:517
  32.9 5.3 %collective-permute-start.5 = (bf16[432,128]{1,0:T(8,128)(2,1)S(1)}, bf16[432,128]{1,0:T(8,128)(2,1)S(1)}, u32[]{:S(2)}, u32[]{:S(2)}) collective-permute-start(bf16[432,128]{1,0:T(8,128)(2,1)S(1)} %get-tuple-element.62), channel_id=1, source_target_pairs={{0,4},{4,0},{8,12},{12,8},{1,5},{5,1},{9,13},{13,9},{2,6},{6,2},{1... | collective-permute-start | bytes 331784 | tf_op jit(solution)/shard_map/ppermute | solution.py:545
  36.5 10.3 %collective-permute-start.7 = (bf16[64,2304]{1,0:T(8,128)(2,1)S(1)}, bf16[64,2304]{1,0:T(8,128)(2,1)S(1)}, u32[]{:S(2)}, u32[]{:S(2)}) collective-permute-start(bf16[64,2304]{1,0:T(8,128)(2,1)S(1)} %get-tuple-element.67), channel_id=1, source_target_pairs={{0,2},{2,0},{1,3},{3,1},{4,6},{6,4},{5,7},{7,5},{8,10},{10,8},{9,1... | collective-permute-start | bytes 884744 | tf_op jit(solution)/shard_map/ppermute | solution.py:528
  38.2 7.8 %collective-permute-start.6 = (bf16[432,128]{1,0:T(8,128)(2,1)S(1)}, bf16[432,128]{1,0:T(8,128)(2,1)S(1)}, u32[]{:S(2)}, u32[]{:S(2)}) collective-permute-start(bf16[432,128]{1,0:T(8,128)(2,1)S(1)} %merge_1.1.refs_0_.refs_1_), channel_id=1, source_target_pairs={{0,8},{4,12},{8,0},{12,4},{1,9},{5,13},{9,1},{13,5},{2,10},{6,14},... | collective-permute-start | bytes 331784 | tf_op jit(solution)/shard_map/ppermute | solution.py:563
  42.7 9.0 %collective-permute-start.8 = (bf16[64,2304]{1,0:T(8,128)(2,1)S(1)}, bf16[64,2304]{1,0:T(8,128)(2,1)S(1)}, u32[]{:S(2)}, u32[]{:S(2)}) collective-permute-start(bf16[64,2304]{1,0:T(8,128)(2,1)S(1)} %get-tuple-element.69), channel_id=1, source_target_pairs={{0,2},{2,0},{1,3},{3,1},{4,6},{6,4},{5,7},{7,5},{8,10},{10,8},{9,1... | collective-permute-start | bytes 884744 | tf_op jit(solution)/shard_map/ppermute | solution.py:528
  46.0 4.8 %collective-permute-start.9 = (bf16[432,128]{1,0:T(8,128)(2,1)S(1)}, bf16[432,128]{1,0:T(8,128)(2,1)S(1)}, u32[]{:S(2)}, u32[]{:S(2)}) collective-permute-start(bf16[432,128]{1,0:T(8,128)(2,1)S(1)} %merge_4.1.done.refs_5_), channel_id=1, source_target_pairs={{0,4},{4,0},{8,12},{12,8},{1,5},{5,1},{9,13},{13,9},{2,6},{6,2},{1... | collective-permute-start | bytes 331784 | tf_op jit(solution)/shard_map/ppermute | solution.py:572
  51.7 1.5 %collective-permute-start.10 = (bf16[864,128]{1,0:T(8,128)(2,1)S(1)}, bf16[864,128]{1,0:T(8,128)(2,1)S(1)}, u32[]{:S(2)}, u32[]{:S(2)}) collective-permute-start(bf16[864,128]{1,0:T(8,128)(2,1)S(1)} %gather.1.refs_4_), channel_id=1, source_target_pairs={{0,1},{1,0},{2,3},{3,2},{4,5},{5,4},{6,7},{7,6},{8,9},{9,8},{10,11... | collective-permute-start | bytes 663560 | tf_op jit(solution)/shard_map/ppermute | solution.py:587

commit v14 on v13

--- a/solution.py
+++ b/solution.py
@@ -336,13 +336,13 @@
     sent[...] = total[pl.ds(pl.multiple_of((1 - mine) * half, ROWS), half), :].astype(BF16)
 
 
-def feature_body(part, weights, valid, grads, own, rest):
-    share, sites = own.shape
-    blocks = sites // WIDTH
+def feature_body(first, last, lead_in, weights, valid, grads, *refs):
+    own, rest = refs[-2:]
+    share = own.shape[0]
 
     def block(j, carry):
-        here = pl.ds(pl.multiple_of(j * WIDTH, LANES), WIDTH)
-        start = (part * blocks + j) * TILES + HALO // LANES
+        here = pl.ds(pl.multiple_of((j - lead_in) * WIDTH, LANES), WIDTH)
+        start = j * TILES + HALO // LANES
         total = product(
             weights, grads, valid, start + LEAD // LANES, start, lambda tap: TAPS - 1 - tap
         )
@@ -350,7 +350,7 @@
         rest[:, here] = total[share:].astype(BF16)
         return carry
 
-    lax.fori_loop(0, blocks, block, 0)
+    lax.fori_loop(first, last, block, 0)
 
 
 def split_body(brick, chan, rep, kept, arrived, mine, sent):
@@ -390,14 +390,15 @@
     *terms, out, token = rest
     token[...] = jnp.zeros_like(token)
     sites = own.shape[1]
-    total = cotangent[:, part * sites : (part + 1) * sites].astype(F32) + own[...]
+    begin = part * (cotangent.shape[1] - sites)
+    total = cotangent[:, begin : begin + sites].astype(F32) + own[...]
     for term in terms:
         total += term[...].astype(F32)
     if part == 0:
         out[...] = total.astype(BF16)
     else:
-        out[:, :sites] = done[...]
-        out[:, sites:] = total.astype(BF16)
+        out[:, :begin] = done[...]
+        out[:, begin:] = total.astype(BF16)
 
 
 def line_swap(x):
@@ -516,14 +517,23 @@
     )
     arrived = lax.ppermute(sent, "rep", swap)
 
-    def feature_part(part, first):
-        own, other = kernel(
-            after(functools.partial(feature_body, part), 0),
+    third = sites // WIDTH // 3
+
+    def feature_part(part, ahead, so_far=()):
+        lead_in = 2 * third if part == 2 else 0
+        count = third if part == 2 else 2 * third
+        return kernel(
+            after(
+                functools.partial(feature_body, part * third, (part + 1) * third, lead_in), 0
+            ),
             "grad_features_%d" % part,
-            [shape((share, sites // 2), F32), shape((left, sites // 2))],
-            [first, by_in, valid, grads],
-            flops=flops * total // 2,
+            [shape((share, count * WIDTH), F32), shape((left, count * WIDTH))],
+            [ahead, by_in, valid, grads, *so_far],
+            aliases={4 + i: i for i in range(len(so_far))},
+            flops=flops * total // 3,
         )
+
+    def terms_of(own, other):
         return [own] + [
             lax.ppermute(
                 other if left == share else other[(over - 1) * share : over * share],
@@ -533,17 +543,18 @@
             for over in range(1, chans)
         ]
 
+    parts = feature_part(0, kept)
     mine, sent = kernel(
-        split_body,
+        after(split_body, 3),
         "split",
         [shape((size, total), F32), shape((size, total))],
-        [kept, arrived],
+        [parts[0], kept, arrived],
         scalars=place,
         flops=LATER,
     )
     pairs = [(i, i ^ 1) for i in range(bricks)]
     arrived = lax.ppermute(sent, "brick", pairs)
-    first = feature_part(0, mine)
+    first = terms_of(*feature_part(1, mine, parts))
     mine = kernel(
         after(merge_body, 0),
         "merge_1",
@@ -551,7 +562,7 @@
         [first[0], mine, arrived],
         flops=LATER,
     )
-    second = feature_part(1, mine)
+    second = terms_of(*feature_part(2, mine))
     output, token = kernel(
         after(emit_body, 0),
         "emit",
@@ -573,7 +584,7 @@
     begun, token = kernel(
         functools.partial(add_body, 0),
         "add_0",
-        [shape((share, sites // 2)), shape((8, LANES), F32)],
+        [shape((share, 2 * third * WIDTH)), shape((8, LANES), F32)],
         [mine, cotangent, *first],
     )
     side = kernel(

time: 54.5 us -> 54 us (level)
    ppermute x1, waiting for transfers between devices: 3.92 us -> 0.01 us  [local(): other = lax.ppermute(mine, 'brick', pairs)]
    ppermute x2, waiting for transfers between devices: 0.84 us -> 4.17 us  [terms_of(): lax.ppermute(other if left == share else other[(over - 1) * share:over *...]
    ppermute x1, waiting for transfers between devices: 1.46 us -> 0.32 us  [local(): arrived = lax.ppermute(sent, 'rep', swap)]
    ppermute x1, waiting for transfers between devices: 0.09 us -> 0.71 us  [local(): arrived = lax.ppermute(sent, 'brick', pairs)]
    pallas_call x17 -> x18, Pallas kernels: 28.5 us -> 28.5 us  [kernel(): pl.pallas_call(body, out_shape=outs, in_specs=[SCALAR] * len(scalars) + [...]
where the time goes in v14:
time: 54 us; the launch traced here: 53.8 us
  Pallas kernels  28.5 us (53%)
  starting transfers between devices  12.6 us (23%)
  waiting for transfers between devices  11.9 us (22%)
  between operations  0.77 us (1%)
    pallas_call x18, Pallas kernels, kernel(): pl.pallas_call(body, out_shape=outs, in_specs=[SCALAR] * len(scalars) + [...  28.5 us
    ppermute x2, waiting for transfers between devices, around(): lax.ppermute(x, 'chan', [((i + over) % chans, i) for i in range(chans)])  4.72 us
    ppermute x2, waiting for transfers between devices, terms_of(): lax.ppermute(other if left == share else other[(over - 1) * share:over *...  4.17 us
    ppermute x2, starting transfers between devices, terms_of(): lax.ppermute(other if left == share else other[(over - 1) * share:over *...  3.13 us
    ppermute x2, starting transfers between devices, around(): lax.ppermute(x, 'chan', [((i + over) % chans, i) for i in range(chans)])  3.1 us
    ppermute x1, starting transfers between devices, local(): other = lax.ppermute(mine, 'brick', [(i, i ^ step) for i in range(bricks)])  2.82 us
    ppermute x1, starting transfers between devices, local(): arrived = lax.ppermute(sent, 'brick', pairs)  1.89 us
    ppermute x1, waiting for transfers between devices, local(): other = lax.ppermute(mine, 'brick', [(i, i ^ step) for i in range(bricks)])  1.4 us
  transfers between devices with their start and end apart: 11, of which 8 were waited for; matrix products, arithmetic and copies ran while one was open for 0% of the time, Pallas kernels for 31%

profile of v14, /device:TPU:0, one launch (start us, length us, event | category | flops | bytes accessed | tf_op | source)
XLA Modules:
  0.0 53.8 jit_solution(8199678038850326895)
XLA Ops:
  0.6 3.0 %collective-permute-start = (bf16[64,4608]{1,0:T(8,128)(2,1)}, bf16[64,4608]{1,0:T(8,128)(2,1)S(1)}, u32[]{:S(2)}, u32[]{:S(2)}) collective-permute-start(bf16[64,4608]{1,0:T(8,128)(2,1)} %features.3), channel_id=1, source_target_pairs={{2,0},{0,2},{3,1},{1,3},{6,4},{4,6},{7,5},{5,7},{10,8},{8,10},{11,... | collective-permute-start | bytes 1769480 | tf_op jit(solution)/shard_map/ppermute | solution.py:421
  3.6 1.1 %pack.1 = (bf16[128,768]{1,0:T(8,128)(2,1)S(1)}, bf16[128,768]{1,0:T(8,128)(2,1)S(1)}) custom-call(s32[1]{0:T(128)} %bitcast.brick.refs_0_, s32[1]{0:T(128)} %bitcast.1.chan.refs_1_, s32[1]{0:T(128)} %bitcast.2.rep.refs_2_, bf16[64,4608]{1,0:T(8,128)(2,1)} %features.3, bf16[64,4608]{1,0:T(8,128)(2,1)} %cotangent.7, s32[27,4608]{1,0:T(8,128)} %neighbours.3), custom_call_target="tpu_custom_call" | custom-call | bytes 1048576 | tf_op jit(solution)/shard_map/pack/pallas_call | solution.py:40
  4.7 0.1 collective-permute-start.1
  4.8 0.7 %collective-permute-start.2 = (bf16[128,768]{1,0:T(8,128)(2,1)S(1)}, bf16[128,768]{1,0:T(8,128)(2,1)S(1)}, u32[]{:S(2)}, u32[]{:S(2)}) collective-permute-start(bf16[128,768]{1,0:T(8,128)(2,1)S(1)} %get-tuple-element.42), channel_id=1, source_target_pairs={{1,4},{4,1},{5,8},{8,5},{9,12},{12,9},{3,6},{6,3},{7,10},{10,7},{1... | collective-permute-start | bytes 589832 | tf_op jit(solution)/shard_map/ppermute | solution.py:407
  5.5 3.5 %prepare.1 = (bf16[64,1728]{1,0:T(8,128)(2,1)S(1)}, bf16[64,1728]{1,0:T(8,128)(2,1)S(1)}, bf16[128,1792]{1,0:T(8,128)(2,1)S(1)}, bf16[9,48,64,128]{3,2,1,0:T(8,128)(2,1)S(1)}, bf16[27,42,16,128]{3,2,1,0:T(8,128)(2,1)S(1)}) custom-call(s32[1]{0:T(128)} %bitcast.brick.refs_0_, s32[1]{0:T(128)} %bitcast.1.chan.refs_1_, s32[1]{0:T(128)} %bitcast.2.rep.refs_2_, ...), custom_call_target="tpu_custom_call" | custom-call | bytes 1048576 | tf_op jit(solution)/shard_map/prepare/pallas_call | solution.py:40
  9.0 0.0 collective-permute-done.1.refs_4_
  9.0 0.0 collective-permute-done.2.refs_5_
  9.0 0.1 ends.1
  9.1 0.1 collective-permute-start.3
  9.2 0.0 copy-start
  9.2 4.8 %forward_own.1 = (f32[64,5376]{1,0:T(8,128)S(1)}, bf16[9,48,64,128]{3,2,1,0:T(8,128)(2,1)S(1)}, bf16[27,42,16,128]{3,2,1,0:T(8,128)(2,1)S(1)}) custom-call(bf16[128,768]{1,0:T(8,128)(2,1)S(1)} %get-tuple-element.43.left, bf16[128,768]{1,0:T(8,128)(2,1)S(1)} %get-tuple-element.44.right, ...), custom_call_target="tpu_custom_call", output_to_operand_aliasing={{1}: (3, {}), {2}: (4, {})} | custom-call | bytes 1048576 | tf_op jit(solution)/shard_map/forward_own/pallas_call | solution.py:40
  14.0 4.0 %collective-permute-done.rest = bf16[64,4608]{1,0:T(8,128)(2,1)S(1)} collective-permute-done((bf16[64,4608]{1,0:T(8,128)(2,1)}, bf16[64,4608]{1,0:T(8,128)(2,1)S(1)}, u32[]{:S(2)}, u32[]{:S(2)}) %collective-permute-start) | collective-permute-done | bytes 589856 | tf_op jit(solution)/shard_map/ppermute | solution.py:421
  18.0 2.0 %arrive.1 = (bf16[9,48,64,128]{3,2,1,0:T(8,128)(2,1)S(1)}, bf16[4608,128]{1,0:T(8,128)(2,1)S(1)}, bf16[9,48,64,128]{3,2,1,0:T(8,128)(2,1)S(1)}) custom-call(bf16[64,4608]{1,0:T(8,128)(2,1)S(1)} %collective-permute-done.rest, bf16[9,48,64,128]{3,2,1,0:T(8,128)(2,1)S(1)} %get-tuple-element.47.own_in), custom_call_target="tpu_custom_call", output_to_operand_aliasing={{2}: (1, {})} | custom-call | bytes 1048576 | tf_op jit(solution)/shard_map/arrive/pallas_call | solution.py:40
  20.0 0.7 %collective-permute-done.3.ends = bf16[64,1280]{1,0:T(8,128)(2,1)S(1)} collective-permute-done((bf16[64,1280]{1,0:T(8,128)(2,1)S(1)}, bf16[64,1280]{1,0:T(8,128)(2,1)S(1)}, u32[]{:S(2)}, u32[]{:S(2)}) %collective-permute-start.3) | collective-permute-done | bytes 163872 | tf_op jit(solution)/shard_map/ppermute | solution.py:421
  20.7 0.0 copy-done
  20.7 5.9 %forward_rest.1 = (bf16[64,6144]{1,0:T(8,128)(2,1)S(1)}, bf16[9,48,64,128]{3,2,1,0:T(8,128)(2,1)S(1)}, bf16[27,42,16,128]{3,2,1,0:T(8,128)(2,1)S(1)}, bf16[9,48,64,128]{3,2,1,0:T(8,128)(2,1)S(1)}) custom-call(bf16[64,1280]{1,0:T(8,128)(2,1)S(1)} %collective-permute-done.3.ends, ...), custom_call_target="tpu_custom_call", output_to_operand_aliasing={{3}: (1, {}), {2}: (3, {})} | custom-call | flops 1019215872 | bytes 1048576 | tf_op jit(solution)/shard_map/forward_rest/pallas_call | solution.py:40
  26.6 4.7 %grad_weight.1 = (f32[864,128]{1,0:T(8,128)S(1)}, bf16[864,128]{1,0:T(8,128)(2,1)S(1)}, bf16[27,42,16,128]{3,2,1,0:T(8,128)(2,1)S(1)}, bf16[9,48,64,128]{3,2,1,0:T(8,128)(2,1)S(1)}) custom-call(s32[1]{0:T(128)} %bitcast.brick.refs_0_, s32[1]{0:T(128)} %bitcast.1.chan.refs_1_, s32[1]{0:T(128)} %bitcast.2.rep.refs_2_, ...), custom_call_target="tpu_custom_call", output_to_operand_aliasing={{2}: (4, {}), {3}: (5, {})} | custom-call | flops 2038431744 | bytes 1048576 | tf_op jit(solution)/shard_map/grad_weight/pallas_call | solution.py:40
  31.3 0.1 collective-permute-start.4
  31.4 1.1 %grad_features_0.1 = (f32[64,3072]{1,0:T(8,128)S(1)}, bf16[64,3072]{1,0:T(8,128)(2,1)S(1)}) custom-call(f32[864,128]{1,0:T(8,128)S(1)} %get-tuple-element.57.refs_0_.refs_4_, bf16[128,1792]{1,0:T(8,128)(2,1)S(1)} %get-tuple-element.58.refs_1_, bf16[27,42,16,128]{3,2,1,0:T(8,128)(2,1)S(1)} %get-tuple-element.59.refs_2_, ...), custom_call_target="tpu_custom_call" | custom-call | flops 679477248 | bytes 1048576 | tf_op jit(solution)/shard_map/grad_features_0/pallas_call | solution.py:40
  32.5 0.3 collective-permute-done.4.refs_5_
  32.9 1.9 %collective-permute-start.5 = (bf16[432,128]{1,0:T(8,128)(2,1)S(1)}, bf16[432,128]{1,0:T(8,128)(2,1)S(1)}, u32[]{:S(2)}, u32[]{:S(2)}) collective-permute-start(bf16[432,128]{1,0:T(8,128)(2,1)S(1)} %get-tuple-element.66), channel_id=1, source_target_pairs={{0,4},{4,0},{8,12},{12,8},{1,5},{5,1},{9,13},{13,9},{2,6},{6,2},{1... | collective-permute-start | bytes 331784 | tf_op jit(solution)/shard_map/ppermute | solution.py:556
  34.8 1.1 %grad_features_1.1 = (f32[64,3072]{1,0:T(8,128)S(1)}, bf16[64,3072]{1,0:T(8,128)(2,1)S(1)}) custom-call(f32[432,128]{1,0:T(8,128)S(1)} %get-tuple-element.63.refs_0_.refs_1_, bf16[128,1792]{1,0:T(8,128)(2,1)S(1)} %get-tuple-element.58.refs_1_, bf16[27,42,16,128]{3,2,1,0:T(8,128)(2,1)S(1)} %get-tuple-element.59.refs_2_, ...), custom_call_target="tpu_custom_call", output_to_operand_aliasing={{0}: (4, {}), {1}: (5, {})} | custom-call | flops 679477248 | bytes 1048576 | tf_op jit(solution)/shard_map/grad_features_1/pallas_call | solution.py:40
  35.9 1.6 %collective-permute-start.7 = (bf16[64,3072]{1,0:T(8,128)(2,1)S(1)}, bf16[64,3072]{1,0:T(8,128)(2,1)S(1)}, u32[]{:S(2)}, u32[]{:S(2)}) collective-permute-start(bf16[64,3072]{1,0:T(8,128)(2,1)S(1)} %get-tuple-element.71), channel_id=1, source_target_pairs={{0,2},{2,0},{1,3},{3,1},{4,6},{6,4},{5,7},{7,5},{8,10},{10,8},{9,1... | collective-permute-start | bytes 1179656 | tf_op jit(solution)/shard_map/ppermute | solution.py:538
  37.5 0.7 %collective-permute-done.5.refs_2_ = bf16[432,128]{1,0:T(8,128)(2,1)S(1)} collective-permute-done((bf16[432,128]{1,0:T(8,128)(2,1)S(1)}, bf16[432,128]{1,0:T(8,128)(2,1)S(1)}, u32[]{:S(2)}, u32[]{:S(2)}) %collective-permute-start.5) | collective-permute-done | bytes 110624 | tf_op jit(solution)/shard_map/ppermute | solution.py:556
  38.2 2.8 %collective-permute-start.6 = (bf16[432,128]{1,0:T(8,128)(2,1)S(1)}, bf16[432,128]{1,0:T(8,128)(2,1)S(1)}, u32[]{:S(2)}, u32[]{:S(2)}) collective-permute-start(bf16[432,128]{1,0:T(8,128)(2,1)S(1)} %merge_1.1.refs_0_.refs_1_), channel_id=1, source_target_pairs={{0,8},{4,12},{8,0},{12,4},{1,9},{5,13},{9,1},{13,5},{2,10},{6,14},... | collective-permute-start | bytes 331784 | tf_op jit(solution)/shard_map/ppermute | solution.py:574
  41.0 1.1 %grad_features_2.1 = (f32[64,1536]{1,0:T(8,128)S(1)}, bf16[64,1536]{1,0:T(8,128)(2,1)S(1)}) custom-call(bf16[432,128]{1,0:T(8,128)(2,1)S(1)} %merge_1.1.refs_0_.refs_1_, bf16[128,1792]{1,0:T(8,128)(2,1)S(1)} %get-tuple-element.58.refs_1_, bf16[27,42,16,128]{3,2,1,0:T(8,128)(2,1)S(1)} %get-tuple-element.59.refs_2_, ...), custom_call_target="tpu_custom_call" | custom-call | flops 679477248 | bytes 1048576 | tf_op jit(solution)/shard_map/grad_features_2/pallas_call | solution.py:40
  42.2 1.6 %collective-permute-start.8 = (bf16[64,1536]{1,0:T(8,128)(2,1)S(1)}, bf16[64,1536]{1,0:T(8,128)(2,1)S(1)}, u32[]{:S(2)}, u32[]{:S(2)}) collective-permute-start(bf16[64,1536]{1,0:T(8,128)(2,1)S(1)} %get-tuple-element.73), channel_id=1, source_target_pairs={{0,2},{2,0},{1,3},{3,1},{4,6},{6,4},{5,7},{7,5},{8,10},{10,8},{9,1... | collective-permute-start | bytes 589832 | tf_op jit(solution)/shard_map/ppermute | solution.py:538
  43.7 0.9 %emit.1 = (bf16[64,4608]{1,0:T(8,128)(2,1)}, f32[8,128]{1,0:T(8,128)S(1)}) custom-call(f32[64,1536]{1,0:T(8,128)S(1)} %get-tuple-element.67.refs_0_.own, bf16[64,6144]{1,0:T(8,128)(2,1)S(1)} %get-tuple-element.68.refs_1_), custom_call_target="tpu_custom_call" | custom-call | bytes 1048576 | tf_op jit(solution)/shard_map/emit/pallas_call | solution.py:40
  44.6 1.4 %collective-permute-done.6.refs_2_ = bf16[432,128]{1,0:T(8,128)(2,1)S(1)} collective-permute-done((bf16[432,128]{1,0:T(8,128)(2,1)S(1)}, bf16[432,128]{1,0:T(8,128)(2,1)S(1)}, u32[]{:S(2)}, u32[]{:S(2)}) %collective-permute-start.6) | collective-permute-done | bytes 110624 | tf_op jit(solution)/shard_map/ppermute | solution.py:574
  46.0 0.8 %collective-permute-start.9 = (bf16[432,128]{1,0:T(8,128)(2,1)S(1)}, bf16[432,128]{1,0:T(8,128)(2,1)S(1)}, u32[]{:S(2)}, u32[]{:S(2)}) collective-permute-start(bf16[432,128]{1,0:T(8,128)(2,1)S(1)} %merge_4.1.done.refs_5_), channel_id=1, source_target_pairs={{0,4},{4,0},{8,12},{12,8},{1,5},{5,1},{9,13},{13,9},{2,6},{6,2},{1... | collective-permute-start | bytes 331784 | tf_op jit(solution)/shard_map/ppermute | solution.py:583
  46.8 1.2 %collective-permute-done.7.rest_0_ = bf16[64,3072]{1,0:T(8,128)(2,1)S(1)} collective-permute-done((bf16[64,3072]{1,0:T(8,128)(2,1)S(1)}, bf16[64,3072]{1,0:T(8,128)(2,1)S(1)}, u32[]{:S(2)}, u32[]{:S(2)}) %collective-permute-start.7) | collective-permute-done | bytes 393248 | tf_op jit(solution)/shard_map/ppermute | solution.py:538
  48.0 0.1 add_0.1
  48.1 3.0 %collective-permute-done.8.rest_0_.refs_4_ = bf16[64,1536]{1,0:T(8,128)(2,1)S(1)} collective-permute-done((bf16[64,1536]{1,0:T(8,128)(2,1)S(1)}, bf16[64,1536]{1,0:T(8,128)(2,1)S(1)}, u32[]{:S(2)}, u32[]{:S(2)}) %collective-permute-start.8) | collective-permute-done | bytes 196640 | tf_op jit(solution)/shard_map/ppermute | solution.py:538
  51.1 0.0 collective-permute-done.9.refs_6_
  51.1 0.1 collective-permute-start.10
  51.2 0.9 %add_1.1 = (bf16[64,4608]{1,0:T(8,128)(2,1)}, f32[8,128]{1,0:T(8,128)S(1)}) custom-call(bf16[64,3072]{1,0:T(8,128)(2,1)S(1)} %get-tuple-element.72.done, bf16[64,4608]{1,0:T(8,128)(2,1)S(1)} %copy-done, f32[64,1536]{1,0:T(8,128)S(1)} %get-tuple-element.67.refs_0_.own, bf16[64,1536]{1,0:T(8,128)(2,1)S(1)} %collective-permute-done.8.rest_0_.refs_4_), custom_call_target="tpu_custom_call" | custom-call | bytes 1048576 | tf_op jit(solution)/shard_map/add_1/pallas_call | solution.py:40
  52.1 0.6 %collective-permute-done.10.refs_5_ = bf16[864,128]{1,0:T(8,128)(2,1)S(1)} collective-permute-done((bf16[864,128]{1,0:T(8,128)(2,1)S(1)}, bf16[864,128]{1,0:T(8,128)(2,1)S(1)}, u32[]{:S(2)}, u32[]{:S(2)}) %collective-permute-start.10) | collective-permute-done | bytes 221216 | tf_op jit(solution)/shard_map/ppermute | solution.py:598
  52.7 1.1 %join.1 = f32[1728,128]{1,0:T(8,128)} custom-call(s32[1]{0:T(128)} %bitcast.brick.refs_0_, s32[1]{0:T(128)} %bitcast.1.chan.refs_1_, s32[1]{0:T(128)} %bitcast.2.rep.refs_2_, f32[8,128]{1,0:T(8,128)S(1)} %get-tuple-element.75.refs_3_, bf16[864,128]{1,0:T(8,128)(2,1)S(1)} %gather.1.refs_4_, bf16[864,128]{1,0:T(8,128)(2,1)S(1)} %collective-permute-done.10.refs_5_), custom_call_target="tpu_custom_call" | custom-call | flops 1200000000 | bytes 1048576 | tf_op jit(solution)/shard_map/join/pallas_call | solution.py:40
  (4 shorter events, 0.1 us)
Async XLA Ops:
  0.6 17.4 %collective-permute-start = (bf16[64,4608]{1,0:T(8,128)(2,1)}, bf16[64,4608]{1,0:T(8,128)(2,1)S(1)}, u32[]{:S(2)}, u32[]{:S(2)}) collective-permute-start(bf16[64,4608]{1,0:T(8,128)(2,1)} %features.3), channel_id=1, source_target_pairs={{2,0},{0,2},{3,1},{1,3},{6,4},{4,6},{7,5},{5,7},{10,8},{8,10},{11,... | collective-permute-start | bytes 1769480 | tf_op jit(solution)/shard_map/ppermute | solution.py:421
  4.7 4.3 %collective-permute-start.1 = (bf16[128,768]{1,0:T(8,128)(2,1)S(1)}, bf16[128,768]{1,0:T(8,128)(2,1)S(1)}, u32[]{:S(2)}, u32[]{:S(2)}) collective-permute-start(bf16[128,768]{1,0:T(8,128)(2,1)S(1)} %get-tuple-element.41), channel_id=1, source_target_pairs={{0,1},{1,0},{2,3},{3,2},{4,5},{5,4},{6,7},{7,6},{8,9},{9,8},{10,11... | collective-permute-start | bytes 589832 | tf_op jit(solution)/shard_map/ppermute | solution.py:441
  4.8 4.2 %collective-permute-start.2 = (bf16[128,768]{1,0:T(8,128)(2,1)S(1)}, bf16[128,768]{1,0:T(8,128)(2,1)S(1)}, u32[]{:S(2)}, u32[]{:S(2)}) collective-permute-start(bf16[128,768]{1,0:T(8,128)(2,1)S(1)} %get-tuple-element.42), channel_id=1, source_target_pairs={{1,4},{4,1},{5,8},{8,5},{9,12},{12,9},{3,6},{6,3},{7,10},{10,7},{1... | collective-permute-start | bytes 589832 | tf_op jit(solution)/shard_map/ppermute | solution.py:407
  9.1 11.6 %collective-permute-start.3 = (bf16[64,1280]{1,0:T(8,128)(2,1)S(1)}, bf16[64,1280]{1,0:T(8,128)(2,1)S(1)}, u32[]{:S(2)}, u32[]{:S(2)}) collective-permute-start(bf16[64,1280]{1,0:T(8,128)(2,1)S(1)} %get-tuple-element.49), channel_id=1, source_target_pairs={{2,0},{0,2},{3,1},{1,3},{6,4},{4,6},{7,5},{5,7},{10,8},{8,10},{11,... | collective-permute-start | bytes 491528 | tf_op jit(solution)/shard_map/ppermute | solution.py:421
  9.2 11.5 %copy-start = (bf16[64,4608]{1,0:T(8,128)(2,1)S(1)}, bf16[64,4608]{1,0:T(8,128)(2,1)}, u32[]{:S(2)}) copy-start(bf16[64,4608]{1,0:T(8,128)(2,1)} %cotangent.7) | copy-start | bytes 1769476
  31.3 1.5 %collective-permute-start.4 = (bf16[864,128]{1,0:T(8,128)(2,1)S(1)}, bf16[864,128]{1,0:T(8,128)(2,1)S(1)}, u32[]{:S(2)}, u32[]{:S(2)}) collective-permute-start(bf16[864,128]{1,0:T(8,128)(2,1)S(1)} %get-tuple-element.62), channel_id=1, source_target_pairs={{0,1},{1,0},{2,3},{3,2},{4,5},{5,4},{6,7},{7,6},{8,9},{9,8},{10,11... | collective-permute-start | bytes 663560 | tf_op jit(solution)/shard_map/ppermute | solution.py:518
  32.9 5.3 %collective-permute-start.5 = (bf16[432,128]{1,0:T(8,128)(2,1)S(1)}, bf16[432,128]{1,0:T(8,128)(2,1)S(1)}, u32[]{:S(2)}, u32[]{:S(2)}) collective-permute-start(bf16[432,128]{1,0:T(8,128)(2,1)S(1)} %get-tuple-element.66), channel_id=1, source_target_pairs={{0,4},{4,0},{8,12},{12,8},{1,5},{5,1},{9,13},{13,9},{2,6},{6,2},{1... | collective-permute-start | bytes 331784 | tf_op jit(solution)/shard_map/ppermute | solution.py:556
  35.9 12.1 %collective-permute-start.7 = (bf16[64,3072]{1,0:T(8,128)(2,1)S(1)}, bf16[64,3072]{1,0:T(8,128)(2,1)S(1)}, u32[]{:S(2)}, u32[]{:S(2)}) collective-permute-start(bf16[64,3072]{1,0:T(8,128)(2,1)S(1)} %get-tuple-element.71), channel_id=1, source_target_pairs={{0,2},{2,0},{1,3},{3,1},{4,6},{6,4},{5,7},{7,5},{8,10},{10,8},{9,1... | collective-permute-start | bytes 1179656 | tf_op jit(solution)/shard_map/ppermute | solution.py:538
  38.2 7.8 %collective-permute-start.6 = (bf16[432,128]{1,0:T(8,128)(2,1)S(1)}, bf16[432,128]{1,0:T(8,128)(2,1)S(1)}, u32[]{:S(2)}, u32[]{:S(2)}) collective-permute-start(bf16[432,128]{1,0:T(8,128)(2,1)S(1)} %merge_1.1.refs_0_.refs_1_), channel_id=1, source_target_pairs={{0,8},{4,12},{8,0},{12,4},{1,9},{5,13},{9,1},{13,5},{2,10},{6,14},... | collective-permute-start | bytes 331784 | tf_op jit(solution)/shard_map/ppermute | solution.py:574
  42.2 8.9 %collective-permute-start.8 = (bf16[64,1536]{1,0:T(8,128)(2,1)S(1)}, bf16[64,1536]{1,0:T(8,128)(2,1)S(1)}, u32[]{:S(2)}, u32[]{:S(2)}) collective-permute-start(bf16[64,1536]{1,0:T(8,128)(2,1)S(1)} %get-tuple-element.73), channel_id=1, source_target_pairs={{0,2},{2,0},{1,3},{3,1},{4,6},{6,4},{5,7},{7,5},{8,10},{10,8},{9,1... | collective-permute-start | bytes 589832 | tf_op jit(solution)/shard_map/ppermute | solution.py:538
  46.0 5.1 %collective-permute-start.9 = (bf16[432,128]{1,0:T(8,128)(2,1)S(1)}, bf16[432,128]{1,0:T(8,128)(2,1)S(1)}, u32[]{:S(2)}, u32[]{:S(2)}) collective-permute-start(bf16[432,128]{1,0:T(8,128)(2,1)S(1)} %merge_4.1.done.refs_5_), channel_id=1, source_target_pairs={{0,4},{4,0},{8,12},{12,8},{1,5},{5,1},{9,13},{13,9},{2,6},{6,2},{1... | collective-permute-start | bytes 331784 | tf_op jit(solution)/shard_map/ppermute | solution.py:583
  51.1 1.5 %collective-permute-start.10 = (bf16[864,128]{1,0:T(8,128)(2,1)S(1)}, bf16[864,128]{1,0:T(8,128)(2,1)S(1)}, u32[]{:S(2)}, u32[]{:S(2)}) collective-permute-start(bf16[864,128]{1,0:T(8,128)(2,1)S(1)} %gather.1.refs_4_), channel_id=1, source_target_pairs={{0,1},{1,0},{2,3},{3,2},{4,5},{5,4},{6,7},{7,6},{8,9},{9,8},{10,11... | collective-permute-start | bytes 663560 | tf_op jit(solution)/shard_map/ppermute | solution.py:598

commit v15 on v14

--- a/solution.py
+++ b/solution.py
@@ -315,22 +315,20 @@
     del valid_in, grads_in
     share, sites = grads.shape[2], across.shape[0]
     halo, lead = HALO // LANES, LEAD // LANES
-    total[...] = jnp.zeros_like(total)
-
-    def block(j, carry):
+    if total.shape[0] > TAPS * share:
+        total[...] = jnp.zeros_like(total)
+
+    for j in range(sites // (DEEP * LANES)):
         start = j * DEEP + halo
-        here = pl.ds(pl.multiple_of(j * DEEP * LANES, LANES), DEEP * LANES)
+        here = pl.ds(j * DEEP * LANES, DEEP * LANES)
         features = across[here, :]
         for group in groups(MANY):
             rows = []
             for tap in group:
                 rows += masked(grads, valid, TAPS - 1 - tap, start + lead, start, DEEP)
-            total[group[0] * share : (group[-1] + 1) * share, :] += jnp.dot(
-                jnp.concatenate(rows, axis=0), features, preferred_element_type=F32
-            )
-        return carry
-
-    lax.fori_loop(0, sites // (DEEP * LANES), block, 0)
+            part = jnp.dot(jnp.concatenate(rows, axis=0), features, preferred_element_type=F32)
+            here = slice(group[0] * share, (group[-1] + 1) * share)
+            total[here, :] = part if j == 0 else total[here, :] + part
     mine = rep[0]
     kept[...] = total[pl.ds(pl.multiple_of(mine * half, ROWS), half), :]
     sent[...] = total[pl.ds(pl.multiple_of((1 - mine) * half, ROWS), half), :].astype(BF16)

time: 54 us -> 53.7 us (level)
  transfers between devices with their start and end apart: 11 -> 11, of which waited for: 8 -> 8; matrix products, arithmetic and copies ran while one was open for 0% -> 0% of each run, Pallas kernels for 31% -> 32%
where the time goes in v15:
time: 53.7 us; the launch traced here: 53.6 us
  Pallas kernels  28.4 us (53%)
  starting transfers between devices  12.6 us (23%)
  waiting for transfers between devices  11.7 us (22%)
  between operations  0.77 us (1%)
    pallas_call x18, Pallas kernels, kernel(): pl.pallas_call(body, out_shape=outs, in_specs=[SCALAR] * len(scalars) + [...  28.4 us
    ppermute x2, waiting for transfers between devices, around(): lax.ppermute(x, 'chan', [((i + over) % chans, i) for i in range(chans)])  4.55 us
    ppermute x2, waiting for transfers between devices, terms_of(): lax.ppermute(other if left == share else other[(over - 1) * share:over *...  4.17 us
    ppermute x2, starting transfers between devices, terms_of(): lax.ppermute(other if left == share else other[(over - 1) * share:over *...  3.11 us
    ppermute x2, starting transfers between devices, around(): lax.ppermute(x, 'chan', [((i + over) % chans, i) for i in range(chans)])  3.1 us
    ppermute x1, starting transfers between devices, local(): other = lax.ppermute(mine, 'brick', [(i, i ^ step) for i in range(bricks)])  2.82 us
    ppermute x1, starting transfers between devices, local(): arrived = lax.ppermute(sent, 'brick', pairs)  1.89 us
    ppermute x1, waiting for transfers between devices, local(): other = lax.ppermute(mine, 'brick', [(i, i ^ step) for i in range(bricks)])  1.41 us
  transfers between devices with their start and end apart: 11, of which 8 were waited for; matrix products, arithmetic and copies ran while one was open for 0% of the time, Pallas kernels for 32%

profile of v15, /device:TPU:0, one launch (start us, length us, event | category | flops | bytes accessed | tf_op | source)
XLA Modules:
  0.0 53.6 jit_solution(6494957939928603481)
XLA Ops:
  0.6 3.0 %collective-permute-start = (bf16[64,4608]{1,0:T(8,128)(2,1)}, bf16[64,4608]{1,0:T(8,128)(2,1)S(1)}, u32[]{:S(2)}, u32[]{:S(2)}) collective-permute-start(bf16[64,4608]{1,0:T(8,128)(2,1)} %features.3), channel_id=1, source_target_pairs={{2,0},{0,2},{3,1},{1,3},{6,4},{4,6},{7,5},{5,7},{10,8},{8,10},{11,... | collective-permute-start | bytes 1769480 | tf_op jit(solution)/shard_map/ppermute | solution.py:419
  3.6 1.1 %pack.1 = (bf16[128,768]{1,0:T(8,128)(2,1)S(1)}, bf16[128,768]{1,0:T(8,128)(2,1)S(1)}) custom-call(s32[1]{0:T(128)} %bitcast.brick.refs_0_, s32[1]{0:T(128)} %bitcast.1.chan.refs_1_, s32[1]{0:T(128)} %bitcast.2.rep.refs_2_, bf16[64,4608]{1,0:T(8,128)(2,1)} %features.3, bf16[64,4608]{1,0:T(8,128)(2,1)} %cotangent.7, s32[27,4608]{1,0:T(8,128)} %neighbours.3), custom_call_target="tpu_custom_call" | custom-call | bytes 1048576 | tf_op jit(solution)/shard_map/pack/pallas_call | solution.py:40
  4.7 0.1 collective-permute-start.1
  4.8 0.7 %collective-permute-start.2 = (bf16[128,768]{1,0:T(8,128)(2,1)S(1)}, bf16[128,768]{1,0:T(8,128)(2,1)S(1)}, u32[]{:S(2)}, u32[]{:S(2)}) collective-permute-start(bf16[128,768]{1,0:T(8,128)(2,1)S(1)} %get-tuple-element.42), channel_id=1, source_target_pairs={{1,4},{4,1},{5,8},{8,5},{9,12},{12,9},{3,6},{6,3},{7,10},{10,7},{1... | collective-permute-start | bytes 589832 | tf_op jit(solution)/shard_map/ppermute | solution.py:405
  5.5 3.5 %prepare.1 = (bf16[64,1728]{1,0:T(8,128)(2,1)S(1)}, bf16[64,1728]{1,0:T(8,128)(2,1)S(1)}, bf16[128,1792]{1,0:T(8,128)(2,1)S(1)}, bf16[9,48,64,128]{3,2,1,0:T(8,128)(2,1)S(1)}, bf16[27,42,16,128]{3,2,1,0:T(8,128)(2,1)S(1)}) custom-call(s32[1]{0:T(128)} %bitcast.brick.refs_0_, s32[1]{0:T(128)} %bitcast.1.chan.refs_1_, s32[1]{0:T(128)} %bitcast.2.rep.refs_2_, ...), custom_call_target="tpu_custom_call" | custom-call | bytes 1048576 | tf_op jit(solution)/shard_map/prepare/pallas_call | solution.py:40
  9.0 0.0 collective-permute-done.1.refs_4_
  9.0 0.0 collective-permute-done.2.refs_5_
  9.0 0.2 ends.1
  9.2 0.1 collective-permute-start.3
  9.3 0.0 copy-start
  9.3 4.8 %forward_own.1 = (f32[64,5376]{1,0:T(8,128)S(1)}, bf16[9,48,64,128]{3,2,1,0:T(8,128)(2,1)S(1)}, bf16[27,42,16,128]{3,2,1,0:T(8,128)(2,1)S(1)}) custom-call(bf16[128,768]{1,0:T(8,128)(2,1)S(1)} %get-tuple-element.43.left, bf16[128,768]{1,0:T(8,128)(2,1)S(1)} %get-tuple-element.44.right, ...), custom_call_target="tpu_custom_call", output_to_operand_aliasing={{1}: (3, {}), {2}: (4, {})} | custom-call | bytes 1048576 | tf_op jit(solution)/shard_map/forward_own/pallas_call | solution.py:40
  14.1 3.9 %collective-permute-done.rest = bf16[64,4608]{1,0:T(8,128)(2,1)S(1)} collective-permute-done((bf16[64,4608]{1,0:T(8,128)(2,1)}, bf16[64,4608]{1,0:T(8,128)(2,1)S(1)}, u32[]{:S(2)}, u32[]{:S(2)}) %collective-permute-start) | collective-permute-done | bytes 589856 | tf_op jit(solution)/shard_map/ppermute | solution.py:419
  18.0 2.0 %arrive.1 = (bf16[9,48,64,128]{3,2,1,0:T(8,128)(2,1)S(1)}, bf16[4608,128]{1,0:T(8,128)(2,1)S(1)}, bf16[9,48,64,128]{3,2,1,0:T(8,128)(2,1)S(1)}) custom-call(bf16[64,4608]{1,0:T(8,128)(2,1)S(1)} %collective-permute-done.rest, bf16[9,48,64,128]{3,2,1,0:T(8,128)(2,1)S(1)} %get-tuple-element.47.own_in), custom_call_target="tpu_custom_call", output_to_operand_aliasing={{2}: (1, {})} | custom-call | bytes 1048576 | tf_op jit(solution)/shard_map/arrive/pallas_call | solution.py:40
  20.0 0.7 %collective-permute-done.3.ends = bf16[64,1280]{1,0:T(8,128)(2,1)S(1)} collective-permute-done((bf16[64,1280]{1,0:T(8,128)(2,1)S(1)}, bf16[64,1280]{1,0:T(8,128)(2,1)S(1)}, u32[]{:S(2)}, u32[]{:S(2)}) %collective-permute-start.3) | collective-permute-done | bytes 163872 | tf_op jit(solution)/shard_map/ppermute | solution.py:419
  20.7 0.0 copy-done
  20.7 5.9 %forward_rest.1 = (bf16[64,6144]{1,0:T(8,128)(2,1)S(1)}, bf16[9,48,64,128]{3,2,1,0:T(8,128)(2,1)S(1)}, bf16[27,42,16,128]{3,2,1,0:T(8,128)(2,1)S(1)}, bf16[9,48,64,128]{3,2,1,0:T(8,128)(2,1)S(1)}) custom-call(bf16[64,1280]{1,0:T(8,128)(2,1)S(1)} %collective-permute-done.3.ends, ...), custom_call_target="tpu_custom_call", output_to_operand_aliasing={{3}: (1, {}), {2}: (3, {})} | custom-call | flops 1019215872 | bytes 1048576 | tf_op jit(solution)/shard_map/forward_rest/pallas_call | solution.py:40
  26.6 4.4 %grad_weight.1 = (f32[864,128]{1,0:T(8,128)S(1)}, bf16[864,128]{1,0:T(8,128)(2,1)S(1)}, bf16[27,42,16,128]{3,2,1,0:T(8,128)(2,1)S(1)}, bf16[9,48,64,128]{3,2,1,0:T(8,128)(2,1)S(1)}) custom-call(s32[1]{0:T(128)} %bitcast.brick.refs_0_, s32[1]{0:T(128)} %bitcast.1.chan.refs_1_, s32[1]{0:T(128)} %bitcast.2.rep.refs_2_, ...), custom_call_target="tpu_custom_call", output_to_operand_aliasing={{2}: (4, {}), {3}: (5, {})} | custom-call | flops 2038431744 | bytes 1048576 | tf_op jit(solution)/shard_map/grad_weight/pallas_call | solution.py:40
  31.0 0.1 collective-permute-start.4
  31.1 1.1 %grad_features_0.1 = (f32[64,3072]{1,0:T(8,128)S(1)}, bf16[64,3072]{1,0:T(8,128)(2,1)S(1)}) custom-call(f32[864,128]{1,0:T(8,128)S(1)} %get-tuple-element.57.refs_0_.refs_4_, bf16[128,1792]{1,0:T(8,128)(2,1)S(1)} %get-tuple-element.58.refs_1_, bf16[27,42,16,128]{3,2,1,0:T(8,128)(2,1)S(1)} %get-tuple-element.59.refs_2_, ...), custom_call_target="tpu_custom_call" | custom-call | flops 679477248 | bytes 1048576 | tf_op jit(solution)/shard_map/grad_features_0/pallas_call | solution.py:40
  32.2 0.3 collective-permute-done.4.refs_5_
  32.6 1.9 %collective-permute-start.5 = (bf16[432,128]{1,0:T(8,128)(2,1)S(1)}, bf16[432,128]{1,0:T(8,128)(2,1)S(1)}, u32[]{:S(2)}, u32[]{:S(2)}) collective-permute-start(bf16[432,128]{1,0:T(8,128)(2,1)S(1)} %get-tuple-element.66), channel_id=1, source_target_pairs={{0,4},{4,0},{8,12},{12,8},{1,5},{5,1},{9,13},{13,9},{2,6},{6,2},{1... | collective-permute-start | bytes 331784 | tf_op jit(solution)/shard_map/ppermute | solution.py:554
  34.5 1.1 %grad_features_1.1 = (f32[64,3072]{1,0:T(8,128)S(1)}, bf16[64,3072]{1,0:T(8,128)(2,1)S(1)}) custom-call(f32[432,128]{1,0:T(8,128)S(1)} %get-tuple-element.63.refs_0_.refs_1_, bf16[128,1792]{1,0:T(8,128)(2,1)S(1)} %get-tuple-element.58.refs_1_, bf16[27,42,16,128]{3,2,1,0:T(8,128)(2,1)S(1)} %get-tuple-element.59.refs_2_, ...), custom_call_target="tpu_custom_call", output_to_operand_aliasing={{0}: (4, {}), {1}: (5, {})} | custom-call | flops 679477248 | bytes 1048576 | tf_op jit(solution)/shard_map/grad_features_1/pallas_call | solution.py:40
  35.6 1.6 %collective-permute-start.7 = (bf16[64,3072]{1,0:T(8,128)(2,1)S(1)}, bf16[64,3072]{1,0:T(8,128)(2,1)S(1)}, u32[]{:S(2)}, u32[]{:S(2)}) collective-permute-start(bf16[64,3072]{1,0:T(8,128)(2,1)S(1)} %get-tuple-element.71), channel_id=1, source_target_pairs={{0,2},{2,0},{1,3},{3,1},{4,6},{6,4},{5,7},{7,5},{8,10},{10,8},{9,1... | collective-permute-start | bytes 1179656 | tf_op jit(solution)/shard_map/ppermute | solution.py:536
  37.2 0.7 %collective-permute-done.5.refs_2_ = bf16[432,128]{1,0:T(8,128)(2,1)S(1)} collective-permute-done((bf16[432,128]{1,0:T(8,128)(2,1)S(1)}, bf16[432,128]{1,0:T(8,128)(2,1)S(1)}, u32[]{:S(2)}, u32[]{:S(2)}) %collective-permute-start.5) | collective-permute-done | bytes 110624 | tf_op jit(solution)/shard_map/ppermute | solution.py:554
  37.9 2.8 %collective-permute-start.6 = (bf16[432,128]{1,0:T(8,128)(2,1)S(1)}, bf16[432,128]{1,0:T(8,128)(2,1)S(1)}, u32[]{:S(2)}, u32[]{:S(2)}) collective-permute-start(bf16[432,128]{1,0:T(8,128)(2,1)S(1)} %merge_1.1.refs_0_.refs_1_), channel_id=1, source_target_pairs={{0,8},{4,12},{8,0},{12,4},{1,9},{5,13},{9,1},{13,5},{2,10},{6,14},... | collective-permute-start | bytes 331784 | tf_op jit(solution)/shard_map/ppermute | solution.py:572
  40.8 1.1 %grad_features_2.1 = (f32[64,1536]{1,0:T(8,128)S(1)}, bf16[64,1536]{1,0:T(8,128)(2,1)S(1)}) custom-call(bf16[432,128]{1,0:T(8,128)(2,1)S(1)} %merge_1.1.refs_0_.refs_1_, bf16[128,1792]{1,0:T(8,128)(2,1)S(1)} %get-tuple-element.58.refs_1_, bf16[27,42,16,128]{3,2,1,0:T(8,128)(2,1)S(1)} %get-tuple-element.59.refs_2_, ...), custom_call_target="tpu_custom_call" | custom-call | flops 679477248 | bytes 1048576 | tf_op jit(solution)/shard_map/grad_features_2/pallas_call | solution.py:40
  41.9 1.6 %collective-permute-start.8 = (bf16[64,1536]{1,0:T(8,128)(2,1)S(1)}, bf16[64,1536]{1,0:T(8,128)(2,1)S(1)}, u32[]{:S(2)}, u32[]{:S(2)}) collective-permute-start(bf16[64,1536]{1,0:T(8,128)(2,1)S(1)} %get-tuple-element.73), channel_id=1, source_target_pairs={{0,2},{2,0},{1,3},{3,1},{4,6},{6,4},{5,7},{7,5},{8,10},{10,8},{9,1... | collective-permute-start | bytes 589832 | tf_op jit(solution)/shard_map/ppermute | solution.py:536
  43.5 0.9 %emit.1 = (bf16[64,4608]{1,0:T(8,128)(2,1)}, f32[8,128]{1,0:T(8,128)S(1)}) custom-call(f32[64,1536]{1,0:T(8,128)S(1)} %get-tuple-element.67.refs_0_.own, bf16[64,6144]{1,0:T(8,128)(2,1)S(1)} %get-tuple-element.68.refs_1_), custom_call_target="tpu_custom_call" | custom-call | bytes 1048576 | tf_op jit(solution)/shard_map/emit/pallas_call | solution.py:40
  44.3 1.4 %collective-permute-done.6.refs_2_ = bf16[432,128]{1,0:T(8,128)(2,1)S(1)} collective-permute-done((bf16[432,128]{1,0:T(8,128)(2,1)S(1)}, bf16[432,128]{1,0:T(8,128)(2,1)S(1)}, u32[]{:S(2)}, u32[]{:S(2)}) %collective-permute-start.6) | collective-permute-done | bytes 110624 | tf_op jit(solution)/shard_map/ppermute | solution.py:572
  45.8 0.8 %collective-permute-start.9 = (bf16[432,128]{1,0:T(8,128)(2,1)S(1)}, bf16[432,128]{1,0:T(8,128)(2,1)S(1)}, u32[]{:S(2)}, u32[]{:S(2)}) collective-permute-start(bf16[432,128]{1,0:T(8,128)(2,1)S(1)} %merge_4.1.done.refs_5_), channel_id=1, source_target_pairs={{0,4},{4,0},{8,12},{12,8},{1,5},{5,1},{9,13},{13,9},{2,6},{6,2},{1... | collective-permute-start | bytes 331784 | tf_op jit(solution)/shard_map/ppermute | solution.py:581
  46.5 1.2 %collective-permute-done.7.rest_0_ = bf16[64,3072]{1,0:T(8,128)(2,1)S(1)} collective-permute-done((bf16[64,3072]{1,0:T(8,128)(2,1)S(1)}, bf16[64,3072]{1,0:T(8,128)(2,1)S(1)}, u32[]{:S(2)}, u32[]{:S(2)}) %collective-permute-start.7) | collective-permute-done | bytes 393248 | tf_op jit(solution)/shard_map/ppermute | solution.py:536
  47.7 0.1 add_0.1
  47.8 3.0 %collective-permute-done.8.rest_0_.refs_4_ = bf16[64,1536]{1,0:T(8,128)(2,1)S(1)} collective-permute-done((bf16[64,1536]{1,0:T(8,128)(2,1)S(1)}, bf16[64,1536]{1,0:T(8,128)(2,1)S(1)}, u32[]{:S(2)}, u32[]{:S(2)}) %collective-permute-start.8) | collective-permute-done | bytes 196640 | tf_op jit(solution)/shard_map/ppermute | solution.py:536
  50.9 0.0 collective-permute-done.9.refs_6_
  50.9 0.1 collective-permute-start.10
  51.0 0.9 %add_1.1 = (bf16[64,4608]{1,0:T(8,128)(2,1)}, f32[8,128]{1,0:T(8,128)S(1)}) custom-call(bf16[64,3072]{1,0:T(8,128)(2,1)S(1)} %get-tuple-element.72.done, bf16[64,4608]{1,0:T(8,128)(2,1)S(1)} %copy-done, f32[64,1536]{1,0:T(8,128)S(1)} %get-tuple-element.67.refs_0_.own, bf16[64,1536]{1,0:T(8,128)(2,1)S(1)} %collective-permute-done.8.rest_0_.refs_4_), custom_call_target="tpu_custom_call" | custom-call | bytes 1048576 | tf_op jit(solution)/shard_map/add_1/pallas_call | solution.py:40
  51.9 0.6 %collective-permute-done.10.refs_5_ = bf16[864,128]{1,0:T(8,128)(2,1)S(1)} collective-permute-done((bf16[864,128]{1,0:T(8,128)(2,1)S(1)}, bf16[864,128]{1,0:T(8,128)(2,1)S(1)}, u32[]{:S(2)}, u32[]{:S(2)}) %collective-permute-start.10) | collective-permute-done | bytes 221216 | tf_op jit(solution)/shard_map/ppermute | solution.py:596
  52.4 1.1 %join.1 = f32[1728,128]{1,0:T(8,128)} custom-call(s32[1]{0:T(128)} %bitcast.brick.refs_0_, s32[1]{0:T(128)} %bitcast.1.chan.refs_1_, s32[1]{0:T(128)} %bitcast.2.rep.refs_2_, f32[8,128]{1,0:T(8,128)S(1)} %get-tuple-element.75.refs_3_, bf16[864,128]{1,0:T(8,128)(2,1)S(1)} %gather.1.refs_4_, bf16[864,128]{1,0:T(8,128)(2,1)S(1)} %collective-permute-done.10.refs_5_), custom_call_target="tpu_custom_call" | custom-call | flops 1200000000 | bytes 1048576 | tf_op jit(solution)/shard_map/join/pallas_call | solution.py:40
  (4 shorter events, 0.1 us)
Async XLA Ops:
  0.6 17.4 %collective-permute-start = (bf16[64,4608]{1,0:T(8,128)(2,1)}, bf16[64,4608]{1,0:T(8,128)(2,1)S(1)}, u32[]{:S(2)}, u32[]{:S(2)}) collective-permute-start(bf16[64,4608]{1,0:T(8,128)(2,1)} %features.3), channel_id=1, source_target_pairs={{2,0},{0,2},{3,1},{1,3},{6,4},{4,6},{7,5},{5,7},{10,8},{8,10},{11,... | collective-permute-start | bytes 1769480 | tf_op jit(solution)/shard_map/ppermute | solution.py:419
  4.7 4.3 %collective-permute-start.1 = (bf16[128,768]{1,0:T(8,128)(2,1)S(1)}, bf16[128,768]{1,0:T(8,128)(2,1)S(1)}, u32[]{:S(2)}, u32[]{:S(2)}) collective-permute-start(bf16[128,768]{1,0:T(8,128)(2,1)S(1)} %get-tuple-element.41), channel_id=1, source_target_pairs={{0,1},{1,0},{2,3},{3,2},{4,5},{5,4},{6,7},{7,6},{8,9},{9,8},{10,11... | collective-permute-start | bytes 589832 | tf_op jit(solution)/shard_map/ppermute | solution.py:439
  4.8 4.2 %collective-permute-start.2 = (bf16[128,768]{1,0:T(8,128)(2,1)S(1)}, bf16[128,768]{1,0:T(8,128)(2,1)S(1)}, u32[]{:S(2)}, u32[]{:S(2)}) collective-permute-start(bf16[128,768]{1,0:T(8,128)(2,1)S(1)} %get-tuple-element.42), channel_id=1, source_target_pairs={{1,4},{4,1},{5,8},{8,5},{9,12},{12,9},{3,6},{6,3},{7,10},{10,7},{1... | collective-permute-start | bytes 589832 | tf_op jit(solution)/shard_map/ppermute | solution.py:405
  9.2 11.4 %collective-permute-start.3 = (bf16[64,1280]{1,0:T(8,128)(2,1)S(1)}, bf16[64,1280]{1,0:T(8,128)(2,1)S(1)}, u32[]{:S(2)}, u32[]{:S(2)}) collective-permute-start(bf16[64,1280]{1,0:T(8,128)(2,1)S(1)} %get-tuple-element.49), channel_id=1, source_target_pairs={{2,0},{0,2},{3,1},{1,3},{6,4},{4,6},{7,5},{5,7},{10,8},{8,10},{11,... | collective-permute-start | bytes 491528 | tf_op jit(solution)/shard_map/ppermute | solution.py:419
  9.3 11.3 %copy-start = (bf16[64,4608]{1,0:T(8,128)(2,1)S(1)}, bf16[64,4608]{1,0:T(8,128)(2,1)}, u32[]{:S(2)}) copy-start(bf16[64,4608]{1,0:T(8,128)(2,1)} %cotangent.7) | copy-start | bytes 1769476
  31.0 1.5 %collective-permute-start.4 = (bf16[864,128]{1,0:T(8,128)(2,1)S(1)}, bf16[864,128]{1,0:T(8,128)(2,1)S(1)}, u32[]{:S(2)}, u32[]{:S(2)}) collective-permute-start(bf16[864,128]{1,0:T(8,128)(2,1)S(1)} %get-tuple-element.62), channel_id=1, source_target_pairs={{0,1},{1,0},{2,3},{3,2},{4,5},{5,4},{6,7},{7,6},{8,9},{9,8},{10,11... | collective-permute-start | bytes 663560 | tf_op jit(solution)/shard_map/ppermute | solution.py:516
  32.6 5.3 %collective-permute-start.5 = (bf16[432,128]{1,0:T(8,128)(2,1)S(1)}, bf16[432,128]{1,0:T(8,128)(2,1)S(1)}, u32[]{:S(2)}, u32[]{:S(2)}) collective-permute-start(bf16[432,128]{1,0:T(8,128)(2,1)S(1)} %get-tuple-element.66), channel_id=1, source_target_pairs={{0,4},{4,0},{8,12},{12,8},{1,5},{5,1},{9,13},{13,9},{2,6},{6,2},{1... | collective-permute-start | bytes 331784 | tf_op jit(solution)/shard_map/ppermute | solution.py:554
  35.6 12.1 %collective-permute-start.7 = (bf16[64,3072]{1,0:T(8,128)(2,1)S(1)}, bf16[64,3072]{1,0:T(8,128)(2,1)S(1)}, u32[]{:S(2)}, u32[]{:S(2)}) collective-permute-start(bf16[64,3072]{1,0:T(8,128)(2,1)S(1)} %get-tuple-element.71), channel_id=1, source_target_pairs={{0,2},{2,0},{1,3},{3,1},{4,6},{6,4},{5,7},{7,5},{8,10},{10,8},{9,1... | collective-permute-start | bytes 1179656 | tf_op jit(solution)/shard_map/ppermute | solution.py:536
  37.9 7.8 %collective-permute-start.6 = (bf16[432,128]{1,0:T(8,128)(2,1)S(1)}, bf16[432,128]{1,0:T(8,128)(2,1)S(1)}, u32[]{:S(2)}, u32[]{:S(2)}) collective-permute-start(bf16[432,128]{1,0:T(8,128)(2,1)S(1)} %merge_1.1.refs_0_.refs_1_), channel_id=1, source_target_pairs={{0,8},{4,12},{8,0},{12,4},{1,9},{5,13},{9,1},{13,5},{2,10},{6,14},... | collective-permute-start | bytes 331784 | tf_op jit(solution)/shard_map/ppermute | solution.py:572
  41.9 8.9 %collective-permute-start.8 = (bf16[64,1536]{1,0:T(8,128)(2,1)S(1)}, bf16[64,1536]{1,0:T(8,128)(2,1)S(1)}, u32[]{:S(2)}, u32[]{:S(2)}) collective-permute-start(bf16[64,1536]{1,0:T(8,128)(2,1)S(1)} %get-tuple-element.73), channel_id=1, source_target_pairs={{0,2},{2,0},{1,3},{3,1},{4,6},{6,4},{5,7},{7,5},{8,10},{10,8},{9,1... | collective-permute-start | bytes 589832 | tf_op jit(solution)/shard_map/ppermute | solution.py:536
  45.8 5.1 %collective-permute-start.9 = (bf16[432,128]{1,0:T(8,128)(2,1)S(1)}, bf16[432,128]{1,0:T(8,128)(2,1)S(1)}, u32[]{:S(2)}, u32[]{:S(2)}) collective-permute-start(bf16[432,128]{1,0:T(8,128)(2,1)S(1)} %merge_4.1.done.refs_5_), channel_id=1, source_target_pairs={{0,4},{4,0},{8,12},{12,8},{1,5},{5,1},{9,13},{13,9},{2,6},{6,2},{1... | collective-permute-start | bytes 331784 | tf_op jit(solution)/shard_map/ppermute | solution.py:581
  50.9 1.5 %collective-permute-start.10 = (bf16[864,128]{1,0:T(8,128)(2,1)S(1)}, bf16[864,128]{1,0:T(8,128)(2,1)S(1)}, u32[]{:S(2)}, u32[]{:S(2)}) collective-permute-start(bf16[864,128]{1,0:T(8,128)(2,1)S(1)} %gather.1.refs_4_), channel_id=1, source_target_pairs={{0,1},{1,0},{2,3},{3,2},{4,5},{5,4},{6,7},{7,6},{8,9},{9,8},{10,11... | collective-permute-start | bytes 663560 | tf_op jit(solution)/shard_map/ppermute | solution.py:596
